TPU v7x, 32 devices: a whole 2x2x4 slice. The times are simulated.
32 devices in a mesh: fsdp: 16 (over z, y, core), tp: 2 (over x).
Axes of the slice: x: 2, y: 2, z: 4, core: 2. Of those that a mesh axis runs over, the one named last changes fastest.
Arguments:
- inputs: bfloat16 [32768, 1024], P(('fsdp', 'tp')), may hold values from -6 to 6
- segments: int32 [32768], P('fsdp'), may hold values from 0 to 512, as said below
- teacher: bfloat16 [32768, 1024], P('fsdp', 'tp'), may hold values from -6 to 6
- first_norm_gain: float32 [1024], P(('fsdp', 'tp')), may hold values from 0.5 to 1.5
- first_norm_bias: float32 [1024], P(('fsdp', 'tp')), may hold values from -1 to 1
- time_decay: float32 [1024], P(('fsdp', 'tp')), may hold values from -6.5 to -2
- time_first: float32 [1024], P(('fsdp', 'tp')), may hold values from -1 to 1
- time_mix_key: float32 [1024], P(('fsdp', 'tp')), may hold values from 0.1 to 0.9
- time_mix_value: float32 [1024], P(('fsdp', 'tp')), may hold values from 0.1 to 0.9
- time_mix_recept: float32 [1024], P(('fsdp', 'tp')), may hold values from 0.1 to 0.9
- time_key: bfloat16 [1024, 1024], P('fsdp', 'tp'), may hold values from -0.1875 to 0.1875
- time_value: bfloat16 [1024, 1024], P('fsdp', 'tp'), may hold values from -0.1875 to 0.1875
- time_recept: bfloat16 [1024, 1024], P('fsdp', 'tp'), may hold values from -0.1875 to 0.1875
- time_output: bfloat16 [1024, 1024], P('tp', 'fsdp'), may hold values from -0.75 to 0.75
- second_norm_gain: float32 [1024], P(('fsdp', 'tp')), may hold values from 0.5 to 1.5
- second_norm_bias: float32 [1024], P(('fsdp', 'tp')), may hold values from -1 to 1
- channel_mix_key: float32 [1024], P(('fsdp', 'tp')), may hold values from 0.1 to 0.9
- channel_mix_recept: float32 [1024], P(('fsdp', 'tp')), may hold values from 0.1 to 0.9
- channel_key: bfloat16 [1024, 4096], P('fsdp', 'tp'), may hold values from -0.1875 to 0.1875
- channel_recept: bfloat16 [1024, 1024], P('fsdp', 'tp'), may hold values from -0.1875 to 0.1875
- channel_value: bfloat16 [4096, 1024], P('tp', 'fsdp'), may hold values from -0.09375 to 0.09375
Outputs:
- outputs: bfloat16 [32768, 1024], P('fsdp', 'tp')
- loss: float32 [], replicated
- input_grad: float32 [32768, 1024], P(('fsdp', 'tp'))
- first_norm_gain_grad: float32 [1024], P(('fsdp', 'tp'))
- first_norm_bias_grad: float32 [1024], P(('fsdp', 'tp'))
- time_decay_grad: float32 [1024], P(('fsdp', 'tp'))
- time_first_grad: float32 [1024], P(('fsdp', 'tp'))
- time_mix_key_grad: float32 [1024], P(('fsdp', 'tp'))
- time_mix_value_grad: float32 [1024], P(('fsdp', 'tp'))
- time_mix_recept_grad: float32 [1024], P(('fsdp', 'tp'))
- time_key_grad: float32 [1024, 1024], P('fsdp', 'tp')
- time_value_grad: float32 [1024, 1024], P('fsdp', 'tp')
- time_recept_grad: float32 [1024, 1024], P('fsdp', 'tp')
- time_output_grad: float32 [1024, 1024], P('tp', 'fsdp')
- second_norm_gain_grad: float32 [1024], P(('fsdp', 'tp'))
- second_norm_bias_grad: float32 [1024], P(('fsdp', 'tp'))
- channel_mix_key_grad: float32 [1024], P(('fsdp', 'tp'))
- channel_mix_recept_grad: float32 [1024], P(('fsdp', 'tp'))
- channel_key_grad: float32 [1024, 4096], P('fsdp', 'tp')
- channel_recept_grad: float32 [1024, 1024], P('fsdp', 'tp')
- channel_value_grad: float32 [4096, 1024], P('tp', 'fsdp')
Inputs may be any that keep to these rules, and one draw needn't show every extreme that they name: `segments`: within each sequence of 1024 tokens the document numbers start at 1 on its first token, never fall, never exceed 1024 // 2, and end in a run of 1 to 512 padding tokens (0).
All inputs are finite; a program needn't handle non-finite values.
Results may differ from a plain program's by a relative error of at most 0.009.
Values may be sent and summed in bfloat16 or wider, within the bound.
No kernel may reach another device: no remote copies, remote signals or barrier semaphores. Data moves between devices by JAX's collectives and lax.ppermute only.
A program may use at most 320 MiB of HBM per device.

v0:
```python
import math

import jax
import jax.numpy as jnp
from jax import lax
from jax.sharding import PartitionSpec as P

SEQ_LEN = 1024


EPSILON = 1e-05


def shift_down(values, persist_filter):
    moved = jnp.concatenate([jnp.zeros_like(values[:1]), values[:-1]], axis=0)
    return moved * persist_filter[:, None]


def shift_up(values, persist_filter):
    masked = values * persist_filter[:, None]
    return jnp.concatenate([masked[1:], jnp.zeros_like(masked[:1])], axis=0)


def norm_forward(values, gain, bias):
    centre = values - jnp.mean(values, axis=-1, keepdims=True)
    scaled = lax.rsqrt(jnp.mean(centre * centre, axis=-1, keepdims=True) + EPSILON)
    unit_rows = centre * scaled
    return (unit_rows * gain + bias, unit_rows, scaled)


def norm_backward(grad_rows, unit_rows, scaled, gain):
    weighted = grad_rows * gain
    return scaled * (
        weighted
        - jnp.mean(weighted, axis=-1, keepdims=True)
        - unit_rows * jnp.mean(weighted * unit_rows, axis=-1, keepdims=True)
    )


def blend(normed, behind, mix_rate):
    return normed * mix_rate + behind * (1.0 - mix_rate)


def mix_back(normed, behind, persist_filter, grad_pairs):
    differ = normed - behind
    direct = jnp.zeros_like(normed)
    lagged = jnp.zeros_like(normed)
    mix_grads = []
    for grad_part, mix_part in grad_pairs:
        direct = direct + grad_part * mix_part
        lagged = lagged + grad_part * (1.0 - mix_part)
        mix_grads.append(jnp.sum(differ * grad_part, axis=0))
    return (direct + shift_up(lagged, persist_filter), mix_grads)


def doubled(values):
    return jnp.concatenate([values, values], axis=-1)


def wkv_tables(persist_filter, attenuation_multiplier):
    total_rows = persist_filter.shape[0]
    span_len = math.gcd(64, total_rows)
    block_count = total_rows // span_len
    decay_speed = jnp.exp(attenuation_multiplier)
    offsets = jnp.arange(span_len, dtype=jnp.float32)[:, None]
    growth = jnp.exp(offsets * decay_speed[None, :])
    fading = jnp.exp(-offsets * decay_speed[None, :])
    fading_rev = jnp.exp(-(span_len - 1.0 - offsets) * decay_speed[None, :])
    retain = jnp.exp(-decay_speed)
    breaks_seen = jnp.cumsum(1.0 - persist_filter.reshape(block_count, span_len), axis=1)
    order_idx = jnp.arange(span_len, dtype=jnp.int32)
    strictly = order_idx[:, None] > order_idx[None, :]
    links_mat = ((breaks_seen[:, :, None] == breaks_seen[:, None, :]) & strictly[None]).astype(
        jnp.float32
    )
    fresh_rows = (breaks_seen == 0.0).astype(jnp.float32)
    tail_rows = (breaks_seen == breaks_seen[:, -1:]).astype(jnp.float32)
    reach_all = fresh_rows[:, -1:] * jnp.exp(-span_len * decay_speed)[None, :]
    return (
        span_len,
        block_count,
        decay_speed,
        retain,
        growth,
        fading,
        fading_rev,
        links_mat,
        fresh_rows,
        tail_rows,
        reach_all,
    )


def attention_recurrence_evaluate(lookup_mapped, content_mapped, reward_tempo, reference_arrays):
    (
        span_len,
        block_count,
        decay_speed,
        retain,
        growth,
        fading,
        fading_rev,
        links_mat,
        fresh_rows,
        tail_rows,
        reach_all,
    ) = reference_arrays
    total_rows, width = lookup_mapped.shape
    lookup_array = jnp.exp(lookup_mapped)
    source = jnp.concatenate([lookup_array * content_mapped, lookup_array], axis=1).reshape(
        block_count, span_len, 2 * width
    )
    scaled_src = source * doubled(growth)[None]
    inner_part = (
        jnp.einsum("nts,nsc->ntc", links_mat, scaled_src, precision=lax.Precision.HIGHEST)
        * doubled(fading / retain[None, :])[None]
    )
    end_states = jnp.einsum(
        "ns,nsc->nc", tail_rows, scaled_src, precision=lax.Precision.HIGHEST
    ) * doubled(fading[-1:])

    def pass_on(state, item):
        reach_one, end_one = item
        return (reach_one * state + end_one, state)

    _, entering = lax.scan(
        pass_on, jnp.zeros((2 * width,), jnp.float32), (doubled(reach_all), end_states)
    )
    prior_part = inner_part + fresh_rows[:, :, None] * doubled(fading)[None] * entering[:, None, :]
    prior_part = prior_part.reshape(total_rows, 2 * width)
    prior_memory_alpha = prior_part[:, :width]
    prior_memory_beta = prior_part[:, width:]
    reward_array = jnp.exp(reward_tempo[None, :] + lookup_mapped)
    normalizer_sum = prior_memory_beta + reward_array
    attention_recurrence_result = (
        prior_memory_alpha + reward_array * content_mapped
    ) / normalizer_sum
    return (
        attention_recurrence_result,
        (prior_memory_alpha, prior_memory_beta, normalizer_sum, reward_array, lookup_array),
    )


def weighted_kv_backward(
    grad_wkv, attention_recurrence_result, content_mapped, stored_residuals, reference_arrays
):
    (
        span_len,
        block_count,
        decay_speed,
        retain,
        growth,
        fading,
        fading_rev,
        links_mat,
        fresh_rows,
        tail_rows,
        reach_all,
    ) = reference_arrays
    prior_memory_alpha, prior_memory_beta, normalizer_sum, reward_array, lookup_array = (
        stored_residuals
    )
    total_rows, width = content_mapped.shape
    slope_multiplied = grad_wkv / normalizer_sum
    source = jnp.concatenate(
        [slope_multiplied, -slope_multiplied * attention_recurrence_result], axis=1
    ).reshape(block_count, span_len, 2 * width)
    scaled_src = source * doubled(fading)[None]
    inner_part = (
        jnp.einsum("nut,nuc->ntc", links_mat, scaled_src, precision=lax.Precision.HIGHEST)
        * doubled(growth / retain[None, :])[None]
    )
    start_sums = jnp.einsum("nu,nuc->nc", fresh_rows, scaled_src, precision=lax.Precision.HIGHEST)

    def pass_back(state, item):
        start_one, reach_one = item
        return (start_one + reach_one * state, state)

    _, leaving = lax.scan(
        pass_back,
        jnp.zeros((2 * width,), jnp.float32),
        (start_sums, doubled(reach_all)),
        reverse=True,
    )
    later_part = (
        inner_part + tail_rows[:, :, None] * doubled(fading_rev)[None] * leaving[:, None, :]
    )
    later_part = later_part.reshape(total_rows, 2 * width)
    memory_slope_alpha = later_part[:, :width]
    memory_slope_beta = later_part[:, width:]
    reward_summand = (
        reward_array * slope_multiplied * (content_mapped - attention_recurrence_result)
    )
    lookup_slope = (
        lookup_array * (memory_slope_alpha * content_mapped + memory_slope_beta) + reward_summand
    )
    content_slope = lookup_array * memory_slope_alpha + reward_array * slope_multiplied
    reward_slope = jnp.sum(reward_summand, axis=0)
    attenuation_slope = (
        -retain
        * decay_speed
        * jnp.sum(
            memory_slope_alpha * prior_memory_alpha + memory_slope_beta * prior_memory_beta, axis=0
        )
    )
    return (lookup_slope, content_slope, attenuation_slope, reward_slope)


def matmul(left, right):
    return jnp.dot(left, right, preferred_element_type=jnp.float32)


def inner_left(left, right):
    return lax.dot_general(
        left, right, (((0,), (0,)), ((), ())), preferred_element_type=jnp.float32
    )


def inner_right(left, right):
    return lax.dot_general(
        left, right, (((1,), (1,)), ((), ())), preferred_element_type=jnp.float32
    )


def on_device(
    inputs,
    segments,
    teacher,
    first_norm_gain,
    first_norm_bias,
    time_decay,
    time_first,
    time_mix_key,
    time_mix_value,
    time_mix_recept,
    time_key,
    time_value,
    time_recept,
    time_output,
    second_norm_gain,
    second_norm_bias,
    channel_mix_key,
    channel_mix_recept,
    channel_key,
    channel_recept,
    channel_value,
):
    group_rows = segments.shape[0]
    local_rows = inputs.shape[0]
    model_width = inputs.shape[1]
    half_columns = time_key.shape[1]
    tp_index = lax.axis_index("tp")
    feedfwd_start_index = tp_index * half_columns
    row_start = tp_index * local_rows
    positions = jnp.arange(group_rows, dtype=jnp.int32) % SEQ_LEN
    previous_ids = jnp.concatenate([jnp.zeros((1,), jnp.int32), segments[:-1]])
    persist_filter = ((segments == previous_ids) & (segments > 0) & (positions > 0)).astype(
        jnp.float32
    )
    valid_rows = (segments > 0).astype(jnp.float32)
    own_count = jnp.sum(lax.dynamic_slice_in_dim(valid_rows, row_start, local_rows)).reshape(1)
    whole_vectors = (
        lax.all_gather(first_norm_gain, ("fsdp", "tp"), axis=0, tiled=True),
        lax.all_gather(first_norm_bias, ("fsdp", "tp"), axis=0, tiled=True),
        lax.all_gather(time_decay, ("fsdp", "tp"), axis=0, tiled=True),
        lax.all_gather(time_first, ("fsdp", "tp"), axis=0, tiled=True),
        lax.all_gather(time_mix_key, ("fsdp", "tp"), axis=0, tiled=True),
        lax.all_gather(time_mix_value, ("fsdp", "tp"), axis=0, tiled=True),
        lax.all_gather(time_mix_recept, ("fsdp", "tp"), axis=0, tiled=True),
        lax.all_gather(second_norm_gain, ("fsdp", "tp"), axis=0, tiled=True),
        lax.all_gather(second_norm_bias, ("fsdp", "tp"), axis=0, tiled=True),
        lax.all_gather(channel_mix_key, ("fsdp", "tp"), axis=0, tiled=True),
        lax.all_gather(channel_mix_recept, ("fsdp", "tp"), axis=0, tiled=True),
        lax.all_gather(own_count, ("fsdp", "tp"), axis=0, tiled=True),
    )
    (
        initial_standardize_gain,
        initial_standardize_shift,
        decay_full,
        reward_entire,
        initial_lookup_mixing,
        initial_content_mixing,
        initial_gating_mixing,
        latter_standardize_gain,
        latter_standardize_shift,
        latter_lookup_mixing,
        latter_gating_mixing,
        count_pieces,
    ) = whole_vectors
    count = jnp.sum(count_pieces)
    decay_mine = lax.dynamic_slice_in_dim(decay_full, feedfwd_start_index, half_columns)
    reward_device = lax.dynamic_slice_in_dim(reward_entire, feedfwd_start_index, half_columns)
    time_mats = (
        lax.all_gather(time_key, "fsdp", axis=0, tiled=True),
        lax.all_gather(time_value, "fsdp", axis=0, tiled=True),
        lax.all_gather(time_recept, "fsdp", axis=0, tiled=True),
        lax.all_gather(time_output, "fsdp", axis=1, tiled=True),
    )
    key_full, value_full, recept_full, output_full = time_mats
    whole_inputs = lax.all_gather(inputs, "tp", axis=0, tiled=True)
    residual = whole_inputs.astype(jnp.float32)
    normed_one, unit_one, scale_one = norm_forward(
        residual, initial_standardize_gain, initial_standardize_shift
    )
    behind_one = shift_down(normed_one, persist_filter)
    mixed_key = blend(normed_one, behind_one, initial_lookup_mixing).astype(jnp.bfloat16)
    mixed_value = blend(normed_one, behind_one, initial_content_mixing).astype(jnp.bfloat16)
    mixed_recept = blend(normed_one, behind_one, initial_gating_mixing).astype(jnp.bfloat16)
    lookup_mapped = matmul(mixed_key, key_full)
    content_mapped = matmul(mixed_value, value_full)
    recept_gate = jax.nn.sigmoid(matmul(mixed_recept, recept_full))
    reference_arrays = wkv_tables(persist_filter, decay_mine)
    attention_recurrence_result, weighted_kv_stored = attention_recurrence_evaluate(
        lookup_mapped, content_mapped, reward_device, reference_arrays
    )
    gated = (recept_gate * attention_recurrence_result).astype(jnp.bfloat16)
    time_part = matmul(gated, output_full)
    time_total = lax.psum(time_part, "tp")
    middle = residual + time_total
    chan_mats = (
        lax.all_gather(channel_key, "fsdp", axis=0, tiled=True),
        lax.all_gather(channel_recept, "fsdp", axis=0, tiled=True),
        lax.all_gather(channel_value, "fsdp", axis=1, tiled=True),
    )
    chan_key_full, chan_recept_full, chan_value_full = chan_mats
    normed_two, unit_two, scale_two = norm_forward(
        middle, latter_standardize_gain, latter_standardize_shift
    )
    behind_two = shift_down(normed_two, persist_filter)
    mixed_key_two = blend(normed_two, behind_two, latter_lookup_mixing).astype(jnp.bfloat16)
    mixed_recept_two = blend(normed_two, behind_two, latter_gating_mixing).astype(jnp.bfloat16)
    active = jnp.maximum(matmul(mixed_key_two, chan_key_full), 0.0)
    hidden = (active * active).astype(jnp.bfloat16)
    value_part = matmul(hidden, chan_value_full)
    value_mine = lax.psum_scatter(
        value_part.astype(jnp.bfloat16), "tp", scatter_dimension=1, tiled=True
    ).astype(jnp.float32)
    recept_two = jax.nn.sigmoid(matmul(mixed_recept_two, chan_recept_full))
    middle_mine = lax.dynamic_slice_in_dim(middle, feedfwd_start_index, half_columns, axis=1)
    result = middle_mine + recept_two * value_mine
    outputs = result.astype(jnp.bfloat16)
    error = (result - teacher.astype(jnp.float32)) * valid_rows[:, None]
    loss_part = jnp.sum(error * error)
    total_rows = group_rows * lax.axis_size("fsdp")
    grad_result = error * (total_rows / count)
    content_slope = (grad_result * recept_two).astype(jnp.bfloat16)
    grad_recept_two = (grad_result * value_mine * recept_two * (1.0 - recept_two)).astype(
        jnp.bfloat16
    )
    chan_key_back, chan_recept_back, chan_value_back = (
        lax.all_gather(channel_key, "fsdp", axis=0, tiled=True),
        lax.all_gather(channel_recept, "fsdp", axis=0, tiled=True),
        lax.all_gather(channel_value, "fsdp", axis=1, tiled=True),
    )
    key_back, value_back, recept_back, output_back = (
        lax.all_gather(time_key, "fsdp", axis=0, tiled=True),
        lax.all_gather(time_value, "fsdp", axis=0, tiled=True),
        lax.all_gather(time_recept, "fsdp", axis=0, tiled=True),
        lax.all_gather(time_output, "fsdp", axis=1, tiled=True),
    )
    grad_value_full = lax.all_gather(content_slope, "tp", axis=1, tiled=True)
    grad_chan_value = inner_left(hidden, grad_value_full)
    grad_hidden = inner_right(grad_value_full, chan_value_back)
    grad_key_two = (2.0 * active * grad_hidden).astype(jnp.bfloat16)
    grad_chan_key = inner_left(mixed_key_two, grad_key_two)
    grad_chan_recept = inner_left(mixed_recept_two, grad_recept_two)
    chan_grads = (
        lax.psum_scatter(grad_chan_key, "fsdp", scatter_dimension=0, tiled=True),
        lax.psum_scatter(grad_chan_recept, "fsdp", scatter_dimension=0, tiled=True),
        lax.psum_scatter(grad_chan_value, "fsdp", scatter_dimension=1, tiled=True),
    )
    grad_mixed_key_two = inner_right(grad_key_two, chan_key_back)
    grad_mixed_recept_two = inner_right(grad_recept_two, chan_recept_back)
    grad_normed_two, chan_mix_grads = mix_back(
        normed_two,
        behind_two,
        persist_filter,
        ((grad_mixed_key_two, latter_lookup_mixing), (grad_mixed_recept_two, latter_gating_mixing)),
    )
    grad_gain_two = jnp.sum(grad_normed_two * unit_two, axis=0)
    grad_bias_two = jnp.sum(grad_normed_two, axis=0)
    grad_middle_part = norm_backward(grad_normed_two, unit_two, scale_two, latter_standardize_gain)
    grad_middle_part = grad_middle_part + lax.dynamic_update_slice_in_dim(
        jnp.zeros_like(grad_middle_part), grad_result, feedfwd_start_index, 1
    )
    grad_middle = lax.psum(grad_middle_part.astype(jnp.bfloat16), "tp").astype(jnp.float32)
    grad_time = grad_middle.astype(jnp.bfloat16)
    grad_output_w = inner_left(gated, grad_time)
    grad_gated = inner_right(grad_time, output_back)
    grad_recept_pre = (
        grad_gated * attention_recurrence_result * recept_gate * (1.0 - recept_gate)
    ).astype(jnp.bfloat16)
    grad_wkv = grad_gated * recept_gate
    lookup_mapped_slope, content_mapped_slope, attenuation_slope_device, reward_slope_device = (
        weighted_kv_backward(
            grad_wkv,
            attention_recurrence_result,
            content_mapped,
            weighted_kv_stored,
            reference_arrays,
        )
    )
    grad_key_low = lookup_mapped_slope.astype(jnp.bfloat16)
    grad_value_low = content_mapped_slope.astype(jnp.bfloat16)
    grad_time_key = inner_left(mixed_key, grad_key_low)
    grad_time_value = inner_left(mixed_value, grad_value_low)
    grad_time_recept = inner_left(mixed_recept, grad_recept_pre)
    time_grads = (
        lax.psum_scatter(grad_time_key, "fsdp", scatter_dimension=0, tiled=True),
        lax.psum_scatter(grad_time_value, "fsdp", scatter_dimension=0, tiled=True),
        lax.psum_scatter(grad_time_recept, "fsdp", scatter_dimension=0, tiled=True),
        lax.psum_scatter(grad_output_w, "fsdp", scatter_dimension=1, tiled=True),
    )
    grad_mixed_key = inner_right(grad_key_low, key_back)
    grad_mixed_value = inner_right(grad_value_low, value_back)
    grad_mixed_recept = inner_right(grad_recept_pre, recept_back)
    grad_normed_one, time_mix_grads = mix_back(
        normed_one,
        behind_one,
        persist_filter,
        (
            (grad_mixed_key, initial_lookup_mixing),
            (grad_mixed_value, initial_content_mixing),
            (grad_mixed_recept, initial_gating_mixing),
        ),
    )
    grad_gain_one = jnp.sum(grad_normed_one * unit_one, axis=0)
    grad_bias_one = jnp.sum(grad_normed_one, axis=0)
    input_part = norm_backward(grad_normed_one, unit_one, scale_one, initial_standardize_gain)
    input_back = lax.psum_scatter(
        input_part.astype(jnp.bfloat16), "tp", scatter_dimension=0, tiled=True
    ).astype(jnp.float32)
    input_grad = lax.dynamic_slice_in_dim(grad_middle, row_start, local_rows, 0) + input_back
    blank_columns = jnp.zeros((model_width,), jnp.float32)
    grad_decay_full = lax.dynamic_update_slice_in_dim(
        blank_columns, attenuation_slope_device, feedfwd_start_index, 0
    )
    reward_slope_entire = lax.dynamic_update_slice_in_dim(
        blank_columns, reward_slope_device, feedfwd_start_index, 0
    )
    stacked = jnp.stack(
        [
            grad_gain_one,
            grad_bias_one,
            grad_decay_full,
            reward_slope_entire,
            time_mix_grads[0],
            time_mix_grads[1],
            time_mix_grads[2],
            grad_gain_two,
            grad_bias_two,
            chan_mix_grads[0],
            chan_mix_grads[1],
        ]
    )
    loss_total, vector_total = lax.psum((loss_part, stacked), ("fsdp", "tp"))
    loss = loss_total / (2.0 * count * model_width)
    piece_width = first_norm_gain.shape[0]
    flat_index = lax.axis_index("fsdp") * lax.axis_size("tp") + tp_index
    vector_mine = lax.dynamic_slice_in_dim(
        vector_total, flat_index * piece_width, piece_width, axis=1
    )
    return (
        outputs,
        loss,
        input_grad,
        vector_mine[0],
        vector_mine[1],
        vector_mine[2],
        vector_mine[3],
        vector_mine[4],
        vector_mine[5],
        vector_mine[6],
        time_grads[0],
        time_grads[1],
        time_grads[2],
        time_grads[3],
        vector_mine[7],
        vector_mine[8],
        vector_mine[9],
        vector_mine[10],
        chan_grads[0],
        chan_grads[1],
        chan_grads[2],
    )


def solution(mesh):
    return jax.shard_map(
        on_device,
        mesh=mesh,
        in_specs=(
            P(("fsdp", "tp"), None),
            P("fsdp"),
            P("fsdp", "tp"),
            P(("fsdp", "tp")),
            P(("fsdp", "tp")),
            P(("fsdp", "tp")),
            P(("fsdp", "tp")),
            P(("fsdp", "tp")),
            P(("fsdp", "tp")),
            P(("fsdp", "tp")),
            P("fsdp", "tp"),
            P("fsdp", "tp"),
            P("fsdp", "tp"),
            P("tp", "fsdp"),
            P(("fsdp", "tp")),
            P(("fsdp", "tp")),
            P(("fsdp", "tp")),
            P(("fsdp", "tp")),
            P("fsdp", "tp"),
            P("fsdp", "tp"),
            P("tp", "fsdp"),
        ),
        out_specs=(
            P("fsdp", "tp"),
            P(),
            P(("fsdp", "tp"), None),
            P(("fsdp", "tp")),
            P(("fsdp", "tp")),
            P(("fsdp", "tp")),
            P(("fsdp", "tp")),
            P(("fsdp", "tp")),
            P(("fsdp", "tp")),
            P(("fsdp", "tp")),
            P("fsdp", "tp"),
            P("fsdp", "tp"),
            P("fsdp", "tp"),
            P("tp", "fsdp"),
            P(("fsdp", "tp")),
            P(("fsdp", "tp")),
            P(("fsdp", "tp")),
            P(("fsdp", "tp")),
            P("fsdp", "tp"),
            P("fsdp", "tp"),
            P("tp", "fsdp"),
        ),
        check_vma=False,
    )
```

profile of v0, /device:TPU:0, one launch (start us, length us, event | category | flops | bytes accessed | tf_op | source)
XLA Modules:
  0.0 1618.2 jit_solution(17226568120817549145)
XLA Ops:
  21.9 43.4 %all-reduce.17 = (f32[1024]{0:T(1024)S(1)}, f32[1024]{0:T(1024)S(1)}, f32[1024]{0:T(1024)S(1)}, f32[1024]{0:T(1024)S(1)}, f32[1024]{0:T(1024)S(1)}, /*index=5*/f...) all-reduce(f32[1024]{0:T(1024)S(1)} %dynamic-update-slice.2, ...), channel_id=1, replica_groups=mesh['fsdp'=16,'tp'=2] {'fsdp','tp'}, use_global_device_ids=true, to_apply=%add.5 | all-reduce | flops 11296 | bytes 90368
  81.4 8.9 add_convert_fusion.2
  90.3 20.3 %all-gather.14.cloned.1.call-done = bf16[1024,512]{1,0:T(8,128)(2,1)} async-done(((bf16[64,512]{1,0:T(8,128)(2,1)}), bf16[1024,512]{1,0:T(8,128)(2,1)}) %all-gather.14.cloned.1.call-update) | async-done | bytes 1048592 | tf_op jit(solution)/shard_map/all_gather | solution.py:294
  110.6 6.9 fusion.67
  117.5 32.2 %all-gather.16.cloned.1.call-done = bf16[1024,512]{1,0:T(8,128)(2,1)} async-done(((bf16[64,512]{1,0:T(8,128)(2,1)}), bf16[1024,512]{1,0:T(8,128)(2,1)}) %all-gather.16.cloned.1.call-update) | async-done | bytes 1048592 | tf_op jit(solution)/shard_map/all_gather | solution.py:295
  149.7 9.8 exponential_multiply_fusion
  174.7 25.4 %multiply_add_fusion.4 = f32[32,64,1024]{2,1,0:T(8,128)} fusion(f32[32,1024]{1,0:T(8,128)S(1)} %get-tuple-element.151, f32[64,1024]{1,0:T(8,128)S(1)} %get-tuple-element.309, f32[32,64]{1,0:T(8,128)S(1)} %get-tuple-element.293, f32[64,1024]{1,0:T(8,128)S(1)} %get-tuple-element.308, f32[32,64,1024]{2,1,0:T(8,128)} %bitcast.118, ...), kind=kOutput, calls=%fused_computation.54 | convolution fusion | flops 1621360640 | bytes 17715200 | tf_op jit(solution)/shard_map/nts,nsc->ntc/dot_general | solution.py:115
  200.2 14.7 multiply_convert_fusion.4
  214.9 12.6 all-gather.18.cloned.1.call-done
  227.5 6.9 fusion.68
  236.6 194.8 %all-reduce.21.cloned.1.call-done = f32[2048,1024]{1,0:T(8,128)} async-done(((f32[2048,1024]{1,0:T(8,128)}), f32[2048,1024]{1,0:T(8,128)}) %all-reduce.21.cloned.1.call-update) | async-done | bytes 8388624 | tf_op jit(solution)/shard_map/psum | solution.py:318
  442.9 6.5 add_convert_fusion
  449.4 35.2 %all-gather.22.cloned.1.call-done = bf16[1024,2048]{1,0:T(8,128)(2,1)} async-done(((bf16[64,2048]{1,0:T(8,128)(2,1)}), bf16[1024,2048]{1,0:T(8,128)(2,1)}) %all-gather.22.cloned.1.call-update) | async-done | bytes 4194320 | tf_op jit(solution)/shard_map/all_gather | solution.py:321
  484.7 15.3 fusion.69
  499.9 36.0 %all-gather.24.cloned.1.call-done = bf16[2048,1024]{0,1:T(8,128)(2,1)} async-done(((bf16[2048,64]{0,1:T(8,128)(2,1)}), bf16[2048,1024]{0,1:T(8,128)(2,1)}) %all-gather.24.cloned.1.call-update) | async-done | bytes 4194320 | tf_op jit(solution)/shard_map/all_gather | solution.py:323
  535.9 15.0 convolution_convert_fusion
  552.3 22.3 %all-gather.20.cloned.1.call-done = bf16[1024,512]{1,0:T(8,128)(2,1)} async-done(((bf16[64,512]{1,0:T(8,128)(2,1)}), bf16[1024,512]{1,0:T(8,128)(2,1)}) %all-gather.20.cloned.1.call-update) | async-done | bytes 1048592 | tf_op jit(solution)/shard_map/all_gather | solution.py:322
  574.6 55.4 %reduce-scatter.10.cloned.1.call-done = bf16[2048,512]{1,0:T(8,128)(2,1)} async-done(((bf16[2048,1024]{1,0:T(8,128)(2,1)}), bf16[2048,512]{1,0:T(8,128)(2,1)}) %reduce-scatter.10.cloned.1.call-update) | async-done | bytes 2097168 | tf_op jit(solution)/shard_map/reduce_scatter | solution.py:335
  629.9 12.0 multiply_convert_fusion.3
  648.7 7.1 fusion.71
  655.8 43.1 %all-gather.26.cloned.1.call-done = bf16[2048,1024]{1,0:T(8,128)(2,1)} async-done(((bf16[2048,512]{1,0:T(8,128)(2,1)}), bf16[2048,1024]{1,0:T(8,128)(2,1)}) %all-gather.26.cloned.1.call-update) | async-done | bytes 4194320 | tf_op jit(solution)/shard_map/all_gather | solution.py:361
  698.9 16.9 %multiply_convert_fusion = bf16[2048,2048]{1,0:T(8,128)(2,1)} fusion(f32[2048,2048]{1,0:T(8,128)} %fusion.69, bf16[2048,1024]{1,0:T(8,128)(2,1)} %all-gather.26.cloned.1.call-done, bf16[2048,1024]{0,1:T(8,128)(2,1)} %all-gather.24.cloned.1.call-done), kind=kOutput, calls=%fused_computation.8 | convolution fusion | flops 8606711808 | bytes 33554432 | tf_op jit(solution)/shard_map/dot_general | solution.py:220
  715.8 14.6 fusion.70
  730.4 6.6 fusion.17
  737.1 13.8 multiply_reduce_fusion.2
  763.3 107.9 %all-reduce.23.cloned.1.call-done = bf16[2048,1024]{1,0:T(8,128)(2,1)} async-done(((bf16[2048,1024]{1,0:T(8,128)(2,1)}), bf16[2048,1024]{1,0:T(8,128)(2,1)}) %all-reduce.23.cloned.1.call-update) | async-done | bytes 4194320 | tf_op jit(solution)/shard_map/psum | solution.py:386
  871.3 15.5 fusion.61
  900.0 29.8 %while.31 = (s32[]{:T(128)}, f32[1024]{0:T(1024)S(1)}, f32[32,1024]{1,0:T(8,128)S(1)}, f32[32,1024]{1,0:T(8,128)S(1)}, f32[32,1024]{1,0:T(8,128)}, /*index=5*/s32[]{:T(128)}, s32[]{:T(128)}, s32[]{:T(128)}) while((s32[]{:T(128)}, f32[1024]{0:T(1024)S(1)}, f32[32,1024]{1,0:T(8,128)S(1)}, f32[32,1024]{1,0:T(8,128)S(1)}, ...), condition=%wide.region_17.18_spmd.clone, body=%wide.region_16.17_spmd.clone.sunk | while | flops 3076 | bytes 45179 | solution.py:179
  929.8 9.1 multiply_add_fusion.2
  939.0 10.3 add_convert_fusion.5
  966.0 9.8 fusion.14
  975.9 28.9 %fusion.11 = (f32[1024]{0:T(1024)S(1)}, f32[2048]{0:T(1024)S(1)}, f32[2048]{0:T(1024)S(1)}, f32[1024]{0:T(1024)S(1)}, f32[1024]{0:T(1024)S(1)}, /*index=5*/f32[1...) fusion(bf16[2048,1024]{1,0:T(8,128)(2,1)} %all-gather.10.cloned.1.call-done, ...), kind=kLoop, calls=%fused_computation.24 | loop fusion | flops 75486208 | bytes 88182784 | tf_op jit(solution)/shard_map/reduce_sum | solution.py:427
  1004.8 7.3 fusion.10
  1012.2 5.9 fusion.80
  1018.2 6.8 fusion.78
  1025.1 5.9 fusion.77
  1031.4 7.0 fusion.76
  1038.4 6.0 fusion.75
  1044.5 15.9 fusion.41
  1060.7 14.8 fusion.79
  1076.3 40.7 %all-reduce.16 = (f32[]{:T(128)}, f32[11,1024]{1,0:T(8,128)S(1)}) all-reduce(f32[]{:T(128)} %get-tuple-element.278, f32[11,1024]{1,0:T(8,128)S(1)} %stack.50), channel_id=1, replica_groups=mesh['fsdp'=16,'tp'=2] {'fsdp','tp'}, use_global_device_ids=true, to_apply=%region_10.11 | all-reduce | flops 11265 | bytes 90120 | tf_op jit(solution)/shard_map/psum | solution.py:456
  1123.5 9.4 reduce-scatter.24.cloned.1.call-done
  1133.0 64.7 %reduce-scatter.20.cloned.1.call-done = f32[512,64]{0,1:T(8,128)} async-done(((f32[512,1024]{0,1:T(8,128)}), f32[512,64]{0,1:T(8,128)}) %reduce-scatter.20.cloned.1.call-update) | async-done | bytes 131088 | tf_op jit(solution)/shard_map/reduce_scatter | solution.py:412
  1197.7 65.2 %reduce-scatter.18.cloned.1.call-done = f32[64,512]{1,0:T(8,128)} async-done(((f32[1024,512]{1,0:T(8,128)}), f32[64,512]{1,0:T(8,128)}) %reduce-scatter.18.cloned.1.call-update) | async-done | bytes 131088 | tf_op jit(solution)/shard_map/reduce_scatter | solution.py:411
  1262.9 64.8 %reduce-scatter.16.cloned.1.call-done = f32[64,512]{1,0:T(8,128)} async-done(((f32[1024,512]{1,0:T(8,128)}), f32[64,512]{1,0:T(8,128)}) %reduce-scatter.16.cloned.1.call-update) | async-done | bytes 131088 | tf_op jit(solution)/shard_map/reduce_scatter | solution.py:410
  1327.7 65.2 %reduce-scatter.14.cloned.1.call-done = f32[64,512]{1,0:T(8,128)} async-done(((f32[1024,512]{1,0:T(8,128)}), f32[64,512]{1,0:T(8,128)}) %reduce-scatter.14.cloned.1.call-update) | async-done | bytes 131088 | tf_op jit(solution)/shard_map/reduce_scatter | solution.py:409
  1392.8 108.3 %reduce-scatter.26.cloned.1.call-done = f32[2048,64]{0,1:T(8,128)} async-done(((f32[2048,1024]{0,1:T(8,128)}), f32[2048,64]{0,1:T(8,128)}) %reduce-scatter.26.cloned.1.call-update) | async-done | bytes 524304 | tf_op jit(solution)/shard_map/reduce_scatter | solution.py:370
  1501.1 108.9 %reduce-scatter.22.cloned.1.call-done = f32[64,2048]{1,0:T(8,128)} async-done(((f32[1024,2048]{1,0:T(8,128)}), f32[64,2048]{1,0:T(8,128)}) %reduce-scatter.22.cloned.1.call-update) | async-done | bytes 524304 | tf_op jit(solution)/shard_map/reduce_scatter | solution.py:368
  (461 shorter events, 148.5 us)
Async XLA Ops:
  7.2 63.3 %all-gather.10.cloned.1.call-start = ((), (), s32[]{:S(2)}) async-start(), calls=%async_computation.9 | async-start | bytes 6291456 | tf_op jit(solution)/shard_map/all_gather | solution.py:300
  7.9 102.7 %all-gather.14.cloned.1.call-start = ((), (), s32[]{:S(2)}) async-start(), calls=%async_computation.11 | async-start | bytes 1114112 | tf_op jit(solution)/shard_map/all_gather | solution.py:294
  8.7 141.0 %all-gather.16.cloned.1.call-start = ((), (), s32[]{:S(2)}) async-start(), calls=%async_computation.12 | async-start | bytes 1114112 | tf_op jit(solution)/shard_map/all_gather | solution.py:295
  9.4 190.7 %all-gather.12.cloned.1.call-start = ((), (), s32[]{:S(2)}) async-start(), calls=%async_computation.10 | async-start | bytes 1114112 | tf_op jit(solution)/shard_map/all_gather | solution.py:296
  10.0 217.5 %all-gather.18.cloned.1.call-start = ((), (), s32[]{:S(2)}) async-start(), calls=%async_computation.13 | async-start | bytes 1114112 | tf_op jit(solution)/shard_map/all_gather | solution.py:297
  10.6 420.9 %all-reduce.21.cloned.1.call-start = ((), (), s32[]{:S(2)}) async-start(), calls=%async_computation.14 | async-start | bytes 16777216 | tf_op jit(solution)/shard_map/psum | solution.py:318
  10.7 164.0 %copy-start.32 = (pred[64,64]{0,1:T(8,128)(4,1)}, pred[64,64]{0,1:T(8,128)(4,1)S(1)}, u32[]{:S(2)}) copy-start(pred[64,64]{0,1:T(8,128)(4,1)S(1)} %iota_compare_fusion) | copy-start | bytes 12292
  65.3 12.8 copy-start.34
  65.3 12.8 copy-start.37
  65.3 12.8 copy-start.39
  65.3 12.8 copy-start.43
  65.3 12.8 copy-start.45
  65.4 374.2 %copy-start.51 = (f32[1024]{0:T(1024)}, f32[1024]{0:T(1024)S(1)}, u32[]{:S(2)}) copy-start(f32[1024]{0:T(1024)S(1)} %get-tuple-element.236) | copy-start | bytes 12292
  65.5 134.6 %copy-start.57 = (f32[512]{0:T(512)}, f32[512]{0:T(512)S(1)}, u32[]{:S(2)}) copy-start(f32[512]{0:T(512)S(1)} %dynamic_slice.44) | copy-start | bytes 6148
  65.5 12.6 copy-start.41
  66.7 108.0 %copy-start.23 = (f32[32,64]{1,0:T(8,128)}, f32[32,64]{1,0:T(8,128)S(1)}, u32[]{:S(2)}) copy-start(f32[32,64]{1,0:T(8,128)S(1)} %reduce_window_sum.11) | copy-start | bytes 24580
  69.4 105.3 %copy-start.16 = (f32[64,1024]{1,0:T(8,128)}, f32[64,1024]{1,0:T(8,128)S(1)}, u32[]{:S(2)}) copy-start(f32[64,1024]{1,0:T(8,128)S(1)} %get-tuple-element.309) | copy-start | bytes 786436
  76.5 13.8 copy-start.29
  174.7 25.4 %copy-start.28 = (f32[32,1024]{1,0:T(8,128)}, f32[32,1024]{1,0:T(8,128)S(1)}, u32[]{:S(2)}) copy-start(f32[32,1024]{1,0:T(8,128)S(1)} %get-tuple-element.490) | copy-start | bytes 393220
  214.9 19.5 %copy-start.61 = (bf16[2048,512]{1,0:T(8,128)(2,1)}, bf16[2048,512]{1,0:T(8,128)(2,1)S(1)}, u32[]{:S(2)}) copy-start(bf16[2048,512]{1,0:T(8,128)(2,1)S(1)} %get-tuple-element.256) | copy-start | bytes 6291460
  234.4 250.3 %all-gather.22.cloned.1.call-start = ((), (), s32[]{:S(2)}) async-start(), calls=%async_computation.16 | async-start | bytes 4456448 | tf_op jit(solution)/shard_map/all_gather | solution.py:321
  235.1 300.8 %all-gather.24.cloned.1.call-start = ((), (), s32[]{:S(2)}) async-start(), calls=%async_computation.17 | async-start | bytes 4456448 | tf_op jit(solution)/shard_map/all_gather | solution.py:323
  235.9 338.7 %all-gather.20.cloned.1.call-start = ((), (), s32[]{:S(2)}) async-start(), calls=%async_computation.15 | async-start | bytes 1114112 | tf_op jit(solution)/shard_map/all_gather | solution.py:322
  236.6 393.4 %reduce-scatter.10.cloned.1.call-start = ((), (), s32[]{:S(2)}) async-start(), calls=%async_computation.18 | async-start | bytes 6291456 | tf_op jit(solution)/shard_map/reduce_scatter | solution.py:335
  499.9 130.0 %copy-start.11 = (bf16[2048,512]{1,0:T(8,128)(2,1)S(1)}, bf16[2048,512]{1,0:T(8,128)(2,1)}, u32[]{:S(2)}) copy-start(bf16[2048,512]{1,0:T(8,128)(2,1)} %param.27) | copy-start | bytes 6291460
  550.9 148.0 %all-gather.26.cloned.1.call-start = ((), (), s32[]{:S(2)}) async-start(), calls=%async_computation.19 | async-start | bytes 6291456 | tf_op jit(solution)/shard_map/all_gather | solution.py:361
  642.0 229.3 %all-reduce.23.cloned.1.call-start = ((), (), s32[]{:S(2)}) async-start(), calls=%async_computation.20 | async-start | bytes 8388608 | tf_op jit(solution)/shard_map/psum | solution.py:386
  698.9 38.2 %slice-start = ((s8[8388608]{0:T(1024)(128)(4,1)}), s8[4194304]{0:T(1024)(128)(4,1)S(1)}, s32[]{:S(2)}) async-start(s8[8388608]{0:T(1024)(128)(4,1)} %bitcast.107), calls=%async_computation.29 | async-start | bytes 8388608
  715.8 14.6 copy-start.6
  715.8 21.3 %slice-start.1 = ((s8[8388608]{0:T(1024)(128)(4,1)}), s8[4194304]{0:T(1024)(128)(4,1)S(1)}, s32[]{:S(2)}) async-start(s8[8388608]{0:T(1024)(128)(4,1)} %bitcast.107), calls=%async_computation.30 | async-start | bytes 8388608
  760.5 110.8 %copy-start.58 = (f32[512]{0:T(512)S(1)}, f32[512]{0:T(512)}, u32[]{:S(2)}) copy-start(f32[512]{0:T(512)} %copy-done.57) | copy-start | bytes 6148
  763.2 355.1 %reduce-scatter.12.cloned.1.call-start = ((), (), s32[]{:S(2)}) async-start(), calls=%async_computation.21 | async-start | bytes 6291456 | tf_op jit(solution)/shard_map/reduce_scatter | solution.py:430
  871.3 15.6 copy-start.18
  893.5 36.3 %copy-start.21 = (f32[64,1024]{1,0:T(8,128)S(1)}, f32[64,1024]{1,0:T(8,128)}, u32[]{:S(2)}) copy-start(f32[64,1024]{1,0:T(8,128)} %get-tuple-element.310) | copy-start | bytes 786436
  893.5 36.3 %copy-start.24 = (f32[32,64]{1,0:T(8,128)S(1)}, f32[32,64]{1,0:T(8,128)}, u32[]{:S(2)}) copy-start(f32[32,64]{1,0:T(8,128)} %copy-done.23) | copy-start | bytes 24580
  893.5 36.3 %copy-start.33 = (pred[64,64]{0,1:T(8,128)(4,1)S(1)}, pred[64,64]{0,1:T(8,128)(4,1)}, u32[]{:S(2)}) copy-start(pred[64,64]{0,1:T(8,128)(4,1)} %copy-done.32) | copy-start | bytes 12292
  893.5 36.3 %copy-start.36 = (f32[32,64]{1,0:T(8,128)S(1)}, f32[32,64]{1,0:T(8,128)}, u32[]{:S(2)}) copy-start(f32[32,64]{1,0:T(8,128)} %get-tuple-element.249) | copy-start | bytes 24580
  939.0 10.3 copy-start.22
  949.3 10.7 copy-start.12
  954.2 11.7 copy-start.9
  960.1 15.7 slice-start.2
  1012.2 120.8 %reduce-scatter.24.cloned.1.call-start = ((), (), s32[]{:S(2)}) async-start(), calls=%async_computation.27 | async-start | bytes 2228224 | tf_op jit(solution)/shard_map/reduce_scatter | solution.py:369
  1018.2 179.5 %reduce-scatter.20.cloned.1.call-start = ((), (), s32[]{:S(2)}) async-start(), calls=%async_computation.25 | async-start | bytes 2228224 | tf_op jit(solution)/shard_map/reduce_scatter | solution.py:412
  1025.1 237.8 %reduce-scatter.18.cloned.1.call-start = ((), (), s32[]{:S(2)}) async-start(), calls=%async_computation.24 | async-start | bytes 2228224 | tf_op jit(solution)/shard_map/reduce_scatter | solution.py:411
  1031.1 296.6 %reduce-scatter.16.cloned.1.call-start = ((), (), s32[]{:S(2)}) async-start(), calls=%async_computation.23 | async-start | bytes 2228224 | tf_op jit(solution)/shard_map/reduce_scatter | solution.py:410
  1038.4 354.5 %reduce-scatter.14.cloned.1.call-start = ((), (), s32[]{:S(2)}) async-start(), calls=%async_computation.22 | async-start | bytes 2228224 | tf_op jit(solution)/shard_map/reduce_scatter | solution.py:409
  1044.5 456.6 %reduce-scatter.26.cloned.1.call-start = ((), (), s32[]{:S(2)}) async-start(), calls=%async_computation.28 | async-start | bytes 8912896 | tf_op jit(solution)/shard_map/reduce_scatter | solution.py:370
  1060.4 549.6 %reduce-scatter.22.cloned.1.call-start = ((), (), s32[]{:S(2)}) async-start(), calls=%async_computation.26 | async-start | bytes 8912896 | tf_op jit(solution)/shard_map/reduce_scatter | solution.py:368
  (38 other events, 234.8 us)
Sparse Core Ops, SparseCore 0:
  9.6 60.8 all-gather.9
  72.7 37.8 all-gather.13
  112.8 36.8 all-gather.15
  151.7 36.8 all-gather.11
  190.6 36.8 all-gather.17
  234.5 196.9 all-reduce.20
  433.6 51.0 all-gather.21
  486.8 49.0 all-gather.23
  538.1 36.4 all-gather.19
  576.7 53.1 reduce-scatter.9
  642.1 56.7 all-gather.25
  763.4 107.8 all-reduce.22
  1012.3 54.2 reduce-scatter.11
  1071.2 61.6 reduce-scatter.23
  1137.1 60.5 reduce-scatter.19
  1202.3 60.5 reduce-scatter.17
  1267.0 60.5 reduce-scatter.15
  1332.3 60.4 reduce-scatter.13
  1397.5 103.5 reduce-scatter.25
  1505.6 104.3 reduce-scatter.21
where the time goes:
time: 1630 us; the launch traced here: 1620 us
  waiting for transfers between devices  1050 us (64%)
  matrix products  254 us (16%)
  other arithmetic  146 us (9%)
  blocking collectives  84 us (5%)
  local copies, waits for them, and re-layouts  58.3 us (4%)
  between operations  18.8 us (1%)
    psum x1, waiting for transfers between devices, on_device(): time_total = lax.psum(time_part, 'tp')  195 us
    reduce_scatter x1, waiting for transfers between devices, on_device(): lax.psum_scatter(grad_chan_key, 'fsdp', scatter_dimension=0, tiled=True)  109 us
    reduce_scatter x1, waiting for transfers between devices, on_device(): lax.psum_scatter(grad_chan_value, 'fsdp', scatter_dimension=1, tiled=True)  108 us
    psum x1, waiting for transfers between devices, on_device(): lax.psum(grad_middle_part.astype(jnp.bfloat16), 'tp').astype(jnp.float32)  108 us
    dot_general x7, matrix products, matmul(): return jnp.dot(left, right, preferred_element_type=jnp.float32)  80.4 us
    dot_general x7, matrix products, inner_right(): lax.dot_general(left, right, (((1,), (1,)), ((), ())), preferred_element_...  70.7 us
    reduce_scatter x1, waiting for transfers between devices, on_device(): lax.psum_scatter(grad_time_recept, 'fsdp', scatter_dimension=0, tiled=True)  65.2 us
    reduce_scatter x1, waiting for transfers between devices, on_device(): lax.psum_scatter(grad_time_key, 'fsdp', scatter_dimension=0, tiled=True)  65.2 us
  transfers between devices with their start and end apart: 20, of which 18 were waited for; matrix products, arithmetic and copies ran while one was open for 14% of the time, Pallas kernels for 0%

commit v1 on v0

v1 whole, which is shorter than its diff:
```python
import functools
import itertools

import jax
import jax.numpy as jnp
from jax import lax
from jax.experimental import pallas as pl
from jax.experimental.pallas import tpu as pltpu
from jax.sharding import Mesh
from jax.sharding import PartitionSpec as P

BF = jnp.bfloat16
F32 = jnp.float32
EPSILON = 1e-05
SLOT = 64
CHUNK = 16
VMEM_LIMIT = 58 << 20
SIZES = {"z": 4, "y": 2, "x": 2}
EVERY = ("z", "y", "c", "x")
SWAP = [(0, 1), (1, 0)]

NN = (((1,), (0,)), ((), ()))
NT = (((1,), (1,)), ((), ()))
TN = (((0,), (0,)), ((), ()))


def dot(left, right, dims):
    return lax.dot_general(left, right, dims, preferred_element_type=F32)


def slot_list(order):
    dims = order[::-1]
    for index in itertools.product(*[range(SIZES[d]) for d in dims]):
        yield index, dict(zip(dims, index))


def slot_place(co, rel, other_core):
    block = ((co[0] + 4 - rel["z"]) & 3) * 4 + (co[1] ^ rel["y"]) * 2 + (co[2] ^ other_core)
    return pl.multiple_of(block * SLOT, SLOT), co[3] ^ rel["x"]


def weight_copies(co, own, other, whole, sems, order):
    copies = []
    for other_core, source in ((0, own), (1, other)):
        for index, rel in slot_list(order):
            row, half = slot_place(co, rel, other_core)
            copy = pltpu.make_async_copy(
                source.at[index], whole.at[half, pl.ds(row, SLOT), :], sems.at[len(copies)]
            )
            copies.append((rel["x"], copy))
    return copies


def start_all(copies):
    for _, copy in copies:
        copy.start()


def wait_half(copies, half):
    for which, copy in copies:
        if which == half:
            copy.wait()


def norm_rows(values, gain, bias):
    centre = values - jnp.mean(values, axis=-1, keepdims=True)
    scaled = lax.rsqrt(jnp.mean(centre * centre, axis=-1, keepdims=True) + EPSILON)
    unit = centre * scaled
    return unit * gain + bias, unit, scaled


def norm_rows_back(grad, unit, scaled, gain):
    weighted = grad * gain
    return scaled * (
        weighted
        - jnp.mean(weighted, axis=-1, keepdims=True)
        - unit * jnp.mean(weighted * unit, axis=-1, keepdims=True)
    )


def first_row(shape):
    return lax.broadcasted_iota(jnp.int32, shape, 0) == 0


def last_row(shape):
    return lax.broadcasted_iota(jnp.int32, shape, 0) == shape[0] - 1


def move_down(values, before):
    return jnp.where(first_row(values.shape), before, pltpu.roll(values, 1, 0))


def move_up(values, after):
    return jnp.where(last_row(values.shape), after, pltpu.roll(values, values.shape[0] - 1, 0))


def fold_rows(values):
    return values[:8] + values[8:]


def params(semantics=1):
    return pltpu.CompilerParams(vmem_limit_bytes=VMEM_LIMIT)


def anywhere():
    return pl.BlockSpec(memory_space=pl.ANY)


def cost(units, traffic):
    return pl.CostEstimate(
        flops=int(units * 2 * 1024**3), bytes_accessed=int(traffic), transcendentals=0
    )


def first_mix_kernel(x_ref, carry_ref, vec_ref, mk_ref, mv_ref, mr_ref):
    gain, bias = vec_ref[0:1, :], vec_ref[1:2, :]
    mixes = [vec_ref[i : i + 1, :] for i in (4, 5, 6)]
    width = x_ref.shape[1]

    def step(i, before):
        rows = pl.ds(pl.multiple_of(i * CHUNK, CHUNK), CHUNK)
        normed, _, _ = norm_rows(x_ref[rows, :].astype(F32), gain, bias)
        behind = move_down(normed, before) * carry_ref[rows, :]
        for mix, out in zip(mixes, (mk_ref, mv_ref, mr_ref)):
            out[rows, :] = (normed * mix + behind * (1.0 - mix)).astype(BF)
        return normed[CHUNK - 1 :, :]

    lax.fori_loop(0, x_ref.shape[0] // CHUNK, step, jnp.zeros((1, width), F32), unroll=2)


def first_mix(x, carry, vectors):
    shape = jax.ShapeDtypeStruct(x.shape, BF)
    return pl.pallas_call(
        first_mix_kernel,
        out_shape=[shape] * 3,
        compiler_params=params(),
        cost_estimate=cost(0, 8 << 20),
    )(x, carry, vectors)


TILE = 256


def scan_rates(decay):
    speed = jnp.exp(decay)
    return [jnp.exp(-float(n) * speed) for n in (1, 2, 4, 8)]


def twice(values):
    return jnp.concatenate([values] * (TILE // 128), axis=1)


def time_forward_kernel(
    co, mk, mv, mr, ko, kx, vo, vx, ro, rx, vec, masks,
    key_ref, val_ref, rec_ref, pa_ref, pb_ref, gated_ref, kw, vw, rw, sems,
):
    j = pl.program_id(0)
    per_half = kw.shape[2] // TILE
    groups = [
        weight_copies(co, own, other, whole, sems.at[n], order)
        for n, (own, other, whole, order) in enumerate(
            ((ko, kx, kw, ORDERS[0]), (vo, vx, vw, ORDERS[1]), (ro, rx, rw, ORDERS[2]))
        )
    ]

    @pl.when(j == 0)
    def _():
        for copies in groups:
            start_all(copies)
        for copies in groups:
            wait_half(copies, 0)

    @pl.when(j == per_half)
    def _():
        for copies in groups:
            wait_half(copies, 1)

    half = co[3] ^ lax.div(j, per_half)
    columns = pl.ds(pl.multiple_of(lax.rem(j, per_half) * TILE, TILE), TILE)
    key_ref[...] = dot(mk[...], kw[half, :, columns], NN)
    val_ref[...] = dot(mv[...], vw[half, :, columns], NN)
    rec_ref[...] = dot(mr[...], rw[half, :, columns], NN)

    spread = (8, TILE)
    decay = jnp.broadcast_to(vec[2:3, :], spread)
    first = jnp.broadcast_to(vec[3:4, :], spread)
    r1, r2, r4, r8 = scan_rates(decay)
    powers = jnp.exp(-lax.broadcasted_iota(jnp.int32, spread, 0).astype(F32) * jnp.exp(decay))

    def group(start, state):
        rows = pl.ds(start, 8)
        key, val, pre = key_ref[rows, :], val_ref[rows, :], rec_ref[rows, :]
        m1, m2, m4, mf, ml = (twice(masks[n, rows, :]) for n in range(5))
        rec = 1.0 / (1.0 + jnp.exp(-pre))
        power = jnp.exp(key)
        bonus = jnp.exp(first + key)
        c1, c2, c4, cf, cl = m1 * r1, m2 * r2, m4 * r4, mf * powers, ml * r8
        priors, ends = [], []
        for local, entering in ((power * val, state[0]), (power, state[1])):
            local = local + c1 * pltpu.roll(local, 1, 0)
            local = local + c2 * pltpu.roll(local, 2, 0)
            local = local + c4 * pltpu.roll(local, 4, 0)
            priors.append(m1 * pltpu.roll(local, 1, 0) + cf * entering)
            ends.append(jnp.broadcast_to(local[7:8, :], spread) + cl * entering)
        wkv = (priors[0] + bonus * val) / (priors[1] + bonus)
        rec_ref[rows, :] = rec
        pa_ref[rows, :] = priors[0]
        pb_ref[rows, :] = priors[1]
        return rec * wkv, tuple(ends)

    def step(i, state):
        start = pl.multiple_of(i * CHUNK, CHUNK)
        upper, state = group(start, state)
        lower, state = group(pl.multiple_of(start + 8, 8), state)
        gated_ref[pl.ds(start, CHUNK), :] = jnp.concatenate([upper, lower], axis=0).astype(BF)
        return state

    zero = jnp.zeros(spread, F32)
    lax.fori_loop(0, key_ref.shape[0] // CHUNK, step, (zero, zero))


def time_forward(co, mixed, weights, vectors, masks):
    tokens, width = mixed[0].shape
    half = width // 2
    per_half = half // TILE

    def tile(j, co):
        return 0, (co[3] ^ lax.div(j, per_half)) * per_half + lax.rem(j, per_half)

    fixed = pl.BlockSpec((tokens, width), lambda j, co: (0, 0))
    block = pl.BlockSpec((tokens, TILE), tile)
    return pl.pallas_call(
        time_forward_kernel,
        grid_spec=pltpu.PrefetchScalarGridSpec(
            num_scalar_prefetch=1,
            grid=(width // TILE,),
            in_specs=[fixed] * 3
            + [anywhere()] * 6
            + [
                pl.BlockSpec((vectors.shape[0], TILE), tile),
                pl.BlockSpec(masks.shape, lambda j, co: (0, 0, 0)),
            ],
            out_specs=[block] * 6,
            scratch_shapes=[pltpu.VMEM((2, width, half), BF)] * 3
            + [pltpu.SemaphoreType.DMA((3, 32))],
        ),
        out_shape=[jax.ShapeDtypeStruct((tokens, width), F32)] * 5
        + [jax.ShapeDtypeStruct((tokens, width), BF)],
        compiler_params=params(),
        cost_estimate=cost(8, 34 << 20),
    )(co, *mixed, *[part for pair in weights for part in pair], vectors, masks)


def time_output_kernel(
    co, gated, x_ref, carry_ref, vec_ref, oo, ox, middle_ref, mk_ref, mr_ref, ow, last, sems
):
    i = pl.program_id(0)
    copies = weight_copies(co, oo, ox, ow, sems, ORDERS[3])

    @pl.when(i == 0)
    def _():
        start_all(copies)
        last[...] = jnp.zeros_like(last)
        wait_half(copies, 0)
        wait_half(copies, 1)

    half = ow.shape[2]
    middle_ref[...] = dot(gated[:, :half], ow[0], NT) + dot(gated[:, half:], ow[1], NT)
    gain, bias = vec_ref[7:8, :], vec_ref[8:9, :]
    mixes = [vec_ref[n : n + 1, :] for n in (9, 10)]

    def step(n, before):
        rows = pl.ds(pl.multiple_of(n * CHUNK, CHUNK), CHUNK)
        middle = middle_ref[rows, :] + x_ref[rows, :].astype(F32)
        middle_ref[rows, :] = middle
        normed, _, _ = norm_rows(middle, gain, bias)
        behind = move_down(normed, before) * carry_ref[rows, :]
        for mix, out in zip(mixes, (mk_ref, mr_ref)):
            out[rows, :] = (normed * mix + behind * (1.0 - mix)).astype(BF)
        return normed[CHUNK - 1 :, :]

    last[...] = lax.fori_loop(0, x_ref.shape[0] // CHUNK, step, last[...], unroll=2)


def time_output_step(co, gated, x, carry, vectors, weight):
    tokens, width = x.shape
    rows = tokens // 4
    tall = pl.BlockSpec((rows, width), lambda i, co: (i, 0))
    return pl.pallas_call(
        time_output_kernel,
        grid_spec=pltpu.PrefetchScalarGridSpec(
            num_scalar_prefetch=1,
            grid=(4,),
            in_specs=[
                tall,
                tall,
                pl.BlockSpec((rows, 1), lambda i, co: (i, 0)),
                pl.BlockSpec(vectors.shape, lambda i, co: (0, 0)),
                anywhere(),
                anywhere(),
            ],
            out_specs=[tall] * 3,
            scratch_shapes=[
                pltpu.VMEM((2, width, width // 2), BF),
                pltpu.VMEM((1, width), F32),
                pltpu.SemaphoreType.DMA((32,)),
            ],
        ),
        out_shape=[jax.ShapeDtypeStruct((tokens, width), t) for t in (F32, BF, BF)],
        compiler_params=params(),
        cost_estimate=cost(3, 14 << 20),
    )(co, gated, x, carry, vectors, *weight)


WIDE = 512


def hidden_kernel(co, mk, wo, wx, hidden_ref, active_ref, whole, sems):
    j = pl.program_id(0)
    per_half = whole.shape[2] // WIDE
    copies = weight_copies(co, wo, wx, whole, sems, ORDERS[4])

    @pl.when(j == 0)
    def _():
        start_all(copies)
        wait_half(copies, 0)

    @pl.when(j == per_half)
    def _():
        wait_half(copies, 1)

    half = co[3] ^ lax.div(j, per_half)
    columns = pl.ds(pl.multiple_of(lax.rem(j, per_half) * WIDE, WIDE), WIDE)
    active = jnp.maximum(dot(mk[...], whole[half, :, columns], NN), 0.0)
    active_ref[...] = active.astype(BF)
    hidden_ref[...] = (active * active).astype(BF)


def column_tile(per_half):
    return lambda j, co: (0, (co[3] ^ lax.div(j, per_half)) * per_half + lax.rem(j, per_half))


def hidden_step(co, mixed, weight):
    tokens, width = mixed.shape
    half = weight[0].shape[-1]
    block = pl.BlockSpec((tokens, WIDE), column_tile(half // WIDE))
    return pl.pallas_call(
        hidden_kernel,
        grid_spec=pltpu.PrefetchScalarGridSpec(
            num_scalar_prefetch=1,
            grid=(2 * half // WIDE,),
            in_specs=[
                pl.BlockSpec((tokens, width), lambda j, co: (0, 0)),
                anywhere(),
                anywhere(),
            ],
            out_specs=[block] * 2,
            scratch_shapes=[
                pltpu.VMEM((2, width, half), BF),
                pltpu.SemaphoreType.DMA((32,)),
            ],
        ),
        out_shape=[jax.ShapeDtypeStruct((tokens, 2 * half), BF)] * 2,
        compiler_params=params(),
        cost_estimate=cost(4.5, 26 << 20),
    )(co, mixed, *weight)


def result_kernel(
    co, scale, hidden, mr, middle_ref, teacher_ref, valid_ref, wo, wx, ro, rx,
    out_ref, dres_ref, dkv_ref, drec_ref, loss_ref, ww, rw, kv_ref, pre_ref, sems,
):
    i = pl.program_id(0)
    copies = weight_copies(co, wo, wx, ww, sems.at[0], ORDERS[6])
    recept = weight_copies(co, ro, rx, rw, sems.at[1], ORDERS[5])

    @pl.when(i == 0)
    def _():
        start_all(recept)
        start_all(copies)
        loss_ref[...] = jnp.zeros_like(loss_ref)
        for half in (0, 1):
            wait_half(recept, half)
        for half in (0, 1):
            wait_half(copies, half)

    wide, narrow = ww.shape[2], rw.shape[2]
    kv_ref[...] = dot(hidden[:, :wide], ww[0], NT) + dot(hidden[:, wide:], ww[1], NT)
    pre_ref[:, :narrow] = dot(mr[...], rw[0], NN)
    pre_ref[:, narrow:] = dot(mr[...], rw[1], NN)
    factor = scale[0]

    def step(n, total):
        rows = pl.ds(pl.multiple_of(n * CHUNK, CHUNK), CHUNK)
        kv = kv_ref[rows, :]
        rec = 1.0 / (1.0 + jnp.exp(-pre_ref[rows, :]))
        result = middle_ref[rows, :] + rec * kv
        out_ref[rows, :] = result.astype(BF)
        error = (result - teacher_ref[rows, :].astype(F32)) * valid_ref[rows, :]
        grad = error * factor
        dres_ref[rows, :] = grad
        dkv_ref[rows, :] = (grad * rec).astype(BF)
        drec_ref[rows, :] = (grad * kv * rec * (1.0 - rec)).astype(BF)
        return total + fold_rows(error * error)

    total = lax.fori_loop(
        0, kv_ref.shape[0] // CHUNK, step, jnp.zeros((8, kv_ref.shape[1]), F32)
    )
    loss_ref[...] += total


def result_step(co, scale, hidden, mixed, middle, teacher, valid, weight, recept):
    tokens, width = mixed.shape
    rows = tokens // 4
    wide = weight[0].shape[-1]
    tall = pl.BlockSpec((rows, width), lambda i, co, s: (i, 0))
    return pl.pallas_call(
        result_kernel,
        grid_spec=pltpu.PrefetchScalarGridSpec(
            num_scalar_prefetch=2,
            grid=(4,),
            in_specs=[
                pl.BlockSpec((rows, 2 * wide), lambda i, co, s: (i, 0)),
                tall,
                tall,
                tall,
                pl.BlockSpec((rows, 1), lambda i, co, s: (i, 0)),
            ]
            + [anywhere()] * 4,
            out_specs=[tall] * 4 + [pl.BlockSpec((8, width), lambda i, co, s: (0, 0))],
            scratch_shapes=[
                pltpu.VMEM((2, width, wide), BF),
                pltpu.VMEM((2, width, width // 2), BF),
                pltpu.VMEM((rows, width), F32),
                pltpu.VMEM((rows, width), F32),
                pltpu.SemaphoreType.DMA((2, 32)),
            ],
        ),
        out_shape=[jax.ShapeDtypeStruct((tokens, width), t) for t in (BF, F32, BF, BF)]
        + [jax.ShapeDtypeStruct((8, width), F32)],
        compiler_params=params(),
        cost_estimate=cost(7, 38 << 20),
    )(co, scale, hidden, mixed, middle, teacher, valid, *weight, *recept)


def weight_grad_kernel(co, model_ref, chan_ref, own, other, whole, sems, *, order):
    j = pl.program_id(0)
    per_half = whole.shape[2] // WIDE
    part = lax.rem(j, per_half)
    columns = pl.ds(pl.multiple_of(part * WIDE, WIDE), WIDE)
    turn = lax.div(j, per_half)
    whole[co[3] ^ turn, :, columns] = dot(model_ref[...], chan_ref[...], TN).astype(BF)

    def copies(piece):
        found = []
        for other_core, target in ((0, own), (1, other)):
            for index, rel in slot_list(order):
                row, half = slot_place(co, rel, other_core)
                copy = pltpu.make_async_copy(
                    whole.at[half, pl.ds(row, SLOT), piece],
                    target.at[index + (slice(None), piece)],
                    sems.at[len(found)],
                )
                found.append((rel["x"], copy))
        return found

    for which in (0, 1):

        @pl.when(turn == which)
        def _(which=which):
            for rel_x, copy in copies(columns):
                if rel_x == which:
                    copy.start()

    @pl.when(j == pl.num_programs(0) - 1)
    def _():
        for _, copy in copies(slice(None)):
            copy.wait()


def weight_grad(co, model, chan, order):
    tokens, width = model.shape
    half = chan.shape[1] // 2
    dims = tuple(SIZES[d] for d in order[::-1])
    shape = jax.ShapeDtypeStruct(dims + (SLOT, half), BF)
    return pl.pallas_call(
        functools.partial(weight_grad_kernel, order=order),
        grid_spec=pltpu.PrefetchScalarGridSpec(
            num_scalar_prefetch=1,
            grid=(2 * half // WIDE,),
            in_specs=[
                pl.BlockSpec((tokens, width), lambda j, co: (0, 0)),
                pl.BlockSpec((tokens, WIDE), column_tile(half // WIDE)),
            ],
            out_specs=[anywhere()] * 2,
            scratch_shapes=[
                pltpu.VMEM((2, width, half), BF),
                pltpu.SemaphoreType.DMA((32,)),
            ],
        ),
        out_shape=[shape] * 2,
        compiler_params=params(),
        cost_estimate=cost(half / 512 * 1.2, (2 << 20) * (1 + half / 256)),
    )(co, model, chan)


def hidden_back_kernel(co, dkv, active_ref, wo, wx, out_ref, whole, sems):
    j = pl.program_id(0)
    per_half = whole.shape[2] // WIDE
    copies = weight_copies(co, wo, wx, whole, sems, ORDERS[6])

    @pl.when(j == 0)
    def _():
        start_all(copies)
        wait_half(copies, 0)

    @pl.when(j == per_half)
    def _():
        wait_half(copies, 1)

    half = co[3] ^ lax.div(j, per_half)
    columns = pl.ds(pl.multiple_of(lax.rem(j, per_half) * WIDE, WIDE), WIDE)
    grad = dot(dkv[...], whole[half, :, columns], NN)
    out_ref[...] = (2.0 * active_ref[...].astype(F32) * grad).astype(BF)


def hidden_back(co, dkv, active, weight):
    tokens, width = dkv.shape
    half = weight[0].shape[-1]
    block = pl.BlockSpec((tokens, WIDE), column_tile(half // WIDE))
    return pl.pallas_call(
        hidden_back_kernel,
        grid_spec=pltpu.PrefetchScalarGridSpec(
            num_scalar_prefetch=1,
            grid=(2 * half // WIDE,),
            in_specs=[
                pl.BlockSpec((tokens, width), lambda j, co: (0, 0)),
                block,
                anywhere(),
                anywhere(),
            ],
            out_specs=block,
            scratch_shapes=[
                pltpu.VMEM((2, width, half), BF),
                pltpu.SemaphoreType.DMA((32,)),
            ],
        ),
        out_shape=jax.ShapeDtypeStruct((tokens, 2 * half), BF),
        compiler_params=params(),
        cost_estimate=cost(4.5, 26 << 20),
    )(co, dkv, active, *weight)


def middle_back_kernel(
    co, dkey, drec, middle_ref, dres_ref, lead_ref, vec_ref, wo, wx, ro, rx,
    dmid_ref, dtime_ref, sums_ref, ww, rw, gk_ref, gr_ref, next_ref, sems,
):
    i = pl.program_id(0)
    copies = weight_copies(co, wo, wx, ww, sems.at[0], ORDERS[4])
    recept = weight_copies(co, ro, rx, rw, sems.at[1], ORDERS[5])

    @pl.when(i == 0)
    def _():
        start_all(recept)
        start_all(copies)
        sums_ref[...] = jnp.zeros_like(sums_ref)
        next_ref[...] = jnp.zeros_like(next_ref)
        for half in (0, 1):
            wait_half(recept, half)
        for half in (0, 1):
            wait_half(copies, half)

    wide, narrow = ww.shape[2], rw.shape[2]
    gk_ref[...] = dot(dkey[:, :wide], ww[0], NT) + dot(dkey[:, wide:], ww[1], NT)
    gr_ref[...] = dot(drec[:, :narrow], rw[0], NT) + dot(drec[:, narrow:], rw[1], NT)
    gain, bias = vec_ref[7:8, :], vec_ref[8:9, :]
    mix_k, mix_r = vec_ref[9:10, :], vec_ref[10:11, :]
    steps = middle_ref.shape[0] // CHUNK

    def step(n, after):
        rows = pl.ds(pl.multiple_of((steps - 1 - n) * CHUNK, CHUNK), CHUNK)
        normed, unit, scaled = norm_rows(middle_ref[rows, :], gain, bias)
        lead = lead_ref[rows, :]
        gk, gr = gk_ref[rows, :], gr_ref[rows, :]
        uk = move_up(gk, after[0]) * lead
        ur = move_up(gr, after[1]) * lead
        grad = gk * mix_k + gr * mix_r + uk * (1.0 - mix_k) + ur * (1.0 - mix_r)
        sums_ref[0] += fold_rows(grad * unit)
        sums_ref[1] += fold_rows(grad)
        sums_ref[2] += fold_rows(normed * (gk - uk))
        sums_ref[3] += fold_rows(normed * (gr - ur))
        dmid = dres_ref[rows, :] + norm_rows_back(grad, unit, scaled, gain)
        dmid_ref[rows, :] = dmid
        dtime_ref[rows, :] = dmid.astype(BF)
        return gk[:1, :], gr[:1, :]

    after = lax.fori_loop(0, steps, step, (next_ref[0:1, :], next_ref[1:2, :]))
    next_ref[0:1, :] = after[0]
    next_ref[1:2, :] = after[1]


def middle_back(co, dkey, drec, middle, dres, lead, vectors, weight, recept):
    tokens, width = middle.shape
    rows = tokens // 4
    wide = weight[0].shape[-1]
    tall = pl.BlockSpec((rows, width), lambda i, co: (3 - i, 0))
    return pl.pallas_call(
        middle_back_kernel,
        grid_spec=pltpu.PrefetchScalarGridSpec(
            num_scalar_prefetch=1,
            grid=(4,),
            in_specs=[
                pl.BlockSpec((rows, 2 * wide), lambda i, co: (3 - i, 0)),
                tall,
                tall,
                tall,
                pl.BlockSpec((rows, 1), lambda i, co: (3 - i, 0)),
                pl.BlockSpec(vectors.shape, lambda i, co: (0, 0)),
            ]
            + [anywhere()] * 4,
            out_specs=[tall] * 2 + [pl.BlockSpec((4, 8, width), lambda i, co: (0, 0, 0))],
            scratch_shapes=[
                pltpu.VMEM((2, width, wide), BF),
                pltpu.VMEM((2, width, width // 2), BF),
                pltpu.VMEM((rows, width), F32),
                pltpu.VMEM((rows, width), F32),
                pltpu.VMEM((8, width), F32),
                pltpu.SemaphoreType.DMA((2, 32)),
            ],
        ),
        out_shape=[
            jax.ShapeDtypeStruct((tokens, width), F32),
            jax.ShapeDtypeStruct((tokens, width), BF),
            jax.ShapeDtypeStruct((4, 8, width), F32),
        ],
        compiler_params=params(),
        cost_estimate=cost(8, 36 << 20),
    )(co, dkey, drec, middle, dres, lead, vectors, *weight, *recept)


def time_back_kernel(
    co, dtime, key_ref, val_ref, rec_ref, pa_ref, pb_ref, vec, masks, oo, ox,
    dkey_ref, dval_ref, drec_ref, sums_ref, ow, dg_ref, sems,
):
    j = pl.program_id(0)
    per_half = ow.shape[2] // TILE
    copies = weight_copies(co, oo, ox, ow, sems, ORDERS[3])

    @pl.when(j == 0)
    def _():
        start_all(copies)
        wait_half(copies, 0)

    @pl.when(j == per_half)
    def _():
        wait_half(copies, 1)

    half = co[3] ^ lax.div(j, per_half)
    columns = pl.ds(pl.multiple_of(lax.rem(j, per_half) * TILE, TILE), TILE)
    dg_ref[...] = dot(dtime[...], ow[half, :, columns], NN)

    spread = (8, TILE)
    decay = jnp.broadcast_to(vec[2:3, :], spread)
    first = jnp.broadcast_to(vec[3:4, :], spread)
    r1, r2, r4, r8 = scan_rates(decay)
    left = 7.0 - lax.broadcasted_iota(jnp.int32, spread, 0).astype(F32)
    powers = jnp.exp(-left * jnp.exp(decay))

    def group(start, state):
        rows = pl.ds(start, 8)
        n1, n2, n4, nf, c0, ml = (twice(masks[n, rows, :]) for n in (5, 6, 7, 8, 9, 4))
        key, val, rec, dg = key_ref[rows, :], val_ref[rows, :], rec_ref[rows, :], dg_ref[rows, :]
        pa, pb = pa_ref[rows, :], pb_ref[rows, :]
        power = jnp.exp(key)
        bonus = jnp.exp(first + key)
        inverse = 1.0 / (pb + bonus)
        wkv = (pa + bonus * val) * inverse
        slope = dg * rec * inverse
        drec = dg * wkv * rec * (1.0 - rec)
        c1, c2, c4, cf, cl = n1 * r1, n2 * r2, n4 * r4, nf * powers, ml * r8
        found, starts = [], []
        for local, leaving in ((slope, state[0]), (-slope * wkv, state[1])):
            local = local + c1 * pltpu.roll(local, 7, 0)
            local = local + c2 * pltpu.roll(local, 6, 0)
            local = local + c4 * pltpu.roll(local, 4, 0)
            found.append(n1 * pltpu.roll(local, 7, 0) + cf * leaving)
            starts.append(c0 * jnp.broadcast_to(local[0:1, :], spread) + cl * leaving)
        later_a, later_b = found
        summand = bonus * slope * (val - wkv)
        dkey = power * (later_a * val + later_b) + summand
        dval = power * later_a + bonus * slope
        state = (
            starts[0],
            starts[1],
            state[2] + summand,
            state[3] + later_a * pa + later_b * pb,
        )
        return (dkey, dval, drec), state

    steps = key_ref.shape[0] // CHUNK

    def step(n, state):
        start = pl.multiple_of((steps - 1 - n) * CHUNK, CHUNK)
        lower, state = group(pl.multiple_of(start + 8, 8), state)
        upper, state = group(start, state)
        for up, low, out in zip(upper, lower, (dkey_ref, dval_ref, drec_ref)):
            out[pl.ds(start, CHUNK), :] = jnp.concatenate([up, low], axis=0).astype(BF)
        return state

    zero = jnp.zeros(spread, F32)
    _, _, first_sum, decay_sum = lax.fori_loop(0, steps, step, (zero,) * 4)
    sums_ref[0] = -r1 * jnp.exp(decay) * decay_sum
    sums_ref[1] = first_sum


def time_back(co, dtime, saved, vectors, masks, weight):
    tokens, width = dtime.shape
    half = width // 2
    tile = column_tile(half // TILE)
    block = pl.BlockSpec((tokens, TILE), tile)
    return pl.pallas_call(
        time_back_kernel,
        grid_spec=pltpu.PrefetchScalarGridSpec(
            num_scalar_prefetch=1,
            grid=(width // TILE,),
            in_specs=[pl.BlockSpec((tokens, width), lambda j, co: (0, 0))]
            + [block] * 5
            + [
                pl.BlockSpec((vectors.shape[0], TILE), tile),
                pl.BlockSpec(masks.shape, lambda j, co: (0, 0, 0)),
                anywhere(),
                anywhere(),
            ],
            out_specs=[block] * 3
            + [pl.BlockSpec((2, 8, TILE), lambda j, co: (0,) + tile(j, co))],
            scratch_shapes=[
                pltpu.VMEM((2, width, half), BF),
                pltpu.VMEM((tokens, TILE), F32),
                pltpu.SemaphoreType.DMA((32,)),
            ],
        ),
        out_shape=[jax.ShapeDtypeStruct((tokens, width), BF)] * 3
        + [jax.ShapeDtypeStruct((2, 8, width), F32)],
        compiler_params=params(),
        cost_estimate=cost(9, 34 << 20),
    )(co, dtime, *saved, vectors, masks, *weight)


def input_back_kernel(
    co, dkey, dval, drec, x_ref, dmid_ref, lead_ref, vec_ref, ko, kx, vo, vx, ro, rx,
    out_ref, sums_ref, kw, vw, rw, gk_ref, gv_ref, gr_ref, next_ref, sems,
):
    i = pl.program_id(0)
    groups = [
        weight_copies(co, own, other, whole, sems.at[n], order)
        for n, (own, other, whole, order) in enumerate(
            ((ko, kx, kw, ORDERS[0]), (vo, vx, vw, ORDERS[1]), (ro, rx, rw, ORDERS[2]))
        )
    ]

    @pl.when(i == 0)
    def _():
        for copies in groups:
            start_all(copies)
        sums_ref[...] = jnp.zeros_like(sums_ref)
        next_ref[...] = jnp.zeros_like(next_ref)
        for copies in groups:
            wait_half(copies, 0)
            wait_half(copies, 1)

    half = kw.shape[2]
    for grad, whole, out in ((dkey, kw, gk_ref), (dval, vw, gv_ref), (drec, rw, gr_ref)):
        out[...] = dot(grad[:, :half], whole[0], NT) + dot(grad[:, half:], whole[1], NT)
    gain, bias = vec_ref[0:1, :], vec_ref[1:2, :]
    mixes = [vec_ref[n : n + 1, :] for n in (4, 5, 6)]
    steps = x_ref.shape[0] // CHUNK

    def step(n, after):
        rows = pl.ds(pl.multiple_of((steps - 1 - n) * CHUNK, CHUNK), CHUNK)
        normed, unit, scaled = norm_rows(x_ref[rows, :].astype(F32), gain, bias)
        lead = lead_ref[rows, :]
        total = jnp.zeros_like(normed)
        firsts = []
        for m, (part, mix) in enumerate(zip((gk_ref, gv_ref, gr_ref), mixes)):
            grad = part[rows, :]
            up = move_up(grad, after[m]) * lead
            total = total + grad * mix + up * (1.0 - mix)
            sums_ref[2 + m] += fold_rows(normed * (grad - up))
            firsts.append(grad[:1, :])
        sums_ref[0] += fold_rows(total * unit)
        sums_ref[1] += fold_rows(total)
        out_ref[rows, :] = dmid_ref[rows, :] + norm_rows_back(total, unit, scaled, gain)
        return tuple(firsts)

    after = lax.fori_loop(0, steps, step, tuple(next_ref[m : m + 1, :] for m in range(3)))
    for m in range(3):
        next_ref[m : m + 1, :] = after[m]


def input_back(co, grads, x, dmid, lead, vectors, weights):
    tokens, width = x.shape
    rows = tokens // 4
    tall = pl.BlockSpec((rows, width), lambda i, co: (3 - i, 0))
    return pl.pallas_call(
        input_back_kernel,
        grid_spec=pltpu.PrefetchScalarGridSpec(
            num_scalar_prefetch=1,
            grid=(4,),
            in_specs=[tall] * 5
            + [
                pl.BlockSpec((rows, 1), lambda i, co: (3 - i, 0)),
                pl.BlockSpec(vectors.shape, lambda i, co: (0, 0)),
            ]
            + [anywhere()] * 6,
            out_specs=[tall, pl.BlockSpec((5, 8, width), lambda i, co: (0, 0, 0))],
            scratch_shapes=[pltpu.VMEM((2, width, width // 2), BF)] * 3
            + [pltpu.VMEM((rows, width), F32)] * 3
            + [pltpu.VMEM((8, width), F32), pltpu.SemaphoreType.DMA((3, 32))],
        ),
        out_shape=[
            jax.ShapeDtypeStruct((tokens, width), F32),
            jax.ShapeDtypeStruct((5, 8, width), F32),
        ],
        compiler_params=params(),
        cost_estimate=cost(7, 26 << 20),
    )(co, *grads, x, dmid, lead, vectors, *[part for pair in weights for part in pair])


ORDERS = ("xzy", "yzx", "zyx", "zxy", "xzy", "zyx", "yzx")
RING_UP = [(0, 1), (1, 2), (2, 3), (3, 0)]
RING_DOWN = [(1, 0), (2, 1), (3, 2), (0, 3)]


class Links:
    def __init__(self):
        self.co = jnp.stack([lax.axis_index(a) for a in ("z", "y", "c", "x")]).astype(jnp.int32)

    def gather(self, shard, order):
        held = shard
        for axis in order:
            if axis == "z":
                parts = [held]
                for _ in range(3):
                    parts.append(lax.ppermute(parts[-1], "z", RING_UP))
                held = jnp.stack(parts)
            else:
                held = jnp.stack([held, lax.ppermute(held, axis, SWAP)])
        return held, lax.ppermute(held, "c", SWAP)

    def reduce(self, own, other, order):
        held = own + lax.ppermute(other, "c", SWAP)
        for n, axis in enumerate(order[::-1]):
            wide = (lambda v: v.astype(F32)) if n == 2 else (lambda v: v)
            if axis == "z":
                moving = held[3]
                for place in (2, 1):
                    moving = held[place] + lax.ppermute(moving, "z", RING_DOWN)
                held = wide(held[0]) + wide(lax.ppermute(moving, "z", RING_DOWN))
            else:
                held = wide(held[0]) + wide(lax.ppermute(held[1], axis, SWAP))
        return held

    def total(self, values):
        for axis in ("x", "y", "c"):
            values = values + lax.ppermute(values, axis, SWAP)
        values = values + lax.ppermute(values, "z", [(0, 1), (1, 0), (2, 3), (3, 2)])
        return values + lax.ppermute(values, "z", [(0, 2), (2, 0), (1, 3), (3, 1)])


class Plain:
    def __init__(self, blocks):
        self.blocks = blocks
        self.co = jnp.zeros((4,), jnp.int32)

    def gather(self, shard, order):
        whole = lax.all_gather(shard, ("z", "y", "c"), axis=0, tiled=True)
        whole = lax.all_gather(whole, "x", axis=1, tiled=True)
        half = whole.shape[1] // 2
        dims = tuple(SIZES[d] for d in order[::-1])
        found = []
        for core in (0, 1):
            parts = []
            for _, rel in slot_list(order):
                block = ((4 - rel["z"]) & 3) * 4 + rel["y"] * 2 + core
                part = whole[block * SLOT : (block + 1) * SLOT]
                parts.append(part[:, rel["x"] * half : (rel["x"] + 1) * half])
            found.append(jnp.stack(parts).reshape(dims + (SLOT, half)))
        return tuple(found)

    def reduce(self, own, other, order):
        half = own.shape[-1]
        table = {}
        for core, source in ((0, own), (1, other)):
            for index, rel in slot_list(order):
                block = ((4 - rel["z"]) & 3) * 4 + rel["y"] * 2 + core
                table[block, rel["x"]] = source[index]
        whole = jnp.concatenate(
            [jnp.concatenate([table[b, 0], table[b, 1]], axis=1) for b in range(16)], axis=0
        )
        whole = lax.psum_scatter(whole, ("z", "y", "c"), scatter_dimension=0, tiled=True)
        whole = lax.psum_scatter(whole, "x", scatter_dimension=1, tiled=True)
        return whole.astype(F32)

    def total(self, values):
        return lax.psum(values, EVERY)


def scan_masks(carry):
    c = carry.reshape(-1, 8)
    place = jnp.arange(8)[None, :]

    def behind(values, n):
        return jnp.where(place >= n, jnp.roll(values, n, axis=1), 0.0)

    def ahead(values, n):
        return jnp.where(place < 8 - n, jnp.roll(values, -n, axis=1), 0.0)

    m1 = jnp.where(place >= 1, c, 0.0)
    m2 = m1 * behind(m1, 1)
    m4 = m2 * behind(m2, 2)
    mf = jnp.cumprod(c, axis=1)
    ml = jnp.broadcast_to(mf[:, 7:], c.shape)
    n1 = ahead(c, 1)
    n2 = n1 * ahead(n1, 1)
    n4 = n2 * ahead(n2, 2)
    back = jnp.cumprod(c[:, ::-1], axis=1)[:, ::-1]
    nf = jnp.where(place < 7, jnp.roll(back, -1, axis=1), 1.0)
    c0 = jnp.broadcast_to(c[:, :1], c.shape)
    table = jnp.stack([m1, m2, m4, mf, ml, n1, n2, n4, nf, c0]).reshape(10, -1, 1)
    return jnp.broadcast_to(table, table.shape[:2] + (128,))


def on_device(
    inputs,
    segments,
    teacher,
    first_norm_gain,
    first_norm_bias,
    time_decay,
    time_first,
    time_mix_key,
    time_mix_value,
    time_mix_recept,
    time_key,
    time_value,
    time_recept,
    time_output,
    second_norm_gain,
    second_norm_bias,
    channel_mix_key,
    channel_mix_recept,
    channel_key,
    channel_recept,
    channel_value,
):
    tokens, width = inputs.shape
    sizes = {a: lax.axis_size(a) for a in EVERY}
    devices = sizes["z"] * sizes["y"] * sizes["c"] * sizes["x"]
    fast = (sizes["z"], sizes["y"], sizes["c"], sizes["x"]) == (4, 2, 2, 2)
    links = Links() if fast else Plain(width // SLOT)
    co = links.co
    side = lax.axis_index("x")

    ids = lax.dynamic_slice_in_dim(segments, side * tokens, tokens)
    previous = jnp.concatenate([jnp.zeros((1,), jnp.int32), ids[:-1]])
    started = jnp.arange(tokens, dtype=jnp.int32) > 0
    carry = ((ids == previous) & (ids > 0) & started).astype(F32)
    valid = (ids > 0).astype(F32)
    lead = jnp.concatenate([carry[1:], jnp.zeros((1,), F32)])
    masks = scan_masks(carry)
    carry, valid_rows, lead = carry[:, None], valid[:, None], lead[:, None]

    flat = ((lax.axis_index("z") * sizes["y"] + lax.axis_index("y")) * sizes["c"] + lax.axis_index("c")) * sizes["x"] + side
    own_vectors = jnp.stack(
        [
            first_norm_gain,
            first_norm_bias,
            time_decay,
            time_first,
            time_mix_key,
            time_mix_value,
            time_mix_recept,
            second_norm_gain,
            second_norm_bias,
            channel_mix_key,
            channel_mix_recept,
        ]
    )
    piece = own_vectors.shape[1]
    spread = jnp.where(
        jnp.arange(width)[None, :] // piece == flat, jnp.tile(own_vectors, (1, width // piece)), 0.0
    )
    counts = jnp.broadcast_to(jnp.sum(valid), (1, width))
    vectors = links.total(jnp.concatenate([spread, counts, jnp.zeros((4, width), F32)]))
    count = vectors[11, 0]

    shards = (
        time_key,
        time_value,
        time_recept,
        time_output.T,
        channel_key,
        channel_recept,
        channel_value.T,
    )
    key_w, value_w, recept_w, output_w, ckey_w, crecept_w, cvalue_w = (
        links.gather(shard, order) for shard, order in zip(shards, ORDERS)
    )

    if sizes["x"] == 2:
        mine = lax.dynamic_slice_in_dim(teacher, side * tokens, tokens)
        theirs = lax.dynamic_slice_in_dim(teacher, (1 - side) * tokens, tokens)
        theirs = lax.ppermute(theirs, "x", SWAP)
        teacher_rows = jnp.where(
            side == 0,
            jnp.concatenate([mine, theirs], axis=1),
            jnp.concatenate([theirs, mine], axis=1),
        )
    else:
        teacher_rows = teacher

    mixed = first_mix(inputs, carry, vectors)
    *saved, gated = time_forward(co, mixed, (key_w, value_w, recept_w), vectors, masks)
    middle, mixed_k2, mixed_r2 = time_output_step(co, gated, inputs, carry, vectors, output_w)
    hidden, active = hidden_step(co, mixed_k2, ckey_w)
    scale = (float(tokens * devices) / count).reshape(1)
    result, dres, dkv, drec2, loss_rows = result_step(
        co, scale, hidden, mixed_r2, middle, teacher_rows, valid_rows, cvalue_w, crecept_w
    )
    if sizes["x"] == 2:
        half = width // 2
        kept = lax.dynamic_slice_in_dim(result, side * half, half, axis=1)
        sent = lax.dynamic_slice_in_dim(result, (1 - side) * half, half, axis=1)
        arrived = lax.ppermute(sent, "x", SWAP)
        outputs = jnp.where(
            side == 0,
            jnp.concatenate([kept, arrived], axis=0),
            jnp.concatenate([arrived, kept], axis=0),
        )
    else:
        outputs = result

    cvalue_g = links.reduce(*weight_grad(co, dkv, hidden, ORDERS[6]), ORDERS[6])
    dkey2 = hidden_back(co, dkv, active, cvalue_w)
    ckey_g = links.reduce(*weight_grad(co, mixed_k2, dkey2, ORDERS[4]), ORDERS[4])
    crecept_g = links.reduce(*weight_grad(co, mixed_r2, drec2, ORDERS[5]), ORDERS[5])
    dmid, dtime, sums2 = middle_back(
        co, dkey2, drec2, middle, dres, lead, vectors, ckey_w, crecept_w
    )
    output_g = links.reduce(*weight_grad(co, dtime, gated, ORDERS[3]), ORDERS[3])
    *dmix, sums_t = time_back(co, dtime, saved, vectors, masks, output_w)
    time_g = [
        links.reduce(*weight_grad(co, m, d, order), order)
        for m, d, order in zip(mixed, dmix, ORDERS)
    ]
    input_grad, sums1 = input_back(
        co, dmix, inputs, dmid, lead, vectors, (key_w, value_w, recept_w)
    )

    rows = jnp.concatenate([sums1[:2], sums_t, sums1[2:], sums2, loss_rows[None]])
    totals = links.total(jnp.sum(rows, axis=1))
    loss = jnp.sum(totals[11]) / (2.0 * count * width)
    vector_g = lax.dynamic_slice_in_dim(totals, flat * piece, piece, axis=1)
    return (
        outputs,
        loss,
        input_grad,
        *[vector_g[n] for n in range(7)],
        *time_g,
        output_g.T,
        *[vector_g[n] for n in range(7, 11)],
        ckey_g,
        crecept_g,
        cvalue_g.T,
    )


def solution(mesh):
    fsdp, tp = mesh.shape["fsdp"], mesh.shape["tp"]
    core = 2 if fsdp % 4 == 0 else 1
    split = Mesh(mesh.devices.reshape(fsdp // (core * core), core, core, tp), EVERY)
    rows = ("z", "y", "c")
    vector = P(EVERY)
    matrix = P(rows, "x")
    turned = P("x", rows)
    tall = P(EVERY, None)
    return jax.shard_map(
        on_device,
        mesh=split,
        in_specs=(
            (tall, P(rows), matrix)
            + (vector,) * 7
            + (matrix, matrix, matrix, turned)
            + (vector,) * 4
            + (matrix, matrix, turned)
        ),
        out_specs=(
            (matrix, P(), tall)
            + (vector,) * 7
            + (matrix, matrix, matrix, turned)
            + (vector,) * 4
            + (matrix, matrix, turned)
        ),
        check_vma=False,
    )
```

time: 1630 us -> 783 us (0.48)
  waiting for transfers between devices: 1050 us -> 265 us
  Pallas kernels: 0 us -> 294 us
  matrix products: 254 us -> 0 us
  starting transfers between devices: 1.67 us -> 110 us
  blocking collectives: 84 us -> 0 us
  other arithmetic: 146 us -> 68.5 us
  local copies, waits for them, and re-layouts: 58.3 us -> 30.9 us
    reduce_scatter x9 -> x0, waiting for transfers between devices: 542 us -> none  [the longest x1 109 us: on_device(): lax.psum_scatter(grad_chan_key, 'fsdp', scatter_dimension=0, tiled=True)]
    psum x2 -> x0, waiting for transfers between devices: 303 us -> none  [the longest x1 195 us: on_device(): time_total = lax.psum(time_part, 'tp')]
    pallas_call x0 -> x16, Pallas kernels: none -> 294 us  [the longest x7 63.6 us: weight_grad(): pl.pallas_call(functools.partial(weight_grad_kernel, order=order), grid_s...]
    ppermute x0 -> x96, waiting for transfers between devices: none -> 265 us  [the longest x21 72.3 us: gather(): parts.append(lax.ppermute(parts[-1], 'z', RING_UP))]
    dot_general x25 -> x0, matrix products: 254 us -> none  [the longest x7 80.4 us: matmul(): return jnp.dot(left, right, preferred_element_type=jnp.float32)]
    all_gather x9 -> x0, waiting for transfers between devices: 203 us -> none  [the longest x1 43.1 us: on_device(): grad_value_full = lax.all_gather(content_slope, 'tp', axis=1, tiled=True)]
    ppermute x0 -> x96, starting transfers between devices: none -> 110 us  [the longest x14 40 us: reduce(): moving = held[place] + lax.ppermute(moving, 'z', RING_DOWN)]
    reduce_sum x8 -> x2, other arithmetic: 56.5 us -> 0.7 us  [the longest x1 0.61 us: on_device(): loss = jnp.sum(totals[11]) / (2.0 * count * width)]
  transfers between devices with their start and end apart: 20 -> 96, of which waited for: 18 -> 41; matrix products, arithmetic and copies ran while one was open for 14% -> 11% of each run, Pallas kernels for 0% -> 16%
where the time goes in v1:
time: 783 us; the launch traced here: 774 us
  Pallas kernels  294 us (38%)
  waiting for transfers between devices  265 us (34%)
  starting transfers between devices  110 us (14%)
  other arithmetic  68.5 us (9%)
  local copies, waits for them, and re-layouts  30.9 us (4%)
    ppermute x21, waiting for transfers between devices, gather(): parts.append(lax.ppermute(parts[-1], 'z', RING_UP))  72.3 us
    pallas_call x7, Pallas kernels, weight_grad(): pl.pallas_call(functools.partial(weight_grad_kernel, order=order), grid_s...  63.6 us
    ppermute x14, waiting for transfers between devices, reduce(): held = wide(held[0]) + wide(lax.ppermute(held[1], axis, SWAP))  59.6 us
    pallas_call x1, Pallas kernels, middle_back(): pl.pallas_call(middle_back_kernel, grid_spec=pltpu.PrefetchScalarGridSpec...  42.3 us
    ppermute x14, waiting for transfers between devices, reduce(): moving = held[place] + lax.ppermute(moving, 'z', RING_DOWN)  42.1 us
    ppermute x14, starting transfers between devices, reduce(): moving = held[place] + lax.ppermute(moving, 'z', RING_DOWN)  40 us
    pallas_call x1, Pallas kernels, input_back(): pl.pallas_call(input_back_kernel, grid_spec=pltpu.PrefetchScalarGridSpec(...  37.1 us
    ppermute x14, waiting for transfers between devices, gather(): held = jnp.stack([held, lax.ppermute(held, axis, SWAP)])  33.2 us
  transfers between devices with their start and end apart: 96, of which 41 were waited for; matrix products, arithmetic and copies ran while one was open for 11% of the time, Pallas kernels for 16%

profile of v1, /device:TPU:0, one launch (start us, length us, event | category | flops | bytes accessed | tf_op | source)
XLA Modules:
  0.0 773.9 jit_solution(10617391858895170981)
XLA Ops:
  23.2 12.5 %collective-permute-done.30 = bf16[2,64,2048]{2,1,0:T(8,128)(2,1)S(1)} collective-permute-done((bf16[2,64,2048]{2,1,0:T(8,128)(2,1)S(1)}, bf16[2,64,2048]{2,1,0:T(8,128)(2,1)S(1)}, u32[]{:S(2)}, u32[]{:S(2)}) %collective-permute-start.30) | collective-permute-done | bytes 524320 | tf_op jit(solution)/shard_map/ppermute | solution.py:844
  37.4 9.5 %collective-permute-done.37 = bf16[2,64,2048]{2,1,0:T(8,128)(2,1)S(1)} collective-permute-done((bf16[2,64,2048]{2,1,0:T(8,128)(2,1)S(1)}, bf16[2,64,2048]{2,1,0:T(8,128)(2,1)S(1)}, u32[]{:S(2)}, u32[]{:S(2)}) %collective-permute-start.37) | collective-permute-done | bytes 524320 | tf_op jit(solution)/shard_map/ppermute | solution.py:844
  46.9 11.3 %collective-permute-done.31 = bf16[2,64,2048]{2,1,0:T(8,128)(2,1)} collective-permute-done((bf16[2,64,2048]{2,1,0:T(8,128)(2,1)S(1)}, bf16[2,64,2048]{2,1,0:T(8,128)(2,1)}, u32[]{:S(2)}, u32[]{:S(2)}) %collective-permute-start.31) | collective-permute-done | bytes 524320 | tf_op jit(solution)/shard_map/ppermute | solution.py:844
  59.9 9.5 %collective-permute-done.38 = bf16[2,64,2048]{2,1,0:T(8,128)(2,1)S(1)} collective-permute-done((bf16[2,64,2048]{2,1,0:T(8,128)(2,1)S(1)}, bf16[2,64,2048]{2,1,0:T(8,128)(2,1)S(1)}, u32[]{:S(2)}, u32[]{:S(2)}) %collective-permute-start.38) | collective-permute-done | bytes 524320 | tf_op jit(solution)/shard_map/ppermute | solution.py:844
  69.4 11.3 %collective-permute-done.32 = bf16[2,64,2048]{2,1,0:T(8,128)(2,1)} collective-permute-done((bf16[2,64,2048]{2,1,0:T(8,128)(2,1)}, bf16[2,64,2048]{2,1,0:T(8,128)(2,1)}, u32[]{:S(2)}, u32[]{:S(2)}) %collective-permute-start.32) | collective-permute-done | bytes 524320 | tf_op jit(solution)/shard_map/ppermute | solution.py:844
  98.3 31.6 %collective-permute-done.1 = f32[16,1024]{1,0:T(8,128)S(1)} collective-permute-done((f32[16,1024]{1,0:T(8,128)S(1)}, f32[16,1024]{1,0:T(8,128)S(1)}, u32[]{:S(2)}, u32[]{:S(2)}) %collective-permute-start.1) | collective-permute-done | bytes 65568 | tf_op jit(solution)/shard_map/ppermute | solution.py:865
  178.7 4.2 collective-permute-done.4
  199.2 14.0 %collective-permute-done.15 = bf16[4,2,64,512]{3,2,1,0:T(8,128)(2,1)S(1)} collective-permute-done((bf16[4,2,64,512]{3,2,1,0:T(8,128)(2,1)S(1)}, bf16[4,2,64,512]{3,2,1,0:T(8,128)(2,1)S(1)}, u32[]{:S(2)}, u32[]{:S(2)}) %collective-permute-start.15) | collective-permute-done | bytes 524320 | tf_op jit(solution)/shard_map/ppermute | solution.py:847
  219.2 5.2 collective-permute-done.21
  226.0 6.2 collective-permute-done.46
  238.4 14.4 %shard_map.364 = (bf16[1024,1024]{1,0:T(8,128)(2,1)}, bf16[1024,1024]{1,0:T(8,128)(2,1)}, bf16[1024,1024]{1,0:T(8,128)(2,1)}) custom-call(bf16[1024,1024]{1,0:T(8,128)(2,1)} %x_ref.5, f32[1024,1]{1,0:T(8,128)} %copy.92.carry_ref, f32[16,1024]{1,0:T(8,128)} %copy-done.27), custom_call_target="tpu_custom_call" | custom-call | bytes 8388608 | tf_op jit(solution)/shard_map/pallas_call | solution.py:133
  260.5 30.3 %shard_map.365 = (f32[1024,1024]{1,0:T(8,128)}, f32[1024,1024]{1,0:T(8,128)}, f32[1024,1024]{1,0:T(8,128)}, f32[1024,1024]{1,0:T(8,128)}, f32[1024,1024]{1,0:T(8,128)}, /*index=5*/bf16[1024,1024]{1,0:T(8,128)(2,1)}) custom-call(s32[4]{0:T(128)} %pad_add_fusion.co, bf16[1024,1024]{1,0:T(8,128)(2,1)} %get-tuple-element.63.mk.model_ref, ...), custom_call_target="tpu_custom_call" | custom-call | flops 17179869184 | bytes 35651584 | tf_op jit(solution)/shard_map/pallas_call | solution.py:232
  291.8 16.8 %shard_map.366 = (f32[1024,1024]{1,0:T(8,128)}, bf16[1024,1024]{1,0:T(8,128)(2,1)}, bf16[1024,1024]{1,0:T(8,128)(2,1)}) custom-call(s32[4]{0:T(128)} %pad_add_fusion.co, bf16[1024,1024]{1,0:T(8,128)(2,1)} %get-tuple-element.66.gated.chan_ref, bf16[1024,1024]{1,0:T(8,128)(2,1)} %x_ref.5, f32[1024,1]{1,0:T(8,128)} %copy.92.carry_ref, f32[16,1024]{1,0:T(8,128)} %copy-done.27, ...), custom_call_target="tpu_custom_call" | custom-call | flops 6442450944 | bytes 14680064 | tf_op jit(solution)/shard_map/pallas_call | solution.py:289
  308.6 17.9 %shard_map.367 = (bf16[1024,4096]{1,0:T(8,128)(2,1)}, bf16[1024,4096]{1,0:T(8,128)(2,1)}) custom-call(s32[4]{0:T(128)} %pad_add_fusion.co, bf16[1024,1024]{1,0:T(8,128)(2,1)} %get-tuple-element.67.mk.model_ref, bf16[2,4,2,64,2048]{4,3,2,1,0:T(8,128)(2,1)} %pad_maximum_fusion.wo, bf16[2,4,2,64,2048]{4,3,2,1,0:T(8,128)(2,1)} %collective-permute-done.34.wx), custom_call_target="tpu_custom_call" | custom-call | flops 9663676416 | bytes 27262976 | tf_op jit(solution)/shard_map/pallas_call | solution.py:347
  327.5 27.3 %shard_map.368 = (bf16[1024,1024]{1,0:T(8,128)(2,1)}, f32[1024,1024]{1,0:T(8,128)}, bf16[1024,1024]{1,0:T(8,128)(2,1)}, bf16[1024,1024]{1,0:T(8,128)(2,1)}, f32[8,1024]{1,0:T(8,128)}) custom-call(s32[4]{0:T(128)} %pad_add_fusion.co, f32[1]{0:T(128)} %bitcast.15.scale, bf16[1024,4096]{1,0:T(8,128)(2,1)} %get-tuple-element.68.hidden.chan_ref, ...), custom_call_target="tpu_custom_call" | custom-call | flops 15032385536 | bytes 39845888 | tf_op jit(solution)/shard_map/pallas_call | solution.py:417
  354.8 18.2 %shard_map.369.dkey.chan_ref = bf16[1024,4096]{1,0:T(8,128)(2,1)} custom-call(s32[4]{0:T(128)} %pad_add_fusion.co, bf16[1024,1024]{1,0:T(8,128)(2,1)} %get-tuple-element.72.dkv.model_ref, bf16[1024,4096]{1,0:T(8,128)(2,1)} %get-tuple-element.73.active_ref, bf16[2,4,2,64,2048]{4,3,2,1,0:T(8,128)(2,1)} %pad_maximum_fusion.1.wo, ...), custom_call_target="tpu_custom_call" | custom-call | flops 9663676416 | bytes 27262976 | tf_op jit(solution)/shard_map/pallas_call | solution.py:531
  373.0 15.4 %shard_map.377 = (bf16[2,4,2,64,2048]{4,3,2,1,0:T(8,128)(2,1)}, bf16[2,4,2,64,2048]{4,3,2,1,0:T(8,128)(2,1)}) custom-call(s32[4]{0:T(128)} %pad_add_fusion.co, bf16[1024,1024]{1,0:T(8,128)(2,1)} %get-tuple-element.67.mk.model_ref, bf16[1024,4096]{1,0:T(8,128)(2,1)} %shard_map.369.dkey.chan_ref), custom_call_target="tpu_custom_call" | custom-call | flops 10307921920 | bytes 18874368 | tf_op jit(solution)/shard_map/pallas_call | solution.py:486
  388.4 42.3 %shard_map.370 = (f32[1024,1024]{1,0:T(8,128)}, bf16[1024,1024]{1,0:T(8,128)(2,1)}, f32[4,8,1024]{2,1,0:T(8,128)}) custom-call(s32[4]{0:T(128)} %pad_add_fusion.co, bf16[1024,4096]{1,0:T(8,128)(2,1)} %shard_map.369.dkey.chan_ref, bf16[1024,1024]{1,0:T(8,128)(2,1)} %get-tuple-element.74.drec.chan_ref, f32[1024,1024]{1,0:T(8,128)} %get-tuple-element.70.middle_ref, ...), custom_call_target="tpu_custom_call" | custom-call | flops 17179869184 | bytes 37748736 | tf_op jit(solution)/shard_map/pallas_call | solution.py:607
  430.7 25.9 %shard_map.371 = (bf16[1024,1024]{1,0:T(8,128)(2,1)}, bf16[1024,1024]{1,0:T(8,128)(2,1)}, bf16[1024,1024]{1,0:T(8,128)(2,1)}, f32[2,8,1024]{2,1,0:T(8,128)}) custom-call(s32[4]{0:T(128)} %pad_add_fusion.co, bf16[1024,1024]{1,0:T(8,128)(2,1)} %get-tuple-element.76.dtime.model_ref, f32[1024,1024]{1,0:T(8,128)} %get-tuple-element.77.key_ref, ...), custom_call_target="tpu_custom_call" | custom-call | flops 19327352832 | bytes 35651584 | tf_op jit(solution)/shard_map/pallas_call | solution.py:721
  456.6 37.1 %shard_map.372 = (f32[1024,1024]{1,0:T(8,128)}, f32[5,8,1024]{2,1,0:T(8,128)}) custom-call(s32[4]{0:T(128)} %pad_add_fusion.co, bf16[1024,1024]{1,0:T(8,128)(2,1)} %get-tuple-element.82.dkey.chan_ref, bf16[1024,1024]{1,0:T(8,128)(2,1)} %get-tuple-element.83.dval.chan_ref, bf16[1024,1024]{1,0:T(8,128)(2,1)} %get-tuple-element.84.drec.chan_ref, ...), custom_call_target="tpu_custom_call" | custom-call | flops 15032385536 | bytes 27262976 | tf_op jit(solution)/shard_map/pallas_call | solution.py:804
  496.2 6.5 shard_map.373
  503.6 6.5 shard_map.374
  510.2 6.5 shard_map.375
  517.4 6.5 shard_map.376
  526.3 6.7 shard_map.378
  534.2 15.5 %shard_map.379 = (bf16[2,4,2,64,2048]{4,3,2,1,0:T(8,128)(2,1)}, bf16[2,4,2,64,2048]{4,3,2,1,0:T(8,128)(2,1)}) custom-call(s32[4]{0:T(128)} %pad_add_fusion.co, bf16[1024,1024]{1,0:T(8,128)(2,1)} %get-tuple-element.72.dkv.model_ref, bf16[1024,4096]{1,0:T(8,128)(2,1)} %get-tuple-element.68.hidden.chan_ref), custom_call_target="tpu_custom_call" | custom-call | flops 10307921920 | bytes 18874368 | tf_op jit(solution)/shard_map/pallas_call | solution.py:486
  564.1 13.7 %collective-permute-done.48 = bf16[1024,512]{1,0:T(8,128)(2,1)} collective-permute-done((bf16[1024,512]{1,0:T(8,128)(2,1)}, bf16[1024,512]{1,0:T(8,128)(2,1)}, u32[]{:S(2)}, u32[]{:S(2)}) %collective-permute-start.48) | collective-permute-done | bytes 1048608 | tf_op jit(solution)/shard_map/ppermute | solution.py:1034
  582.8 6.1 collective-permute-done.61
  589.9 10.3 %collective-permute-done.67 = bf16[2,4,64,512]{3,2,1,0:T(8,128)(2,1)S(1)} collective-permute-done((bf16[2,4,64,512]{3,2,1,0:T(8,128)(2,1)S(1)}, bf16[2,4,64,512]{3,2,1,0:T(8,128)(2,1)S(1)}, u32[]{:S(2)}, u32[]{:S(2)}) %collective-permute-start.67) | collective-permute-done | bytes 524320 | tf_op jit(solution)/shard_map/ppermute | solution.py:860
  602.5 8.4 %collective-permute-done.85 = bf16[2,4,64,512]{3,2,1,0:T(8,128)(2,1)S(1)} collective-permute-done((bf16[2,4,64,512]{3,2,1,0:T(8,128)(2,1)S(1)}, bf16[2,4,64,512]{3,2,1,0:T(8,128)(2,1)S(1)}, u32[]{:S(2)}, u32[]{:S(2)}) %collective-permute-start.85) | collective-permute-done | bytes 524320 | tf_op jit(solution)/shard_map/ppermute | solution.py:860
  618.1 4.2 collective-permute-start.63
  625.1 4.3 collective-permute-start.58
  631.2 4.2 collective-permute-start.69
  637.5 4.3 collective-permute-start.75
  643.7 4.2 collective-permute-start.87
  650.3 4.3 collective-permute-start.70
  671.1 28.1 %collective-permute-done.65 = bf16[64,512]{1,0:T(8,128)(2,1)} collective-permute-done((bf16[64,512]{1,0:T(8,128)(2,1)S(1)}, bf16[64,512]{1,0:T(8,128)(2,1)}, u32[]{:S(2)}, u32[]{:S(2)}) %collective-permute-start.65) | collective-permute-done | bytes 65568 | tf_op jit(solution)/shard_map/ppermute | solution.py:860
  702.0 4.1 collective-permute-start.80
  706.8 11.7 %collective-permute-done.80 = bf16[2,64,2048]{2,1,0:T(8,128)(2,1)S(1)} collective-permute-done((bf16[2,64,2048]{2,1,0:T(8,128)(2,1)S(1)}, bf16[2,64,2048]{2,1,0:T(8,128)(2,1)S(1)}, u32[]{:S(2)}, u32[]{:S(2)}) %collective-permute-start.80) | collective-permute-done | bytes 524320 | tf_op jit(solution)/shard_map/ppermute | solution.py:857
  718.6 4.3 collective-permute-start.81
  723.6 6.2 collective-permute-done.92
  729.8 4.3 collective-permute-start.93
  734.1 6.8 collective-permute-done.81
  741.0 4.3 collective-permute-start.82
  746.1 6.2 collective-permute-done.93
  752.3 4.3 collective-permute-start.94
  760.0 5.0 collective-permute-done.94
  766.8 4.7 collective-permute-done.95
  (465 shorter events, 204.8 us)
Async XLA Ops:
  5.9 80.2 %collective-permute-start = (f32[16,1024]{1,0:T(8,128)}, f32[16,1024]{1,0:T(8,128)}, u32[]{:S(2)}, u32[]{:S(2)}) collective-permute-start(f32[16,1024]{1,0:T(8,128)} %maximum_maximum_fusion), channel_id=1, source_target_pairs={{0,1},{1,0},{2,3},{3,2},{4,5},{5,4},{6,7},{7,6},{8,9},{9,8},{10,11... | collective-permute-start | bytes 196616 | tf_op jit(solution)/shard_map/ppermute | solution.py:865
  8.8 86.7 %collective-permute-start.5 = (bf16[64,512]{1,0:T(8,128)(2,1)}, bf16[64,512]{1,0:T(8,128)(2,1)}, u32[]{:S(2)}, u32[]{:S(2)}) collective-permute-start(bf16[64,512]{1,0:T(8,128)(2,1)} %param.31), channel_id=1, source_target_pairs={{0,1},{1,0},{2,3},{3,2},{4,5},{5,4},{6,7},{7,6},{8,9},{9,8},{10,11... | collective-permute-start | bytes 196616 | tf_op jit(solution)/shard_map/ppermute | solution.py:847
  8.8 88.1 %collective-permute-start.11 = (bf16[64,512]{1,0:T(8,128)(2,1)}, bf16[64,512]{1,0:T(8,128)(2,1)}, u32[]{:S(2)}, u32[]{:S(2)}) collective-permute-start(bf16[64,512]{1,0:T(8,128)(2,1)} %param.32), channel_id=1, source_target_pairs={{0,4},{4,0},{1,5},{5,1},{2,6},{6,2},{3,7},{7,3},{8,12},{12,8},{9,1... | collective-permute-start | bytes 196616 | tf_op jit(solution)/shard_map/ppermute | solution.py:847
  21.5 25.4 %collective-permute-start.37 = (bf16[2,64,2048]{2,1,0:T(8,128)(2,1)S(1)}, bf16[2,64,2048]{2,1,0:T(8,128)(2,1)S(1)}, u32[]{:S(2)}, u32[]{:S(2)}) collective-permute-start(bf16[2,64,2048]{2,1,0:T(8,128)(2,1)S(1)} %get-tuple-element.122), channel_id=1, source_target_pairs={{0,8},{8,16},{16,24},{24,0},{1,9},{9,17},{17,25},{25,1},{2,10},{10... | collective-permute-start | bytes 1572872 | tf_op jit(solution)/shard_map/ppermute | solution.py:844
  35.7 22.6 %collective-permute-start.31 = (bf16[2,64,2048]{2,1,0:T(8,128)(2,1)S(1)}, bf16[2,64,2048]{2,1,0:T(8,128)(2,1)}, u32[]{:S(2)}, u32[]{:S(2)}) collective-permute-start(bf16[2,64,2048]{2,1,0:T(8,128)(2,1)S(1)} %collective-permute-done.30), channel_id=1, source_target_pairs={{0,8},{8,16},{16,24},{24,0},{1,9},{9,17},{17,25},{25,1},{2,10},{10... | collective-permute-start | bytes 1572872 | tf_op jit(solution)/shard_map/ppermute | solution.py:844
  46.9 22.5 %collective-permute-start.38 = (bf16[2,64,2048]{2,1,0:T(8,128)(2,1)S(1)}, bf16[2,64,2048]{2,1,0:T(8,128)(2,1)S(1)}, u32[]{:S(2)}, u32[]{:S(2)}) collective-permute-start(bf16[2,64,2048]{2,1,0:T(8,128)(2,1)S(1)} %collective-permute-done.37), channel_id=1, source_target_pairs={{0,8},{8,16},{16,24},{24,0},{1,9},{9,17},{17,25},{25,1},{2,10},{10... | collective-permute-start | bytes 1572872 | tf_op jit(solution)/shard_map/ppermute | solution.py:844
  58.3 22.5 %collective-permute-start.32 = (bf16[2,64,2048]{2,1,0:T(8,128)(2,1)}, bf16[2,64,2048]{2,1,0:T(8,128)(2,1)}, u32[]{:S(2)}, u32[]{:S(2)}) collective-permute-start(bf16[2,64,2048]{2,1,0:T(8,128)(2,1)} %collective-permute-done.31), channel_id=1, source_target_pairs={{0,8},{8,16},{16,24},{24,0},{1,9},{9,17},{17,25},{25,1},{2,10},{10... | collective-permute-start | bytes 1572872 | tf_op jit(solution)/shard_map/ppermute | solution.py:844
  69.4 21.0 %collective-permute-start.39 = (bf16[2,64,2048]{2,1,0:T(8,128)(2,1)S(1)}, bf16[2,64,2048]{2,1,0:T(8,128)(2,1)}, u32[]{:S(2)}, u32[]{:S(2)}) collective-permute-start(bf16[2,64,2048]{2,1,0:T(8,128)(2,1)S(1)} %collective-permute-done.38), channel_id=1, source_target_pairs={{0,8},{8,16},{16,24},{24,0},{1,9},{9,17},{17,25},{25,1},{2,10},{10... | collective-permute-start | bytes 1572872 | tf_op jit(solution)/shard_map/ppermute | solution.py:844
  84.3 100.6 %collective-permute-start.33 = (bf16[4,2,64,2048]{3,2,1,0:T(8,128)(2,1)}, bf16[4,2,64,2048]{3,2,1,0:T(8,128)(2,1)}, u32[]{:S(2)}, u32[]{:S(2)}) collective-permute-start(bf16[4,2,64,2048]{3,2,1,0:T(8,128)(2,1)} %get-tuple-element.118), channel_id=1, source_target_pairs={{0,4},{4,0},{1,5},{5,1},{2,6},{6,2},{3,7},{7,3},{8,12},{12,8},{9,1... | collective-permute-start | bytes 6291464 | tf_op jit(solution)/shard_map/ppermute | solution.py:847
  90.4 39.5 %collective-permute-start.1 = (f32[16,1024]{1,0:T(8,128)S(1)}, f32[16,1024]{1,0:T(8,128)S(1)}, u32[]{:S(2)}, u32[]{:S(2)}) collective-permute-start(f32[16,1024]{1,0:T(8,128)S(1)} %fusion.60), channel_id=1, source_target_pairs={{0,4},{4,0},{1,5},{5,1},{2,6},{6,2},{3,7},{7,3},{8,12},{12,8},{9,1... | collective-permute-start | bytes 196616 | tf_op jit(solution)/shard_map/ppermute | solution.py:865
  95.6 118.3 %collective-permute-start.40 = (bf16[4,2,64,2048]{3,2,1,0:T(8,128)(2,1)}, bf16[4,2,64,2048]{3,2,1,0:T(8,128)(2,1)}, u32[]{:S(2)}, u32[]{:S(2)}) collective-permute-start(bf16[4,2,64,2048]{3,2,1,0:T(8,128)(2,1)} %get-tuple-element.114), channel_id=1, source_target_pairs={{0,1},{1,0},{2,3},{3,2},{4,5},{5,4},{6,7},{7,6},{8,9},{9,8},{10,11... | collective-permute-start | bytes 6291464 | tf_op jit(solution)/shard_map/ppermute | solution.py:847
  97.0 34.5 %collective-permute-start.23 = (bf16[64,512]{1,0:T(8,128)(2,1)S(1)}, bf16[64,512]{1,0:T(8,128)(2,1)S(1)}, u32[]{:S(2)}, u32[]{:S(2)}) collective-permute-start(bf16[64,512]{1,0:T(8,128)(2,1)S(1)} %bitcast.368), channel_id=1, source_target_pairs={{0,8},{8,16},{16,24},{24,0},{1,9},{9,17},{17,25},{25,1},{2,10},{10... | collective-permute-start | bytes 196616 | tf_op jit(solution)/shard_map/ppermute | solution.py:844
  97.0 35.7 %collective-permute-start.42 = (bf16[64,512]{1,0:T(8,128)(2,1)S(1)}, bf16[64,512]{1,0:T(8,128)(2,1)S(1)}, u32[]{:S(2)}, u32[]{:S(2)}) collective-permute-start(bf16[64,512]{1,0:T(8,128)(2,1)S(1)} %copy-done.33), channel_id=1, source_target_pairs={{0,8},{8,16},{16,24},{24,0},{1,9},{9,17},{17,25},{25,1},{2,10},{10... | collective-permute-start | bytes 196616 | tf_op jit(solution)/shard_map/ppermute | solution.py:844
  172.7 59.5 %collective-permute-start.35 = (bf16[1024,512]{1,0:T(8,128)(2,1)S(1)}, bf16[1024,512]{1,0:T(8,128)(2,1)S(1)}, u32[]{:S(2)}, u32[]{:S(2)}) collective-permute-start(bf16[1024,512]{1,0:T(8,128)(2,1)S(1)} %copy-done.6), channel_id=1, source_target_pairs={{0,1},{1,0},{2,3},{3,2},{4,5},{5,4},{6,7},{7,6},{8,9},{9,8},{10,11... | collective-permute-start | bytes 3145736 | tf_op jit(solution)/shard_map/ppermute | solution.py:1013
  184.9 28.3 %collective-permute-start.15 = (bf16[4,2,64,512]{3,2,1,0:T(8,128)(2,1)S(1)}, bf16[4,2,64,512]{3,2,1,0:T(8,128)(2,1)S(1)}, u32[]{:S(2)}, u32[]{:S(2)}) collective-permute-start(bf16[4,2,64,512]{3,2,1,0:T(8,128)(2,1)S(1)} %get-tuple-element.130), channel_id=1, source_target_pairs={{0,1},{1,0},{2,3},{3,2},{4,5},{5,4},{6,7},{7,6},{8,9},{9,8},{10,11... | collective-permute-start | bytes 1572872 | tf_op jit(solution)/shard_map/ppermute | solution.py:847
  191.9 116.6 %collective-permute-start.34 = (bf16[2,4,2,64,2048]{4,3,2,1,0:T(8,128)(2,1)}, bf16[2,4,2,64,2048]{4,3,2,1,0:T(8,128)(2,1)}, u32[]{:S(2)}, u32[]{:S(2)}) collective-permute-start(bf16[2,4,2,64,2048]{4,3,2,1,0:T(8,128)(2,1)} %pad_maximum_fusion.wo), channel_id=1, source_target_pairs={{0,2},{2,0},{1,3},{3,1},{4,6},{6,4},{5,7},{7,5},{8,10},{10,8},{9,1... | collective-permute-start | bytes 12582920 | tf_op jit(solution)/shard_map/ppermute | solution.py:848
  197.6 26.8 %collective-permute-start.21 = (bf16[2,4,64,512]{3,2,1,0:T(8,128)(2,1)S(1)}, bf16[2,4,64,512]{3,2,1,0:T(8,128)(2,1)S(1)}, u32[]{:S(2)}, u32[]{:S(2)}) collective-permute-start(bf16[2,4,64,512]{3,2,1,0:T(8,128)(2,1)S(1)} %get-tuple-element.128), channel_id=1, source_target_pairs={{0,1},{1,0},{2,3},{3,2},{4,5},{5,4},{6,7},{7,6},{8,9},{9,8},{10,11... | collective-permute-start | bytes 1572872 | tf_op jit(solution)/shard_map/ppermute | solution.py:847
  224.4 102.2 %collective-permute-start.41 = (bf16[2,4,2,64,2048]{4,3,2,1,0:T(8,128)(2,1)}, bf16[2,4,2,64,2048]{4,3,2,1,0:T(8,128)(2,1)}, u32[]{:S(2)}, u32[]{:S(2)}) collective-permute-start(bf16[2,4,2,64,2048]{4,3,2,1,0:T(8,128)(2,1)} %pad_maximum_fusion.1.wo), channel_id=1, source_target_pairs={{0,2},{2,0},{1,3},{3,1},{4,6},{6,4},{5,7},{7,5},{8,10},{10,8},{9,1... | collective-permute-start | bytes 12582920 | tf_op jit(solution)/shard_map/ppermute | solution.py:848
  225.5 31.0 %collective-permute-start.10 = (bf16[2,4,2,64,512]{4,3,2,1,0:T(8,128)(2,1)}, bf16[2,4,2,64,512]{4,3,2,1,0:T(8,128)(2,1)}, u32[]{:S(2)}, u32[]{:S(2)}) collective-permute-start(bf16[2,4,2,64,512]{4,3,2,1,0:T(8,128)(2,1)} %pad_maximum_fusion.4.ko), channel_id=1, source_target_pairs={{0,2},{2,0},{1,3},{3,1},{4,6},{6,4},{5,7},{7,5},{8,10},{10,8},{9,1... | collective-permute-start | bytes 3145736 | tf_op jit(solution)/shard_map/ppermute | solution.py:848
  232.2 24.3 %collective-permute-start.16 = (bf16[2,4,2,64,512]{4,3,2,1,0:T(8,128)(2,1)}, bf16[2,4,2,64,512]{4,3,2,1,0:T(8,128)(2,1)}, u32[]{:S(2)}, u32[]{:S(2)}) collective-permute-start(bf16[2,4,2,64,512]{4,3,2,1,0:T(8,128)(2,1)} %pad_maximum_fusion.5.vo), channel_id=1, source_target_pairs={{0,2},{2,0},{1,3},{3,1},{4,6},{6,4},{5,7},{7,5},{8,10},{10,8},{9,1... | collective-permute-start | bytes 3145736 | tf_op jit(solution)/shard_map/ppermute | solution.py:848
  233.2 23.8 %collective-permute-start.22 = (bf16[2,2,4,64,512]{4,3,2,1,0:T(8,128)(2,1)}, bf16[2,2,4,64,512]{4,3,2,1,0:T(8,128)(2,1)}, u32[]{:S(2)}, u32[]{:S(2)}) collective-permute-start(bf16[2,2,4,64,512]{4,3,2,1,0:T(8,128)(2,1)} %pad_maximum_fusion.6.ro), channel_id=1, source_target_pairs={{0,2},{2,0},{1,3},{3,1},{4,6},{6,4},{5,7},{7,5},{8,10},{10,8},{9,1... | collective-permute-start | bytes 3145736 | tf_op jit(solution)/shard_map/ppermute | solution.py:848
  256.5 34.3 %collective-permute-start.28 = (bf16[2,2,4,64,512]{4,3,2,1,0:T(8,128)(2,1)S(1)}, bf16[2,2,4,64,512]{4,3,2,1,0:T(8,128)(2,1)S(1)}, u32[]{:S(2)}, u32[]{:S(2)}) collective-permute-start(bf16[2,2,4,64,512]{4,3,2,1,0:T(8,128)(2,1)S(1)} %pad_maximum_fusion.7.oo), channel_id=1, source_target_pairs={{0,2},{2,0},{1,3},{3,1},{4,6},{6,4},{5,7},{7,5},{8,10},{10,8},{9,1... | collective-permute-start | bytes 3145736 | tf_op jit(solution)/shard_map/ppermute | solution.py:848
  256.5 70.0 %collective-permute-start.47 = (bf16[2,2,4,64,512]{4,3,2,1,0:T(8,128)(2,1)S(1)}, bf16[2,2,4,64,512]{4,3,2,1,0:T(8,128)(2,1)S(1)}, u32[]{:S(2)}, u32[]{:S(2)}) collective-permute-start(bf16[2,2,4,64,512]{4,3,2,1,0:T(8,128)(2,1)S(1)} %pad_maximum_fusion.8.ro), channel_id=1, source_target_pairs={{0,2},{2,0},{1,3},{3,1},{4,6},{6,4},{5,7},{7,5},{8,10},{10,8},{9,1... | collective-permute-start | bytes 3145736 | tf_op jit(solution)/shard_map/ppermute | solution.py:848
  533.0 18.5 %collective-permute-start.54 = (bf16[2,4,2,64,512]{4,3,2,1,0:T(8,128)(2,1)}, bf16[2,4,2,64,512]{4,3,2,1,0:T(8,128)(2,1)}, u32[]{:S(2)}, u32[]{:S(2)}) collective-permute-start(bf16[2,4,2,64,512]{4,3,2,1,0:T(8,128)(2,1)} %get-tuple-element.92), channel_id=1, source_target_pairs={{0,2},{2,0},{1,3},{3,1},{4,6},{6,4},{5,7},{7,5},{8,10},{10,8},{9,1... | collective-permute-start | bytes 3145736 | tf_op jit(solution)/shard_map/ppermute | solution.py:851
  533.1 22.2 %collective-permute-start.60 = (bf16[2,4,2,64,512]{4,3,2,1,0:T(8,128)(2,1)}, bf16[2,4,2,64,512]{4,3,2,1,0:T(8,128)(2,1)}, u32[]{:S(2)}, u32[]{:S(2)}) collective-permute-start(bf16[2,4,2,64,512]{4,3,2,1,0:T(8,128)(2,1)} %get-tuple-element.94), channel_id=1, source_target_pairs={{0,2},{2,0},{1,3},{3,1},{4,6},{6,4},{5,7},{7,5},{8,10},{10,8},{9,1... | collective-permute-start | bytes 3145736 | tf_op jit(solution)/shard_map/ppermute | solution.py:851
  533.6 23.6 %collective-permute-start.66 = (bf16[2,2,4,64,512]{4,3,2,1,0:T(8,128)(2,1)}, bf16[2,2,4,64,512]{4,3,2,1,0:T(8,128)(2,1)}, u32[]{:S(2)}, u32[]{:S(2)}) collective-permute-start(bf16[2,2,4,64,512]{4,3,2,1,0:T(8,128)(2,1)} %get-tuple-element.96), channel_id=1, source_target_pairs={{0,2},{2,0},{1,3},{3,1},{4,6},{6,4},{5,7},{7,5},{8,10},{10,8},{9,1... | collective-permute-start | bytes 3145736 | tf_op jit(solution)/shard_map/ppermute | solution.py:851
  533.7 25.5 %collective-permute-start.72 = (bf16[2,2,4,64,512]{4,3,2,1,0:T(8,128)(2,1)}, bf16[2,2,4,64,512]{4,3,2,1,0:T(8,128)(2,1)}, u32[]{:S(2)}, u32[]{:S(2)}) collective-permute-start(bf16[2,2,4,64,512]{4,3,2,1,0:T(8,128)(2,1)} %get-tuple-element.98), channel_id=1, source_target_pairs={{0,2},{2,0},{1,3},{3,1},{4,6},{6,4},{5,7},{7,5},{8,10},{10,8},{9,1... | collective-permute-start | bytes 3145736 | tf_op jit(solution)/shard_map/ppermute | solution.py:851
  534.1 27.3 %collective-permute-start.84 = (bf16[2,2,4,64,512]{4,3,2,1,0:T(8,128)(2,1)}, bf16[2,2,4,64,512]{4,3,2,1,0:T(8,128)(2,1)}, u32[]{:S(2)}, u32[]{:S(2)}) collective-permute-start(bf16[2,2,4,64,512]{4,3,2,1,0:T(8,128)(2,1)} %get-tuple-element.102), channel_id=1, source_target_pairs={{0,2},{2,0},{1,3},{3,1},{4,6},{6,4},{5,7},{7,5},{8,10},{10,8},{9,1... | collective-permute-start | bytes 3145736 | tf_op jit(solution)/shard_map/ppermute | solution.py:851
  551.5 26.3 %collective-permute-start.48 = (bf16[1024,512]{1,0:T(8,128)(2,1)}, bf16[1024,512]{1,0:T(8,128)(2,1)}, u32[]{:S(2)}, u32[]{:S(2)}) collective-permute-start(bf16[1024,512]{1,0:T(8,128)(2,1)} %get-tuple-element.112), channel_id=1, source_target_pairs={{0,1},{1,0},{2,3},{3,2},{4,5},{5,4},{6,7},{7,6},{8,9},{9,8},{10,11... | collective-permute-start | bytes 3145736 | tf_op jit(solution)/shard_map/ppermute | solution.py:1034
  555.3 99.7 %collective-permute-start.78 = (bf16[2,4,2,64,2048]{4,3,2,1,0:T(8,128)(2,1)}, bf16[2,4,2,64,2048]{4,3,2,1,0:T(8,128)(2,1)S(1)}, u32[]{:S(2)}, u32[]{:S(2)}) collective-permute-start(bf16[2,4,2,64,2048]{4,3,2,1,0:T(8,128)(2,1)} %get-tuple-element.100), channel_id=1, source_target_pairs={{0,2},{2,0},{1,3},{3,1},{4,6},{6,4},{5,7},{7,5},{8,10},{10,8},{9,1... | collective-permute-start | bytes 12582920 | tf_op jit(solution)/shard_map/ppermute | solution.py:851
  557.2 101.5 %collective-permute-start.90 = (bf16[2,4,2,64,2048]{4,3,2,1,0:T(8,128)(2,1)}, bf16[2,4,2,64,2048]{4,3,2,1,0:T(8,128)(2,1)S(1)}, u32[]{:S(2)}, u32[]{:S(2)}) collective-permute-start(bf16[2,4,2,64,2048]{4,3,2,1,0:T(8,128)(2,1)} %get-tuple-element.104), channel_id=1, source_target_pairs={{0,2},{2,0},{1,3},{3,1},{4,6},{6,4},{5,7},{7,5},{8,10},{10,8},{9,1... | collective-permute-start | bytes 12582920 | tf_op jit(solution)/shard_map/ppermute | solution.py:851
  559.2 23.0 %collective-permute-start.55 = (bf16[4,2,64,512]{3,2,1,0:T(8,128)(2,1)S(1)}, bf16[4,2,64,512]{3,2,1,0:T(8,128)(2,1)S(1)}, u32[]{:S(2)}, u32[]{:S(2)}) collective-permute-start(bf16[4,2,64,512]{3,2,1,0:T(8,128)(2,1)S(1)} %slice_bitcast_fusion.20), channel_id=1, source_target_pairs={{0,4},{4,0},{1,5},{5,1},{2,6},{6,2},{3,7},{7,3},{8,12},{12,8},{9,1... | collective-permute-start | bytes 1572872 | tf_op jit(solution)/shard_map/ppermute | solution.py:860
  561.4 27.5 %collective-permute-start.61 = (bf16[4,2,64,512]{3,2,1,0:T(8,128)(2,1)S(1)}, bf16[4,2,64,512]{3,2,1,0:T(8,128)(2,1)S(1)}, u32[]{:S(2)}, u32[]{:S(2)}) collective-permute-start(bf16[4,2,64,512]{3,2,1,0:T(8,128)(2,1)S(1)} %slice_bitcast_fusion.18), channel_id=1, source_target_pairs={{0,1},{1,0},{2,3},{3,2},{4,5},{5,4},{6,7},{7,6},{8,9},{9,8},{10,11... | collective-permute-start | bytes 1572872 | tf_op jit(solution)/shard_map/ppermute | solution.py:860
  577.8 22.4 %collective-permute-start.67 = (bf16[2,4,64,512]{3,2,1,0:T(8,128)(2,1)S(1)}, bf16[2,4,64,512]{3,2,1,0:T(8,128)(2,1)S(1)}, u32[]{:S(2)}, u32[]{:S(2)}) collective-permute-start(bf16[2,4,64,512]{3,2,1,0:T(8,128)(2,1)S(1)} %slice_bitcast_fusion.16), channel_id=1, source_target_pairs={{0,1},{1,0},{2,3},{3,2},{4,5},{5,4},{6,7},{7,6},{8,9},{9,8},{10,11... | collective-permute-start | bytes 1572872 | tf_op jit(solution)/shard_map/ppermute | solution.py:860
  582.2 19.6 %collective-permute-start.73 = (bf16[2,4,64,512]{3,2,1,0:T(8,128)(2,1)S(1)}, bf16[2,4,64,512]{3,2,1,0:T(8,128)(2,1)S(1)}, u32[]{:S(2)}, u32[]{:S(2)}) collective-permute-start(bf16[2,4,64,512]{3,2,1,0:T(8,128)(2,1)S(1)} %slice_bitcast_fusion.14), channel_id=1, source_target_pairs={{0,4},{4,0},{1,5},{5,1},{2,6},{6,2},{3,7},{7,3},{8,12},{12,8},{9,1... | collective-permute-start | bytes 1572872 | tf_op jit(solution)/shard_map/ppermute | solution.py:860
  588.9 22.0 %collective-permute-start.85 = (bf16[2,4,64,512]{3,2,1,0:T(8,128)(2,1)S(1)}, bf16[2,4,64,512]{3,2,1,0:T(8,128)(2,1)S(1)}, u32[]{:S(2)}, u32[]{:S(2)}) collective-permute-start(bf16[2,4,64,512]{3,2,1,0:T(8,128)(2,1)S(1)} %slice_bitcast_fusion.8), channel_id=1, source_target_pairs={{0,1},{1,0},{2,3},{3,2},{4,5},{5,4},{6,7},{7,6},{8,9},{9,8},{10,11... | collective-permute-start | bytes 1572872 | tf_op jit(solution)/shard_map/ppermute | solution.py:860
  625.1 29.5 %collective-permute-start.58 = (bf16[2,64,512]{2,1,0:T(8,128)(2,1)S(1)}, bf16[2,64,512]{2,1,0:T(8,128)(2,1)S(1)}, u32[]{:S(2)}, u32[]{:S(2)}) collective-permute-start(bf16[2,64,512]{2,1,0:T(8,128)(2,1)S(1)} %fusion.21), channel_id=1, source_target_pairs={{8,0},{16,8},{24,16},{0,24},{9,1},{17,9},{25,17},{1,25},{10,2},{18... | collective-permute-start | bytes 393224 | tf_op jit(solution)/shard_map/ppermute | solution.py:858
  629.4 25.3 %collective-permute-start.64 = (bf16[2,64,512]{2,1,0:T(8,128)(2,1)S(1)}, bf16[2,64,512]{2,1,0:T(8,128)(2,1)S(1)}, u32[]{:S(2)}, u32[]{:S(2)}) collective-permute-start(bf16[2,64,512]{2,1,0:T(8,128)(2,1)S(1)} %fusion.18), channel_id=1, source_target_pairs={{8,0},{16,8},{24,16},{0,24},{9,1},{17,9},{25,17},{1,25},{10,2},{18... | collective-permute-start | bytes 393224 | tf_op jit(solution)/shard_map/ppermute | solution.py:858
  657.6 44.1 %collective-permute-start.79 = (bf16[4,2,64,2048]{3,2,1,0:T(8,128)(2,1)S(1)}, bf16[4,2,64,2048]{3,2,1,0:T(8,128)(2,1)S(1)}, u32[]{:S(2)}, u32[]{:S(2)}) collective-permute-start(bf16[4,2,64,2048]{3,2,1,0:T(8,128)(2,1)S(1)} %slice_bitcast_fusion.2), channel_id=1, source_target_pairs={{0,4},{4,0},{1,5},{5,1},{2,6},{6,2},{3,7},{7,3},{8,12},{12,8},{9,1... | collective-permute-start | bytes 6291464 | tf_op jit(solution)/shard_map/ppermute | solution.py:860
  658.6 40.6 %collective-permute-start.65 = (bf16[64,512]{1,0:T(8,128)(2,1)S(1)}, bf16[64,512]{1,0:T(8,128)(2,1)}, u32[]{:S(2)}, u32[]{:S(2)}) collective-permute-start(bf16[64,512]{1,0:T(8,128)(2,1)S(1)} %slice_bitcast_fusion.52), channel_id=1, source_target_pairs={{0,4},{4,0},{1,5},{5,1},{2,6},{6,2},{3,7},{7,3},{8,12},{12,8},{9,1... | collective-permute-start | bytes 196616 | tf_op jit(solution)/shard_map/ppermute | solution.py:860
  662.9 43.2 %collective-permute-start.91 = (bf16[4,2,64,2048]{3,2,1,0:T(8,128)(2,1)S(1)}, bf16[4,2,64,2048]{3,2,1,0:T(8,128)(2,1)S(1)}, u32[]{:S(2)}, u32[]{:S(2)}) collective-permute-start(bf16[4,2,64,2048]{3,2,1,0:T(8,128)(2,1)S(1)} %slice_bitcast_fusion), channel_id=1, source_target_pairs={{0,1},{1,0},{2,3},{3,2},{4,5},{5,4},{6,7},{7,6},{8,9},{9,8},{10,11... | collective-permute-start | bytes 6291464 | tf_op jit(solution)/shard_map/ppermute | solution.py:860
  664.6 36.5 %collective-permute-start.71 = (bf16[64,512]{1,0:T(8,128)(2,1)S(1)}, bf16[64,512]{1,0:T(8,128)(2,1)S(1)}, u32[]{:S(2)}, u32[]{:S(2)}) collective-permute-start(bf16[64,512]{1,0:T(8,128)(2,1)S(1)} %fusion.29), channel_id=1, source_target_pairs={{8,0},{16,8},{24,16},{0,24},{9,1},{17,9},{25,17},{1,25},{10,2},{18... | collective-permute-start | bytes 196616 | tf_op jit(solution)/shard_map/ppermute | solution.py:858
  665.5 57.4 %collective-permute-start.77 = (bf16[64,512]{1,0:T(8,128)(2,1)S(1)}, bf16[64,512]{1,0:T(8,128)(2,1)S(1)}, u32[]{:S(2)}, u32[]{:S(2)}) collective-permute-start(bf16[64,512]{1,0:T(8,128)(2,1)S(1)} %fusion.27), channel_id=1, source_target_pairs={{8,0},{16,8},{24,16},{0,24},{9,1},{17,9},{25,17},{1,25},{10,2},{18... | collective-permute-start | bytes 196616 | tf_op jit(solution)/shard_map/ppermute | solution.py:858
  699.2 46.1 %collective-permute-start.89 = (bf16[64,512]{1,0:T(8,128)(2,1)S(1)}, bf16[64,512]{1,0:T(8,128)(2,1)S(1)}, u32[]{:S(2)}, u32[]{:S(2)}) collective-permute-start(bf16[64,512]{1,0:T(8,128)(2,1)S(1)} %fusion.25), channel_id=1, source_target_pairs={{8,0},{16,8},{24,16},{0,24},{9,1},{17,9},{25,17},{1,25},{10,2},{18... | collective-permute-start | bytes 196616 | tf_op jit(solution)/shard_map/ppermute | solution.py:858
  706.5 23.3 %collective-permute-start.92 = (bf16[2,64,2048]{2,1,0:T(8,128)(2,1)S(1)}, bf16[2,64,2048]{2,1,0:T(8,128)(2,1)S(1)}, u32[]{:S(2)}, u32[]{:S(2)}) collective-permute-start(bf16[2,64,2048]{2,1,0:T(8,128)(2,1)S(1)} %slice_bitcast_fusion.4), channel_id=1, source_target_pairs={{8,0},{16,8},{24,16},{0,24},{9,1},{17,9},{25,17},{1,25},{10,2},{18... | collective-permute-start | bytes 1572872 | tf_op jit(solution)/shard_map/ppermute | solution.py:857
  718.6 22.4 %collective-permute-start.81 = (bf16[2,64,2048]{2,1,0:T(8,128)(2,1)S(1)}, bf16[2,64,2048]{2,1,0:T(8,128)(2,1)S(1)}, u32[]{:S(2)}, u32[]{:S(2)}) collective-permute-start(bf16[2,64,2048]{2,1,0:T(8,128)(2,1)S(1)} %fusion.6), channel_id=1, source_target_pairs={{8,0},{16,8},{24,16},{0,24},{9,1},{17,9},{25,17},{1,25},{10,2},{18... | collective-permute-start | bytes 1572872 | tf_op jit(solution)/shard_map/ppermute | solution.py:857
  729.8 22.4 %collective-permute-start.93 = (bf16[2,64,2048]{2,1,0:T(8,128)(2,1)S(1)}, bf16[2,64,2048]{2,1,0:T(8,128)(2,1)S(1)}, u32[]{:S(2)}, u32[]{:S(2)}) collective-permute-start(bf16[2,64,2048]{2,1,0:T(8,128)(2,1)S(1)} %fusion.2), channel_id=1, source_target_pairs={{8,0},{16,8},{24,16},{0,24},{9,1},{17,9},{25,17},{1,25},{10,2},{18... | collective-permute-start | bytes 1572872 | tf_op jit(solution)/shard_map/ppermute | solution.py:857
  741.0 18.3 %collective-permute-start.82 = (bf16[2,64,2048]{2,1,0:T(8,128)(2,1)S(1)}, bf16[2,64,2048]{2,1,0:T(8,128)(2,1)S(1)}, u32[]{:S(2)}, u32[]{:S(2)}) collective-permute-start(bf16[2,64,2048]{2,1,0:T(8,128)(2,1)S(1)} %fusion.7), channel_id=1, source_target_pairs={{8,0},{16,8},{24,16},{0,24},{9,1},{17,9},{25,17},{1,25},{10,2},{18... | collective-permute-start | bytes 1572872 | tf_op jit(solution)/shard_map/ppermute | solution.py:858
  (103 other events, 1129.0 us)

commit v2 on v1

--- a/solution.py
+++ b/solution.py
@@ -1,5 +1,6 @@
 import functools
 import itertools
+import math
 
 import jax
 import jax.numpy as jnp
@@ -15,8 +16,7 @@
 SLOT = 64
 CHUNK = 16
 VMEM_LIMIT = 58 << 20
-SIZES = {"z": 4, "y": 2, "x": 2}
-EVERY = ("z", "y", "c", "x")
+EVERY = ("w", "u", "y", "c", "x")
 SWAP = [(0, 1), (1, 0)]
 
 NN = (((1,), (0,)), ((), ()))
@@ -28,27 +28,74 @@
     return lax.dot_general(left, right, dims, preferred_element_type=F32)
 
 
-def slot_list(order):
-    dims = order[::-1]
-    for index in itertools.product(*[range(SIZES[d]) for d in dims]):
-        yield index, dict(zip(dims, index))
-
-
-def slot_place(co, rel, other_core):
-    block = ((co[0] + 4 - rel["z"]) & 3) * 4 + (co[1] ^ rel["y"]) * 2 + (co[2] ^ other_core)
-    return pl.multiple_of(block * SLOT, SLOT), co[3] ^ rel["x"]
-
-
-def weight_copies(co, own, other, whole, sems, order):
+def rel_slots(order):
+    for other_core in (0, 1):
+        for last in (0, 1):
+            for index in itertools.product((0, 1), repeat=3):
+                rel = dict(zip(order[2::-1], index))
+                rel[order[3]] = last
+                rel["c"] = other_core
+                yield other_core * 2 + last, index, rel
+
+
+def slot_place(co, rel):
+    at = {axis: co[n] ^ rel[axis] for n, axis in enumerate(EVERY)}
+    block = at["w"] * 8 + at["u"] * 4 + at["y"] * 2 + at["c"]
+    return pl.multiple_of(block * SLOT, SLOT), at["x"]
+
+
+def weight_copies(co, refs, whole, sems, layout):
     copies = []
-    for other_core, source in ((0, own), (1, other)):
-        for index, rel in slot_list(order):
-            row, half = slot_place(co, rel, other_core)
-            copy = pltpu.make_async_copy(
-                source.at[index], whole.at[half, pl.ds(row, SLOT), :], sems.at[len(copies)]
-            )
-            copies.append((rel["x"], copy))
+    refs = list(refs)
+    for kind, order, first, columns in layout:
+        target = pl.ds(first, columns)
+        if kind == "rel":
+            arrays, refs = refs[:4], refs[4:]
+            for which, index, rel in rel_slots(order):
+                row, half = slot_place(co, rel)
+                copies.append(
+                    (
+                        rel["x"],
+                        pltpu.make_async_copy(
+                            arrays[which].at[index],
+                            whole.at[half, pl.ds(row, SLOT), target],
+                            sems.at[len(copies)],
+                        ),
+                    )
+                )
+        else:
+            array, refs = refs[0], refs[1:]
+            for rel_x in (0, 1):
+                half = co[4] ^ rel_x
+                for block in range(16):
+                    copies.append(
+                        (
+                            rel_x,
+                            pltpu.make_async_copy(
+                                array.at[block, half, :, pl.ds(order, columns)],
+                                whole.at[half, pl.ds(block * SLOT, SLOT), target],
+                                sems.at[len(copies)],
+                            ),
+                        )
+                    )
     return copies
+
+
+def take_refs(refs, layout):
+    count = sum(4 if part[0] == "rel" else 1 for part in layout)
+    return refs[:count], refs[count:]
+
+
+def arrays_of(*weights):
+    return [array for _, arrays in weights for array in arrays]
+
+
+def weight_width(weight):
+    return sum(part[3] for part in weight[0])
+
+
+def sem_count(weight):
+    return 32 * len(weight[0])
 
 
 def start_all(copies):
@@ -151,16 +198,17 @@
 
 
 def time_forward_kernel(
-    co, mk, mv, mr, ko, kx, vo, vx, ro, rx, vec, masks,
-    key_ref, val_ref, rec_ref, pa_ref, pb_ref, gated_ref, kw, vw, rw, sems,
+    co, mk, mv, mr, vec, masks, *refs, layouts,
 ):
+    key_w, refs = take_refs(refs, layouts[0])
+    val_w, refs = take_refs(refs, layouts[1])
+    rec_w, refs = take_refs(refs, layouts[2])
+    key_ref, val_ref, rec_ref, pa_ref, pb_ref, gated_ref, kw, vw, rw, sems = refs
     j = pl.program_id(0)
     per_half = kw.shape[2] // TILE
     groups = [
-        weight_copies(co, own, other, whole, sems.at[n], order)
-        for n, (own, other, whole, order) in enumerate(
-            ((ko, kx, kw, ORDERS[0]), (vo, vx, vw, ORDERS[1]), (ro, rx, rw, ORDERS[2]))
-        )
+        weight_copies(co, arrays, whole, sems.at[n], layout)
+        for n, (arrays, whole, layout) in enumerate(zip((key_w, val_w, rec_w), (kw, vw, rw), layouts))
     ]
 
     @pl.when(j == 0)
@@ -175,7 +223,7 @@
         for copies in groups:
             wait_half(copies, 1)
 
-    half = co[3] ^ lax.div(j, per_half)
+    half = co[4] ^ lax.div(j, per_half)
     columns = pl.ds(pl.multiple_of(lax.rem(j, per_half) * TILE, TILE), TILE)
     key_ref[...] = dot(mk[...], kw[half, :, columns], NN)
     val_ref[...] = dot(mv[...], vw[half, :, columns], NN)
@@ -225,21 +273,21 @@
     per_half = half // TILE
 
     def tile(j, co):
-        return 0, (co[3] ^ lax.div(j, per_half)) * per_half + lax.rem(j, per_half)
+        return 0, (co[4] ^ lax.div(j, per_half)) * per_half + lax.rem(j, per_half)
 
     fixed = pl.BlockSpec((tokens, width), lambda j, co: (0, 0))
     block = pl.BlockSpec((tokens, TILE), tile)
     return pl.pallas_call(
-        time_forward_kernel,
+        functools.partial(time_forward_kernel, layouts=[w[0] for w in weights]),
         grid_spec=pltpu.PrefetchScalarGridSpec(
             num_scalar_prefetch=1,
             grid=(width // TILE,),
             in_specs=[fixed] * 3
-            + [anywhere()] * 6
             + [
                 pl.BlockSpec((vectors.shape[0], TILE), tile),
                 pl.BlockSpec(masks.shape, lambda j, co: (0, 0, 0)),
-            ],
+            ]
+            + [anywhere()] * len(arrays_of(*weights)),
             out_specs=[block] * 6,
             scratch_shapes=[pltpu.VMEM((2, width, half), BF)] * 3
             + [pltpu.SemaphoreType.DMA((3, 32))],
@@ -248,14 +296,16 @@
         + [jax.ShapeDtypeStruct((tokens, width), BF)],
         compiler_params=params(),
         cost_estimate=cost(8, 34 << 20),
-    )(co, *mixed, *[part for pair in weights for part in pair], vectors, masks)
+    )(co, *mixed, vectors, masks, *arrays_of(*weights))
 
 
 def time_output_kernel(
-    co, gated, x_ref, carry_ref, vec_ref, oo, ox, middle_ref, mk_ref, mr_ref, ow, last, sems
+    co, gated, x_ref, carry_ref, vec_ref, *refs, layout
 ):
+    arrays, refs = take_refs(refs, layout)
+    middle_ref, mk_ref, mr_ref, ow, last, sems = refs
     i = pl.program_id(0)
-    copies = weight_copies(co, oo, ox, ow, sems, ORDERS[3])
+    copies = weight_copies(co, arrays, ow, sems, layout)
 
     @pl.when(i == 0)
     def _():
@@ -287,7 +337,7 @@
     rows = tokens // 4
     tall = pl.BlockSpec((rows, width), lambda i, co: (i, 0))
     return pl.pallas_call(
-        time_output_kernel,
+        functools.partial(time_output_kernel, layout=weight[0]),
         grid_spec=pltpu.PrefetchScalarGridSpec(
             num_scalar_prefetch=1,
             grid=(4,),
@@ -296,9 +346,8 @@
                 tall,
                 pl.BlockSpec((rows, 1), lambda i, co: (i, 0)),
                 pl.BlockSpec(vectors.shape, lambda i, co: (0, 0)),
-                anywhere(),
-                anywhere(),
-            ],
+            ]
+            + [anywhere()] * len(weight[1]),
             out_specs=[tall] * 3,
             scratch_shapes=[
                 pltpu.VMEM((2, width, width // 2), BF),
@@ -309,16 +358,17 @@
         out_shape=[jax.ShapeDtypeStruct((tokens, width), t) for t in (F32, BF, BF)],
         compiler_params=params(),
         cost_estimate=cost(3, 14 << 20),
-    )(co, gated, x, carry, vectors, *weight)
+    )(co, gated, x, carry, vectors, *weight[1])
 
 
 WIDE = 512
 
 
-def hidden_kernel(co, mk, wo, wx, hidden_ref, active_ref, whole, sems):
+def hidden_kernel(co, mk, *refs, layout):
+    arrays, (hidden_ref, active_ref, whole, sems) = take_refs(refs, layout)
     j = pl.program_id(0)
     per_half = whole.shape[2] // WIDE
-    copies = weight_copies(co, wo, wx, whole, sems, ORDERS[4])
+    copies = weight_copies(co, arrays, whole, sems, layout)
 
     @pl.when(j == 0)
     def _():
@@ -329,7 +379,7 @@
     def _():
         wait_half(copies, 1)
 
-    half = co[3] ^ lax.div(j, per_half)
+    half = co[4] ^ lax.div(j, per_half)
     columns = pl.ds(pl.multiple_of(lax.rem(j, per_half) * WIDE, WIDE), WIDE)
     active = jnp.maximum(dot(mk[...], whole[half, :, columns], NN), 0.0)
     active_ref[...] = active.astype(BF)
@@ -337,42 +387,41 @@
 
 
 def column_tile(per_half):
-    return lambda j, co: (0, (co[3] ^ lax.div(j, per_half)) * per_half + lax.rem(j, per_half))
+    return lambda j, co: (0, (co[4] ^ lax.div(j, per_half)) * per_half + lax.rem(j, per_half))
 
 
 def hidden_step(co, mixed, weight):
     tokens, width = mixed.shape
-    half = weight[0].shape[-1]
+    half = weight_width(weight)
     block = pl.BlockSpec((tokens, WIDE), column_tile(half // WIDE))
     return pl.pallas_call(
-        hidden_kernel,
+        functools.partial(hidden_kernel, layout=weight[0]),
         grid_spec=pltpu.PrefetchScalarGridSpec(
             num_scalar_prefetch=1,
             grid=(2 * half // WIDE,),
-            in_specs=[
-                pl.BlockSpec((tokens, width), lambda j, co: (0, 0)),
-                anywhere(),
-                anywhere(),
-            ],
+            in_specs=[pl.BlockSpec((tokens, width), lambda j, co: (0, 0))]
+            + [anywhere()] * len(weight[1]),
             out_specs=[block] * 2,
             scratch_shapes=[
                 pltpu.VMEM((2, width, half), BF),
-                pltpu.SemaphoreType.DMA((32,)),
+                pltpu.SemaphoreType.DMA((sem_count(weight),)),
             ],
         ),
         out_shape=[jax.ShapeDtypeStruct((tokens, 2 * half), BF)] * 2,
         compiler_params=params(),
         cost_estimate=cost(4.5, 26 << 20),
-    )(co, mixed, *weight)
+    )(co, mixed, *weight[1])
 
 
 def result_kernel(
-    co, scale, hidden, mr, middle_ref, teacher_ref, valid_ref, wo, wx, ro, rx,
-    out_ref, dres_ref, dkv_ref, drec_ref, loss_ref, ww, rw, kv_ref, pre_ref, sems,
+    co, scale, hidden, mr, middle_ref, teacher_ref, valid_ref, *refs, layouts,
 ):
+    value_w, refs = take_refs(refs, layouts[0])
+    recept_w, refs = take_refs(refs, layouts[1])
+    out_ref, dres_ref, dkv_ref, drec_ref, loss_ref, ww, rw, kv_ref, pre_ref, sems, sems_r = refs
     i = pl.program_id(0)
-    copies = weight_copies(co, wo, wx, ww, sems.at[0], ORDERS[6])
-    recept = weight_copies(co, ro, rx, rw, sems.at[1], ORDERS[5])
+    copies = weight_copies(co, value_w, ww, sems, layouts[0])
+    recept = weight_copies(co, recept_w, rw, sems_r, layouts[1])
 
     @pl.when(i == 0)
     def _():
@@ -412,10 +461,10 @@
 def result_step(co, scale, hidden, mixed, middle, teacher, valid, weight, recept):
     tokens, width = mixed.shape
     rows = tokens // 4
-    wide = weight[0].shape[-1]
+    wide = weight_width(weight)
     tall = pl.BlockSpec((rows, width), lambda i, co, s: (i, 0))
     return pl.pallas_call(
-        result_kernel,
+        functools.partial(result_kernel, layouts=[weight[0], recept[0]]),
         grid_spec=pltpu.PrefetchScalarGridSpec(
             num_scalar_prefetch=2,
             grid=(4,),
@@ -426,42 +475,42 @@
                 tall,
                 pl.BlockSpec((rows, 1), lambda i, co, s: (i, 0)),
             ]
-            + [anywhere()] * 4,
+            + [anywhere()] * len(arrays_of(weight, recept)),
             out_specs=[tall] * 4 + [pl.BlockSpec((8, width), lambda i, co, s: (0, 0))],
             scratch_shapes=[
                 pltpu.VMEM((2, width, wide), BF),
                 pltpu.VMEM((2, width, width // 2), BF),
                 pltpu.VMEM((rows, width), F32),
                 pltpu.VMEM((rows, width), F32),
-                pltpu.SemaphoreType.DMA((2, 32)),
+                pltpu.SemaphoreType.DMA((sem_count(weight),)),
+                pltpu.SemaphoreType.DMA((sem_count(recept),)),
             ],
         ),
         out_shape=[jax.ShapeDtypeStruct((tokens, width), t) for t in (BF, F32, BF, BF)]
         + [jax.ShapeDtypeStruct((8, width), F32)],
         compiler_params=params(),
         cost_estimate=cost(7, 38 << 20),
-    )(co, scale, hidden, mixed, middle, teacher, valid, *weight, *recept)
-
-
-def weight_grad_kernel(co, model_ref, chan_ref, own, other, whole, sems, *, order):
+    )(co, scale, hidden, mixed, middle, teacher, valid, *arrays_of(weight, recept))
+
+
+def weight_grad_kernel(co, model_ref, chan_ref, *refs, order):
+    targets, (whole, sems) = refs[:4], refs[4:]
     j = pl.program_id(0)
     per_half = whole.shape[2] // WIDE
-    part = lax.rem(j, per_half)
-    columns = pl.ds(pl.multiple_of(part * WIDE, WIDE), WIDE)
+    columns = pl.ds(pl.multiple_of(lax.rem(j, per_half) * WIDE, WIDE), WIDE)
     turn = lax.div(j, per_half)
-    whole[co[3] ^ turn, :, columns] = dot(model_ref[...], chan_ref[...], TN).astype(BF)
+    whole[co[4] ^ turn, :, columns] = dot(model_ref[...], chan_ref[...], TN).astype(BF)
 
     def copies(piece):
         found = []
-        for other_core, target in ((0, own), (1, other)):
-            for index, rel in slot_list(order):
-                row, half = slot_place(co, rel, other_core)
-                copy = pltpu.make_async_copy(
-                    whole.at[half, pl.ds(row, SLOT), piece],
-                    target.at[index + (slice(None), piece)],
-                    sems.at[len(found)],
-                )
-                found.append((rel["x"], copy))
+        for which, index, rel in rel_slots(order):
+            row, half = slot_place(co, rel)
+            copy = pltpu.make_async_copy(
+                whole.at[half, pl.ds(row, SLOT), piece],
+                targets[which].at[index + (slice(None), piece)],
+                sems.at[len(found)],
+            )
+            found.append((rel["x"], copy))
         return found
 
     for which in (0, 1):
@@ -478,36 +527,42 @@
             copy.wait()
 
 
-def weight_grad(co, model, chan, order):
+def weight_grad(co, model, chan, order, first=0, half=None):
     tokens, width = model.shape
-    half = chan.shape[1] // 2
-    dims = tuple(SIZES[d] for d in order[::-1])
-    shape = jax.ShapeDtypeStruct(dims + (SLOT, half), BF)
+    each = chan.shape[1] // 2
+    half = half or each
+    per_half, skip, stride = half // WIDE, first // WIDE, each // WIDE
+
+    def tile(j, co):
+        return 0, (co[4] ^ lax.div(j, per_half)) * stride + skip + lax.rem(j, per_half)
+
+    shape = jax.ShapeDtypeStruct((2, 2, 2, SLOT, half), BF)
     return pl.pallas_call(
         functools.partial(weight_grad_kernel, order=order),
         grid_spec=pltpu.PrefetchScalarGridSpec(
             num_scalar_prefetch=1,
-            grid=(2 * half // WIDE,),
+            grid=(2 * per_half,),
             in_specs=[
                 pl.BlockSpec((tokens, width), lambda j, co: (0, 0)),
-                pl.BlockSpec((tokens, WIDE), column_tile(half // WIDE)),
+                pl.BlockSpec((tokens, WIDE), tile),
             ],
-            out_specs=[anywhere()] * 2,
+            out_specs=[anywhere()] * 4,
             scratch_shapes=[
                 pltpu.VMEM((2, width, half), BF),
                 pltpu.SemaphoreType.DMA((32,)),
             ],
         ),
-        out_shape=[shape] * 2,
+        out_shape=[shape] * 4,
         compiler_params=params(),
         cost_estimate=cost(half / 512 * 1.2, (2 << 20) * (1 + half / 256)),
     )(co, model, chan)
 
 
-def hidden_back_kernel(co, dkv, active_ref, wo, wx, out_ref, whole, sems):
+def hidden_back_kernel(co, dkv, active_ref, *refs, layout):
+    arrays, (out_ref, whole, sems) = take_refs(refs, layout)
     j = pl.program_id(0)
     per_half = whole.shape[2] // WIDE
-    copies = weight_copies(co, wo, wx, whole, sems, ORDERS[6])
+    copies = weight_copies(co, arrays, whole, sems, layout)
 
     @pl.when(j == 0)
     def _():
@@ -518,7 +573,7 @@
     def _():
         wait_half(copies, 1)
 
-    half = co[3] ^ lax.div(j, per_half)
+    half = co[4] ^ lax.div(j, per_half)
     columns = pl.ds(pl.multiple_of(lax.rem(j, per_half) * WIDE, WIDE), WIDE)
     grad = dot(dkv[...], whole[half, :, columns], NN)
     out_ref[...] = (2.0 * active_ref[...].astype(F32) * grad).astype(BF)
@@ -526,38 +581,39 @@
 
 def hidden_back(co, dkv, active, weight):
     tokens, width = dkv.shape
-    half = weight[0].shape[-1]
+    half = weight_width(weight)
     block = pl.BlockSpec((tokens, WIDE), column_tile(half // WIDE))
     return pl.pallas_call(
-        hidden_back_kernel,
+        functools.partial(hidden_back_kernel, layout=weight[0]),
         grid_spec=pltpu.PrefetchScalarGridSpec(
             num_scalar_prefetch=1,
             grid=(2 * half // WIDE,),
             in_specs=[
                 pl.BlockSpec((tokens, width), lambda j, co: (0, 0)),
                 block,
-                anywhere(),
-                anywhere(),
-            ],
+            ]
+            + [anywhere()] * len(weight[1]),
             out_specs=block,
             scratch_shapes=[
                 pltpu.VMEM((2, width, half), BF),
-                pltpu.SemaphoreType.DMA((32,)),
+                pltpu.SemaphoreType.DMA((sem_count(weight),)),
             ],
         ),
         out_shape=jax.ShapeDtypeStruct((tokens, 2 * half), BF),
         compiler_params=params(),
         cost_estimate=cost(4.5, 26 << 20),
-    )(co, dkv, active, *weight)
+    )(co, dkv, active, *weight[1])
 
 
 def middle_back_kernel(
-    co, dkey, drec, middle_ref, dres_ref, lead_ref, vec_ref, wo, wx, ro, rx,
-    dmid_ref, dtime_ref, sums_ref, ww, rw, gk_ref, gr_ref, next_ref, sems,
+    co, dkey, drec, middle_ref, dres_ref, lead_ref, vec_ref, *refs, layouts,
 ):
+    key_w, refs = take_refs(refs, layouts[0])
+    recept_w, refs = take_refs(refs, layouts[1])
+    dmid_ref, dtime_ref, sums_ref, ww, rw, gk_ref, gr_ref, next_ref, sems, sems_r = refs
     i = pl.program_id(0)
-    copies = weight_copies(co, wo, wx, ww, sems.at[0], ORDERS[4])
-    recept = weight_copies(co, ro, rx, rw, sems.at[1], ORDERS[5])
+    copies = weight_copies(co, key_w, ww, sems, layouts[0])
+    recept = weight_copies(co, recept_w, rw, sems_r, layouts[1])
 
     @pl.when(i == 0)
     def _():
@@ -602,10 +658,10 @@
 def middle_back(co, dkey, drec, middle, dres, lead, vectors, weight, recept):
     tokens, width = middle.shape
     rows = tokens // 4
-    wide = weight[0].shape[-1]
+    wide = weight_width(weight)
     tall = pl.BlockSpec((rows, width), lambda i, co: (3 - i, 0))
     return pl.pallas_call(
-        middle_back_kernel,
+        functools.partial(middle_back_kernel, layouts=[weight[0], recept[0]]),
         grid_spec=pltpu.PrefetchScalarGridSpec(
             num_scalar_prefetch=1,
             grid=(4,),
@@ -617,7 +673,7 @@
                 pl.BlockSpec((rows, 1), lambda i, co: (3 - i, 0)),
                 pl.BlockSpec(vectors.shape, lambda i, co: (0, 0)),
             ]
-            + [anywhere()] * 4,
+            + [anywhere()] * len(arrays_of(weight, recept)),
             out_specs=[tall] * 2 + [pl.BlockSpec((4, 8, width), lambda i, co: (0, 0, 0))],
             scratch_shapes=[
                 pltpu.VMEM((2, width, wide), BF),
@@ -625,7 +681,8 @@
                 pltpu.VMEM((rows, width), F32),
                 pltpu.VMEM((rows, width), F32),
                 pltpu.VMEM((8, width), F32),
-                pltpu.SemaphoreType.DMA((2, 32)),
+                pltpu.SemaphoreType.DMA((sem_count(weight),)),
+                pltpu.SemaphoreType.DMA((sem_count(recept),)),
             ],
         ),
         out_shape=[
@@ -635,16 +692,17 @@
         ],
         compiler_params=params(),
         cost_estimate=cost(8, 36 << 20),
-    )(co, dkey, drec, middle, dres, lead, vectors, *weight, *recept)
+    )(co, dkey, drec, middle, dres, lead, vectors, *arrays_of(weight, recept))
 
 
 def time_back_kernel(
-    co, dtime, key_ref, val_ref, rec_ref, pa_ref, pb_ref, vec, masks, oo, ox,
-    dkey_ref, dval_ref, drec_ref, sums_ref, ow, dg_ref, sems,
+    co, dtime, key_ref, val_ref, rec_ref, pa_ref, pb_ref, vec, masks, *refs, layout,
 ):
+    arrays, refs = take_refs(refs, layout)
+    dkey_ref, dval_ref, drec_ref, sums_ref, ow, dg_ref, sems = refs
     j = pl.program_id(0)
     per_half = ow.shape[2] // TILE
-    copies = weight_copies(co, oo, ox, ow, sems, ORDERS[3])
+    copies = weight_copies(co, arrays, ow, sems, layout)
 
     @pl.when(j == 0)
     def _():
@@ -655,7 +713,7 @@
     def _():
         wait_half(copies, 1)
 
-    half = co[3] ^ lax.div(j, per_half)
+    half = co[4] ^ lax.div(j, per_half)
     columns = pl.ds(pl.multiple_of(lax.rem(j, per_half) * TILE, TILE), TILE)
     dg_ref[...] = dot(dtime[...], ow[half, :, columns], NN)
 
@@ -719,7 +777,7 @@
     tile = column_tile(half // TILE)
     block = pl.BlockSpec((tokens, TILE), tile)
     return pl.pallas_call(
-        time_back_kernel,
+        functools.partial(time_back_kernel, layout=weight[0]),
         grid_spec=pltpu.PrefetchScalarGridSpec(
             num_scalar_prefetch=1,
             grid=(width // TILE,),
@@ -728,9 +786,8 @@
             + [
                 pl.BlockSpec((vectors.shape[0], TILE), tile),
                 pl.BlockSpec(masks.shape, lambda j, co: (0, 0, 0)),
-                anywhere(),
-                anywhere(),
-            ],
+            ]
+            + [anywhere()] * len(weight[1]),
             out_specs=[block] * 3
             + [pl.BlockSpec((2, 8, TILE), lambda j, co: (0,) + tile(j, co))],
             scratch_shapes=[
@@ -743,19 +800,20 @@
         + [jax.ShapeDtypeStruct((2, 8, width), F32)],
         compiler_params=params(),
         cost_estimate=cost(9, 34 << 20),
-    )(co, dtime, *saved, vectors, masks, *weight)
+    )(co, dtime, *saved, vectors, masks, *weight[1])
 
 
 def input_back_kernel(
-    co, dkey, dval, drec, x_ref, dmid_ref, lead_ref, vec_ref, ko, kx, vo, vx, ro, rx,
-    out_ref, sums_ref, kw, vw, rw, gk_ref, gv_ref, gr_ref, next_ref, sems,
+    co, dkey, dval, drec, x_ref, dmid_ref, lead_ref, vec_ref, *refs, layouts,
 ):
+    key_w, refs = take_refs(refs, layouts[0])
+    val_w, refs = take_refs(refs, layouts[1])
+    rec_w, refs = take_refs(refs, layouts[2])
+    out_ref, sums_ref, kw, vw, rw, gk_ref, gv_ref, gr_ref, next_ref, sems = refs
     i = pl.program_id(0)
     groups = [
-        weight_copies(co, own, other, whole, sems.at[n], order)
-        for n, (own, other, whole, order) in enumerate(
-            ((ko, kx, kw, ORDERS[0]), (vo, vx, vw, ORDERS[1]), (ro, rx, rw, ORDERS[2]))
-        )
+        weight_copies(co, arrays, whole, sems.at[n], layout)
+        for n, (arrays, whole, layout) in enumerate(zip((key_w, val_w, rec_w), (kw, vw, rw), layouts))
     ]
 
     @pl.when(i == 0)
@@ -802,7 +860,7 @@
     rows = tokens // 4
     tall = pl.BlockSpec((rows, width), lambda i, co: (3 - i, 0))
     return pl.pallas_call(
-        input_back_kernel,
+        functools.partial(input_back_kernel, layouts=[w[0] for w in weights]),
         grid_spec=pltpu.PrefetchScalarGridSpec(
             num_scalar_prefetch=1,
             grid=(4,),
@@ -811,7 +869,7 @@
                 pl.BlockSpec((rows, 1), lambda i, co: (3 - i, 0)),
                 pl.BlockSpec(vectors.shape, lambda i, co: (0, 0)),
             ]
-            + [anywhere()] * 6,
+            + [anywhere()] * len(arrays_of(*weights)),
             out_specs=[tall, pl.BlockSpec((5, 8, width), lambda i, co: (0, 0, 0))],
             scratch_shapes=[pltpu.VMEM((2, width, width // 2), BF)] * 3
             + [pltpu.VMEM((rows, width), F32)] * 3
@@ -823,86 +881,104 @@
         ],
         compiler_params=params(),
         cost_estimate=cost(7, 26 << 20),
-    )(co, *grads, x, dmid, lead, vectors, *[part for pair in weights for part in pair])
-
-
-ORDERS = ("xzy", "yzx", "zyx", "zxy", "xzy", "zyx", "yzx")
-RING_UP = [(0, 1), (1, 2), (2, 3), (3, 0)]
-RING_DOWN = [(1, 0), (2, 1), (3, 2), (0, 3)]
-
-
-class Links:
-    def __init__(self):
-        self.co = jnp.stack([lax.axis_index(a) for a in ("z", "y", "c", "x")]).astype(jnp.int32)
-
-    def gather(self, shard, order):
-        held = shard
-        for axis in order:
-            if axis == "z":
-                parts = [held]
-                for _ in range(3):
-                    parts.append(lax.ppermute(parts[-1], "z", RING_UP))
-                held = jnp.stack(parts)
-            else:
-                held = jnp.stack([held, lax.ppermute(held, axis, SWAP)])
-        return held, lax.ppermute(held, "c", SWAP)
-
-    def reduce(self, own, other, order):
-        held = own + lax.ppermute(other, "c", SWAP)
-        for n, axis in enumerate(order[::-1]):
-            wide = (lambda v: v.astype(F32)) if n == 2 else (lambda v: v)
-            if axis == "z":
-                moving = held[3]
-                for place in (2, 1):
-                    moving = held[place] + lax.ppermute(moving, "z", RING_DOWN)
-                held = wide(held[0]) + wide(lax.ppermute(moving, "z", RING_DOWN))
-            else:
-                held = wide(held[0]) + wide(lax.ppermute(held[1], axis, SWAP))
-        return held
-
-    def total(self, values):
-        for axis in ("x", "y", "c"):
-            values = values + lax.ppermute(values, axis, SWAP)
-        values = values + lax.ppermute(values, "z", [(0, 1), (1, 0), (2, 3), (3, 2)])
-        return values + lax.ppermute(values, "z", [(0, 2), (2, 0), (1, 3), (3, 1)])
-
-
-class Plain:
-    def __init__(self, blocks):
-        self.blocks = blocks
-        self.co = jnp.zeros((4,), jnp.int32)
-
-    def gather(self, shard, order):
-        whole = lax.all_gather(shard, ("z", "y", "c"), axis=0, tiled=True)
-        whole = lax.all_gather(whole, "x", axis=1, tiled=True)
-        half = whole.shape[1] // 2
-        dims = tuple(SIZES[d] for d in order[::-1])
-        found = []
-        for core in (0, 1):
-            parts = []
-            for _, rel in slot_list(order):
-                block = ((4 - rel["z"]) & 3) * 4 + rel["y"] * 2 + core
-                part = whole[block * SLOT : (block + 1) * SLOT]
-                parts.append(part[:, rel["x"] * half : (rel["x"] + 1) * half])
-            found.append(jnp.stack(parts).reshape(dims + (SLOT, half)))
-        return tuple(found)
-
-    def reduce(self, own, other, order):
-        half = own.shape[-1]
-        table = {}
-        for core, source in ((0, own), (1, other)):
-            for index, rel in slot_list(order):
-                block = ((4 - rel["z"]) & 3) * 4 + rel["y"] * 2 + core
-                table[block, rel["x"]] = source[index]
-        whole = jnp.concatenate(
-            [jnp.concatenate([table[b, 0], table[b, 1]], axis=1) for b in range(16)], axis=0
-        )
-        whole = lax.psum_scatter(whole, ("z", "y", "c"), scatter_dimension=0, tiled=True)
-        whole = lax.psum_scatter(whole, "x", scatter_dimension=1, tiled=True)
-        return whole.astype(F32)
-
-    def total(self, values):
-        return lax.psum(values, EVERY)
+    )(co, *grads, x, dmid, lead, vectors, *arrays_of(*weights))
+
+
+def seal(*values):
+    return lax.optimization_barrier(values)
+
+
+def swap(values, axis):
+    return lax.ppermute(values, axis, SWAP)
+
+
+class Gather:
+    def __init__(self, shard, order):
+        self.order, self.state, self.done = order, (shard,), 0
+
+    def step(self):
+        n = self.done
+        if n and n < 4:
+            self.state = (jnp.stack(self.state),)
+        if n < 3:
+            self.state += (swap(self.state[0], self.order[n]),)
+        elif n == 3:
+            near = self.state[0]
+            self.state = (near, swap(near, self.order[3]), swap(near, "c"))
+        else:
+            near, far, near_other = self.state
+            self.state = (near, far, near_other, swap(far, "c"))
+        self.done += 1
+
+    def part(self, first=0):
+        assert self.done == 5
+        return ("rel", self.order, first, self.state[0].shape[-1]), self.state
+
+
+def weight_of(*parts):
+    layouts, arrays = zip(*parts)
+    return layouts, [array for group in arrays for array in group]
+
+
+class Reduce:
+    def __init__(self, slots, order):
+        self.order, self.state, self.done = order, tuple(slots), 0
+
+    def step(self):
+        n = self.done
+        if n == 0:
+            near, far, near_other, far_other = self.state
+            self.state = (near, far, swap(far_other, "c"), swap(near_other, "c"))
+        elif n == 1:
+            near, far, far_got, near_got = self.state
+            self.state = (near, near_got, swap(far + far_got, self.order[3]))
+        elif n == 2:
+            near, near_got, got = (v.astype(F32) for v in self.state)
+            held = near + near_got + got
+            self.keep(held, 2)
+        elif n < 5:
+            held = self.state[0] + self.state[1].astype(F32)
+            self.keep(held, 4 - n)
+        self.done += 1
+
+    def keep(self, held, place):
+        self.state = (held[0], swap(held[1].astype(BF), self.order[place]))
+
+    def finish(self):
+        assert self.done == 5
+        return self.state[0] + self.state[1].astype(F32)
+
+
+def step_all(*chains):
+    for chain in chains:
+        chain.step()
+
+
+def seal_all(chains, *values):
+    states, values = seal([chain.state for chain in chains], values)
+    for chain, state in zip(chains, states):
+        chain.state = tuple(state)
+    return values
+
+
+def gather_plain(shard, first=0):
+    whole = lax.all_gather(shard, ("w", "u", "y", "c"), axis=0, tiled=True)
+    whole = lax.all_gather(whole, "x", axis=1, tiled=True)
+    half = whole.shape[1] // 2
+    whole = whole.reshape(16, SLOT, 2, half).transpose(0, 2, 1, 3)
+    return ("abs", 0, first, half), (whole,)
+
+
+def reduce_plain(slots, order):
+    table = {}
+    for which, index, rel in rel_slots(order):
+        block = rel["w"] * 8 + rel["u"] * 4 + rel["y"] * 2 + rel["c"]
+        table[block, rel["x"]] = slots[which][index]
+    whole = jnp.concatenate(
+        [jnp.concatenate([table[b, 0], table[b, 1]], axis=1) for b in range(16)], axis=0
+    )
+    whole = lax.psum_scatter(whole, ("w", "u", "y", "c"), scatter_dimension=0, tiled=True)
+    return lax.psum_scatter(whole, "x", scatter_dimension=1, tiled=True).astype(F32)
 
 
 def scan_masks(carry):
@@ -955,11 +1031,13 @@
 ):
     tokens, width = inputs.shape
     sizes = {a: lax.axis_size(a) for a in EVERY}
-    devices = sizes["z"] * sizes["y"] * sizes["c"] * sizes["x"]
-    fast = (sizes["z"], sizes["y"], sizes["c"], sizes["x"]) == (4, 2, 2, 2)
-    links = Links() if fast else Plain(width // SLOT)
-    co = links.co
+    devices = math.prod(sizes.values())
+    fast = all(size == 2 for size in sizes.values())
     side = lax.axis_index("x")
+    if fast:
+        co = jnp.stack([lax.axis_index(a) for a in EVERY]).astype(jnp.int32)
+    else:
+        co = jnp.zeros((5,), jnp.int32)
 
     ids = lax.dynamic_slice_in_dim(segments, side * tokens, tokens)
     previous = jnp.concatenate([jnp.zeros((1,), jnp.int32), ids[:-1]])
@@ -970,7 +1048,9 @@
     masks = scan_masks(carry)
     carry, valid_rows, lead = carry[:, None], valid[:, None], lead[:, None]
 
-    flat = ((lax.axis_index("z") * sizes["y"] + lax.axis_index("y")) * sizes["c"] + lax.axis_index("c")) * sizes["x"] + side
+    flat = 0
+    for axis in EVERY:
+        flat = flat * sizes[axis] + lax.axis_index(axis)
     own_vectors = jnp.stack(
         [
             first_norm_gain,
@@ -991,26 +1071,13 @@
         jnp.arange(width)[None, :] // piece == flat, jnp.tile(own_vectors, (1, width // piece)), 0.0
     )
     counts = jnp.broadcast_to(jnp.sum(valid), (1, width))
-    vectors = links.total(jnp.concatenate([spread, counts, jnp.zeros((4, width), F32)]))
-    count = vectors[11, 0]
-
-    shards = (
-        time_key,
-        time_value,
-        time_recept,
-        time_output.T,
-        channel_key,
-        channel_recept,
-        channel_value.T,
-    )
-    key_w, value_w, recept_w, output_w, ckey_w, crecept_w, cvalue_w = (
-        links.gather(shard, order) for shard, order in zip(shards, ORDERS)
-    )
+    vectors = jnp.concatenate([spread, counts, jnp.zeros((4, width), F32)])
+    output_t, value_t = time_output.T, channel_value.T
 
     if sizes["x"] == 2:
         mine = lax.dynamic_slice_in_dim(teacher, side * tokens, tokens)
         theirs = lax.dynamic_slice_in_dim(teacher, (1 - side) * tokens, tokens)
-        theirs = lax.ppermute(theirs, "x", SWAP)
+        theirs = swap(theirs, "x")
         teacher_rows = jnp.where(
             side == 0,
             jnp.concatenate([mine, theirs], axis=1),
@@ -1019,46 +1086,162 @@
     else:
         teacher_rows = teacher
 
-    mixed = first_mix(inputs, carry, vectors)
+    if fast:
+        rest = lax.all_gather(jnp.concatenate([value_t, channel_recept], axis=1), EVERY)
+        rest = rest.reshape(16, 2, SLOT, rest.shape[-1])
+        cols = value_t.shape[1]
+        cvalue_w = ((("abs", 0, 0, cols),), [rest])
+        crecept_w = ((("abs", cols, 0, width // 2),), [rest])
+
+        key_c, val_c, rec_c = Gather(time_key, "wxuy"), Gather(time_value, "uwyx"), Gather(time_recept, "wyxu")
+        out_c = Gather(output_t, "wuyx")
+        split = channel_key.shape[1] // 2
+        ck_a, ck_b = Gather(channel_key[:, :split], "wxuy"), Gather(channel_key[:, split:], "uwyx")
+        three = (key_c, val_c, rec_c)
+
+        step_all(*three)
+        got = swap(vectors, "x")
+        (vectors, got) = seal_all(three, vectors, got)
+        vectors = vectors + got
+        step_all(*three, out_c)
+        got = swap(vectors, "y")
+        (vectors, got) = seal_all((*three, out_c), vectors, got)
+        vectors = vectors + got
+        step_all(*three, out_c, ck_a, ck_b)
+        vectors = vectors + swap(vectors, "c")
+        got = swap(vectors, "u")
+        (vectors, got) = seal_all((*three, out_c, ck_a, ck_b), vectors, got)
+        vectors = vectors + got
+        step_all(*three, out_c, ck_a, ck_b)
+        vectors = vectors + swap(vectors, "w")
+        mixed = first_mix(inputs, carry, vectors)
+        (mixed, vectors) = seal_all((*three, out_c, ck_a, ck_b), mixed, vectors)
+        step_all(*three, out_c, ck_a, ck_b)
+        (mixed,) = seal_all((*three, out_c, ck_a, ck_b), mixed)
+        key_w, value_w, recept_w = (weight_of(c.part()) for c in three)
+        step_all(out_c, ck_a, ck_b)
+    else:
+        vectors = lax.psum(vectors, EVERY)
+        mixed = first_mix(inputs, carry, vectors)
+        key_w, value_w, recept_w, output_w, ckey_w, crecept_w, cvalue_w = (
+            weight_of(gather_plain(w))
+            for w in (time_key, time_value, time_recept, output_t, channel_key, channel_recept, value_t)
+        )
+    count = vectors[11, 0]
+    scale = (float(tokens * devices) / count).reshape(1)
+
     *saved, gated = time_forward(co, mixed, (key_w, value_w, recept_w), vectors, masks)
+    if fast:
+        (gated,) = seal_all((out_c, ck_a, ck_b), gated)
+        output_w = weight_of(out_c.part())
+        step_all(ck_a, ck_b)
     middle, mixed_k2, mixed_r2 = time_output_step(co, gated, inputs, carry, vectors, output_w)
+    if fast:
+        (middle, mixed_k2, mixed_r2) = seal_all((ck_a, ck_b), middle, mixed_k2, mixed_r2)
+        ckey_w = weight_of(ck_a.part(), ck_b.part(split))
     hidden, active = hidden_step(co, mixed_k2, ckey_w)
-    scale = (float(tokens * devices) / count).reshape(1)
     result, dres, dkv, drec2, loss_rows = result_step(
         co, scale, hidden, mixed_r2, middle, teacher_rows, valid_rows, cvalue_w, crecept_w
     )
-    if sizes["x"] == 2:
-        half = width // 2
+
+    half = width // 2
+    if fast:
         kept = lax.dynamic_slice_in_dim(result, side * half, half, axis=1)
         sent = lax.dynamic_slice_in_dim(result, (1 - side) * half, half, axis=1)
-        arrived = lax.ppermute(sent, "x", SWAP)
+        arrived = swap(sent, "x")
+        split = hidden.shape[1] // 4
+        cv_a = Reduce(weight_grad(co, dkv, hidden, "wxuy", 0, split), "wxuy")
+        (hidden, dkv) = seal_all((cv_a,), hidden, dkv)
+        step_all(cv_a)
+        cv_b = Reduce(weight_grad(co, dkv, hidden, "uwyx", split, split), "uwyx")
+        (dkv, arrived) = seal_all((cv_a, cv_b), dkv, arrived)
+        step_all(cv_a, cv_b)
+        dkey2 = hidden_back(co, dkv, active, cvalue_w)
+        (dkey2,) = seal_all((cv_b,), dkey2)
+        step_all(cv_b)
+        ck_a = Reduce(weight_grad(co, mixed_k2, dkey2, "wyxu", 0, split), "wyxu")
+        (dkey2,) = seal_all((cv_a, ck_a), dkey2)
+        step_all(cv_a, ck_a)
+        ck_b = Reduce(weight_grad(co, mixed_k2, dkey2, "wxuy", split, split), "wxuy")
+        cr = Reduce(weight_grad(co, mixed_r2, drec2, "uwyx"), "uwyx")
+        (dkey2, drec2) = seal_all((ck_a, ck_b, cr), dkey2, drec2)
+        step_all(ck_a, ck_b, cr)
+        dmid, dtime, sums2 = middle_back(
+            co, dkey2, drec2, middle, dres, lead, vectors, ckey_w, crecept_w
+        )
+        chains = (cv_a, cv_b, ck_a, ck_b, cr)
+        (dtime, dmid) = seal_all(chains, dtime, dmid)
+        step_all(*chains)
+        out_c = Reduce(weight_grad(co, dtime, gated, "wuyx"), "wuyx")
+        (dtime,) = seal_all((cv_a, cv_b, ck_a, out_c), dtime)
+        step_all(cv_a, cv_b, ck_a, out_c)
+        *dmix, sums_t = time_back(co, dtime, saved, vectors, masks, output_w)
+        chains = (cv_a, cv_b, ck_a, ck_b, cr, out_c)
+        (dmix, dmid) = seal_all(chains, dmix, dmid)
+        step_all(cv_b, ck_b, cr, out_c)
+        orders = ("wxuy", "uwyx", "wyxu")
+        three = []
+        pending = [cv_b, ck_b, cr, out_c]
+        for m, d, order in zip(mixed, dmix, orders):
+            chain = Reduce(weight_grad(co, m, d, order), order)
+            (dmix,) = seal_all((*three, chain, *pending), dmix)
+            three.append(chain)
+            step_all(*three)
+            if len(three) == 2:
+                step_all(ck_a, ck_b, cr, out_c)
+                pending = [ck_a, ck_b, cr, out_c]
+        input_grad, sums1 = input_back(
+            co, dmix, inputs, dmid, lead, vectors, (key_w, value_w, recept_w)
+        )
+        (input_grad, sums1) = seal_all((*three, *pending), input_grad, sums1)
+        for chain in (ck_b, cr, out_c, *three):
+            while chain.done < 5:
+                chain.step()
+        key_g, val_g, rec_g = (c.finish() for c in three)
+        output_g, crecept_g = out_c.finish(), cr.finish()
+        cvalue_g = jnp.concatenate([cv_a.finish(), cv_b.finish()], axis=1)
+        ckey_g = jnp.concatenate([ck_a.finish(), ck_b.finish()], axis=1)
         outputs = jnp.where(
             side == 0,
             jnp.concatenate([kept, arrived], axis=0),
             jnp.concatenate([arrived, kept], axis=0),
         )
     else:
-        outputs = result
-
-    cvalue_g = links.reduce(*weight_grad(co, dkv, hidden, ORDERS[6]), ORDERS[6])
-    dkey2 = hidden_back(co, dkv, active, cvalue_w)
-    ckey_g = links.reduce(*weight_grad(co, mixed_k2, dkey2, ORDERS[4]), ORDERS[4])
-    crecept_g = links.reduce(*weight_grad(co, mixed_r2, drec2, ORDERS[5]), ORDERS[5])
-    dmid, dtime, sums2 = middle_back(
-        co, dkey2, drec2, middle, dres, lead, vectors, ckey_w, crecept_w
-    )
-    output_g = links.reduce(*weight_grad(co, dtime, gated, ORDERS[3]), ORDERS[3])
-    *dmix, sums_t = time_back(co, dtime, saved, vectors, masks, output_w)
-    time_g = [
-        links.reduce(*weight_grad(co, m, d, order), order)
-        for m, d, order in zip(mixed, dmix, ORDERS)
-    ]
-    input_grad, sums1 = input_back(
-        co, dmix, inputs, dmid, lead, vectors, (key_w, value_w, recept_w)
-    )
+        order = "wuyx"
+
+        def grad(model, chan):
+            return reduce_plain(weight_grad(co, model, chan, order), order)
+
+        if sizes["x"] == 2:
+            kept = lax.dynamic_slice_in_dim(result, side * half, half, axis=1)
+            arrived = swap(lax.dynamic_slice_in_dim(result, (1 - side) * half, half, axis=1), "x")
+            outputs = jnp.where(
+                side == 0,
+                jnp.concatenate([kept, arrived], axis=0),
+                jnp.concatenate([arrived, kept], axis=0),
+            )
+        else:
+            outputs = result
+        cvalue_g = grad(dkv, hidden)
+        dkey2 = hidden_back(co, dkv, active, cvalue_w)
+        ckey_g, crecept_g = grad(mixed_k2, dkey2), grad(mixed_r2, drec2)
+        dmid, dtime, sums2 = middle_back(
+            co, dkey2, drec2, middle, dres, lead, vectors, ckey_w, crecept_w
+        )
+        output_g = grad(dtime, gated)
+        *dmix, sums_t = time_back(co, dtime, saved, vectors, masks, output_w)
+        key_g, val_g, rec_g = (grad(m, d) for m, d in zip(mixed, dmix))
+        input_grad, sums1 = input_back(
+            co, dmix, inputs, dmid, lead, vectors, (key_w, value_w, recept_w)
+        )
 
     rows = jnp.concatenate([sums1[:2], sums_t, sums1[2:], sums2, loss_rows[None]])
-    totals = links.total(jnp.sum(rows, axis=1))
+    totals = jnp.sum(rows, axis=1)
+    if fast:
+        for axis in EVERY:
+            totals = totals + swap(totals, axis)
+    else:
+        totals = lax.psum(totals, EVERY)
     loss = jnp.sum(totals[11]) / (2.0 * count * width)
     vector_g = lax.dynamic_slice_in_dim(totals, flat * piece, piece, axis=1)
     return (
@@ -1066,7 +1249,9 @@
         loss,
         input_grad,
         *[vector_g[n] for n in range(7)],
-        *time_g,
+        key_g,
+        val_g,
+        rec_g,
         output_g.T,
         *[vector_g[n] for n in range(7, 11)],
         ckey_g,
@@ -1077,9 +1262,9 @@
 
 def solution(mesh):
     fsdp, tp = mesh.shape["fsdp"], mesh.shape["tp"]
-    core = 2 if fsdp % 4 == 0 else 1
-    split = Mesh(mesh.devices.reshape(fsdp // (core * core), core, core, tp), EVERY)
-    rows = ("z", "y", "c")
+    two = 2 if fsdp % 8 == 0 else 1
+    split = Mesh(mesh.devices.reshape(fsdp // two**3, two, two, two, tp), EVERY)
+    rows = ("w", "u", "y", "c")
     vector = P(EVERY)
     matrix = P(rows, "x")
     turned = P("x", rows)

time: 783 us -> 661 us (0.84)
  waiting for transfers between devices: 265 us -> 137 us
  between operations: 5.85 us -> 19.8 us
  other arithmetic: 68.5 us -> 55.7 us
  Pallas kernels: 294 us -> 302 us
    ppermute x96 -> x102, waiting for transfers between devices: 265 us -> 137 us  [swap(): return lax.ppermute(values, axis, SWAP)]
    another operation x22 -> x18, other arithmetic: 30.3 us -> 6.73 us  [step(): self.state = (jnp.stack(self.state),)]
    add x50 -> x54, other arithmetic: 22.6 us -> 31.6 us  [the longest x9 14.4 us: step(): self.state = (near, near_got, swap(far + far_got, self.order[3]))]
    pallas_call x7 -> x9, Pallas kernels: 63.6 us -> 71.9 us  [weight_grad(): pl.pallas_call(functools.partial(weight_grad_kernel, order=order), grid_s...]
    ppermute x96 -> x102, starting transfers between devices: 110 us -> 107 us  [swap(): return lax.ppermute(values, axis, SWAP)]
  transfers between devices with their start and end apart: 96 -> 103, of which waited for: 41 -> 33; matrix products, arithmetic and copies ran while one was open for 11% -> 10% of each run, Pallas kernels for 16% -> 39%
where the time goes in v2:
time: 661 us; the launch traced here: 655 us
  Pallas kernels  302 us (46%)
  waiting for transfers between devices  137 us (21%)
  starting transfers between devices  107 us (16%)
  other arithmetic  55.7 us (8%)
  local copies, waits for them, and re-layouts  33.3 us (5%)
  between operations  19.8 us (3%)
    ppermute x102, waiting for transfers between devices, swap(): return lax.ppermute(values, axis, SWAP)  137 us
    ppermute x102, starting transfers between devices, swap(): return lax.ppermute(values, axis, SWAP)  107 us
    pallas_call x9, Pallas kernels, weight_grad(): pl.pallas_call(functools.partial(weight_grad_kernel, order=order), grid_s...  71.9 us
    pallas_call x1, Pallas kernels, middle_back(): pl.pallas_call(functools.partial(middle_back_kernel, layouts=[weight[0],...  43 us
    pallas_call x1, Pallas kernels, input_back(): pl.pallas_call(functools.partial(input_back_kernel, layouts=[w[0] for w i...  37 us
    pallas_call x1, Pallas kernels, time_forward(): pl.pallas_call(functools.partial(time_forward_kernel, layouts=[w[0] for w...  30.4 us
    pallas_call x1, Pallas kernels, result_step(): pl.pallas_call(functools.partial(result_kernel, layouts=[weight[0], recep...  27.1 us
    pallas_call x1, Pallas kernels, time_back(): pl.pallas_call(functools.partial(time_back_kernel, layout=weight[0]), gri...  25.9 us
  transfers between devices with their start and end apart: 103, of which 33 were waited for; matrix products, arithmetic and copies ran while one was open for 10% of the time, Pallas kernels for 39%

profile of v2, /device:TPU:0, one launch (start us, length us, event | category | flops | bytes accessed | tf_op | source)
XLA Modules:
  0.0 655.4 jit_solution(1623361861510280926)
XLA Ops:
  9.0 4.1 collective-permute-start
  34.3 4.1 collective-permute-start.14
  38.4 4.1 collective-permute-done.5
  49.1 14.3 %collective-permute-done.12 = bf16[2,64,512]{2,1,0:T(8,128)(2,1)S(1)} collective-permute-done((bf16[2,64,512]{2,1,0:T(8,128)(2,1)S(1)}, bf16[2,64,512]{2,1,0:T(8,128)(2,1)S(1)}, u32[]{:S(2)}, u32[]{:S(2)}) %collective-permute-start.12) | collective-permute-done | bytes 131104 | tf_op jit(solution)/shard_map/ppermute | solution.py:892
  65.3 5.3 collective-permute-start.17
  80.6 19.0 %collective-permute-done.26 = f32[16,1024]{1,0:T(8,128)S(1)} collective-permute-done((f32[16,1024]{1,0:T(8,128)S(1)}, f32[16,1024]{1,0:T(8,128)S(1)}, u32[]{:S(2)}, u32[]{:S(2)}) %collective-permute-start.26) | collective-permute-done | bytes 65568 | tf_op jit(solution)/shard_map/ppermute | solution.py:892
  102.6 14.5 %shard_map.364 = (bf16[1024,1024]{1,0:T(8,128)(2,1)}, bf16[1024,1024]{1,0:T(8,128)(2,1)}, bf16[1024,1024]{1,0:T(8,128)(2,1)}) custom-call(bf16[1024,1024]{1,0:T(8,128)(2,1)} %x_ref.5, f32[1024,1]{1,0:T(8,128)} %copy.92.carry_ref, f32[16,1024]{1,0:T(8,128)} %add.235.vec_ref.vec), custom_call_target="tpu_custom_call" | custom-call | bytes 8388608 | tf_op jit(solution)/shard_map/pallas_call | solution.py:180
  117.1 5.7 collective-permute-done.21.refs_9_
  134.3 6.2 collective-permute-done.30.refs_1_
  150.3 3.5 broadcast_in_dim.133.masks
  153.8 30.4 %shard_map.365 = (f32[1024,1024]{1,0:T(8,128)}, f32[1024,1024]{1,0:T(8,128)}, f32[1024,1024]{1,0:T(8,128)}, f32[1024,1024]{1,0:T(8,128)}, f32[1024,1024]{1,0:T(8,128)}, /*index=5*/bf16[1024,1024]{1,0:T(8,128)(2,1)}) custom-call(s32[5]{0:T(128)} %stack.234.co, bf16[1024,1024]{1,0:T(8,128)(2,1)} %get-tuple-element.410.mk.model_ref, ...), custom_call_target="tpu_custom_call" | custom-call | flops 17179869184 | bytes 35651584 | tf_op jit(solution)/shard_map/pallas_call | solution.py:280
  188.0 3.7 maximum_select_fusion.teacher_ref
  191.7 16.8 %shard_map.366 = (f32[1024,1024]{1,0:T(8,128)}, bf16[1024,1024]{1,0:T(8,128)(2,1)}, bf16[1024,1024]{1,0:T(8,128)(2,1)}) custom-call(s32[5]{0:T(128)} %stack.234.co, bf16[1024,1024]{1,0:T(8,128)(2,1)} %get-tuple-element.432.gated.chan_ref, bf16[1024,1024]{1,0:T(8,128)(2,1)} %x_ref.5, f32[1024,1]{1,0:T(8,128)} %copy.92.carry_ref, ...), custom_call_target="tpu_custom_call" | custom-call | flops 6442450944 | bytes 14680064 | tf_op jit(solution)/shard_map/pallas_call | solution.py:339
  209.5 18.2 %shard_map.367 = (bf16[1024,4096]{1,0:T(8,128)(2,1)}, bf16[1024,4096]{1,0:T(8,128)(2,1)}) custom-call(s32[5]{0:T(128)} %stack.234.co, bf16[1024,1024]{1,0:T(8,128)(2,1)} %get-tuple-element.440.mk.model_ref, bf16[2,2,2,64,1024]{4,3,2,1,0:T(8,128)(2,1)} %copy-done.14, bf16[2,2,2,64,1024]{4,3,2,1,0:T(8,128)(2,1)} %collective-permute-done.35.refs_1_, ...), custom_call_target="tpu_custom_call" | custom-call | flops 9663676416 | bytes 27262976 | tf_op jit(solution)/shard_map/pallas_call | solution.py:397
  227.8 27.1 %shard_map.368 = (bf16[1024,1024]{1,0:T(8,128)(2,1)}, f32[1024,1024]{1,0:T(8,128)}, bf16[1024,1024]{1,0:T(8,128)(2,1)}, bf16[1024,1024]{1,0:T(8,128)(2,1)}, f32[8,1024]{1,0:T(8,128)}) custom-call(s32[5]{0:T(128)} %stack.234.co, f32[1]{0:T(128)} %bitcast.44.scale, bf16[1024,4096]{1,0:T(8,128)(2,1)} %get-tuple-element.463.hidden.chan_ref, ...), custom_call_target="tpu_custom_call" | custom-call | flops 15032385536 | bytes 39845888 | tf_op jit(solution)/shard_map/pallas_call | solution.py:466
  254.9 9.8 %shard_map.369 = (bf16[2,2,2,64,1024]{4,3,2,1,0:T(8,128)(2,1)}, bf16[2,2,2,64,1024]{4,3,2,1,0:T(8,128)(2,1)}, bf16[2,2,2,64,1024]{4,3,2,1,0:T(8,128)(2,1)}, bf16[2,2,2,64,1024]{4,3,2,1,0:T(8,128)(2,1)}) custom-call(s32[5]{0:T(128)} %stack.234.co, bf16[1024,1024]{1,0:T(8,128)(2,1)} %get-tuple-element.477.model_ref.dkv, ...), custom_call_target="tpu_custom_call" | custom-call | flops 5153960960 | bytes 10485760 | tf_op jit(solution)/shard_map/pallas_call | solution.py:540
  270.0 6.5 shard_map.374
  276.6 9.7 %shard_map.370 = (bf16[2,2,2,64,1024]{4,3,2,1,0:T(8,128)(2,1)}, bf16[2,2,2,64,1024]{4,3,2,1,0:T(8,128)(2,1)}, bf16[2,2,2,64,1024]{4,3,2,1,0:T(8,128)(2,1)}, bf16[2,2,2,64,1024]{4,3,2,1,0:T(8,128)(2,1)}) custom-call(s32[5]{0:T(128)} %stack.234.co, bf16[1024,1024]{1,0:T(8,128)(2,1)} %get-tuple-element.477.model_ref.dkv, ...), custom_call_target="tpu_custom_call" | custom-call | flops 5153960960 | bytes 10485760 | tf_op jit(solution)/shard_map/pallas_call | solution.py:540
  286.2 5.8 collective-permute-done.44
  297.2 17.5 %shard_map.371.chan_ref.dkey = bf16[1024,4096]{1,0:T(8,128)(2,1)} custom-call(s32[5]{0:T(128)} %stack.234.co, bf16[1024,1024]{1,0:T(8,128)(2,1)} %get-tuple-element.477.model_ref.dkv, bf16[1024,4096]{1,0:T(8,128)(2,1)} %get-tuple-element.478.active_ref, bf16[16,2,64,2560]{3,2,1,0:T(8,128)(2,1)} %bitcast.312), custom_call_target="tpu_custom_call" | custom-call | flops 9663676416 | bytes 27262976 | tf_op jit(solution)/shard_map/pallas_call | solution.py:586
  316.7 9.7 %shard_map.372 = (bf16[2,2,2,64,1024]{4,3,2,1,0:T(8,128)(2,1)}, bf16[2,2,2,64,1024]{4,3,2,1,0:T(8,128)(2,1)}, bf16[2,2,2,64,1024]{4,3,2,1,0:T(8,128)(2,1)}, bf16[2,2,2,64,1024]{4,3,2,1,0:T(8,128)(2,1)}) custom-call(s32[5]{0:T(128)} %stack.234.co, bf16[1024,1024]{1,0:T(8,128)(2,1)} %get-tuple-element.440.mk.model_ref, bf16[1024,4096]{1,0:T(8,128)(2,1)} %shard_map.371.chan_ref.dkey), custom_call_target="tpu_custom_call" | custom-call | flops 5153960960 | bytes 10485760 | tf_op jit(solution)/shard_map/pallas_call | solution.py:540
  326.4 2.7 add.242
  334.1 9.7 %shard_map.373 = (bf16[2,2,2,64,1024]{4,3,2,1,0:T(8,128)(2,1)}, bf16[2,2,2,64,1024]{4,3,2,1,0:T(8,128)(2,1)}, bf16[2,2,2,64,1024]{4,3,2,1,0:T(8,128)(2,1)}, bf16[2,2,2,64,1024]{4,3,2,1,0:T(8,128)(2,1)}) custom-call(s32[5]{0:T(128)} %stack.234.co, bf16[1024,1024]{1,0:T(8,128)(2,1)} %get-tuple-element.440.mk.model_ref, bf16[1024,4096]{1,0:T(8,128)(2,1)} %shard_map.371.chan_ref.dkey), custom_call_target="tpu_custom_call" | custom-call | flops 5153960960 | bytes 10485760 | tf_op jit(solution)/shard_map/pallas_call | solution.py:540
  343.8 3.0 add.243
  348.6 5.8 collective-permute-done.49
  354.4 43.0 %shard_map.375 = (f32[1024,1024]{1,0:T(8,128)}, bf16[1024,1024]{1,0:T(8,128)(2,1)}, f32[4,8,1024]{2,1,0:T(8,128)}) custom-call(s32[5]{0:T(128)} %stack.234.co, bf16[1024,4096]{1,0:T(8,128)(2,1)} %shard_map.371.chan_ref.dkey, bf16[1024,1024]{1,0:T(8,128)(2,1)} %get-tuple-element.518.chan_ref.drec, f32[1024,1024]{1,0:T(8,128)} %get-tuple-element.451.middle_ref, ...), custom_call_target="tpu_custom_call" | custom-call | flops 17179869184 | bytes 37748736 | tf_op jit(solution)/shard_map/pallas_call | solution.py:663
  404.9 6.5 shard_map.376
  411.4 2.7 add.252
  419.8 2.7 collective-permute-done.57
  423.8 25.9 %shard_map.377 = (bf16[1024,1024]{1,0:T(8,128)(2,1)}, bf16[1024,1024]{1,0:T(8,128)(2,1)}, bf16[1024,1024]{1,0:T(8,128)(2,1)}, f32[2,8,1024]{2,1,0:T(8,128)}) custom-call(s32[5]{0:T(128)} %stack.234.co, bf16[1024,1024]{1,0:T(8,128)(2,1)} %get-tuple-element.553.model_ref.dtime, f32[1024,1024]{1,0:T(8,128)} %get-tuple-element.554.key_ref, ...), custom_call_target="tpu_custom_call" | custom-call | flops 19327352832 | bytes 35651584 | tf_op jit(solution)/shard_map/pallas_call | solution.py:779
  449.8 4.1 collective-permute-start.60
  455.8 3.3 collective-permute-done.60
  459.1 7.0 %collective-permute-start.62 = (bf16[2,64,1024]{2,1,0:T(8,128)(2,1)S(1)}, bf16[2,64,1024]{2,1,0:T(8,128)(2,1)S(1)}, u32[]{:S(2)}, u32[]{:S(2)}) collective-permute-start(bf16[2,64,1024]{2,1,0:T(8,128)(2,1)S(1)} %fusion.8), channel_id=1, source_target_pairs={{0,4},{4,0},{1,5},{5,1},{2,6},{6,2},{3,7},{7,3},{8,12},{12,8},{9,1... | collective-permute-start | bytes 786440 | tf_op jit(solution)/shard_map/ppermute | solution.py:892
  466.2 4.3 collective-permute-done.61
  475.4 6.8 %shard_map.378 = (bf16[2,2,2,64,512]{4,3,2,1,0:T(8,128)(2,1)}, bf16[2,2,2,64,512]{4,3,2,1,0:T(8,128)(2,1)}, bf16[2,2,2,64,512]{4,3,2,1,0:T(8,128)(2,1)}, bf16[2,2,2,64,512]{4,3,2,1,0:T(8,128)(2,1)}) custom-call(s32[5]{0:T(128)} %stack.234.co, bf16[1024,1024]{1,0:T(8,128)(2,1)} %get-tuple-element.410.mk.model_ref, ...), custom_call_target="tpu_custom_call" | custom-call | flops 2576980480 | bytes 6291456 | tf_op jit(solution)/shard_map/pallas_call | solution.py:540
  488.7 3.3 collective-permute-done.69
  492.0 6.7 %collective-permute-done.68 = bf16[2,2,64,1024]{3,2,1,0:T(8,128)(2,1)S(1)} collective-permute-done((bf16[2,2,64,1024]{3,2,1,0:T(8,128)(2,1)}, bf16[2,2,64,1024]{3,2,1,0:T(8,128)(2,1)S(1)}, u32[]{:S(2)}, u32[]{:S(2)}) %collective-permute-start.68) | collective-permute-done | bytes 524320 | tf_op jit(solution)/shard_map/ppermute | solution.py:892
  502.0 6.5 shard_map.379
  508.6 6.7 %shard_map.380 = (bf16[2,2,2,64,512]{4,3,2,1,0:T(8,128)(2,1)}, bf16[2,2,2,64,512]{4,3,2,1,0:T(8,128)(2,1)}, bf16[2,2,2,64,512]{4,3,2,1,0:T(8,128)(2,1)}, bf16[2,2,2,64,512]{4,3,2,1,0:T(8,128)(2,1)}) custom-call(s32[5]{0:T(128)} %stack.234.co, bf16[1024,1024]{1,0:T(8,128)(2,1)} %get-tuple-element.412.mr.model_ref, ...), custom_call_target="tpu_custom_call" | custom-call | flops 2576980480 | bytes 6291456 | tf_op jit(solution)/shard_map/pallas_call | solution.py:540
  522.6 5.8 collective-permute-done.78
  530.3 6.4 collective-permute-done.79
  541.0 37.0 %shard_map.381 = (f32[1024,1024]{1,0:T(8,128)}, f32[5,8,1024]{2,1,0:T(8,128)}) custom-call(s32[5]{0:T(128)} %stack.234.co, bf16[1024,1024]{1,0:T(8,128)(2,1)} %get-tuple-element.645.chan_ref.dkey, bf16[1024,1024]{1,0:T(8,128)(2,1)} %get-tuple-element.646.chan_ref.dval, bf16[1024,1024]{1,0:T(8,128)(2,1)} %get-tuple-element.647.chan_ref.drec, ...), custom_call_target="tpu_custom_call" | custom-call | flops 15032385536 | bytes 27262976 | tf_op jit(solution)/shard_map/pallas_call | solution.py:862
  591.2 12.3 %collective-permute-done.101 = bf16[64,512]{1,0:T(8,128)(2,1)S(1)} collective-permute-done((bf16[64,512]{1,0:T(8,128)(2,1)S(1)}, bf16[64,512]{1,0:T(8,128)(2,1)S(1)}, u32[]{:S(2)}, u32[]{:S(2)}) %collective-permute-start.101) | collective-permute-done | bytes 65568 | tf_op jit(solution)/shard_map/ppermute | solution.py:892
  605.7 3.1 collective-permute-done.85
  612.3 5.6 collective-permute-done.100
  625.2 3.0 collective-permute-start.92
  637.9 3.1 collective-permute-done.96
  643.5 2.8 collective-permute-done.97
  (538 shorter events, 169.7 us)
Async XLA Ops:
  7.2 220.6 %all-gather.3.cloned.1.call-start = ((), (), s32[]{:S(2)}) async-start(), calls=%async_computation | async-start | bytes 10813440 | tf_op jit(solution)/shard_map/all_gather | solution.py:1090
  9.0 18.0 %collective-permute-start = (bf16[64,512]{1,0:T(8,128)(2,1)}, bf16[64,512]{1,0:T(8,128)(2,1)S(1)}, u32[]{:S(2)}, u32[]{:S(2)}) collective-permute-start(bf16[64,512]{1,0:T(8,128)(2,1)} %param.31), channel_id=1, source_target_pairs={{0,16},{16,0},{1,17},{17,1},{2,18},{18,2},{3,19},{19,3},{4,20},{20... | collective-permute-start | bytes 196616 | tf_op jit(solution)/shard_map/ppermute | solution.py:892
  42.6 21.9 %collective-permute-start.9 = (bf16[2,2,64,512]{3,2,1,0:T(8,128)(2,1)S(1)}, bf16[2,2,64,512]{3,2,1,0:T(8,128)(2,1)S(1)}, u32[]{:S(2)}, u32[]{:S(2)}) collective-permute-start(bf16[2,2,64,512]{3,2,1,0:T(8,128)(2,1)S(1)} %pad_maximum_fusion.10), channel_id=1, source_target_pairs={{0,8},{8,0},{1,9},{9,1},{2,10},{10,2},{3,11},{11,3},{4,12},{12,4},... | collective-permute-start | bytes 786440 | tf_op jit(solution)/shard_map/ppermute | solution.py:892
  42.7 21.8 %collective-permute-start.10 = (bf16[2,2,64,512]{3,2,1,0:T(8,128)(2,1)S(1)}, bf16[2,2,64,512]{3,2,1,0:T(8,128)(2,1)S(1)}, u32[]{:S(2)}, u32[]{:S(2)}) collective-permute-start(bf16[2,2,64,512]{3,2,1,0:T(8,128)(2,1)S(1)} %pad_maximum_fusion.11), channel_id=1, source_target_pairs={{0,4},{4,0},{1,5},{5,1},{2,6},{6,2},{3,7},{7,3},{8,12},{12,8},{9,1... | collective-permute-start | bytes 786440 | tf_op jit(solution)/shard_map/ppermute | solution.py:892
  44.3 20.2 %collective-permute-start.11 = (bf16[2,2,64,512]{3,2,1,0:T(8,128)(2,1)S(1)}, bf16[2,2,64,512]{3,2,1,0:T(8,128)(2,1)S(1)}, u32[]{:S(2)}, u32[]{:S(2)}) collective-permute-start(bf16[2,2,64,512]{3,2,1,0:T(8,128)(2,1)S(1)} %pad_maximum_fusion.12), channel_id=1, source_target_pairs={{0,1},{1,0},{2,3},{3,2},{4,5},{5,4},{6,7},{7,6},{8,9},{9,8},{10,11... | collective-permute-start | bytes 786440 | tf_op jit(solution)/shard_map/ppermute | solution.py:892
  65.3 35.3 %collective-permute-start.17 = (bf16[2,2,2,64,512]{4,3,2,1,0:T(8,128)(2,1)S(1)}, bf16[2,2,2,64,512]{4,3,2,1,0:T(8,128)(2,1)}, u32[]{:S(2)}, u32[]{:S(2)}) collective-permute-start(bf16[2,2,2,64,512]{4,3,2,1,0:T(8,128)(2,1)S(1)} %pad_maximum_fusion.2.refs_0_), channel_id=1, source_target_pairs={{0,4},{4,0},{1,5},{5,1},{2,6},{6,2},{3,7},{7,3},{8,12},{12,8},{9,1... | collective-permute-start | bytes 1572872 | tf_op jit(solution)/shard_map/ppermute | solution.py:892
  70.7 29.0 %collective-permute-start.23 = (bf16[2,2,64,512]{3,2,1,0:T(8,128)(2,1)S(1)}, bf16[2,2,64,512]{3,2,1,0:T(8,128)(2,1)}, u32[]{:S(2)}, u32[]{:S(2)}) collective-permute-start(bf16[2,2,64,512]{3,2,1,0:T(8,128)(2,1)S(1)} %pad_maximum_fusion.13), channel_id=1, source_target_pairs={{0,4},{4,0},{1,5},{5,1},{2,6},{6,2},{3,7},{7,3},{8,12},{12,8},{9,1... | collective-permute-start | bytes 786440 | tf_op jit(solution)/shard_map/ppermute | solution.py:892
  70.8 29.0 %collective-permute-start.24 = (bf16[2,64,1024]{2,1,0:T(8,128)(2,1)S(1)}, bf16[2,64,1024]{2,1,0:T(8,128)(2,1)S(1)}, u32[]{:S(2)}, u32[]{:S(2)}) collective-permute-start(bf16[2,64,1024]{2,1,0:T(8,128)(2,1)S(1)} %pad_maximum_fusion.14), channel_id=1, source_target_pairs={{0,1},{1,0},{2,3},{3,2},{4,5},{5,4},{6,7},{7,6},{8,9},{9,8},{10,11... | collective-permute-start | bytes 786440 | tf_op jit(solution)/shard_map/ppermute | solution.py:892
  72.0 28.3 %collective-permute-start.25 = (bf16[2,64,1024]{2,1,0:T(8,128)(2,1)S(1)}, bf16[2,64,1024]{2,1,0:T(8,128)(2,1)S(1)}, u32[]{:S(2)}, u32[]{:S(2)}) collective-permute-start(bf16[2,64,1024]{2,1,0:T(8,128)(2,1)S(1)} %pad_maximum_fusion.15), channel_id=1, source_target_pairs={{0,16},{16,0},{1,17},{17,1},{2,18},{18,2},{3,19},{19,3},{4,20},{20... | collective-permute-start | bytes 786440 | tf_op jit(solution)/shard_map/ppermute | solution.py:892
  76.0 23.6 %collective-permute-start.26 = (f32[16,1024]{1,0:T(8,128)S(1)}, f32[16,1024]{1,0:T(8,128)S(1)}, u32[]{:S(2)}, u32[]{:S(2)}) collective-permute-start(f32[16,1024]{1,0:T(8,128)S(1)} %add.234), channel_id=1, source_target_pairs={{0,16},{16,0},{1,17},{17,1},{2,18},{18,2},{3,19},{19,3},{4,20},{20... | collective-permute-start | bytes 196616 | tf_op jit(solution)/shard_map/ppermute | solution.py:892
  100.3 22.5 %collective-permute-start.21 = (bf16[2,2,2,64,512]{4,3,2,1,0:T(8,128)(2,1)S(1)}, bf16[2,2,2,64,512]{4,3,2,1,0:T(8,128)(2,1)}, u32[]{:S(2)}, u32[]{:S(2)}) collective-permute-start(bf16[2,2,2,64,512]{4,3,2,1,0:T(8,128)(2,1)S(1)} %pad_maximum_fusion.4.refs_8_), channel_id=1, source_target_pairs={{0,8},{8,0},{1,9},{9,1},{2,10},{10,2},{3,11},{11,3},{4,12},{12,4},... | collective-permute-start | bytes 1572872 | tf_op jit(solution)/shard_map/ppermute | solution.py:892
  100.6 22.2 %collective-permute-start.22 = (bf16[2,2,2,64,512]{4,3,2,1,0:T(8,128)(2,1)S(1)}, bf16[2,2,2,64,512]{4,3,2,1,0:T(8,128)(2,1)}, u32[]{:S(2)}, u32[]{:S(2)}) collective-permute-start(bf16[2,2,2,64,512]{4,3,2,1,0:T(8,128)(2,1)S(1)} %pad_maximum_fusion.4.refs_8_), channel_id=1, source_target_pairs={{0,2},{2,0},{1,3},{3,1},{4,6},{6,4},{5,7},{7,5},{8,10},{10,8},{9,1... | collective-permute-start | bytes 1572872 | tf_op jit(solution)/shard_map/ppermute | solution.py:892
  133.9 54.1 %collective-permute-start.41 = (bf16[1024,512]{1,0:T(8,128)(2,1)S(1)}, bf16[1024,512]{1,0:T(8,128)(2,1)}, u32[]{:S(2)}, u32[]{:S(2)}) collective-permute-start(bf16[1024,512]{1,0:T(8,128)(2,1)S(1)} %get-tuple-element.686), channel_id=1, source_target_pairs={{0,1},{1,0},{2,3},{3,2},{4,5},{5,4},{6,7},{7,6},{8,9},{9,8},{10,11... | collective-permute-start | bytes 3145736 | tf_op jit(solution)/shard_map/ppermute | solution.py:892
  146.7 37.5 %collective-permute-start.35 = (bf16[2,2,2,64,1024]{4,3,2,1,0:T(8,128)(2,1)S(1)}, bf16[2,2,2,64,1024]{4,3,2,1,0:T(8,128)(2,1)}, u32[]{:S(2)}, u32[]{:S(2)}) collective-permute-start(bf16[2,2,2,64,1024]{4,3,2,1,0:T(8,128)(2,1)S(1)} %pad_maximum_fusion.refs_0_), channel_id=1, source_target_pairs={{0,4},{4,0},{1,5},{5,1},{2,6},{6,2},{3,7},{7,3},{8,12},{12,8},{9,1... | collective-permute-start | bytes 3145736 | tf_op jit(solution)/shard_map/ppermute | solution.py:892
  148.4 35.8 %collective-permute-start.36 = (bf16[2,2,2,64,1024]{4,3,2,1,0:T(8,128)(2,1)S(1)}, bf16[2,2,2,64,1024]{4,3,2,1,0:T(8,128)(2,1)}, u32[]{:S(2)}, u32[]{:S(2)}) collective-permute-start(bf16[2,2,2,64,1024]{4,3,2,1,0:T(8,128)(2,1)S(1)} %pad_maximum_fusion.refs_0_), channel_id=1, source_target_pairs={{0,2},{2,0},{1,3},{3,1},{4,6},{6,4},{5,7},{7,5},{8,10},{10,8},{9,1... | collective-permute-start | bytes 3145736 | tf_op jit(solution)/shard_map/ppermute | solution.py:892
  149.8 34.8 %collective-permute-start.37 = (bf16[2,2,2,64,1024]{4,3,2,1,0:T(8,128)(2,1)S(1)}, bf16[2,2,2,64,1024]{4,3,2,1,0:T(8,128)(2,1)}, u32[]{:S(2)}, u32[]{:S(2)}) collective-permute-start(bf16[2,2,2,64,1024]{4,3,2,1,0:T(8,128)(2,1)S(1)} %pad_maximum_fusion.1.refs_4_), channel_id=1, source_target_pairs={{0,1},{1,0},{2,3},{3,2},{4,5},{5,4},{6,7},{7,6},{8,9},{9,8},{10,11... | collective-permute-start | bytes 3145736 | tf_op jit(solution)/shard_map/ppermute | solution.py:892
  150.3 34.3 %collective-permute-start.38 = (bf16[2,2,2,64,1024]{4,3,2,1,0:T(8,128)(2,1)S(1)}, bf16[2,2,2,64,1024]{4,3,2,1,0:T(8,128)(2,1)}, u32[]{:S(2)}, u32[]{:S(2)}) collective-permute-start(bf16[2,2,2,64,1024]{4,3,2,1,0:T(8,128)(2,1)S(1)} %pad_maximum_fusion.1.refs_4_), channel_id=1, source_target_pairs={{0,2},{2,0},{1,3},{3,1},{4,6},{6,4},{5,7},{7,5},{8,10},{10,8},{9,1... | collective-permute-start | bytes 3145736 | tf_op jit(solution)/shard_map/ppermute | solution.py:892
  184.6 23.9 %collective-permute-start.39 = (bf16[2,2,2,64,1024]{4,3,2,1,0:T(8,128)(2,1)}, bf16[2,2,2,64,1024]{4,3,2,1,0:T(8,128)(2,1)S(1)}, u32[]{:S(2)}, u32[]{:S(2)}) collective-permute-start(bf16[2,2,2,64,1024]{4,3,2,1,0:T(8,128)(2,1)} %collective-permute-done.35.refs_1_), channel_id=1, source_target_pairs={{0,2},{2,0},{1,3},{3,1},{4,6},{6,4},{5,7},{7,5},{8,10},{10,8},{9,1... | collective-permute-start | bytes 3145736 | tf_op jit(solution)/shard_map/ppermute | solution.py:892
  184.8 23.7 %collective-permute-start.40 = (bf16[2,2,2,64,1024]{4,3,2,1,0:T(8,128)(2,1)}, bf16[2,2,2,64,1024]{4,3,2,1,0:T(8,128)(2,1)}, u32[]{:S(2)}, u32[]{:S(2)}) collective-permute-start(bf16[2,2,2,64,1024]{4,3,2,1,0:T(8,128)(2,1)} %collective-permute-done.37.refs_5_), channel_id=1, source_target_pairs={{0,2},{2,0},{1,3},{3,1},{4,6},{6,4},{5,7},{7,5},{8,10},{10,8},{9,1... | collective-permute-start | bytes 3145736 | tf_op jit(solution)/shard_map/ppermute | solution.py:892
  264.7 21.5 %collective-permute-start.42 = (bf16[2,2,2,64,1024]{4,3,2,1,0:T(8,128)(2,1)}, bf16[2,2,2,64,1024]{4,3,2,1,0:T(8,128)(2,1)}, u32[]{:S(2)}, u32[]{:S(2)}) collective-permute-start(bf16[2,2,2,64,1024]{4,3,2,1,0:T(8,128)(2,1)} %get-tuple-element.460), channel_id=1, source_target_pairs={{0,2},{2,0},{1,3},{3,1},{4,6},{6,4},{5,7},{7,5},{8,10},{10,8},{9,1... | collective-permute-start | bytes 3145736 | tf_op jit(solution)/shard_map/ppermute | solution.py:892
  265.0 21.2 %collective-permute-start.43 = (bf16[2,2,2,64,1024]{4,3,2,1,0:T(8,128)(2,1)}, bf16[2,2,2,64,1024]{4,3,2,1,0:T(8,128)(2,1)S(1)}, u32[]{:S(2)}, u32[]{:S(2)}) collective-permute-start(bf16[2,2,2,64,1024]{4,3,2,1,0:T(8,128)(2,1)} %get-tuple-element.461), channel_id=1, source_target_pairs={{0,2},{2,0},{1,3},{3,1},{4,6},{6,4},{5,7},{7,5},{8,10},{10,8},{9,1... | collective-permute-start | bytes 3145736 | tf_op jit(solution)/shard_map/ppermute | solution.py:892
  266.5 25.5 %collective-permute-start.44 = (bf16[1024,512]{1,0:T(8,128)(2,1)}, bf16[1024,512]{1,0:T(8,128)(2,1)S(1)}, u32[]{:S(2)}, u32[]{:S(2)}) collective-permute-start(bf16[1024,512]{1,0:T(8,128)(2,1)} %get-tuple-element.684), channel_id=1, source_target_pairs={{0,1},{1,0},{2,3},{3,2},{4,5},{5,4},{6,7},{7,6},{8,9},{9,8},{10,11... | collective-permute-start | bytes 3145736 | tf_op jit(solution)/shard_map/ppermute | solution.py:892
  294.6 31.7 %collective-permute-start.45 = (bf16[2,2,2,64,1024]{4,3,2,1,0:T(8,128)(2,1)}, bf16[2,2,2,64,1024]{4,3,2,1,0:T(8,128)(2,1)}, u32[]{:S(2)}, u32[]{:S(2)}) collective-permute-start(bf16[2,2,2,64,1024]{4,3,2,1,0:T(8,128)(2,1)} %add.239), channel_id=1, source_target_pairs={{0,4},{4,0},{1,5},{5,1},{2,6},{6,2},{3,7},{7,3},{8,12},{12,8},{9,1... | collective-permute-start | bytes 3145736 | tf_op jit(solution)/shard_map/ppermute | solution.py:892
  296.7 20.0 %collective-permute-start.46 = (bf16[2,2,2,64,1024]{4,3,2,1,0:T(8,128)(2,1)}, bf16[2,2,2,64,1024]{4,3,2,1,0:T(8,128)(2,1)}, u32[]{:S(2)}, u32[]{:S(2)}) collective-permute-start(bf16[2,2,2,64,1024]{4,3,2,1,0:T(8,128)(2,1)} %get-tuple-element.475), channel_id=1, source_target_pairs={{0,2},{2,0},{1,3},{3,1},{4,6},{6,4},{5,7},{7,5},{8,10},{10,8},{9,1... | collective-permute-start | bytes 3145736 | tf_op jit(solution)/shard_map/ppermute | solution.py:892
  296.7 20.0 %collective-permute-start.47 = (bf16[2,2,2,64,1024]{4,3,2,1,0:T(8,128)(2,1)}, bf16[2,2,2,64,1024]{4,3,2,1,0:T(8,128)(2,1)S(1)}, u32[]{:S(2)}, u32[]{:S(2)}) collective-permute-start(bf16[2,2,2,64,1024]{4,3,2,1,0:T(8,128)(2,1)} %get-tuple-element.476), channel_id=1, source_target_pairs={{0,2},{2,0},{1,3},{3,1},{4,6},{6,4},{5,7},{7,5},{8,10},{10,8},{9,1... | collective-permute-start | bytes 3145736 | tf_op jit(solution)/shard_map/ppermute | solution.py:892
  329.1 25.3 %collective-permute-start.49 = (bf16[2,2,2,64,1024]{4,3,2,1,0:T(8,128)(2,1)}, bf16[2,2,2,64,1024]{4,3,2,1,0:T(8,128)(2,1)S(1)}, u32[]{:S(2)}, u32[]{:S(2)}) collective-permute-start(bf16[2,2,2,64,1024]{4,3,2,1,0:T(8,128)(2,1)} %add.242), channel_id=1, source_target_pairs={{0,1},{1,0},{2,3},{3,2},{4,5},{5,4},{6,7},{7,6},{8,9},{9,8},{10,11... | collective-permute-start | bytes 3145736 | tf_op jit(solution)/shard_map/ppermute | solution.py:892
  346.8 50.7 %collective-permute-start.52 = (bf16[2,2,2,64,1024]{4,3,2,1,0:T(8,128)(2,1)}, bf16[2,2,2,64,1024]{4,3,2,1,0:T(8,128)(2,1)}, u32[]{:S(2)}, u32[]{:S(2)}) collective-permute-start(bf16[2,2,2,64,1024]{4,3,2,1,0:T(8,128)(2,1)} %add.243), channel_id=1, source_target_pairs={{0,8},{8,0},{1,9},{9,1},{2,10},{10,2},{3,11},{11,3},{4,12},{12,4},... | collective-permute-start | bytes 3145736 | tf_op jit(solution)/shard_map/ppermute | solution.py:892
  348.1 49.5 %collective-permute-start.53 = (bf16[2,2,2,64,1024]{4,3,2,1,0:T(8,128)(2,1)}, bf16[2,2,2,64,1024]{4,3,2,1,0:T(8,128)(2,1)}, u32[]{:S(2)}, u32[]{:S(2)}) collective-permute-start(bf16[2,2,2,64,1024]{4,3,2,1,0:T(8,128)(2,1)} %get-tuple-element.511), channel_id=1, source_target_pairs={{0,2},{2,0},{1,3},{3,1},{4,6},{6,4},{5,7},{7,5},{8,10},{10,8},{9,1... | collective-permute-start | bytes 3145736 | tf_op jit(solution)/shard_map/ppermute | solution.py:892
  348.1 49.5 %collective-permute-start.54 = (bf16[2,2,2,64,1024]{4,3,2,1,0:T(8,128)(2,1)}, bf16[2,2,2,64,1024]{4,3,2,1,0:T(8,128)(2,1)S(1)}, u32[]{:S(2)}, u32[]{:S(2)}) collective-permute-start(bf16[2,2,2,64,1024]{4,3,2,1,0:T(8,128)(2,1)} %get-tuple-element.512), channel_id=1, source_target_pairs={{0,2},{2,0},{1,3},{3,1},{4,6},{6,4},{5,7},{7,5},{8,10},{10,8},{9,1... | collective-permute-start | bytes 3145736 | tf_op jit(solution)/shard_map/ppermute | solution.py:892
  348.6 48.9 %collective-permute-start.55 = (bf16[2,2,2,64,512]{4,3,2,1,0:T(8,128)(2,1)}, bf16[2,2,2,64,512]{4,3,2,1,0:T(8,128)(2,1)}, u32[]{:S(2)}, u32[]{:S(2)}) collective-permute-start(bf16[2,2,2,64,512]{4,3,2,1,0:T(8,128)(2,1)} %get-tuple-element.515), channel_id=1, source_target_pairs={{0,2},{2,0},{1,3},{3,1},{4,6},{6,4},{5,7},{7,5},{8,10},{10,8},{9,1... | collective-permute-start | bytes 1572872 | tf_op jit(solution)/shard_map/ppermute | solution.py:892
  354.4 43.1 %collective-permute-start.56 = (bf16[2,2,2,64,512]{4,3,2,1,0:T(8,128)(2,1)}, bf16[2,2,2,64,512]{4,3,2,1,0:T(8,128)(2,1)S(1)}, u32[]{:S(2)}, u32[]{:S(2)}) collective-permute-start(bf16[2,2,2,64,512]{4,3,2,1,0:T(8,128)(2,1)} %get-tuple-element.516), channel_id=1, source_target_pairs={{0,2},{2,0},{1,3},{3,1},{4,6},{6,4},{5,7},{7,5},{8,10},{10,8},{9,1... | collective-permute-start | bytes 1572872 | tf_op jit(solution)/shard_map/ppermute | solution.py:892
  402.0 20.6 %collective-permute-start.58 = (bf16[2,2,64,1024]{3,2,1,0:T(8,128)(2,1)}, bf16[2,2,64,1024]{3,2,1,0:T(8,128)(2,1)}, u32[]{:S(2)}, u32[]{:S(2)}) collective-permute-start(bf16[2,2,64,1024]{3,2,1,0:T(8,128)(2,1)} %fusion.1), channel_id=1, source_target_pairs={{0,4},{4,0},{1,5},{5,1},{2,6},{6,2},{3,7},{7,3},{8,12},{12,8},{9,1... | collective-permute-start | bytes 1572872 | tf_op jit(solution)/shard_map/ppermute | solution.py:892
  402.0 20.6 %collective-permute-start.59 = (bf16[2,2,64,1024]{3,2,1,0:T(8,128)(2,1)}, bf16[2,2,64,1024]{3,2,1,0:T(8,128)(2,1)}, u32[]{:S(2)}, u32[]{:S(2)}) collective-permute-start(bf16[2,2,64,1024]{3,2,1,0:T(8,128)(2,1)} %fusion.2), channel_id=1, source_target_pairs={{0,1},{1,0},{2,3},{3,2},{4,5},{5,4},{6,7},{7,6},{8,9},{9,8},{10,11... | collective-permute-start | bytes 1572872 | tf_op jit(solution)/shard_map/ppermute | solution.py:892
  404.5 18.0 %collective-permute-start.57 = (bf16[2,64,1024]{2,1,0:T(8,128)(2,1)}, bf16[2,64,1024]{2,1,0:T(8,128)(2,1)S(1)}, u32[]{:S(2)}, u32[]{:S(2)}) collective-permute-start(bf16[2,64,1024]{2,1,0:T(8,128)(2,1)} %fusion.6), channel_id=1, source_target_pairs={{0,1},{1,0},{2,3},{3,2},{4,5},{5,4},{6,7},{7,6},{8,9},{9,8},{10,11... | collective-permute-start | bytes 786440 | tf_op jit(solution)/shard_map/ppermute | solution.py:892
  414.1 56.3 %collective-permute-start.63 = (bf16[2,2,2,64,1024]{4,3,2,1,0:T(8,128)(2,1)}, bf16[2,2,2,64,1024]{4,3,2,1,0:T(8,128)(2,1)}, u32[]{:S(2)}, u32[]{:S(2)}) collective-permute-start(bf16[2,2,2,64,1024]{4,3,2,1,0:T(8,128)(2,1)} %add.252), channel_id=1, source_target_pairs={{0,4},{4,0},{1,5},{5,1},{2,6},{6,2},{3,7},{7,3},{8,12},{12,8},{9,1... | collective-permute-start | bytes 3145736 | tf_op jit(solution)/shard_map/ppermute | solution.py:892
  418.2 37.4 %collective-permute-start.64 = (bf16[2,2,2,64,512]{4,3,2,1,0:T(8,128)(2,1)}, bf16[2,2,2,64,512]{4,3,2,1,0:T(8,128)(2,1)}, u32[]{:S(2)}, u32[]{:S(2)}) collective-permute-start(bf16[2,2,2,64,512]{4,3,2,1,0:T(8,128)(2,1)} %add.253), channel_id=1, source_target_pairs={{0,1},{1,0},{2,3},{3,2},{4,5},{5,4},{6,7},{7,6},{8,9},{9,8},{10,11... | collective-permute-start | bytes 1572872 | tf_op jit(solution)/shard_map/ppermute | solution.py:892
  500.8 20.5 %collective-permute-start.76 = (bf16[64,1024]{1,0:T(8,128)(2,1)}, bf16[64,1024]{1,0:T(8,128)(2,1)S(1)}, u32[]{:S(2)}, u32[]{:S(2)}) collective-permute-start(bf16[64,1024]{1,0:T(8,128)(2,1)} %fusion.22), channel_id=1, source_target_pairs={{0,16},{16,0},{1,17},{17,1},{2,18},{18,2},{3,19},{19,3},{4,20},{20... | collective-permute-start | bytes 393224 | tf_op jit(solution)/shard_map/ppermute | solution.py:892
  517.4 19.2 %collective-permute-start.73 = (bf16[2,2,2,64,512]{4,3,2,1,0:T(8,128)(2,1)S(1)}, bf16[2,2,2,64,512]{4,3,2,1,0:T(8,128)(2,1)S(1)}, u32[]{:S(2)}, u32[]{:S(2)}) collective-permute-start(bf16[2,2,2,64,512]{4,3,2,1,0:T(8,128)(2,1)S(1)} %add.260), channel_id=1, source_target_pairs={{0,4},{4,0},{1,5},{5,1},{2,6},{6,2},{3,7},{7,3},{8,12},{12,8},{9,1... | collective-permute-start | bytes 1572872 | tf_op jit(solution)/shard_map/ppermute | solution.py:892
  518.5 18.2 %collective-permute-start.74 = (bf16[2,2,2,64,512]{4,3,2,1,0:T(8,128)(2,1)S(1)}, bf16[2,2,2,64,512]{4,3,2,1,0:T(8,128)(2,1)S(1)}, u32[]{:S(2)}, u32[]{:S(2)}) collective-permute-start(bf16[2,2,2,64,512]{4,3,2,1,0:T(8,128)(2,1)S(1)} %copy-done.70), channel_id=1, source_target_pairs={{0,2},{2,0},{1,3},{3,1},{4,6},{6,4},{5,7},{7,5},{8,10},{10,8},{9,1... | collective-permute-start | bytes 1572872 | tf_op jit(solution)/shard_map/ppermute | solution.py:892
  518.5 18.2 %collective-permute-start.75 = (bf16[2,2,2,64,512]{4,3,2,1,0:T(8,128)(2,1)S(1)}, bf16[2,2,2,64,512]{4,3,2,1,0:T(8,128)(2,1)S(1)}, u32[]{:S(2)}, u32[]{:S(2)}) collective-permute-start(bf16[2,2,2,64,512]{4,3,2,1,0:T(8,128)(2,1)S(1)} %copy-done.69), channel_id=1, source_target_pairs={{0,2},{2,0},{1,3},{3,1},{4,6},{6,4},{5,7},{7,5},{8,10},{10,8},{9,1... | collective-permute-start | bytes 1572872 | tf_op jit(solution)/shard_map/ppermute | solution.py:892
  537.6 40.5 %collective-permute-start.80 = (bf16[2,2,64,512]{3,2,1,0:T(8,128)(2,1)S(1)}, bf16[2,2,64,512]{3,2,1,0:T(8,128)(2,1)}, u32[]{:S(2)}, u32[]{:S(2)}) collective-permute-start(bf16[2,2,64,512]{3,2,1,0:T(8,128)(2,1)S(1)} %fusion.12), channel_id=1, source_target_pairs={{0,8},{8,0},{1,9},{9,1},{2,10},{10,2},{3,11},{11,3},{4,12},{12,4},... | collective-permute-start | bytes 786440 | tf_op jit(solution)/shard_map/ppermute | solution.py:892
  540.1 38.0 %collective-permute-start.81 = (bf16[2,2,2,64,512]{4,3,2,1,0:T(8,128)(2,1)}, bf16[2,2,2,64,512]{4,3,2,1,0:T(8,128)(2,1)}, u32[]{:S(2)}, u32[]{:S(2)}) collective-permute-start(bf16[2,2,2,64,512]{4,3,2,1,0:T(8,128)(2,1)} %add.268), channel_id=1, source_target_pairs={{0,1},{1,0},{2,3},{3,2},{4,5},{5,4},{6,7},{7,6},{8,9},{9,8},{10,11... | collective-permute-start | bytes 1572872 | tf_op jit(solution)/shard_map/ppermute | solution.py:892
  540.5 37.6 %collective-permute-start.82 = (bf16[2,2,2,64,512]{4,3,2,1,0:T(8,128)(2,1)}, bf16[2,2,2,64,512]{4,3,2,1,0:T(8,128)(2,1)S(1)}, u32[]{:S(2)}, u32[]{:S(2)}) collective-permute-start(bf16[2,2,2,64,512]{4,3,2,1,0:T(8,128)(2,1)} %get-tuple-element.635), channel_id=1, source_target_pairs={{0,2},{2,0},{1,3},{3,1},{4,6},{6,4},{5,7},{7,5},{8,10},{10,8},{9,1... | collective-permute-start | bytes 1572872 | tf_op jit(solution)/shard_map/ppermute | solution.py:892
  540.5 37.6 %collective-permute-start.83 = (bf16[2,2,2,64,512]{4,3,2,1,0:T(8,128)(2,1)}, bf16[2,2,2,64,512]{4,3,2,1,0:T(8,128)(2,1)S(1)}, u32[]{:S(2)}, u32[]{:S(2)}) collective-permute-start(bf16[2,2,2,64,512]{4,3,2,1,0:T(8,128)(2,1)} %get-tuple-element.636), channel_id=1, source_target_pairs={{0,2},{2,0},{1,3},{3,1},{4,6},{6,4},{5,7},{7,5},{8,10},{10,8},{9,1... | collective-permute-start | bytes 1572872 | tf_op jit(solution)/shard_map/ppermute | solution.py:892
  584.6 26.0 %collective-permute-start.89 = (bf16[2,64,512]{2,1,0:T(8,128)(2,1)S(1)}, bf16[2,64,512]{2,1,0:T(8,128)(2,1)S(1)}, u32[]{:S(2)}, u32[]{:S(2)}) collective-permute-start(bf16[2,64,512]{2,1,0:T(8,128)(2,1)S(1)} %fusion.24), channel_id=1, source_target_pairs={{0,1},{1,0},{2,3},{3,2},{4,5},{5,4},{6,7},{7,6},{8,9},{9,8},{10,11... | collective-permute-start | bytes 393224 | tf_op jit(solution)/shard_map/ppermute | solution.py:892
  586.2 38.8 %collective-permute-start.91 = (bf16[2,2,64,512]{3,2,1,0:T(8,128)(2,1)S(1)}, bf16[2,2,64,512]{3,2,1,0:T(8,128)(2,1)S(1)}, u32[]{:S(2)}, u32[]{:S(2)}) collective-permute-start(bf16[2,2,64,512]{3,2,1,0:T(8,128)(2,1)S(1)} %fusion.13), channel_id=1, source_target_pairs={{0,4},{4,0},{1,5},{5,1},{2,6},{6,2},{3,7},{7,3},{8,12},{12,8},{9,1... | collective-permute-start | bytes 786440 | tf_op jit(solution)/shard_map/ppermute | solution.py:892
  587.2 40.9 %collective-permute-start.94 = (bf16[2,2,2,64,512]{4,3,2,1,0:T(8,128)(2,1)S(1)}, bf16[2,2,2,64,512]{4,3,2,1,0:T(8,128)(2,1)S(1)}, u32[]{:S(2)}, u32[]{:S(2)}) collective-permute-start(bf16[2,2,2,64,512]{4,3,2,1,0:T(8,128)(2,1)S(1)} %add.284), channel_id=1, source_target_pairs={{0,8},{8,0},{1,9},{9,1},{2,10},{10,2},{3,11},{11,3},{4,12},{12,4},... | collective-permute-start | bytes 1572872 | tf_op jit(solution)/shard_map/ppermute | solution.py:892
  589.7 21.6 %collective-permute-start.98 = (bf16[2,64,512]{2,1,0:T(8,128)(2,1)S(1)}, bf16[2,64,512]{2,1,0:T(8,128)(2,1)S(1)}, u32[]{:S(2)}, u32[]{:S(2)}) collective-permute-start(bf16[2,64,512]{2,1,0:T(8,128)(2,1)S(1)} %fusion.27), channel_id=1, source_target_pairs={{0,8},{8,0},{1,9},{9,1},{2,10},{10,2},{3,11},{11,3},{4,12},{12,4},... | collective-permute-start | bytes 393224 | tf_op jit(solution)/shard_map/ppermute | solution.py:892
  (126 other events, 1433.6 us)
Sparse Core Ops, SparseCore 0:
  10.9 110.6 all-gather.2

commit v3 on v2

--- a/solution.py
+++ b/solution.py
@@ -50,6 +50,7 @@
     for kind, order, first, columns in layout:
         target = pl.ds(first, columns)
         if kind == "rel":
+            order, skip = order
             arrays, refs = refs[:4], refs[4:]
             for which, index, rel in rel_slots(order):
                 row, half = slot_place(co, rel)
@@ -57,7 +58,7 @@
                     (
                         rel["x"],
                         pltpu.make_async_copy(
-                            arrays[which].at[index],
+                            arrays[which].at[index + (slice(None), pl.ds(skip, columns))],
                             whole.at[half, pl.ds(row, SLOT), target],
                             sems.at[len(copies)],
                         ),
@@ -90,6 +91,12 @@
     return [array for _, arrays in weights for array in arrays]
 
 
+def both_parts(weights, split):
+    (first, arrays_a), (second, arrays_b) = weights
+    second = tuple((kind, order, at + split, columns) for kind, order, at, columns in second)
+    return tuple(first) + second, list(arrays_a) + list(arrays_b)
+
+
 def weight_width(weight):
     return sum(part[3] for part in weight[0])
 
@@ -109,20 +116,34 @@
             copy.wait()
 
 
-def norm_rows(values, gain, bias):
-    centre = values - jnp.mean(values, axis=-1, keepdims=True)
-    scaled = lax.rsqrt(jnp.mean(centre * centre, axis=-1, keepdims=True) + EPSILON)
-    unit = centre * scaled
-    return unit * gain + bias, unit, scaled
-
-
-def norm_rows_back(grad, unit, scaled, gain):
-    weighted = grad * gain
-    return scaled * (
-        weighted
-        - jnp.mean(weighted, axis=-1, keepdims=True)
-        - unit * jnp.mean(weighted * unit, axis=-1, keepdims=True)
-    )
+ROWS = 32
+LANES = 128
+
+
+def strips(width):
+    return [slice(n, n + LANES) for n in range(0, width, LANES)]
+
+
+def row_parts(ref, row=0):
+    return tuple(ref[row : row + 1, strip] for strip in strips(ref.shape[1]))
+
+
+def chunk_rows(n):
+    return pl.ds(pl.multiple_of(n * ROWS, ROWS), ROWS)
+
+
+def spread_mean(total, width):
+    return jnp.broadcast_to(jnp.sum(total, axis=1, keepdims=True) * (1.0 / width), total.shape)
+
+
+def norm_stats(load, width):
+    total = sum(load(strip) for strip in strips(width))
+    mean = spread_mean(total, width)
+    square = 0.0
+    for strip in strips(width):
+        centre = load(strip) - mean
+        square = square + centre * centre
+    return mean, lax.rsqrt(spread_mean(square, width) + EPSILON)
 
 
 def first_row(shape):
@@ -142,7 +163,7 @@
 
 
 def fold_rows(values):
-    return values[:8] + values[8:]
+    return sum(values[n : n + 8] for n in range(0, values.shape[0], 8))
 
 
 def params(semantics=1):
@@ -159,27 +180,48 @@
     )
 
 
-def first_mix_kernel(x_ref, carry_ref, vec_ref, mk_ref, mv_ref, mr_ref):
-    gain, bias = vec_ref[0:1, :], vec_ref[1:2, :]
-    mixes = [vec_ref[i : i + 1, :] for i in (4, 5, 6)]
+def first_mix_kernel(x_ref, carry_ref, vec_ref, mk_ref, mv_ref, mr_ref, last):
     width = x_ref.shape[1]
 
-    def step(i, before):
-        rows = pl.ds(pl.multiple_of(i * CHUNK, CHUNK), CHUNK)
-        normed, _, _ = norm_rows(x_ref[rows, :].astype(F32), gain, bias)
-        behind = move_down(normed, before) * carry_ref[rows, :]
-        for mix, out in zip(mixes, (mk_ref, mv_ref, mr_ref)):
-            out[rows, :] = (normed * mix + behind * (1.0 - mix)).astype(BF)
-        return normed[CHUNK - 1 :, :]
-
-    lax.fori_loop(0, x_ref.shape[0] // CHUNK, step, jnp.zeros((1, width), F32), unroll=2)
+    def step(n, before):
+        rows = chunk_rows(n)
+        mean, scaled = norm_stats(lambda strip: x_ref[rows, strip].astype(F32), width)
+        carry = carry_ref[rows, :]
+        lasts = []
+        for strip in strips(width):
+            unit = (x_ref[rows, strip].astype(F32) - mean) * scaled
+            normed = unit * vec_ref[0:1, strip] + vec_ref[1:2, strip]
+            behind = move_down(normed, before[len(lasts)]) * carry
+            for m, out in ((4, mk_ref), (5, mv_ref), (6, mr_ref)):
+                mix = vec_ref[m : m + 1, strip]
+                out[rows, strip] = (normed * mix + behind * (1.0 - mix)).astype(BF)
+            lasts.append(normed[ROWS - 1 :, :])
+        return tuple(lasts)
+
+    @pl.when(pl.program_id(0) == 0)
+    def _():
+        last[...] = jnp.zeros_like(last)
+
+    lasts = lax.fori_loop(0, x_ref.shape[0] // ROWS, step, row_parts(last), unroll=2)
+    for strip, value in zip(strips(width), lasts):
+        last[0:1, strip] = value
 
 
 def first_mix(x, carry, vectors):
-    shape = jax.ShapeDtypeStruct(x.shape, BF)
+    tokens, width = x.shape
+    rows = tokens // 4
+    tall = pl.BlockSpec((rows, width), lambda i: (i, 0))
     return pl.pallas_call(
         first_mix_kernel,
-        out_shape=[shape] * 3,
+        grid=(4,),
+        in_specs=[
+            tall,
+            pl.BlockSpec((rows, LANES), lambda i: (i, 0)),
+            pl.BlockSpec(vectors.shape, lambda i: (0, 0)),
+        ],
+        out_specs=[tall] * 3,
+        out_shape=[jax.ShapeDtypeStruct(x.shape, BF)] * 3,
+        scratch_shapes=[pltpu.VMEM((8, width), F32)],
         compiler_params=params(),
         cost_estimate=cost(0, 8 << 20),
     )(x, carry, vectors)
@@ -264,7 +306,7 @@
         return state
 
     zero = jnp.zeros(spread, F32)
-    lax.fori_loop(0, key_ref.shape[0] // CHUNK, step, (zero, zero))
+    lax.fori_loop(0, key_ref.shape[0] // CHUNK, step, (zero, zero), unroll=2)
 
 
 def time_forward(co, mixed, weights, vectors, masks):
@@ -316,20 +358,28 @@
 
     half = ow.shape[2]
     middle_ref[...] = dot(gated[:, :half], ow[0], NT) + dot(gated[:, half:], ow[1], NT)
-    gain, bias = vec_ref[7:8, :], vec_ref[8:9, :]
-    mixes = [vec_ref[n : n + 1, :] for n in (9, 10)]
+    width = x_ref.shape[1]
 
     def step(n, before):
-        rows = pl.ds(pl.multiple_of(n * CHUNK, CHUNK), CHUNK)
-        middle = middle_ref[rows, :] + x_ref[rows, :].astype(F32)
-        middle_ref[rows, :] = middle
-        normed, _, _ = norm_rows(middle, gain, bias)
-        behind = move_down(normed, before) * carry_ref[rows, :]
-        for mix, out in zip(mixes, (mk_ref, mr_ref)):
-            out[rows, :] = (normed * mix + behind * (1.0 - mix)).astype(BF)
-        return normed[CHUNK - 1 :, :]
-
-    last[...] = lax.fori_loop(0, x_ref.shape[0] // CHUNK, step, last[...], unroll=2)
+        rows = chunk_rows(n)
+        for strip in strips(width):
+            middle_ref[rows, strip] += x_ref[rows, strip].astype(F32)
+        mean, scaled = norm_stats(lambda strip: middle_ref[rows, strip], width)
+        carry = carry_ref[rows, :]
+        lasts = []
+        for strip in strips(width):
+            unit = (middle_ref[rows, strip] - mean) * scaled
+            normed = unit * vec_ref[7:8, strip] + vec_ref[8:9, strip]
+            behind = move_down(normed, before[len(lasts)]) * carry
+            for m, out in ((9, mk_ref), (10, mr_ref)):
+                mix = vec_ref[m : m + 1, strip]
+                out[rows, strip] = (normed * mix + behind * (1.0 - mix)).astype(BF)
+            lasts.append(normed[ROWS - 1 :, :])
+        return tuple(lasts)
+
+    lasts = lax.fori_loop(0, x_ref.shape[0] // ROWS, step, row_parts(last), unroll=2)
+    for strip, value in zip(strips(width), lasts):
+        last[0:1, strip] = value
 
 
 def time_output_step(co, gated, x, carry, vectors, weight):
@@ -344,14 +394,14 @@
             in_specs=[
                 tall,
                 tall,
-                pl.BlockSpec((rows, 1), lambda i, co: (i, 0)),
+                pl.BlockSpec((rows, LANES), lambda i, co: (i, 0)),
                 pl.BlockSpec(vectors.shape, lambda i, co: (0, 0)),
             ]
             + [anywhere()] * len(weight[1]),
             out_specs=[tall] * 3,
             scratch_shapes=[
                 pltpu.VMEM((2, width, width // 2), BF),
-                pltpu.VMEM((1, width), F32),
+                pltpu.VMEM((8, width), F32),
                 pltpu.SemaphoreType.DMA((32,)),
             ],
         ),
@@ -439,23 +489,24 @@
     pre_ref[:, narrow:] = dot(mr[...], rw[1], NN)
     factor = scale[0]
 
-    def step(n, total):
-        rows = pl.ds(pl.multiple_of(n * CHUNK, CHUNK), CHUNK)
-        kv = kv_ref[rows, :]
-        rec = 1.0 / (1.0 + jnp.exp(-pre_ref[rows, :]))
-        result = middle_ref[rows, :] + rec * kv
-        out_ref[rows, :] = result.astype(BF)
-        error = (result - teacher_ref[rows, :].astype(F32)) * valid_ref[rows, :]
-        grad = error * factor
-        dres_ref[rows, :] = grad
-        dkv_ref[rows, :] = (grad * rec).astype(BF)
-        drec_ref[rows, :] = (grad * kv * rec * (1.0 - rec)).astype(BF)
-        return total + fold_rows(error * error)
-
-    total = lax.fori_loop(
-        0, kv_ref.shape[0] // CHUNK, step, jnp.zeros((8, kv_ref.shape[1]), F32)
-    )
-    loss_ref[...] += total
+    def step(n, _):
+        rows = chunk_rows(n)
+        valid = valid_ref[rows, :]
+        for strip in strips(kv_ref.shape[1]):
+            kv = kv_ref[rows, strip]
+            rec = 1.0 / (1.0 + jnp.exp(-pre_ref[rows, strip]))
+            result = middle_ref[rows, strip] + rec * kv
+            out_ref[rows, strip] = result.astype(BF)
+            error = (result - teacher_ref[rows, strip].astype(F32)) * valid
+            grad = error * factor
+            dres_ref[rows, strip] = grad
+            dkv = grad * rec
+            dkv_ref[rows, strip] = dkv.astype(BF)
+            drec_ref[rows, strip] = (dkv * kv * (1.0 - rec)).astype(BF)
+            loss_ref[:, strip] += fold_rows(error * error)
+        return 0
+
+    lax.fori_loop(0, kv_ref.shape[0] // ROWS, step, 0)
 
 
 def result_step(co, scale, hidden, mixed, middle, teacher, valid, weight, recept):
@@ -473,7 +524,7 @@
                 tall,
                 tall,
                 tall,
-                pl.BlockSpec((rows, 1), lambda i, co, s: (i, 0)),
+                pl.BlockSpec((rows, LANES), lambda i, co, s: (i, 0)),
             ]
             + [anywhere()] * len(arrays_of(weight, recept)),
             out_specs=[tall] * 4 + [pl.BlockSpec((8, width), lambda i, co, s: (0, 0))],
@@ -493,120 +544,211 @@
     )(co, scale, hidden, mixed, middle, teacher, valid, *arrays_of(weight, recept))
 
 
-def weight_grad_kernel(co, model_ref, chan_ref, *refs, order):
-    targets, (whole, sems) = refs[:4], refs[4:]
+def grad_copies(co, whole, targets, n, sems, order, piece, merged=False):
+    found = ([], [])
+    for m, (which, index, rel) in enumerate(rel_slots(order)):
+        row, half = slot_place(co, rel)
+        found[rel["x"]].append(
+            pltpu.make_async_copy(
+                whole.at[half, pl.ds(row, SLOT), piece],
+                targets[which].at[
+                    (index + (n,) if merged else (n,) + index) + (slice(None), piece)
+                ],
+                sems.at[m],
+            )
+        )
+    return found
+
+
+def weight_grads_kernel(co, *refs, orders, merged):
+    count = len(orders)
+    models, chans, refs = refs[:count], refs[count : 2 * count], refs[2 * count :]
+    targets, (held, given, whole, sems_in, sems_out) = refs[:4], refs[4:]
+    half = whole.shape[3]
+    loads = []
+    for n in range(count):
+        for m, (source, place) in enumerate(((models[n], held), (chans[n], given))):
+            loads.append(pltpu.make_async_copy(source, place.at[n], sems_in.at[2 * n + m]))
+            loads[-1].start()
+    for n, order in enumerate(orders):
+        for load in loads[2 * n : 2 * n + 2]:
+            load.wait()
+
+        def step(turn, _, n=n, order=order):
+            at = co[4] ^ turn
+            columns = pl.ds(pl.multiple_of(at * half, half), half)
+            whole[n, at] = dot(held[n], given[n, :, columns], TN).astype(BF)
+            for which in (0, 1):
+
+                @pl.when(turn == which)
+                def _(which=which):
+                    copies = grad_copies(
+                        co, whole.at[n], targets, n, sems_out.at[n], order, slice(None), merged
+                    )
+                    for copy in copies[which]:
+                        copy.start()
+
+            return 0
+
+        lax.fori_loop(0, 2, step, 0)
+    for n, order in enumerate(orders):
+        for copies in grad_copies(
+            co, whole.at[n], targets, n, sems_out.at[n], order, slice(None), merged
+        ):
+            for copy in copies:
+                copy.wait()
+
+
+def weight_grads(co, pairs, merged=False):
+    models, chans, orders = zip(*pairs)
+    tokens, width = models[0].shape
+    half = width // 2
+    count = len(pairs)
+    dims = (2, 2, 2, count) if merged else (count, 2, 2, 2)
+    return pl.pallas_call(
+        functools.partial(weight_grads_kernel, orders=orders, merged=merged),
+        grid_spec=pltpu.PrefetchScalarGridSpec(
+            num_scalar_prefetch=1,
+            grid=(1,),
+            in_specs=[anywhere()] * (2 * count),
+            out_specs=[anywhere()] * 4,
+            scratch_shapes=[
+                pltpu.VMEM((count, tokens, width), BF),
+                pltpu.VMEM((count, tokens, width), BF),
+                pltpu.VMEM((count, 2, width, half), BF),
+                pltpu.SemaphoreType.DMA((2 * count,)),
+                pltpu.SemaphoreType.DMA((count, 32)),
+            ],
+        ),
+        out_shape=[jax.ShapeDtypeStruct(dims + (SLOT, half), BF)] * 4,
+        compiler_params=params(),
+        cost_estimate=cost(count * 1.2, count * (6 << 20)),
+    )(co, *models, *chans)
+
+
+def channel_back_kernel(co, dkv, mixed, hidden, active, *refs, layout, order):
+    arrays, (dkey, *refs) = take_refs(refs, layout)
+    targets, (whole, grads, sems_in, sems) = refs[:-4], refs[-4:]
     j = pl.program_id(0)
-    per_half = whole.shape[2] // WIDE
+    per_half = grads.shape[4] // WIDE
     columns = pl.ds(pl.multiple_of(lax.rem(j, per_half) * WIDE, WIDE), WIDE)
     turn = lax.div(j, per_half)
-    whole[co[4] ^ turn, :, columns] = dot(model_ref[...], chan_ref[...], TN).astype(BF)
-
-    def copies(piece):
+    half = co[4] ^ turn
+    loads = weight_copies(co, arrays, whole, sems_in, layout)
+
+    @pl.when(j == 0)
+    def _():
+        start_all(loads)
+
+    def keep(n, values):
+        grads[n, half, :, :, columns] = values.astype(BF).reshape(16, SLOT, WIDE)
+
+    keep(0, dot(dkv[...], hidden[...], TN))
+
+    for which in (0, 1):
+
+        @pl.when(j == which * per_half)
+        def _(which=which):
+            wait_half(loads, which)
+
+    back = dot(dkv[...], whole[half, :, columns], NN)
+    back = (2.0 * active[...].astype(F32) * back).astype(BF)
+    dkey[...] = back
+    keep(1, dot(mixed[...], back, TN))
+
+    if order is None:
+        wide = grads.shape[4]
+
+        def copies(turn, piece, size):
+            half = co[4] ^ turn
+            return [
+                pltpu.make_async_copy(
+                    grads.at[n, half, :, :, pl.ds(piece, size)],
+                    targets[0].at[:, half, :, pl.ds(n * wide + piece, size)],
+                    sems.at[n],
+                )
+                for n in (0, 1)
+            ]
+
+        for copy in copies(turn, pl.multiple_of(lax.rem(j, per_half) * WIDE, WIDE), WIDE):
+            copy.start()
+
+        @pl.when(j == pl.num_programs(0) - 1)
+        def _():
+            for which in (0, 1):
+                for copy in copies(which, 0, wide):
+                    copy.wait()
+
+        return
+
+    def slot_copies(which, piece):
         found = []
-        for which, index, rel in rel_slots(order):
-            row, half = slot_place(co, rel)
-            copy = pltpu.make_async_copy(
-                whole.at[half, pl.ds(row, SLOT), piece],
-                targets[which].at[index + (slice(None), piece)],
-                sems.at[len(found)],
-            )
-            found.append((rel["x"], copy))
+        for m, (array, index, rel) in enumerate(rel_slots(order)):
+            if rel["x"] != which:
+                continue
+            row, at = slot_place(co, rel)
+            for n in (0, 1):
+                found.append(
+                    pltpu.make_async_copy(
+                        grads.at[n, at, lax.div(row, SLOT), :, piece],
+                        targets[array].at[index + (n, slice(None), piece)],
+                        sems.at[n * 32 + m],
+                    )
+                )
         return found
 
     for which in (0, 1):
 
         @pl.when(turn == which)
         def _(which=which):
-            for rel_x, copy in copies(columns):
-                if rel_x == which:
-                    copy.start()
+            for copy in slot_copies(which, columns):
+                copy.start()
 
     @pl.when(j == pl.num_programs(0) - 1)
     def _():
-        for _, copy in copies(slice(None)):
-            copy.wait()
-
-
-def weight_grad(co, model, chan, order, first=0, half=None):
-    tokens, width = model.shape
-    each = chan.shape[1] // 2
-    half = half or each
-    per_half, skip, stride = half // WIDE, first // WIDE, each // WIDE
+        for which in (0, 1):
+            for copy in slot_copies(which, slice(None)):
+                copy.wait()
+
+
+def channel_back(co, dkv, mixed, hidden, active, weight, first, half, order):
+    tokens, width = dkv.shape
+    per_half = half // WIDE
+    skip, stride = first // WIDE, hidden.shape[1] // 2 // WIDE
 
     def tile(j, co):
         return 0, (co[4] ^ lax.div(j, per_half)) * stride + skip + lax.rem(j, per_half)
 
-    shape = jax.ShapeDtypeStruct((2, 2, 2, SLOT, half), BF)
-    return pl.pallas_call(
-        functools.partial(weight_grad_kernel, order=order),
+    fixed = pl.BlockSpec((tokens, width), lambda j, co: (0, 0))
+    block = pl.BlockSpec((tokens, WIDE), tile)
+    if order is None:
+        shapes = [jax.ShapeDtypeStruct((16, 2, SLOT, 2 * half), BF)]
+    else:
+        shapes = [jax.ShapeDtypeStruct((2, 2, 2, 2, SLOT, half), BF)] * 4
+    dkey, *slots = pl.pallas_call(
+        functools.partial(channel_back_kernel, layout=weight[0], order=order),
         grid_spec=pltpu.PrefetchScalarGridSpec(
             num_scalar_prefetch=1,
             grid=(2 * per_half,),
-            in_specs=[
-                pl.BlockSpec((tokens, width), lambda j, co: (0, 0)),
-                pl.BlockSpec((tokens, WIDE), tile),
-            ],
-            out_specs=[anywhere()] * 4,
+            in_specs=[fixed, fixed, block, block] + [anywhere()] * len(weight[1]),
+            out_specs=[pl.BlockSpec((tokens, WIDE), column_tile(per_half))]
+            + [anywhere()] * len(shapes),
             scratch_shapes=[
                 pltpu.VMEM((2, width, half), BF),
-                pltpu.SemaphoreType.DMA((32,)),
+                pltpu.VMEM((2, 2, 16, SLOT, half), BF),
+                pltpu.SemaphoreType.DMA((sem_count(weight),)),
+                pltpu.SemaphoreType.DMA((64,)),
             ],
         ),
-        out_shape=[shape] * 4,
+        out_shape=[jax.ShapeDtypeStruct((tokens, 2 * half), BF)] + shapes,
         compiler_params=params(),
-        cost_estimate=cost(half / 512 * 1.2, (2 << 20) * (1 + half / 256)),
-    )(co, model, chan)
-
-
-def hidden_back_kernel(co, dkv, active_ref, *refs, layout):
-    arrays, (out_ref, whole, sems) = take_refs(refs, layout)
-    j = pl.program_id(0)
-    per_half = whole.shape[2] // WIDE
-    copies = weight_copies(co, arrays, whole, sems, layout)
-
-    @pl.when(j == 0)
-    def _():
-        start_all(copies)
-        wait_half(copies, 0)
-
-    @pl.when(j == per_half)
-    def _():
-        wait_half(copies, 1)
-
-    half = co[4] ^ lax.div(j, per_half)
-    columns = pl.ds(pl.multiple_of(lax.rem(j, per_half) * WIDE, WIDE), WIDE)
-    grad = dot(dkv[...], whole[half, :, columns], NN)
-    out_ref[...] = (2.0 * active_ref[...].astype(F32) * grad).astype(BF)
-
-
-def hidden_back(co, dkv, active, weight):
-    tokens, width = dkv.shape
-    half = weight_width(weight)
-    block = pl.BlockSpec((tokens, WIDE), column_tile(half // WIDE))
-    return pl.pallas_call(
-        functools.partial(hidden_back_kernel, layout=weight[0]),
-        grid_spec=pltpu.PrefetchScalarGridSpec(
-            num_scalar_prefetch=1,
-            grid=(2 * half // WIDE,),
-            in_specs=[
-                pl.BlockSpec((tokens, width), lambda j, co: (0, 0)),
-                block,
-            ]
-            + [anywhere()] * len(weight[1]),
-            out_specs=block,
-            scratch_shapes=[
-                pltpu.VMEM((2, width, half), BF),
-                pltpu.SemaphoreType.DMA((sem_count(weight),)),
-            ],
-        ),
-        out_shape=jax.ShapeDtypeStruct((tokens, 2 * half), BF),
-        compiler_params=params(),
-        cost_estimate=cost(4.5, 26 << 20),
-    )(co, dkv, active, *weight[1])
+        cost_estimate=cost(half / 512 * 3.3, half / 512 * (14 << 20)),
+    )(co, dkv, mixed, hidden, active, *weight[1])
+    return dkey, slots
 
 
 def middle_back_kernel(
-    co, dkey, drec, middle_ref, dres_ref, lead_ref, vec_ref, *refs, layouts,
+    co, dkey_a, dkey_b, drec, middle_ref, dres_ref, lead_ref, vec_ref, *refs, layouts,
 ):
     key_w, refs = take_refs(refs, layouts[0])
     recept_w, refs = take_refs(refs, layouts[1])
@@ -626,36 +768,55 @@
         for half in (0, 1):
             wait_half(copies, half)
 
-    wide, narrow = ww.shape[2], rw.shape[2]
-    gk_ref[...] = dot(dkey[:, :wide], ww[0], NT) + dot(dkey[:, wide:], ww[1], NT)
+    wide, narrow = dkey_a.shape[1] // 2, rw.shape[2]
+    gk_ref[...] = sum(
+        dot(part[:, half * wide : (half + 1) * wide], ww[half, :, n * wide : (n + 1) * wide], NT)
+        for n, part in enumerate((dkey_a, dkey_b))
+        for half in (0, 1)
+    )
     gr_ref[...] = dot(drec[:, :narrow], rw[0], NT) + dot(drec[:, narrow:], rw[1], NT)
-    gain, bias = vec_ref[7:8, :], vec_ref[8:9, :]
-    mix_k, mix_r = vec_ref[9:10, :], vec_ref[10:11, :]
-    steps = middle_ref.shape[0] // CHUNK
+    steps = middle_ref.shape[0] // ROWS
+    width = middle_ref.shape[1]
 
     def step(n, after):
-        rows = pl.ds(pl.multiple_of((steps - 1 - n) * CHUNK, CHUNK), CHUNK)
-        normed, unit, scaled = norm_rows(middle_ref[rows, :], gain, bias)
+        rows = chunk_rows(steps - 1 - n)
+        mean, scaled = norm_stats(lambda strip: middle_ref[rows, strip], width)
         lead = lead_ref[rows, :]
-        gk, gr = gk_ref[rows, :], gr_ref[rows, :]
-        uk = move_up(gk, after[0]) * lead
-        ur = move_up(gr, after[1]) * lead
-        grad = gk * mix_k + gr * mix_r + uk * (1.0 - mix_k) + ur * (1.0 - mix_r)
-        sums_ref[0] += fold_rows(grad * unit)
-        sums_ref[1] += fold_rows(grad)
-        sums_ref[2] += fold_rows(normed * (gk - uk))
-        sums_ref[3] += fold_rows(normed * (gr - ur))
-        dmid = dres_ref[rows, :] + norm_rows_back(grad, unit, scaled, gain)
-        dmid_ref[rows, :] = dmid
-        dtime_ref[rows, :] = dmid.astype(BF)
-        return gk[:1, :], gr[:1, :]
-
-    after = lax.fori_loop(0, steps, step, (next_ref[0:1, :], next_ref[1:2, :]))
-    next_ref[0:1, :] = after[0]
-    next_ref[1:2, :] = after[1]
-
-
-def middle_back(co, dkey, drec, middle, dres, lead, vectors, weight, recept):
+        firsts = ([], [])
+        plain, along = 0.0, 0.0
+        for strip in strips(width):
+            gain, bias, mix_k, mix_r = (vec_ref[m : m + 1, strip] for m in (7, 8, 9, 10))
+            unit = (middle_ref[rows, strip] - mean) * scaled
+            normed = unit * gain + bias
+            gk, gr = gk_ref[rows, strip], gr_ref[rows, strip]
+            uk = move_up(gk, after[0][len(firsts[0])]) * lead
+            ur = move_up(gr, after[1][len(firsts[0])]) * lead
+            grad = gk * mix_k + gr * mix_r + uk * (1.0 - mix_k) + ur * (1.0 - mix_r)
+            sums_ref[0, :, strip] += fold_rows(grad * unit)
+            sums_ref[1, :, strip] += fold_rows(grad)
+            sums_ref[2, :, strip] += fold_rows(normed * (gk - uk))
+            sums_ref[3, :, strip] += fold_rows(normed * (gr - ur))
+            firsts[0].append(gk[:1, :])
+            firsts[1].append(gr[:1, :])
+            weighted = grad * gain
+            gk_ref[rows, strip] = weighted
+            plain = plain + weighted
+            along = along + weighted * unit
+        plain, along = spread_mean(plain, width), spread_mean(along, width)
+        for strip in strips(width):
+            unit = (middle_ref[rows, strip] - mean) * scaled
+            dmid = dres_ref[rows, strip] + scaled * (gk_ref[rows, strip] - plain - unit * along)
+            dmid_ref[rows, strip] = dmid
+            dtime_ref[rows, strip] = dmid.astype(BF)
+        return tuple(tuple(f) for f in firsts)
+
+    after = lax.fori_loop(0, steps, step, tuple(row_parts(next_ref, m) for m in (0, 1)), unroll=2)
+    for m, values in enumerate(after):
+        for strip, value in zip(strips(width), values):
+            next_ref[m : m + 1, strip] = value
+
+
+def middle_back(co, dkeys, drec, middle, dres, lead, vectors, weight, recept):
     tokens, width = middle.shape
     rows = tokens // 4
     wide = weight_width(weight)
@@ -666,11 +827,12 @@
             num_scalar_prefetch=1,
             grid=(4,),
             in_specs=[
-                pl.BlockSpec((rows, 2 * wide), lambda i, co: (3 - i, 0)),
+                pl.BlockSpec((rows, wide), lambda i, co: (3 - i, 0)),
+                pl.BlockSpec((rows, wide), lambda i, co: (3 - i, 0)),
                 tall,
                 tall,
                 tall,
-                pl.BlockSpec((rows, 1), lambda i, co: (3 - i, 0)),
+                pl.BlockSpec((rows, LANES), lambda i, co: (3 - i, 0)),
                 pl.BlockSpec(vectors.shape, lambda i, co: (0, 0)),
             ]
             + [anywhere()] * len(arrays_of(weight, recept)),
@@ -692,7 +854,7 @@
         ],
         compiler_params=params(),
         cost_estimate=cost(8, 36 << 20),
-    )(co, dkey, drec, middle, dres, lead, vectors, *arrays_of(weight, recept))
+    )(co, *dkeys, drec, middle, dres, lead, vectors, *arrays_of(weight, recept))
 
 
 def time_back_kernel(
@@ -726,7 +888,7 @@
 
     def group(start, state):
         rows = pl.ds(start, 8)
-        n1, n2, n4, nf, c0, ml = (twice(masks[n, rows, :]) for n in (5, 6, 7, 8, 9, 4))
+        n1, n2, n4, nf, c0, ml = (twice(masks[n, rows, :]) for n in (0, 1, 2, 3, 4, 5))
         key, val, rec, dg = key_ref[rows, :], val_ref[rows, :], rec_ref[rows, :], dg_ref[rows, :]
         pa, pb = pa_ref[rows, :], pb_ref[rows, :]
         power = jnp.exp(key)
@@ -766,7 +928,7 @@
         return state
 
     zero = jnp.zeros(spread, F32)
-    _, _, first_sum, decay_sum = lax.fori_loop(0, steps, step, (zero,) * 4)
+    _, _, first_sum, decay_sum = lax.fori_loop(0, steps, step, (zero,) * 4, unroll=2)
     sums_ref[0] = -r1 * jnp.exp(decay) * decay_sum
     sums_ref[1] = first_sum
 
@@ -804,12 +966,12 @@
 
 
 def input_back_kernel(
-    co, dkey, dval, drec, x_ref, dmid_ref, lead_ref, vec_ref, *refs, layouts,
+    co, dkey, dval, drec, x_ref, dmid_ref, lead_ref, vec_ref, after_ref, _, *refs, layouts,
 ):
     key_w, refs = take_refs(refs, layouts[0])
     val_w, refs = take_refs(refs, layouts[1])
     rec_w, refs = take_refs(refs, layouts[2])
-    out_ref, sums_ref, kw, vw, rw, gk_ref, gv_ref, gr_ref, next_ref, sems = refs
+    out_ref, sums_ref, next_ref, kw, vw, rw, gk_ref, gv_ref, gr_ref, sems = refs
     i = pl.program_id(0)
     groups = [
         weight_copies(co, arrays, whole, sems.at[n], layout)
@@ -821,7 +983,7 @@
         for copies in groups:
             start_all(copies)
         sums_ref[...] = jnp.zeros_like(sums_ref)
-        next_ref[...] = jnp.zeros_like(next_ref)
+        next_ref[...] = after_ref[...]
         for copies in groups:
             wait_half(copies, 0)
             wait_half(copies, 1)
@@ -829,59 +991,87 @@
     half = kw.shape[2]
     for grad, whole, out in ((dkey, kw, gk_ref), (dval, vw, gv_ref), (drec, rw, gr_ref)):
         out[...] = dot(grad[:, :half], whole[0], NT) + dot(grad[:, half:], whole[1], NT)
-    gain, bias = vec_ref[0:1, :], vec_ref[1:2, :]
-    mixes = [vec_ref[n : n + 1, :] for n in (4, 5, 6)]
-    steps = x_ref.shape[0] // CHUNK
+    steps = x_ref.shape[0] // ROWS
+    width = x_ref.shape[1]
 
     def step(n, after):
-        rows = pl.ds(pl.multiple_of((steps - 1 - n) * CHUNK, CHUNK), CHUNK)
-        normed, unit, scaled = norm_rows(x_ref[rows, :].astype(F32), gain, bias)
+        rows = chunk_rows(steps - 1 - n)
+        mean, scaled = norm_stats(lambda strip: x_ref[rows, strip].astype(F32), width)
         lead = lead_ref[rows, :]
-        total = jnp.zeros_like(normed)
-        firsts = []
-        for m, (part, mix) in enumerate(zip((gk_ref, gv_ref, gr_ref), mixes)):
-            grad = part[rows, :]
-            up = move_up(grad, after[m]) * lead
-            total = total + grad * mix + up * (1.0 - mix)
-            sums_ref[2 + m] += fold_rows(normed * (grad - up))
-            firsts.append(grad[:1, :])
-        sums_ref[0] += fold_rows(total * unit)
-        sums_ref[1] += fold_rows(total)
-        out_ref[rows, :] = dmid_ref[rows, :] + norm_rows_back(total, unit, scaled, gain)
-        return tuple(firsts)
-
-    after = lax.fori_loop(0, steps, step, tuple(next_ref[m : m + 1, :] for m in range(3)))
-    for m in range(3):
-        next_ref[m : m + 1, :] = after[m]
-
-
-def input_back(co, grads, x, dmid, lead, vectors, weights):
+        firsts = ([], [], [])
+        plain, along = 0.0, 0.0
+        for strip in strips(width):
+            gain, bias = vec_ref[0:1, strip], vec_ref[1:2, strip]
+            unit = (x_ref[rows, strip].astype(F32) - mean) * scaled
+            normed = unit * gain + bias
+            total = 0.0
+            for m, part in enumerate((gk_ref, gv_ref, gr_ref)):
+                mix = vec_ref[4 + m : 5 + m, strip]
+                grad = part[rows, strip]
+                up = move_up(grad, after[m][len(firsts[m])]) * lead
+                total = total + grad * mix + up * (1.0 - mix)
+                sums_ref[2 + m, :, strip] += fold_rows(normed * (grad - up))
+                firsts[m].append(grad[:1, :])
+            sums_ref[0, :, strip] += fold_rows(total * unit)
+            sums_ref[1, :, strip] += fold_rows(total)
+            weighted = total * gain
+            gk_ref[rows, strip] = weighted
+            plain = plain + weighted
+            along = along + weighted * unit
+        plain, along = spread_mean(plain, width), spread_mean(along, width)
+        for strip in strips(width):
+            unit = (x_ref[rows, strip].astype(F32) - mean) * scaled
+            out_ref[rows, strip] = dmid_ref[rows, strip] + scaled * (
+                gk_ref[rows, strip] - plain - unit * along
+            )
+        return tuple(tuple(f) for f in firsts)
+
+    after = lax.fori_loop(0, steps, step, tuple(row_parts(next_ref, m) for m in range(3)), unroll=2)
+    for m, values in enumerate(after):
+        for strip, value in zip(strips(width), values):
+            next_ref[m : m + 1, strip] = value
+
+
+def input_back(co, grads, x, dmid, lead, vectors, weights, part, after, found):
     tokens, width = x.shape
     rows = tokens // 4
-    tall = pl.BlockSpec((rows, width), lambda i, co: (3 - i, 0))
+
+    def at(i, co):
+        return 3 - 2 * part - i, 0
+
+    tall = pl.BlockSpec((rows, width), at)
+    edge = pl.BlockSpec((8, width), lambda i, co: (0, 0))
     return pl.pallas_call(
         functools.partial(input_back_kernel, layouts=[w[0] for w in weights]),
         grid_spec=pltpu.PrefetchScalarGridSpec(
             num_scalar_prefetch=1,
-            grid=(4,),
+            grid=(2,),
             in_specs=[tall] * 5
             + [
-                pl.BlockSpec((rows, 1), lambda i, co: (3 - i, 0)),
+                pl.BlockSpec((rows, LANES), at),
                 pl.BlockSpec(vectors.shape, lambda i, co: (0, 0)),
+                edge,
+                anywhere(),
             ]
             + [anywhere()] * len(arrays_of(*weights)),
-            out_specs=[tall, pl.BlockSpec((5, 8, width), lambda i, co: (0, 0, 0))],
+            out_specs=[
+                tall,
+                pl.BlockSpec((5, 8, width), lambda i, co: (0, 0, 0)),
+                edge,
+            ],
             scratch_shapes=[pltpu.VMEM((2, width, width // 2), BF)] * 3
             + [pltpu.VMEM((rows, width), F32)] * 3
-            + [pltpu.VMEM((8, width), F32), pltpu.SemaphoreType.DMA((3, 32))],
+            + [pltpu.SemaphoreType.DMA((3, 32))],
         ),
         out_shape=[
             jax.ShapeDtypeStruct((tokens, width), F32),
             jax.ShapeDtypeStruct((5, 8, width), F32),
+            jax.ShapeDtypeStruct((8, width), F32),
         ],
+        input_output_aliases={9: 0},
         compiler_params=params(),
-        cost_estimate=cost(7, 26 << 20),
-    )(co, *grads, x, dmid, lead, vectors, *arrays_of(*weights))
+        cost_estimate=cost(4, 16 << 20),
+    )(co, *grads, x, dmid, lead, vectors, after, found, *arrays_of(*weights))
 
 
 def seal(*values):
@@ -910,17 +1100,17 @@
             self.state = (near, far, near_other, swap(far, "c"))
         self.done += 1
 
-    def part(self, first=0):
+    def part(self, first=0, skip=0, columns=None):
         assert self.done == 5
-        return ("rel", self.order, first, self.state[0].shape[-1]), self.state
+        return ("rel", (self.order, skip), first, columns or self.state[0].shape[-1]), self.state
 
 
 def weight_of(*parts):
     layouts, arrays = zip(*parts)
-    return layouts, [array for group in arrays for array in group]
-
-
-class Reduce:
+    return tuple(layouts), [array for group in arrays for array in group]
+
+
+class Merged:
     def __init__(self, slots, order):
         self.order, self.state, self.done = order, tuple(slots), 0
 
@@ -932,21 +1122,52 @@
         elif n == 1:
             near, far, far_got, near_got = self.state
             self.state = (near, near_got, swap(far + far_got, self.order[3]))
-        elif n == 2:
-            near, near_got, got = (v.astype(F32) for v in self.state)
-            held = near + near_got + got
-            self.keep(held, 2)
         elif n < 5:
-            held = self.state[0] + self.state[1].astype(F32)
-            self.keep(held, 4 - n)
+            kept, sent = (
+                sum(part[place].astype(F32) for part in self.state).astype(BF) for place in (0, 1)
+            )
+            self.state = (kept, swap(sent, self.order[4 - n]))
         self.done += 1
-
-    def keep(self, held, place):
-        self.state = (held[0], swap(held[1].astype(BF), self.order[place]))
 
     def finish(self):
         assert self.done == 5
-        return self.state[0] + self.state[1].astype(F32)
+        return list(self.state[0].astype(F32) + self.state[1].astype(F32))
+
+
+class Reduce:
+    def __init__(self, slots, orders):
+        self.orders, self.state, self.done = orders, tuple(slots), 0
+
+    def step(self):
+        n = self.done
+        if n == 0:
+            near, far, near_other, far_other = self.state
+            self.state = (near, far, swap(far_other, "c"), swap(near_other, "c"))
+        elif n == 1:
+            near, far, far_got, near_got = self.state
+            got = [swap(far[m] + far_got[m], order[3]) for m, order in enumerate(self.orders)]
+            self.state = (near, near_got, *got)
+        elif n == 2:
+            near, near_got, *got = self.state
+            self.keep([(near[m], near_got[m], part) for m, part in enumerate(got)], 2)
+        elif n < 5:
+            self.keep(self.state, 4 - n)
+        self.done += 1
+
+    def keep(self, parts, place):
+        kept, sent = (
+            [sum(v[at].astype(F32) for v in part).astype(BF) for part in parts] for at in (0, 1)
+        )
+        if place:
+            sent = [swap(v, order[place]) for v, order in zip(sent, self.orders)]
+            self.state = tuple(zip(kept, sent))
+        else:
+            self.state = (*kept, swap(jnp.stack(sent), self.orders[0][0]))
+
+    def finish(self):
+        assert self.done == 5
+        *kept, got = self.state
+        return [v.astype(F32) + got[n].astype(F32) for n, v in enumerate(kept)]
 
 
 def step_all(*chains):
@@ -961,15 +1182,59 @@
     return values
 
 
-def gather_plain(shard, first=0):
+def pair_up(shard):
+    got = swap(shard, "x")
+    mine = lax.axis_index("x") == 0
+    return jnp.where(mine, jnp.stack([shard, got]), jnp.stack([got, shard]))
+
+
+def gather_plain(shard):
     whole = lax.all_gather(shard, ("w", "u", "y", "c"), axis=0, tiled=True)
     whole = lax.all_gather(whole, "x", axis=1, tiled=True)
     half = whole.shape[1] // 2
-    whole = whole.reshape(16, SLOT, 2, half).transpose(0, 2, 1, 3)
-    return ("abs", 0, first, half), (whole,)
-
-
-def reduce_plain(slots, order):
+    return whole.reshape(16, SLOT, 2, half).transpose(0, 2, 1, 3)
+
+
+def all_of(array, skip=0, columns=None):
+    return (("abs", skip, 0, columns or array.shape[-1]),), [array]
+
+
+def gather_vectors(own, first, last):
+    for axis in EVERY[::-1][first:last]:
+        got = swap(own, axis)
+        mine = lax.axis_index(axis) == 0
+        own = jnp.where(mine, jnp.concatenate([own, got], axis=1), jnp.concatenate([got, own], axis=1))
+    return (own,)
+
+
+def reduce_plain(slots, orders):
+    return [reduce_one([part[n] for part in slots], order) for n, order in enumerate(orders)]
+
+
+def reduce_merged(slots, order):
+    count = slots[0].shape[3]
+    return [reduce_one([part[:, :, :, n] for part in slots], order) for n in range(count)]
+
+
+def scatter_rows(whole):
+    whole = whole.reshape(-1, *whole.shape[1:])
+    return lax.psum_scatter(whole, ("w", "u", "y", "c"), scatter_dimension=0)
+
+
+def pair_sum(sums):
+    side = lax.axis_index("x")
+    sent = lax.dynamic_index_in_dim(sums, 1 - side, keepdims=False)
+    kept = lax.dynamic_index_in_dim(sums, side, keepdims=False)
+    return kept.astype(F32) + swap(sent, "x").astype(F32)
+
+
+def reduce_blocks(blocks):
+    whole = blocks.transpose(0, 2, 1, 3).reshape(16 * SLOT, -1)
+    whole = lax.psum_scatter(whole, ("w", "u", "y", "c"), scatter_dimension=0, tiled=True)
+    return lax.psum_scatter(whole, "x", scatter_dimension=1, tiled=True).astype(F32)
+
+
+def reduce_one(slots, order):
     table = {}
     for which, index, rel in rel_slots(order):
         block = rel["w"] * 8 + rel["u"] * 4 + rel["y"] * 2 + rel["c"]
@@ -1002,8 +1267,8 @@
     back = jnp.cumprod(c[:, ::-1], axis=1)[:, ::-1]
     nf = jnp.where(place < 7, jnp.roll(back, -1, axis=1), 1.0)
     c0 = jnp.broadcast_to(c[:, :1], c.shape)
-    table = jnp.stack([m1, m2, m4, mf, ml, n1, n2, n4, nf, c0]).reshape(10, -1, 1)
-    return jnp.broadcast_to(table, table.shape[:2] + (128,))
+    tables = (jnp.stack(t).reshape(len(t), -1, 1) for t in ((m1, m2, m4, mf, ml), (n1, n2, n4, nf, c0, ml)))
+    return [jnp.broadcast_to(t, t.shape[:2] + (LANES,)) for t in tables]
 
 
 def on_device(
@@ -1045,8 +1310,10 @@
     carry = ((ids == previous) & (ids > 0) & started).astype(F32)
     valid = (ids > 0).astype(F32)
     lead = jnp.concatenate([carry[1:], jnp.zeros((1,), F32)])
-    masks = scan_masks(carry)
-    carry, valid_rows, lead = carry[:, None], valid[:, None], lead[:, None]
+    masks_down, masks_up = scan_masks(carry)
+    carry, valid_rows, lead = (
+        jnp.broadcast_to(v[:, None], (tokens, LANES)) for v in (carry, valid, lead)
+    )
 
     flat = 0
     for axis in EVERY:
@@ -1067,183 +1334,181 @@
         ]
     )
     piece = own_vectors.shape[1]
-    spread = jnp.where(
-        jnp.arange(width)[None, :] // piece == flat, jnp.tile(own_vectors, (1, width // piece)), 0.0
-    )
-    counts = jnp.broadcast_to(jnp.sum(valid), (1, width))
-    vectors = jnp.concatenate([spread, counts, jnp.zeros((4, width), F32)])
+    counts = jnp.where(jnp.arange(piece) == 0, jnp.sum(valid), 0.0)[None, :]
+    own_vectors = jnp.concatenate([own_vectors, counts, jnp.zeros((4, piece), F32)])
     output_t, value_t = time_output.T, channel_value.T
 
-    if sizes["x"] == 2:
-        mine = lax.dynamic_slice_in_dim(teacher, side * tokens, tokens)
-        theirs = lax.dynamic_slice_in_dim(teacher, (1 - side) * tokens, tokens)
-        theirs = swap(theirs, "x")
-        teacher_rows = jnp.where(
+    def teacher_rows_of(mine, theirs):
+        return jnp.where(
             side == 0,
             jnp.concatenate([mine, theirs], axis=1),
             jnp.concatenate([theirs, mine], axis=1),
         )
+
+    if sizes["x"] == 2:
+        mine = lax.dynamic_slice_in_dim(teacher, side * tokens, tokens)
+        theirs = lax.dynamic_slice_in_dim(teacher, (1 - side) * tokens, tokens)
+
+    key_order, val_order, rec_order = three_orders = ("wxuy", "wuyx", "wyxu")
+    half = width // 2
+    if fast:
+        wide = channel_key.shape[1]
+        split = wide // 2
+        keys = [Gather(channel_key[:, :split], "wuyx"), Gather(channel_key[:, split:], "wyux")]
+        first = pair_up(jnp.concatenate([time_key, time_value, time_recept, output_t], axis=1))
+        late = jnp.concatenate([value_t, channel_recept], axis=1)
+        first, late, own_vectors, masks_down, masks_up, mine, theirs = seal_all(
+            keys, first, late, own_vectors, masks_down, masks_up, mine, theirs
+        )
+        first = lax.all_gather(first, ("w", "u", "y", "c"))
+        step_all(*keys)
+        (vectors,) = gather_vectors(own_vectors, 0, 1)
+        late = pair_up(late)
+        late, vectors = seal_all(keys, late, vectors)
+        step_all(*keys)
+        (vectors,) = gather_vectors(vectors, 1, 3)
+        (vectors,) = seal_all(keys, vectors)
+        step_all(*keys)
+        (vectors,) = gather_vectors(vectors, 3, 5)
+        (vectors,) = seal_all(keys, vectors)
+        step_all(*keys)
+        mixed = first_mix(inputs, carry, vectors)
+        first, late, mixed, vectors = seal(first, late, mixed, vectors)
+        late = lax.all_gather(late, ("w", "u", "y", "c"))
+        key_w, value_w, recept_w, output_w = (all_of(first, n * half, half) for n in range(4))
     else:
-        teacher_rows = teacher
-
+        early = gather_plain(channel_key)
+        wide = early.shape[-1]
+        split = wide // 2
+        key_w, value_w, recept_w, output_w, crecept_w = (
+            all_of(gather_plain(w))
+            for w in (time_key, time_value, time_recept, output_t, channel_recept)
+        )
+        ckey_w = all_of(early)
+        late = gather_plain(value_t)
+        cvalue_w = [all_of(late, skip, split) for skip in (0, split)]
+        vectors = lax.all_gather(own_vectors, EVERY, axis=1, tiled=True)
+        mixed = first_mix(inputs, carry, vectors)
+
+    *saved, gated = time_forward(co, mixed, (key_w, value_w, recept_w), vectors, masks_down)
     if fast:
-        rest = lax.all_gather(jnp.concatenate([value_t, channel_recept], axis=1), EVERY)
-        rest = rest.reshape(16, 2, SLOT, rest.shape[-1])
-        cols = value_t.shape[1]
-        cvalue_w = ((("abs", 0, 0, cols),), [rest])
-        crecept_w = ((("abs", cols, 0, width // 2),), [rest])
-
-        key_c, val_c, rec_c = Gather(time_key, "wxuy"), Gather(time_value, "uwyx"), Gather(time_recept, "wyxu")
-        out_c = Gather(output_t, "wuyx")
-        split = channel_key.shape[1] // 2
-        ck_a, ck_b = Gather(channel_key[:, :split], "wxuy"), Gather(channel_key[:, split:], "uwyx")
-        three = (key_c, val_c, rec_c)
-
-        step_all(*three)
-        got = swap(vectors, "x")
-        (vectors, got) = seal_all(three, vectors, got)
-        vectors = vectors + got
-        step_all(*three, out_c)
-        got = swap(vectors, "y")
-        (vectors, got) = seal_all((*three, out_c), vectors, got)
-        vectors = vectors + got
-        step_all(*three, out_c, ck_a, ck_b)
-        vectors = vectors + swap(vectors, "c")
-        got = swap(vectors, "u")
-        (vectors, got) = seal_all((*three, out_c, ck_a, ck_b), vectors, got)
-        vectors = vectors + got
-        step_all(*three, out_c, ck_a, ck_b)
-        vectors = vectors + swap(vectors, "w")
-        mixed = first_mix(inputs, carry, vectors)
-        (mixed, vectors) = seal_all((*three, out_c, ck_a, ck_b), mixed, vectors)
-        step_all(*three, out_c, ck_a, ck_b)
-        (mixed,) = seal_all((*three, out_c, ck_a, ck_b), mixed)
-        key_w, value_w, recept_w = (weight_of(c.part()) for c in three)
-        step_all(out_c, ck_a, ck_b)
-    else:
-        vectors = lax.psum(vectors, EVERY)
-        mixed = first_mix(inputs, carry, vectors)
-        key_w, value_w, recept_w, output_w, ckey_w, crecept_w, cvalue_w = (
-            weight_of(gather_plain(w))
-            for w in (time_key, time_value, time_recept, output_t, channel_key, channel_recept, value_t)
-        )
-    count = vectors[11, 0]
-    scale = (float(tokens * devices) / count).reshape(1)
-
-    *saved, gated = time_forward(co, mixed, (key_w, value_w, recept_w), vectors, masks)
-    if fast:
-        (gated,) = seal_all((out_c, ck_a, ck_b), gated)
-        output_w = weight_of(out_c.part())
-        step_all(ck_a, ck_b)
+        (gated, theirs) = seal_all(keys, gated, theirs)
+        step_all(*keys)
+    if sizes["x"] == 2:
+        theirs = swap(theirs, "x")
     middle, mixed_k2, mixed_r2 = time_output_step(co, gated, inputs, carry, vectors, output_w)
     if fast:
-        (middle, mixed_k2, mixed_r2) = seal_all((ck_a, ck_b), middle, mixed_k2, mixed_r2)
-        ckey_w = weight_of(ck_a.part(), ck_b.part(split))
+        middle, mixed_k2, mixed_r2 = seal_all(keys, middle, mixed_k2, mixed_r2)
+        ckey_w = weight_of(keys[0].part(), keys[1].part(split))
     hidden, active = hidden_step(co, mixed_k2, ckey_w)
+    if fast:
+        hidden, theirs, late = seal(hidden, theirs, late)
+        cvalue_w = [all_of(late, skip, split) for skip in (0, split)]
+        crecept_w = all_of(late, wide, half)
+    teacher_rows = teacher_rows_of(mine, theirs) if sizes["x"] == 2 else teacher
+    count = jnp.sum(vectors[11])
+    scale = (float(tokens * devices) / count).reshape(1)
     result, dres, dkv, drec2, loss_rows = result_step(
-        co, scale, hidden, mixed_r2, middle, teacher_rows, valid_rows, cvalue_w, crecept_w
+        co, scale, hidden, mixed_r2, middle, teacher_rows, valid_rows, both_parts(cvalue_w, split), crecept_w
     )
 
-    half = width // 2
+    kept = lax.dynamic_slice_in_dim(result, side * half, half, axis=1)
+    arrived = lax.dynamic_slice_in_dim(result, (1 - side) * half, half, axis=1)
+    if sizes["x"] == 2:
+        arrived = swap(arrived, "x")
+
+    back = functools.partial(channel_back, co)
+    order_b, order_c = "wyux", "wuxy"
+    edge = jnp.zeros((8, width), F32)
+
+    def input_back_part(dmix, part, after, found):
+        return input_back(
+            co, dmix, inputs, dmid, lead, vectors, (key_w, value_w, recept_w), part, after, found
+        )
+
     if fast:
-        kept = lax.dynamic_slice_in_dim(result, side * half, half, axis=1)
-        sent = lax.dynamic_slice_in_dim(result, (1 - side) * half, half, axis=1)
-        arrived = swap(sent, "x")
-        split = hidden.shape[1] // 4
-        cv_a = Reduce(weight_grad(co, dkv, hidden, "wxuy", 0, split), "wxuy")
-        (hidden, dkv) = seal_all((cv_a,), hidden, dkv)
-        step_all(cv_a)
-        cv_b = Reduce(weight_grad(co, dkv, hidden, "uwyx", split, split), "uwyx")
-        (dkv, arrived) = seal_all((cv_a, cv_b), dkv, arrived)
-        step_all(cv_a, cv_b)
-        dkey2 = hidden_back(co, dkv, active, cvalue_w)
-        (dkey2,) = seal_all((cv_b,), dkey2)
-        step_all(cv_b)
-        ck_a = Reduce(weight_grad(co, mixed_k2, dkey2, "wyxu", 0, split), "wyxu")
-        (dkey2,) = seal_all((cv_a, ck_a), dkey2)
-        step_all(cv_a, ck_a)
-        ck_b = Reduce(weight_grad(co, mixed_k2, dkey2, "wxuy", split, split), "wxuy")
-        cr = Reduce(weight_grad(co, mixed_r2, drec2, "uwyx"), "uwyx")
-        (dkey2, drec2) = seal_all((ck_a, ck_b, cr), dkey2, drec2)
-        step_all(ck_a, ck_b, cr)
+        dkey_b, found = back(dkv, mixed_k2, hidden, active, cvalue_w[1], split, split, order_b)
+        group_b = Merged(found, order_b)
+        (dkv,) = seal_all((group_b,), dkv)
+        group_b.step()
+        dkey_a, (blocks,) = back(dkv, mixed_k2, hidden, active, cvalue_w[0], 0, split, None)
+        blocks = scatter_rows(blocks)
+        (dkey_a, arrived) = seal_all((group_b,), dkey_a, arrived)
+        group_b.step()
         dmid, dtime, sums2 = middle_back(
-            co, dkey2, drec2, middle, dres, lead, vectors, ckey_w, crecept_w
+            co, (dkey_a, dkey_b), drec2, middle, dres, lead, vectors, ckey_w, crecept_w
         )
-        chains = (cv_a, cv_b, ck_a, ck_b, cr)
-        (dtime, dmid) = seal_all(chains, dtime, dmid)
-        step_all(*chains)
-        out_c = Reduce(weight_grad(co, dtime, gated, "wuyx"), "wuyx")
-        (dtime,) = seal_all((cv_a, cv_b, ck_a, out_c), dtime)
-        step_all(cv_a, cv_b, ck_a, out_c)
-        *dmix, sums_t = time_back(co, dtime, saved, vectors, masks, output_w)
-        chains = (cv_a, cv_b, ck_a, ck_b, cr, out_c)
-        (dmix, dmid) = seal_all(chains, dmix, dmid)
-        step_all(cv_b, ck_b, cr, out_c)
-        orders = ("wxuy", "uwyx", "wyxu")
-        three = []
-        pending = [cv_b, ck_b, cr, out_c]
-        for m, d, order in zip(mixed, dmix, orders):
-            chain = Reduce(weight_grad(co, m, d, order), order)
-            (dmix,) = seal_all((*three, chain, *pending), dmix)
-            three.append(chain)
-            step_all(*three)
-            if len(three) == 2:
-                step_all(ck_a, ck_b, cr, out_c)
-                pending = [ck_a, ck_b, cr, out_c]
-        input_grad, sums1 = input_back(
-            co, dmix, inputs, dmid, lead, vectors, (key_w, value_w, recept_w)
+        found = weight_grads(
+            co, ((mixed_r2, drec2, order_c), (dtime, gated, order_c)), merged=True
         )
-        (input_grad, sums1) = seal_all((*three, *pending), input_grad, sums1)
-        for chain in (ck_b, cr, out_c, *three):
-            while chain.done < 5:
-                chain.step()
-        key_g, val_g, rec_g = (c.finish() for c in three)
-        output_g, crecept_g = out_c.finish(), cr.finish()
-        cvalue_g = jnp.concatenate([cv_a.finish(), cv_b.finish()], axis=1)
-        ckey_g = jnp.concatenate([ck_a.finish(), ck_b.finish()], axis=1)
+        group_c = Merged(found, order_c)
+        (dtime,) = seal_all((group_b, group_c), dtime)
+        step_all(group_b, group_c)
+        *dmix, sums_t = time_back(co, dtime, saved, vectors, masks_up, output_w)
+        (dmix, dmid) = seal_all((group_b, group_c), dmix, dmid)
+        step_all(group_b, group_c)
+        found = weight_grads(co, [(m, d, order) for m, d, order in zip(mixed, dmix, three_orders)])
+        group_t = Reduce(found, three_orders)
+        (dmix,) = seal_all((group_b, group_t), dmix)
+        step_all(group_b, group_t)
+        found, sums_l, edge = input_back_part(dmix, 0, edge, jnp.zeros_like(dmid))
+        (dmix, edge, found) = seal_all((group_b, group_c, group_t), dmix, edge, found)
+        step_all(group_c, group_t)
+        input_grad, sums_u, _ = input_back_part(dmix, 1, edge, found)
+    else:
+        dkey_b, found = back(dkv, mixed_k2, hidden, active, cvalue_w[1], split, split, order_b)
+        cv_b, ck_b = reduce_merged(found, order_b)
+        dkey_a, (blocks,) = back(dkv, mixed_k2, hidden, active, cvalue_w[0], 0, split, None)
+        cv_a, ck_a = (
+            reduce_blocks(blocks[..., n * split : (n + 1) * split]) for n in (0, 1)
+        )
+        dmid, dtime, sums2 = middle_back(
+            co, (dkey_a, dkey_b), drec2, middle, dres, lead, vectors, ckey_w, crecept_w
+        )
+        found = weight_grads(
+            co, ((mixed_r2, drec2, order_c), (dtime, gated, order_c)), merged=True
+        )
+        crecept_g, output_g = reduce_merged(found, order_c)
+        *dmix, sums_t = time_back(co, dtime, saved, vectors, masks_up, output_w)
+        found = weight_grads(co, [(m, d, order) for m, d, order in zip(mixed, dmix, three_orders)])
+        key_g, val_g, rec_g = reduce_plain(found, three_orders)
+        found, sums_l, edge = input_back_part(dmix, 0, edge, jnp.zeros_like(dmid))
+        input_grad, sums_u, _ = input_back_part(dmix, 1, edge, found)
+
+    rows = jnp.concatenate([sums_l[:2] + sums_u[:2], sums_t, sums_l[2:] + sums_u[2:], sums2, loss_rows[None]])
+    totals = jnp.sum(rows, axis=1)
+    if fast:
+        (totals,) = seal_all((group_c, group_t), totals)
+        for axes in ("xc", "yu", "w"):
+            step_all(*[group for group in (group_c, group_t) if group.done < 5])
+            for axis in axes:
+                totals = totals + swap(totals, axis)
+            (totals,) = seal_all((group_c, group_t), totals)
+        cv_b, ck_b = group_b.finish()
+        cv_a, ck_a = jnp.split(pair_sum(blocks), 2, axis=1)
+        crecept_g, output_g = group_c.finish()
+        key_g, val_g, rec_g = group_t.finish()
+    else:
+        totals = lax.psum(totals, EVERY)
+    loss = jnp.sum(totals[11]) / (2.0 * count * width)
+    vector_g = lax.dynamic_slice_in_dim(totals, flat * piece, piece, axis=1)
+    if sizes["x"] == 2:
+        cvalue_g = jnp.concatenate([cv_a, cv_b], axis=1)
+        ckey_g = jnp.concatenate([ck_a, ck_b], axis=1)
         outputs = jnp.where(
             side == 0,
             jnp.concatenate([kept, arrived], axis=0),
             jnp.concatenate([arrived, kept], axis=0),
         )
     else:
-        order = "wuyx"
-
-        def grad(model, chan):
-            return reduce_plain(weight_grad(co, model, chan, order), order)
-
-        if sizes["x"] == 2:
-            kept = lax.dynamic_slice_in_dim(result, side * half, half, axis=1)
-            arrived = swap(lax.dynamic_slice_in_dim(result, (1 - side) * half, half, axis=1), "x")
-            outputs = jnp.where(
-                side == 0,
-                jnp.concatenate([kept, arrived], axis=0),
-                jnp.concatenate([arrived, kept], axis=0),
+        cvalue_g, ckey_g = (
+            jnp.concatenate([a.reshape(-1, 2, split), b.reshape(-1, 2, split)], axis=2).reshape(
+                a.shape[0], -1
             )
-        else:
-            outputs = result
-        cvalue_g = grad(dkv, hidden)
-        dkey2 = hidden_back(co, dkv, active, cvalue_w)
-        ckey_g, crecept_g = grad(mixed_k2, dkey2), grad(mixed_r2, drec2)
-        dmid, dtime, sums2 = middle_back(
-            co, dkey2, drec2, middle, dres, lead, vectors, ckey_w, crecept_w
+            for a, b in ((cv_a, cv_b), (ck_a, ck_b))
         )
-        output_g = grad(dtime, gated)
-        *dmix, sums_t = time_back(co, dtime, saved, vectors, masks, output_w)
-        key_g, val_g, rec_g = (grad(m, d) for m, d in zip(mixed, dmix))
-        input_grad, sums1 = input_back(
-            co, dmix, inputs, dmid, lead, vectors, (key_w, value_w, recept_w)
-        )
-
-    rows = jnp.concatenate([sums1[:2], sums_t, sums1[2:], sums2, loss_rows[None]])
-    totals = jnp.sum(rows, axis=1)
-    if fast:
-        for axis in EVERY:
-            totals = totals + swap(totals, axis)
-    else:
-        totals = lax.psum(totals, EVERY)
-    loss = jnp.sum(totals[11]) / (2.0 * count * width)
-    vector_g = lax.dynamic_slice_in_dim(totals, flat * piece, piece, axis=1)
+        outputs = result
+
     return (
         outputs,
         loss,

time: 661 us -> 530 us (0.80)
  starting transfers between devices: 107 us -> 54.6 us
  Pallas kernels: 302 us -> 250 us
  other arithmetic: 55.7 us -> 45.2 us
  waiting for transfers between devices: 137 us -> 129 us
    ppermute x102 -> x51, starting transfers between devices: 107 us -> 54.5 us  [swap(): return lax.ppermute(values, axis, SWAP)]
    pallas_call x11 -> x5, Pallas kernels: 104 us -> 76.1 us  [the longest x2 44.9 us: channel_back(): pl.pallas_call(functools.partial(channel_back_kernel, layout=weight[0], o...]
    ppermute x102 -> x51, waiting for transfers between devices: 137 us -> 122 us  [swap(): return lax.ppermute(values, axis, SWAP)]
    convert_element_type x0 -> x13, other arithmetic: none -> 12.9 us  [the longest x6 10 us: step(): sum((part[place].astype(F32) for part in self.state)).astype(BF)]
    add x40 -> x5, other arithmetic: 17.1 us -> 4.46 us  [the longest x1 2.61 us: step(): far[m] + far_got[m]]
    pallas_call x1, Pallas kernels: 43 us -> 31.9 us  [middle_back(): pl.pallas_call(functools.partial(middle_back_kernel, layouts=[weight[0],...]
    add x9 -> x2, other arithmetic: 14.4 us -> 4.2 us  [step(): self.state = (near, near_got, swap(far + far_got, self.order[3]))]
    all_gather x1 -> x2, waiting for transfers between devices: 0.02 us -> 7.08 us  [the longest x1 7.08 us: on_device(): late = lax.all_gather(late, ('w', 'u', 'y', 'c'))]
  transfers between devices with their start and end apart: 103 -> 54, of which waited for: 33 -> 22; matrix products, arithmetic and copies ran while one was open for 10% -> 10% of each run, Pallas kernels for 39% -> 39%
where the time goes in v3:
time: 530 us; the launch traced here: 524 us
  Pallas kernels  250 us (47%)
  waiting for transfers between devices  129 us (24%)
  starting transfers between devices  54.6 us (10%)
  other arithmetic  45.2 us (9%)
  local copies, waits for them, and re-layouts  27.5 us (5%)
  between operations  18.1 us (3%)
    ppermute x51, waiting for transfers between devices, swap(): return lax.ppermute(values, axis, SWAP)  122 us
    ppermute x51, starting transfers between devices, swap(): return lax.ppermute(values, axis, SWAP)  54.5 us
    pallas_call x2, Pallas kernels, channel_back(): pl.pallas_call(functools.partial(channel_back_kernel, layout=weight[0], o...  44.9 us
    pallas_call x2, Pallas kernels, input_back(): pl.pallas_call(functools.partial(input_back_kernel, layouts=[w[0] for w i...  32.9 us
    pallas_call x1, Pallas kernels, middle_back(): pl.pallas_call(functools.partial(middle_back_kernel, layouts=[weight[0],...  31.9 us
    pallas_call x1, Pallas kernels, time_forward(): pl.pallas_call(functools.partial(time_forward_kernel, layouts=[w[0] for w...  29 us
    pallas_call x1, Pallas kernels, result_step(): pl.pallas_call(functools.partial(result_kernel, layouts=[weight[0], recep...  24.6 us
    pallas_call x1, Pallas kernels, time_back(): pl.pallas_call(functools.partial(time_back_kernel, layout=weight[0]), gri...  23.2 us
  transfers between devices with their start and end apart: 54, of which 22 were waited for; matrix products, arithmetic and copies ran while one was open for 10% of the time, Pallas kernels for 39%

profile of v3, /device:TPU:0, one launch (start us, length us, event | category | flops | bytes accessed | tf_op | source)
XLA Modules:
  0.0 524.4 jit_solution(17670599525737224922)
XLA Ops:
  9.0 2.9 collective-permute-start
  23.3 2.1 maximum_select_fusion.3
  25.4 1.9 broadcast_in_dim.140.masks
  27.3 2.2 broadcast_in_dim.148.masks
  29.7 2.0 collective-permute-start.4
  31.7 2.6 collective-permute-start.1
  34.7 4.4 collective-permute-done.4
  40.1 8.1 %collective-permute-done.1 = bf16[64,1024]{1,0:T(8,128)(2,1)S(1)} collective-permute-done((bf16[64,1024]{1,0:T(8,128)(2,1)S(1)}, bf16[64,1024]{1,0:T(8,128)(2,1)S(1)}, u32[]{:S(2)}, u32[]{:S(2)}) %collective-permute-start.1) | collective-permute-done | bytes 131104 | tf_op jit(solution)/shard_map/ppermute | solution.py:1082
  48.2 8.0 %collective-permute-done.2 = bf16[64,1024]{1,0:T(8,128)(2,1)S(1)} collective-permute-done((bf16[64,1024]{1,0:T(8,128)(2,1)S(1)}, bf16[64,1024]{1,0:T(8,128)(2,1)S(1)}, u32[]{:S(2)}, u32[]{:S(2)}) %collective-permute-start.2) | collective-permute-done | bytes 131104 | tf_op jit(solution)/shard_map/ppermute | solution.py:1082
  56.2 2.5 collective-permute-start.5
  62.0 4.4 collective-permute-done.8
  71.3 34.3 %collective-permute-done.11 = f32[16,256]{1,0:T(8,128)S(1)} collective-permute-done((f32[16,256]{1,0:T(8,128)S(1)}, f32[16,256]{1,0:T(8,128)S(1)}, u32[]{:S(2)}, u32[]{:S(2)}) %collective-permute-start.11) | collective-permute-done | bytes 16416 | tf_op jit(solution)/shard_map/ppermute | solution.py:1082
  105.6 4.6 collective-permute-start.12
  110.1 4.5 collective-permute-done.12
  116.3 8.3 %shard_map.364 = (bf16[1024,1024]{1,0:T(8,128)(2,1)}, bf16[1024,1024]{1,0:T(8,128)(2,1)}, bf16[1024,1024]{1,0:T(8,128)(2,1)}) custom-call(bf16[1024,1024]{1,0:T(8,128)(2,1)} %x_ref.7, f32[1024,128]{1,0:T(8,128)} %broadcast_in_dim.149.carry_ref, f32[16,1024]{1,0:T(8,128)} %maximum_select_fusion.5.vec_ref.vec), custom_call_target="tpu_custom_call" | custom-call | bytes 8388608 | tf_op jit(solution)/shard_map/pallas_call | solution.py:214
  127.9 29.0 %shard_map.365 = (f32[1024,1024]{1,0:T(8,128)}, f32[1024,1024]{1,0:T(8,128)}, f32[1024,1024]{1,0:T(8,128)}, f32[1024,1024]{1,0:T(8,128)}, f32[1024,1024]{1,0:T(8,128)}, /*index=5*/bf16[1024,1024]{1,0:T(8,128)(2,1)}) custom-call(s32[5]{0:T(128)} %stack.160.co, bf16[1024,1024]{1,0:T(8,128)(2,1)} %get-tuple-element.230.mk.refs_0_, ...), custom_call_target="tpu_custom_call" | custom-call | flops 17179869184 | bytes 35651584 | tf_op jit(solution)/shard_map/pallas_call | solution.py:322
  157.0 13.7 %collective-permute-done.15.refs_5_ = bf16[2,2,2,64,1024]{4,3,2,1,0:T(8,128)(2,1)} collective-permute-done((bf16[2,2,2,64,1024]{4,3,2,1,0:T(8,128)(2,1)S(1)}, bf16[2,2,2,64,1024]{4,3,2,1,0:T(8,128)(2,1)}, u32[]{:S(2)}, u32[]{:S(2)}) %collective-permute-start.15) | collective-permute-done | bytes 1048608 | tf_op jit(solution)/shard_map/ppermute | solution.py:1082
  172.4 13.6 %shard_map.366 = (f32[1024,1024]{1,0:T(8,128)}, bf16[1024,1024]{1,0:T(8,128)(2,1)}, bf16[1024,1024]{1,0:T(8,128)(2,1)}) custom-call(s32[5]{0:T(128)} %stack.160.co, bf16[1024,1024]{1,0:T(8,128)(2,1)} %get-tuple-element.243.gated.refs_3_, bf16[1024,1024]{1,0:T(8,128)(2,1)} %x_ref.7, f32[1024,128]{1,0:T(8,128)} %broadcast_in_dim.149.carry_ref, ...), custom_call_target="tpu_custom_call" | custom-call | flops 6442450944 | bytes 14680064 | tf_op jit(solution)/shard_map/pallas_call | solution.py:389
  188.1 18.2 %shard_map.367 = (bf16[1024,4096]{1,0:T(8,128)(2,1)}, bf16[1024,4096]{1,0:T(8,128)(2,1)}) custom-call(s32[5]{0:T(128)} %stack.160.co, bf16[1024,1024]{1,0:T(8,128)(2,1)} %get-tuple-element.247.mk.mixed, bf16[2,2,2,64,1024]{4,3,2,1,0:T(8,128)(2,1)} %copy-done.8, bf16[2,2,2,64,1024]{4,3,2,1,0:T(8,128)(2,1)} %collective-permute-done.13.refs_1_, ...), custom_call_target="tpu_custom_call" | custom-call | flops 9663676416 | bytes 27262976 | tf_op jit(solution)/shard_map/pallas_call | solution.py:447
  206.4 7.1 %all-gather.7.cloned.1.call-done = bf16[32,64,2560]{2,1,0:T(8,128)(2,1)} async-done(((bf16[2,64,2560]{2,1,0:T(8,128)(2,1)}), bf16[32,64,2560]{2,1,0:T(8,128)(2,1)}) %all-gather.7.cloned.1.call-update) | async-done | bytes 10485776 | tf_op jit(solution)/shard_map/all_gather | solution.py:1377
  213.5 2.0 maximum_select_fusion.teacher_ref
  216.4 24.6 %shard_map.368 = (bf16[1024,1024]{1,0:T(8,128)(2,1)}, f32[1024,1024]{1,0:T(8,128)}, bf16[1024,1024]{1,0:T(8,128)(2,1)}, bf16[1024,1024]{1,0:T(8,128)(2,1)}, f32[8,1024]{1,0:T(8,128)}) custom-call(s32[5]{0:T(128)} %stack.160.co, f32[1]{0:T(128)} %bitcast.46.scale, bf16[1024,4096]{1,0:T(8,128)(2,1)} %get-tuple-element.259.hidden, ...), custom_call_target="tpu_custom_call" | custom-call | flops 15032385536 | bytes 39845888 | tf_op jit(solution)/shard_map/pallas_call | solution.py:517
  241.0 22.6 %shard_map.369 = (bf16[1024,2048]{1,0:T(8,128)(2,1)}, bf16[2,2,2,2,64,1024]{5,4,3,2,1,0:T(8,128)(2,1)}, bf16[2,2,2,2,64,1024]{5,4,3,2,1,0:T(8,128)(2,1)}, bf16[2...) custom-call(s32[5]{0:T(128)} %stack.160.co, bf16[1024,1024]{1,0:T(8,128)(2,1)} %get-tuple-element.276.dkv, ...), custom_call_target="tpu_custom_call" | custom-call | flops 14173391872 | bytes 29360128 | tf_op jit(solution)/shard_map/pallas_call | solution.py:728
  264.3 2.7 constant_dynamic-slice_fusion.2
  268.5 22.3 %shard_map.370 = (bf16[1024,2048]{1,0:T(8,128)(2,1)}, bf16[16,2,64,2048]{3,2,1,0:T(8,128)(2,1)}) custom-call(s32[5]{0:T(128)} %stack.160.co, bf16[1024,1024]{1,0:T(8,128)(2,1)} %get-tuple-element.276.dkv, bf16[1024,1024]{1,0:T(8,128)(2,1)} %get-tuple-element.247.mk.mixed, bf16[1024,4096]{1,0:T(8,128)(2,1)} %get-tuple-element.259.hidden, ...), custom_call_target="tpu_custom_call" | custom-call | flops 14173391872 | bytes 29360128 | tf_op jit(solution)/shard_map/pallas_call | solution.py:728
  292.7 2.2 add.271
  297.5 31.9 %shard_map.371 = (f32[1024,1024]{1,0:T(8,128)}, bf16[1024,1024]{1,0:T(8,128)(2,1)}, f32[4,8,1024]{2,1,0:T(8,128)}) custom-call(s32[5]{0:T(128)} %stack.160.co, bf16[1024,2048]{1,0:T(8,128)(2,1)} %get-tuple-element.283.dkey_a, bf16[1024,2048]{1,0:T(8,128)(2,1)} %get-tuple-element.284.dkey_b, bf16[1024,1024]{1,0:T(8,128)(2,1)} %get-tuple-element.285.drec.refs_2_, ...), custom_call_target="tpu_custom_call" | custom-call | flops 17179869184 | bytes 37748736 | tf_op jit(solution)/shard_map/pallas_call | solution.py:824
  329.4 10.0 %shard_map.372 = (bf16[2,2,2,2,64,512]{5,4,3,2,1,0:T(8,128)(2,1)}, bf16[2,2,2,2,64,512]{5,4,3,2,1,0:T(8,128)(2,1)}, bf16[2,2,2,2,64,512]{5,4,3,2,1,0:T(8,128)(2,1)}, bf16[2,2,2,2,64,512]{5,4,3,2,1,0:T(8,128)(2,1)}) custom-call(s32[5]{0:T(128)} %stack.160.co, bf16[1024,1024]{1,0:T(8,128)(2,1)} %get-tuple-element.260.mr.refs_0_, ...), custom_call_target="tpu_custom_call" | custom-call | flops 5153960960 | bytes 12582912 | tf_op jit(solution)/shard_map/pallas_call | solution.py:608
  339.4 2.8 collective-permute-done.23
  342.2 4.8 fusion.1
  348.0 23.2 %shard_map.373 = (bf16[1024,1024]{1,0:T(8,128)(2,1)}, bf16[1024,1024]{1,0:T(8,128)(2,1)}, bf16[1024,1024]{1,0:T(8,128)(2,1)}, f32[2,8,1024]{2,1,0:T(8,128)}) custom-call(s32[5]{0:T(128)} %stack.160.co, bf16[1024,1024]{1,0:T(8,128)(2,1)} %get-tuple-element.299.refs_1_.dtime, f32[1024,1024]{1,0:T(8,128)} %get-tuple-element.300.key_ref, ...), custom_call_target="tpu_custom_call" | custom-call | flops 19327352832 | bytes 35651584 | tf_op jit(solution)/shard_map/pallas_call | solution.py:941
  371.2 12.5 %collective-permute-done.24 = bf16[2,2,2,64,1024]{4,3,2,1,0:T(8,128)(2,1)S(1)} collective-permute-done((bf16[2,2,2,64,1024]{4,3,2,1,0:T(8,128)(2,1)}, bf16[2,2,2,64,1024]{4,3,2,1,0:T(8,128)(2,1)S(1)}, u32[]{:S(2)}, u32[]{:S(2)}) %collective-permute-start.24) | collective-permute-done | bytes 1048608 | tf_op jit(solution)/shard_map/ppermute | solution.py:1082
  386.7 12.8 %shard_map.374 = (bf16[3,2,2,2,64,512]{5,4,3,2,1,0:T(8,128)(2,1)}, bf16[3,2,2,2,64,512]{5,4,3,2,1,0:T(8,128)(2,1)}, bf16[3,2,2,2,64,512]{5,4,3,2,1,0:T(8,128)(2,1)}, bf16[3,2,2,2,64,512]{5,4,3,2,1,0:T(8,128)(2,1)}) custom-call(s32[5]{0:T(128)} %stack.160.co, bf16[1024,1024]{1,0:T(8,128)(2,1)} %get-tuple-element.230.mk.refs_0_, ...), custom_call_target="tpu_custom_call" | custom-call | flops 7730940928 | bytes 18874368 | tf_op jit(solution)/shard_map/pallas_call | solution.py:608
  399.6 4.9 collective-permute-done.27
  406.5 2.0 add.280
  412.7 2.5 broadcast_in_dim.153._
  415.3 16.4 %shard_map.375 = (f32[1024,1024]{1,0:T(8,128)}, f32[5,8,1024]{2,1,0:T(8,128)}, f32[8,1024]{1,0:T(8,128)}) custom-call(s32[5]{0:T(128)} %stack.160.co, bf16[1024,1024]{1,0:T(8,128)(2,1)} %get-tuple-element.343.refs_3_.dkey, bf16[1024,1024]{1,0:T(8,128)(2,1)} %get-tuple-element.344.refs_4_.dval, ...), custom_call_target="tpu_custom_call", output_to_operand_aliasing={{0}: (9, {})} | custom-call | flops 8589934592 | bytes 16777216 | tf_op jit(solution)/shard_map/pallas_call | solution.py:1044
  433.7 3.4 fusion.5
  438.6 2.6 add_bitcast_fusion
  443.5 16.5 %shard_map.376 = (f32[1024,1024]{1,0:T(8,128)}, f32[5,8,1024]{2,1,0:T(8,128)}, f32[8,1024]{1,0:T(8,128)}) custom-call(s32[5]{0:T(128)} %stack.160.co, bf16[1024,1024]{1,0:T(8,128)(2,1)} %get-tuple-element.343.refs_3_.dkey, bf16[1024,1024]{1,0:T(8,128)(2,1)} %get-tuple-element.344.refs_4_.dval, ...), custom_call_target="tpu_custom_call", output_to_operand_aliasing={{0}: (9, {})} | custom-call | flops 8589934592 | bytes 16777216 | tf_op jit(solution)/shard_map/pallas_call | solution.py:1044
  470.9 2.6 fusion.6
  474.7 3.5 maximum_select_fusion.1
  480.6 2.7 collective-permute-start.42
  487.4 2.3 collective-permute-done.46
  490.7 3.9 collective-permute-done.47
  495.7 2.2 collective-permute-start.49
  497.9 7.2 %collective-permute-done.49 = f32[12,1024]{1,0:T(8,128)S(1)} collective-permute-done((f32[12,1024]{1,0:T(8,128)S(1)}, f32[12,1024]{1,0:T(8,128)S(1)}, u32[]{:S(2)}, u32[]{:S(2)}) %collective-permute-start.49) | collective-permute-done | bytes 49184 | tf_op jit(solution)/shard_map/ppermute | solution.py:1082
  510.9 2.9 collective-permute-done.50
  (274 shorter events, 81.8 us)
Async XLA Ops:
  7.2 117.4 %all-gather.5.cloned.1.call-start = ((), (), s32[]{:S(2)}) async-start(), calls=%async_computation.2 | async-start | bytes 8912896 | tf_op jit(solution)/shard_map/all_gather | solution.py:1363
  9.0 14.3 %collective-permute-start = (bf16[64,2048]{1,0:T(8,128)(2,1)}, bf16[64,2048]{1,0:T(8,128)(2,1)}, u32[]{:S(2)}, u32[]{:S(2)}) collective-permute-start(bf16[64,2048]{1,0:T(8,128)(2,1)} %get-tuple-element.443), channel_id=1, source_target_pairs={{0,1},{1,0},{2,3},{3,2},{4,5},{5,4},{6,7},{7,6},{8,9},{9,8},{10,11... | collective-permute-start | bytes 786440 | tf_op jit(solution)/shard_map/ppermute | solution.py:1082
  29.6 183.9 %all-gather.7.cloned.1.call-start = ((), (), s32[]{:S(2)}) async-start(), calls=%async_computation.3 | async-start | bytes 11141120 | tf_op jit(solution)/shard_map/all_gather | solution.py:1377
  29.6 9.5 %collective-permute-start.3 = (bf16[64,2560]{1,0:T(8,128)(2,1)S(1)}, bf16[64,2560]{1,0:T(8,128)(2,1)S(1)}, u32[]{:S(2)}, u32[]{:S(2)}) collective-permute-start(bf16[64,2560]{1,0:T(8,128)(2,1)S(1)} %pad_maximum_fusion.5), channel_id=1, source_target_pairs={{0,1},{1,0},{2,3},{3,2},{4,5},{5,4},{6,7},{7,6},{8,9},{9,8},{10,11... | collective-permute-start | bytes 983048 | tf_op jit(solution)/shard_map/ppermute | solution.py:1082
  29.7 9.3 %collective-permute-start.4 = (f32[16,32]{1,0:T(8,128)S(1)}, f32[16,32]{1,0:T(8,128)S(1)}, u32[]{:S(2)}, u32[]{:S(2)}) collective-permute-start(f32[16,32]{1,0:T(8,128)S(1)} %concatenate.144), channel_id=1, source_target_pairs={{0,1},{1,0},{2,3},{3,2},{4,5},{5,4},{6,7},{7,6},{8,9},{9,8},{10,11... | collective-permute-start | bytes 6152 | tf_op jit(solution)/shard_map/ppermute | solution.py:1082
  31.7 16.4 %collective-permute-start.1 = (bf16[64,1024]{1,0:T(8,128)(2,1)S(1)}, bf16[64,1024]{1,0:T(8,128)(2,1)S(1)}, u32[]{:S(2)}, u32[]{:S(2)}) collective-permute-start(bf16[64,1024]{1,0:T(8,128)(2,1)S(1)} %get-tuple-element.211), channel_id=1, source_target_pairs={{0,16},{16,0},{1,17},{17,1},{2,18},{18,2},{3,19},{19,3},{4,20},{20... | collective-permute-start | bytes 393224 | tf_op jit(solution)/shard_map/ppermute | solution.py:1082
  34.3 21.8 %collective-permute-start.2 = (bf16[64,1024]{1,0:T(8,128)(2,1)S(1)}, bf16[64,1024]{1,0:T(8,128)(2,1)S(1)}, u32[]{:S(2)}, u32[]{:S(2)}) collective-permute-start(bf16[64,1024]{1,0:T(8,128)(2,1)S(1)} %get-tuple-element.213), channel_id=1, source_target_pairs={{0,16},{16,0},{1,17},{17,1},{2,18},{18,2},{3,19},{19,3},{4,20},{20... | collective-permute-start | bytes 393224 | tf_op jit(solution)/shard_map/ppermute | solution.py:1082
  56.2 11.4 %collective-permute-start.5 = (bf16[2,64,1024]{2,1,0:T(8,128)(2,1)S(1)}, bf16[2,64,1024]{2,1,0:T(8,128)(2,1)S(1)}, u32[]{:S(2)}, u32[]{:S(2)}) collective-permute-start(bf16[2,64,1024]{2,1,0:T(8,128)(2,1)S(1)} %pad_maximum_fusion.7), channel_id=1, source_target_pairs={{0,8},{8,0},{1,9},{9,1},{2,10},{10,2},{3,11},{11,3},{4,12},{12,4},... | collective-permute-start | bytes 786440 | tf_op jit(solution)/shard_map/ppermute | solution.py:1082
  58.7 8.9 %collective-permute-start.6 = (bf16[2,64,1024]{2,1,0:T(8,128)(2,1)S(1)}, bf16[2,64,1024]{2,1,0:T(8,128)(2,1)S(1)}, u32[]{:S(2)}, u32[]{:S(2)}) collective-permute-start(bf16[2,64,1024]{2,1,0:T(8,128)(2,1)S(1)} %pad_maximum_fusion.8), channel_id=1, source_target_pairs={{0,4},{4,0},{1,5},{5,1},{2,6},{6,2},{3,7},{7,3},{8,12},{12,8},{9,1... | collective-permute-start | bytes 786440 | tf_op jit(solution)/shard_map/ppermute | solution.py:1082
  67.6 47.7 %collective-permute-start.9 = (bf16[2,2,64,1024]{3,2,1,0:T(8,128)(2,1)S(1)}, bf16[2,2,64,1024]{3,2,1,0:T(8,128)(2,1)S(1)}, u32[]{:S(2)}, u32[]{:S(2)}) collective-permute-start(bf16[2,2,64,1024]{3,2,1,0:T(8,128)(2,1)S(1)} %pad_maximum_fusion.2), channel_id=1, source_target_pairs={{0,4},{4,0},{1,5},{5,1},{2,6},{6,2},{3,7},{7,3},{8,12},{12,8},{9,1... | collective-permute-start | bytes 1572872 | tf_op jit(solution)/shard_map/ppermute | solution.py:1082
  69.2 46.1 %collective-permute-start.10 = (bf16[2,2,64,1024]{3,2,1,0:T(8,128)(2,1)S(1)}, bf16[2,2,64,1024]{3,2,1,0:T(8,128)(2,1)S(1)}, u32[]{:S(2)}, u32[]{:S(2)}) collective-permute-start(bf16[2,2,64,1024]{3,2,1,0:T(8,128)(2,1)S(1)} %pad_maximum_fusion.3), channel_id=1, source_target_pairs={{0,8},{8,0},{1,9},{9,1},{2,10},{10,2},{3,11},{11,3},{4,12},{12,4},... | collective-permute-start | bytes 1572872 | tf_op jit(solution)/shard_map/ppermute | solution.py:1082
  69.9 35.7 %collective-permute-start.11 = (f32[16,256]{1,0:T(8,128)S(1)}, f32[16,256]{1,0:T(8,128)S(1)}, u32[]{:S(2)}, u32[]{:S(2)}) collective-permute-start(f32[16,256]{1,0:T(8,128)S(1)} %maximum_select_fusion.7), channel_id=1, source_target_pairs={{0,8},{8,0},{1,9},{9,1},{2,10},{10,2},{3,11},{11,3},{4,12},{12,4},... | collective-permute-start | bytes 49160 | tf_op jit(solution)/shard_map/ppermute | solution.py:1082
  105.6 9.1 %collective-permute-start.12 = (f32[16,512]{1,0:T(8,128)S(1)}, f32[16,512]{1,0:T(8,128)S(1)}, u32[]{:S(2)}, u32[]{:S(2)}) collective-permute-start(f32[16,512]{1,0:T(8,128)S(1)} %maximum_select_fusion.6), channel_id=1, source_target_pairs={{0,16},{16,0},{1,17},{17,1},{2,18},{18,2},{3,19},{19,3},{4,20},{20... | collective-permute-start | bytes 98312 | tf_op jit(solution)/shard_map/ppermute | solution.py:1082
  124.6 381.8 %reduce-scatter.2.cloned.1.call-start = ((), (), s32[]{:S(2)}) async-start(), calls=%async_computation.1 | async-start | bytes 8912896 | tf_op jit(solution)/shard_map/reduce_scatter | solution.py:1221
  125.4 31.6 %collective-permute-start.13 = (bf16[2,2,2,64,1024]{4,3,2,1,0:T(8,128)(2,1)S(1)}, bf16[2,2,2,64,1024]{4,3,2,1,0:T(8,128)(2,1)}, u32[]{:S(2)}, u32[]{:S(2)}) collective-permute-start(bf16[2,2,2,64,1024]{4,3,2,1,0:T(8,128)(2,1)S(1)} %pad_maximum_fusion.refs_0_), channel_id=1, source_target_pairs={{0,1},{1,0},{2,3},{3,2},{4,5},{5,4},{6,7},{7,6},{8,9},{9,8},{10,11... | collective-permute-start | bytes 3145736 | tf_op jit(solution)/shard_map/ppermute | solution.py:1082
  126.0 31.0 %collective-permute-start.14 = (bf16[2,2,2,64,1024]{4,3,2,1,0:T(8,128)(2,1)S(1)}, bf16[2,2,2,64,1024]{4,3,2,1,0:T(8,128)(2,1)}, u32[]{:S(2)}, u32[]{:S(2)}) collective-permute-start(bf16[2,2,2,64,1024]{4,3,2,1,0:T(8,128)(2,1)S(1)} %pad_maximum_fusion.refs_0_), channel_id=1, source_target_pairs={{0,2},{2,0},{1,3},{3,1},{4,6},{6,4},{5,7},{7,5},{8,10},{10,8},{9,1... | collective-permute-start | bytes 3145736 | tf_op jit(solution)/shard_map/ppermute | solution.py:1082
  126.1 44.6 %collective-permute-start.15 = (bf16[2,2,2,64,1024]{4,3,2,1,0:T(8,128)(2,1)S(1)}, bf16[2,2,2,64,1024]{4,3,2,1,0:T(8,128)(2,1)}, u32[]{:S(2)}, u32[]{:S(2)}) collective-permute-start(bf16[2,2,2,64,1024]{4,3,2,1,0:T(8,128)(2,1)S(1)} %pad_maximum_fusion.1.refs_4_), channel_id=1, source_target_pairs={{0,1},{1,0},{2,3},{3,2},{4,5},{5,4},{6,7},{7,6},{8,9},{9,8},{10,11... | collective-permute-start | bytes 3145736 | tf_op jit(solution)/shard_map/ppermute | solution.py:1082
  127.7 43.0 %collective-permute-start.16 = (bf16[2,2,2,64,1024]{4,3,2,1,0:T(8,128)(2,1)S(1)}, bf16[2,2,2,64,1024]{4,3,2,1,0:T(8,128)(2,1)S(1)}, u32[]{:S(2)}, u32[]{:S(2)}) collective-permute-start(bf16[2,2,2,64,1024]{4,3,2,1,0:T(8,128)(2,1)S(1)} %pad_maximum_fusion.1.refs_4_), channel_id=1, source_target_pairs={{0,2},{2,0},{1,3},{3,1},{4,6},{6,4},{5,7},{7,5},{8,10},{10,8},{9,1... | collective-permute-start | bytes 3145736 | tf_op jit(solution)/shard_map/ppermute | solution.py:1082
  170.7 17.4 %collective-permute-start.17 = (bf16[2,2,2,64,1024]{4,3,2,1,0:T(8,128)(2,1)}, bf16[2,2,2,64,1024]{4,3,2,1,0:T(8,128)(2,1)}, u32[]{:S(2)}, u32[]{:S(2)}) collective-permute-start(bf16[2,2,2,64,1024]{4,3,2,1,0:T(8,128)(2,1)} %collective-permute-done.13.refs_1_), channel_id=1, source_target_pairs={{0,2},{2,0},{1,3},{3,1},{4,6},{6,4},{5,7},{7,5},{8,10},{10,8},{9,1... | collective-permute-start | bytes 3145736 | tf_op jit(solution)/shard_map/ppermute | solution.py:1082
  171.7 16.4 %collective-permute-start.18 = (bf16[2,2,2,64,1024]{4,3,2,1,0:T(8,128)(2,1)}, bf16[2,2,2,64,1024]{4,3,2,1,0:T(8,128)(2,1)}, u32[]{:S(2)}, u32[]{:S(2)}) collective-permute-start(bf16[2,2,2,64,1024]{4,3,2,1,0:T(8,128)(2,1)} %collective-permute-done.15.refs_5_), channel_id=1, source_target_pairs={{0,2},{2,0},{1,3},{3,1},{4,6},{6,4},{5,7},{7,5},{8,10},{10,8},{9,1... | collective-permute-start | bytes 3145736 | tf_op jit(solution)/shard_map/ppermute | solution.py:1082
  171.7 34.7 %collective-permute-start.19 = (bf16[1024,512]{1,0:T(8,128)(2,1)S(1)}, bf16[1024,512]{1,0:T(8,128)(2,1)S(1)}, u32[]{:S(2)}, u32[]{:S(2)}) collective-permute-start(bf16[1024,512]{1,0:T(8,128)(2,1)S(1)} %copy-done.6), channel_id=1, source_target_pairs={{0,1},{1,0},{2,3},{3,2},{4,5},{5,4},{6,7},{7,6},{8,9},{9,8},{10,11... | collective-permute-start | bytes 3145736 | tf_op jit(solution)/shard_map/ppermute | solution.py:1082
  263.7 29.0 %collective-permute-start.20 = (bf16[2,2,2,2,64,1024]{5,4,3,2,1,0:T(8,128)(2,1)}, bf16[2,2,2,2,64,1024]{5,4,3,2,1,0:T(8,128)(2,1)S(1)}, u32[]{:S(2)}, u32[]{:S(2)}) collective-permute-start(bf16[2,2,2,2,64,1024]{5,4,3,2,1,0:T(8,128)(2,1)} %get-tuple-element.274), channel_id=1, source_target_pairs={{0,2},{2,0},{1,3},{3,1},{4,6},{6,4},{5,7},{7,5},{8,10},{10,8},{9,1... | collective-permute-start | bytes 6291464 | tf_op jit(solution)/shard_map/ppermute | solution.py:1082
  264.0 28.6 %collective-permute-start.21 = (bf16[2,2,2,2,64,1024]{5,4,3,2,1,0:T(8,128)(2,1)}, bf16[2,2,2,2,64,1024]{5,4,3,2,1,0:T(8,128)(2,1)}, u32[]{:S(2)}, u32[]{:S(2)}) collective-permute-start(bf16[2,2,2,2,64,1024]{5,4,3,2,1,0:T(8,128)(2,1)} %get-tuple-element.275), channel_id=1, source_target_pairs={{0,2},{2,0},{1,3},{3,1},{4,6},{6,4},{5,7},{7,5},{8,10},{10,8},{9,1... | collective-permute-start | bytes 6291464 | tf_op jit(solution)/shard_map/ppermute | solution.py:1082
  267.0 25.6 %collective-permute-start.22 = (bf16[1024,512]{1,0:T(8,128)(2,1)}, bf16[1024,512]{1,0:T(8,128)(2,1)}, u32[]{:S(2)}, u32[]{:S(2)}) collective-permute-start(bf16[1024,512]{1,0:T(8,128)(2,1)} %get-tuple-element.415), channel_id=1, source_target_pairs={{0,1},{1,0},{2,3},{3,2},{4,5},{5,4},{6,7},{7,6},{8,9},{9,8},{10,11... | collective-permute-start | bytes 3145736 | tf_op jit(solution)/shard_map/ppermute | solution.py:1082
  294.9 47.3 %collective-permute-start.23 = (bf16[2,2,2,2,64,1024]{5,4,3,2,1,0:T(8,128)(2,1)}, bf16[2,2,2,2,64,1024]{5,4,3,2,1,0:T(8,128)(2,1)}, u32[]{:S(2)}, u32[]{:S(2)}) collective-permute-start(bf16[2,2,2,2,64,1024]{5,4,3,2,1,0:T(8,128)(2,1)} %add.271), channel_id=1, source_target_pairs={{0,1},{1,0},{2,3},{3,2},{4,5},{5,4},{6,7},{7,6},{8,9},{9,8},{10,11... | collective-permute-start | bytes 6291464 | tf_op jit(solution)/shard_map/ppermute | solution.py:1082
  347.0 36.8 %collective-permute-start.24 = (bf16[2,2,2,64,1024]{4,3,2,1,0:T(8,128)(2,1)}, bf16[2,2,2,64,1024]{4,3,2,1,0:T(8,128)(2,1)S(1)}, u32[]{:S(2)}, u32[]{:S(2)}) collective-permute-start(bf16[2,2,2,64,1024]{4,3,2,1,0:T(8,128)(2,1)} %get-tuple-element.395), channel_id=1, source_target_pairs={{0,8},{8,0},{1,9},{9,1},{2,10},{10,2},{3,11},{11,3},{4,12},{12,4},... | collective-permute-start | bytes 3145736 | tf_op jit(solution)/shard_map/ppermute | solution.py:1082
  347.5 36.3 %collective-permute-start.25 = (bf16[2,2,2,2,64,512]{5,4,3,2,1,0:T(8,128)(2,1)}, bf16[2,2,2,2,64,512]{5,4,3,2,1,0:T(8,128)(2,1)S(1)}, u32[]{:S(2)}, u32[]{:S(2)}) collective-permute-start(bf16[2,2,2,2,64,512]{5,4,3,2,1,0:T(8,128)(2,1)} %get-tuple-element.297), channel_id=1, source_target_pairs={{0,2},{2,0},{1,3},{3,1},{4,6},{6,4},{5,7},{7,5},{8,10},{10,8},{9,1... | collective-permute-start | bytes 3145736 | tf_op jit(solution)/shard_map/ppermute | solution.py:1082
  347.5 36.3 %collective-permute-start.26 = (bf16[2,2,2,2,64,512]{5,4,3,2,1,0:T(8,128)(2,1)}, bf16[2,2,2,2,64,512]{5,4,3,2,1,0:T(8,128)(2,1)S(1)}, u32[]{:S(2)}, u32[]{:S(2)}) collective-permute-start(bf16[2,2,2,2,64,512]{5,4,3,2,1,0:T(8,128)(2,1)} %get-tuple-element.298), channel_id=1, source_target_pairs={{0,2},{2,0},{1,3},{3,1},{4,6},{6,4},{5,7},{7,5},{8,10},{10,8},{9,1... | collective-permute-start | bytes 3145736 | tf_op jit(solution)/shard_map/ppermute | solution.py:1082
  385.2 19.3 %collective-permute-start.27 = (bf16[2,2,64,1024]{3,2,1,0:T(8,128)(2,1)S(1)}, bf16[2,2,64,1024]{3,2,1,0:T(8,128)(2,1)S(1)}, u32[]{:S(2)}, u32[]{:S(2)}) collective-permute-start(bf16[2,2,64,1024]{3,2,1,0:T(8,128)(2,1)S(1)} %get-tuple-element.412), channel_id=1, source_target_pairs={{0,4},{4,0},{1,5},{5,1},{2,6},{6,2},{3,7},{7,3},{8,12},{12,8},{9,1... | collective-permute-start | bytes 1572872 | tf_op jit(solution)/shard_map/ppermute | solution.py:1082
  405.3 28.4 %collective-permute-start.30 = (bf16[3,2,2,2,64,512]{5,4,3,2,1,0:T(8,128)(2,1)}, bf16[3,2,2,2,64,512]{5,4,3,2,1,0:T(8,128)(2,1)}, u32[]{:S(2)}, u32[]{:S(2)}) collective-permute-start(bf16[3,2,2,2,64,512]{5,4,3,2,1,0:T(8,128)(2,1)} %get-tuple-element.327), channel_id=1, source_target_pairs={{0,2},{2,0},{1,3},{3,1},{4,6},{6,4},{5,7},{7,5},{8,10},{10,8},{9,1... | collective-permute-start | bytes 4718600 | tf_op jit(solution)/shard_map/ppermute | solution.py:1082
  405.3 28.4 %collective-permute-start.31 = (bf16[3,2,2,2,64,512]{5,4,3,2,1,0:T(8,128)(2,1)}, bf16[3,2,2,2,64,512]{5,4,3,2,1,0:T(8,128)(2,1)S(1)}, u32[]{:S(2)}, u32[]{:S(2)}) collective-permute-start(bf16[3,2,2,2,64,512]{5,4,3,2,1,0:T(8,128)(2,1)} %get-tuple-element.328), channel_id=1, source_target_pairs={{0,2},{2,0},{1,3},{3,1},{4,6},{6,4},{5,7},{7,5},{8,10},{10,8},{9,1... | collective-permute-start | bytes 4718600 | tf_op jit(solution)/shard_map/ppermute | solution.py:1082
  408.4 25.2 %collective-permute-start.29 = (bf16[2,2,2,2,64,512]{5,4,3,2,1,0:T(8,128)(2,1)S(1)}, bf16[2,2,2,2,64,512]{5,4,3,2,1,0:T(8,128)(2,1)}, u32[]{:S(2)}, u32[]{:S(2)}) collective-permute-start(bf16[2,2,2,2,64,512]{5,4,3,2,1,0:T(8,128)(2,1)S(1)} %add.280), channel_id=1, source_target_pairs={{0,4},{4,0},{1,5},{5,1},{2,6},{6,2},{3,7},{7,3},{8,12},{12,8},{9,1... | collective-permute-start | bytes 3145736 | tf_op jit(solution)/shard_map/ppermute | solution.py:1082
  410.3 21.4 %collective-permute-start.28 = (bf16[2,64,1024]{2,1,0:T(8,128)(2,1)S(1)}, bf16[2,64,1024]{2,1,0:T(8,128)(2,1)S(1)}, u32[]{:S(2)}, u32[]{:S(2)}) collective-permute-start(bf16[2,64,1024]{2,1,0:T(8,128)(2,1)S(1)} %get-tuple-element.420), channel_id=1, source_target_pairs={{0,16},{16,0},{1,17},{17,1},{2,18},{18,2},{3,19},{19,3},{4,20},{20... | collective-permute-start | bytes 786440 | tf_op jit(solution)/shard_map/ppermute | solution.py:1082
  437.1 29.1 %collective-permute-start.32 = (bf16[2,2,2,64,512]{4,3,2,1,0:T(8,128)(2,1)}, bf16[2,2,2,64,512]{4,3,2,1,0:T(8,128)(2,1)}, u32[]{:S(2)}, u32[]{:S(2)}) collective-permute-start(bf16[2,2,2,64,512]{4,3,2,1,0:T(8,128)(2,1)} %get-tuple-element.410), channel_id=1, source_target_pairs={{0,1},{1,0},{2,3},{3,2},{4,5},{5,4},{6,7},{7,6},{8,9},{9,8},{10,11... | collective-permute-start | bytes 1572872 | tf_op jit(solution)/shard_map/ppermute | solution.py:1082
  441.2 25.1 %collective-permute-start.33 = (bf16[2,2,2,64,512]{4,3,2,1,0:T(8,128)(2,1)}, bf16[2,2,2,64,512]{4,3,2,1,0:T(8,128)(2,1)}, u32[]{:S(2)}, u32[]{:S(2)}) collective-permute-start(bf16[2,2,2,64,512]{4,3,2,1,0:T(8,128)(2,1)} %get-tuple-element.409), channel_id=1, source_target_pairs={{0,4},{4,0},{1,5},{5,1},{2,6},{6,2},{3,7},{7,3},{8,12},{12,8},{9,1... | collective-permute-start | bytes 1572872 | tf_op jit(solution)/shard_map/ppermute | solution.py:1082
  442.9 23.4 %collective-permute-start.34 = (bf16[2,2,2,64,512]{4,3,2,1,0:T(8,128)(2,1)}, bf16[2,2,2,64,512]{4,3,2,1,0:T(8,128)(2,1)}, u32[]{:S(2)}, u32[]{:S(2)}) collective-permute-start(bf16[2,2,2,64,512]{4,3,2,1,0:T(8,128)(2,1)} %get-tuple-element.408), channel_id=1, source_target_pairs={{0,1},{1,0},{2,3},{3,2},{4,5},{5,4},{6,7},{7,6},{8,9},{9,8},{10,11... | collective-permute-start | bytes 1572872 | tf_op jit(solution)/shard_map/ppermute | solution.py:1082
  443.4 22.8 %collective-permute-start.35 = (bf16[2,2,2,64,512]{4,3,2,1,0:T(8,128)(2,1)}, bf16[2,2,2,64,512]{4,3,2,1,0:T(8,128)(2,1)}, u32[]{:S(2)}, u32[]{:S(2)}) collective-permute-start(bf16[2,2,2,64,512]{4,3,2,1,0:T(8,128)(2,1)} %get-tuple-element.407), channel_id=1, source_target_pairs={{0,8},{8,0},{1,9},{9,1},{2,10},{10,2},{3,11},{11,3},{4,12},{12,4},... | collective-permute-start | bytes 1572872 | tf_op jit(solution)/shard_map/ppermute | solution.py:1082
  467.5 10.8 %collective-permute-start.36 = (bf16[2,2,64,512]{3,2,1,0:T(8,128)(2,1)S(1)}, bf16[2,2,64,512]{3,2,1,0:T(8,128)(2,1)S(1)}, u32[]{:S(2)}, u32[]{:S(2)}) collective-permute-start(bf16[2,2,64,512]{3,2,1,0:T(8,128)(2,1)S(1)} %get-tuple-element.418), channel_id=1, source_target_pairs={{0,8},{8,0},{1,9},{9,1},{2,10},{10,2},{3,11},{11,3},{4,12},{12,4},... | collective-permute-start | bytes 786440 | tf_op jit(solution)/shard_map/ppermute | solution.py:1082
  473.5 6.4 %collective-permute-start.37 = (bf16[2,2,64,512]{3,2,1,0:T(8,128)(2,1)S(1)}, bf16[2,2,64,512]{3,2,1,0:T(8,128)(2,1)S(1)}, u32[]{:S(2)}, u32[]{:S(2)}) collective-permute-start(bf16[2,2,64,512]{3,2,1,0:T(8,128)(2,1)S(1)} %get-tuple-element.406), channel_id=1, source_target_pairs={{0,8},{8,0},{1,9},{9,1},{2,10},{10,2},{3,11},{11,3},{4,12},{12,4},... | collective-permute-start | bytes 786440 | tf_op jit(solution)/shard_map/ppermute | solution.py:1082
  473.7 6.4 %collective-permute-start.38 = (bf16[2,2,64,512]{3,2,1,0:T(8,128)(2,1)S(1)}, bf16[2,2,64,512]{3,2,1,0:T(8,128)(2,1)S(1)}, u32[]{:S(2)}, u32[]{:S(2)}) collective-permute-start(bf16[2,2,64,512]{3,2,1,0:T(8,128)(2,1)S(1)} %get-tuple-element.404), channel_id=1, source_target_pairs={{0,4},{4,0},{1,5},{5,1},{2,6},{6,2},{3,7},{7,3},{8,12},{12,8},{9,1... | collective-permute-start | bytes 786440 | tf_op jit(solution)/shard_map/ppermute | solution.py:1082
  474.1 6.4 %collective-permute-start.39 = (bf16[2,2,64,512]{3,2,1,0:T(8,128)(2,1)S(1)}, bf16[2,2,64,512]{3,2,1,0:T(8,128)(2,1)S(1)}, u32[]{:S(2)}, u32[]{:S(2)}) collective-permute-start(bf16[2,2,64,512]{3,2,1,0:T(8,128)(2,1)S(1)} %get-tuple-element.397), channel_id=1, source_target_pairs={{0,1},{1,0},{2,3},{3,2},{4,5},{5,4},{6,7},{7,6},{8,9},{9,8},{10,11... | collective-permute-start | bytes 786440 | tf_op jit(solution)/shard_map/ppermute | solution.py:1082
  480.6 14.1 %collective-permute-start.42 = (bf16[2,64,512]{2,1,0:T(8,128)(2,1)S(1)}, bf16[2,64,512]{2,1,0:T(8,128)(2,1)S(1)}, u32[]{:S(2)}, u32[]{:S(2)}) collective-permute-start(bf16[2,64,512]{2,1,0:T(8,128)(2,1)S(1)} %get-tuple-element.432), channel_id=1, source_target_pairs={{0,16},{16,0},{1,17},{17,1},{2,18},{18,2},{3,19},{19,3},{4,20},{20... | collective-permute-start | bytes 393224 | tf_op jit(solution)/shard_map/ppermute | solution.py:1082
  483.3 11.3 %collective-permute-start.43 = (bf16[2,64,512]{2,1,0:T(8,128)(2,1)S(1)}, bf16[2,64,512]{2,1,0:T(8,128)(2,1)S(1)}, u32[]{:S(2)}, u32[]{:S(2)}) collective-permute-start(bf16[2,64,512]{2,1,0:T(8,128)(2,1)S(1)} %get-tuple-element.430), channel_id=1, source_target_pairs={{0,1},{1,0},{2,3},{3,2},{4,5},{5,4},{6,7},{7,6},{8,9},{9,8},{10,11... | collective-permute-start | bytes 393224 | tf_op jit(solution)/shard_map/ppermute | solution.py:1082
  484.0 10.7 %collective-permute-start.44 = (bf16[2,64,512]{2,1,0:T(8,128)(2,1)S(1)}, bf16[2,64,512]{2,1,0:T(8,128)(2,1)S(1)}, u32[]{:S(2)}, u32[]{:S(2)}) collective-permute-start(bf16[2,64,512]{2,1,0:T(8,128)(2,1)S(1)} %get-tuple-element.428), channel_id=1, source_target_pairs={{0,8},{8,0},{1,9},{9,1},{2,10},{10,2},{3,11},{11,3},{4,12},{12,4},... | collective-permute-start | bytes 393224 | tf_op jit(solution)/shard_map/ppermute | solution.py:1082
  486.8 7.9 %collective-permute-start.45 = (bf16[2,64,512]{2,1,0:T(8,128)(2,1)S(1)}, bf16[2,64,512]{2,1,0:T(8,128)(2,1)S(1)}, u32[]{:S(2)}, u32[]{:S(2)}) collective-permute-start(bf16[2,64,512]{2,1,0:T(8,128)(2,1)S(1)} %get-tuple-element.426), channel_id=1, source_target_pairs={{0,4},{4,0},{1,5},{5,1},{2,6},{6,2},{3,7},{7,3},{8,12},{12,8},{9,1... | collective-permute-start | bytes 393224 | tf_op jit(solution)/shard_map/ppermute | solution.py:1082
  494.9 10.2 %collective-permute-start.48 = (bf16[3,64,512]{2,1,0:T(8,128)(2,1)S(1)}, bf16[3,64,512]{2,1,0:T(8,128)(2,1)S(1)}, u32[]{:S(2)}, u32[]{:S(2)}) collective-permute-start(bf16[3,64,512]{2,1,0:T(8,128)(2,1)S(1)} %pad_maximum_fusion.9), channel_id=1, source_target_pairs={{0,16},{16,0},{1,17},{17,1},{2,18},{18,2},{3,19},{19,3},{4,20},{20... | collective-permute-start | bytes 589832 | tf_op jit(solution)/shard_map/ppermute | solution.py:1082
  495.7 9.4 %collective-permute-start.49 = (f32[12,1024]{1,0:T(8,128)S(1)}, f32[12,1024]{1,0:T(8,128)S(1)}, u32[]{:S(2)}, u32[]{:S(2)}) collective-permute-start(f32[12,1024]{1,0:T(8,128)S(1)} %add.324), channel_id=1, source_target_pairs={{0,16},{16,0},{1,17},{17,1},{2,18},{18,2},{3,19},{19,3},{4,20},{20... | collective-permute-start | bytes 147464 | tf_op jit(solution)/shard_map/ppermute | solution.py:1082
  507.4 6.4 %collective-permute-start.50 = (bf16[64,2048]{1,0:T(8,128)(2,1)S(1)}, bf16[64,2048]{1,0:T(8,128)(2,1)S(1)}, u32[]{:S(2)}, u32[]{:S(2)}) collective-permute-start(bf16[64,2048]{1,0:T(8,128)(2,1)S(1)} %dynamic-slice_bitcast_fusion), channel_id=1, source_target_pairs={{0,1},{1,0},{2,3},{3,2},{4,5},{5,4},{6,7},{7,6},{8,9},{9,8},{10,11... | collective-permute-start | bytes 786440 | tf_op jit(solution)/shard_map/ppermute | solution.py:1082
  (32 other events, 336.9 us)
Sparse Core Ops, SparseCore 0:
  29.7 92.1 all-gather.4
  124.8 88.6 all-gather.6
  296.6 117.8 reduce-scatter.1

commit v4 on v3

--- a/solution.py
+++ b/solution.py
@@ -50,8 +50,11 @@
     for kind, order, first, columns in layout:
         target = pl.ds(first, columns)
         if kind == "rel":
-            order, skip = order
-            arrays, refs = refs[:4], refs[4:]
+            order, skip, base = order
+            if base is None:
+                arrays, refs = refs[:4], refs[4:]
+            else:
+                arrays, refs = [*refs[:2], refs[2].at[base], refs[2].at[base + 1]], refs[3:]
             for which, index, rel in rel_slots(order):
                 row, half = slot_place(co, rel)
                 copies.append(
@@ -83,7 +86,9 @@
 
 
 def take_refs(refs, layout):
-    count = sum(4 if part[0] == "rel" else 1 for part in layout)
+    count = 0
+    for kind, order, _, _ in layout:
+        count += 1 if kind == "abs" else 4 if order[2] is None else 3
     return refs[:count], refs[count:]
 
 
@@ -134,6 +139,12 @@
 
 def spread_mean(total, width):
     return jnp.broadcast_to(jnp.sum(total, axis=1, keepdims=True) * (1.0 / width), total.shape)
+
+
+def wait_at_first(copies, half):
+    @pl.when(pl.program_id(0) == 0)
+    def _():
+        wait_half(copies, half)
 
 
 def norm_stats(load, width):
@@ -174,9 +185,12 @@
     return pl.BlockSpec(memory_space=pl.ANY)
 
 
+COST = 0.01
+
+
 def cost(units, traffic):
     return pl.CostEstimate(
-        flops=int(units * 2 * 1024**3), bytes_accessed=int(traffic), transcendentals=0
+        flops=int(units * 2 * 1024**3 * COST), bytes_accessed=int(traffic * COST), transcendentals=0
     )
 
 
@@ -464,11 +478,11 @@
 
 
 def result_kernel(
-    co, scale, hidden, mr, middle_ref, teacher_ref, valid_ref, *refs, layouts,
+    co, scale, hidden, mr, middle_ref, mine_ref, theirs_ref, valid_ref, *refs, layouts,
 ):
     value_w, refs = take_refs(refs, layouts[0])
     recept_w, refs = take_refs(refs, layouts[1])
-    out_ref, dres_ref, dkv_ref, drec_ref, loss_ref, ww, rw, kv_ref, pre_ref, sems, sems_r = refs
+    *outs, dres_ref, dkv_ref, drec_ref, loss_ref, ww, rw, kv_ref, pre_ref, sems, sems_r = refs
     i = pl.program_id(0)
     copies = weight_copies(co, value_w, ww, sems, layouts[0])
     recept = weight_copies(co, recept_w, rw, sems_r, layouts[1])
@@ -480,24 +494,27 @@
         loss_ref[...] = jnp.zeros_like(loss_ref)
         for half in (0, 1):
             wait_half(recept, half)
-        for half in (0, 1):
             wait_half(copies, half)
 
     wide, narrow = ww.shape[2], rw.shape[2]
-    kv_ref[...] = dot(hidden[:, :wide], ww[0], NT) + dot(hidden[:, wide:], ww[1], NT)
     pre_ref[:, :narrow] = dot(mr[...], rw[0], NN)
     pre_ref[:, narrow:] = dot(mr[...], rw[1], NN)
+    kv_ref[...] = dot(hidden[:, :wide], ww[0], NT) + dot(hidden[:, wide:], ww[1], NT)
     factor = scale[0]
 
     def step(n, _):
         rows = chunk_rows(n)
         valid = valid_ref[rows, :]
-        for strip in strips(kv_ref.shape[1]):
+        width = kv_ref.shape[1]
+        for part, at in itertools.product((0, 1), range(0, width // 2, LANES)):
+            first = pl.multiple_of((co[4] ^ part) * (width // 2) + at, LANES)
+            strip = pl.ds(first, LANES)
             kv = kv_ref[rows, strip]
             rec = 1.0 / (1.0 + jnp.exp(-pre_ref[rows, strip]))
             result = middle_ref[rows, strip] + rec * kv
-            out_ref[rows, strip] = result.astype(BF)
-            error = (result - teacher_ref[rows, strip].astype(F32)) * valid
+            outs[part][rows, at : at + LANES] = result.astype(BF)
+            teacher = (mine_ref, theirs_ref)[part][rows, at : at + LANES].astype(F32)
+            error = (result - teacher) * valid
             grad = error * factor
             dres_ref[rows, strip] = grad
             dkv = grad * rec
@@ -509,11 +526,12 @@
     lax.fori_loop(0, kv_ref.shape[0] // ROWS, step, 0)
 
 
-def result_step(co, scale, hidden, mixed, middle, teacher, valid, weight, recept):
+def result_step(co, scale, hidden, mixed, middle, teachers, valid, weight, recept):
     tokens, width = mixed.shape
     rows = tokens // 4
     wide = weight_width(weight)
     tall = pl.BlockSpec((rows, width), lambda i, co, s: (i, 0))
+    thin = pl.BlockSpec((rows, width // 2), lambda i, co, s: (i, 0))
     return pl.pallas_call(
         functools.partial(result_kernel, layouts=[weight[0], recept[0]]),
         grid_spec=pltpu.PrefetchScalarGridSpec(
@@ -523,11 +541,14 @@
                 pl.BlockSpec((rows, 2 * wide), lambda i, co, s: (i, 0)),
                 tall,
                 tall,
-                tall,
+                thin,
+                thin,
                 pl.BlockSpec((rows, LANES), lambda i, co, s: (i, 0)),
             ]
             + [anywhere()] * len(arrays_of(weight, recept)),
-            out_specs=[tall] * 4 + [pl.BlockSpec((8, width), lambda i, co, s: (0, 0))],
+            out_specs=[pl.BlockSpec((rows, width // 2), lambda i, co, s: (co[4] * 4 + i, 0)), thin]
+            + [tall] * 3
+            + [pl.BlockSpec((8, width), lambda i, co, s: (0, 0))],
             scratch_shapes=[
                 pltpu.VMEM((2, width, wide), BF),
                 pltpu.VMEM((2, width, width // 2), BF),
@@ -537,11 +558,12 @@
                 pltpu.SemaphoreType.DMA((sem_count(recept),)),
             ],
         ),
-        out_shape=[jax.ShapeDtypeStruct((tokens, width), t) for t in (BF, F32, BF, BF)]
+        out_shape=[jax.ShapeDtypeStruct((n * tokens, width // 2), BF) for n in (2, 1)]
+        + [jax.ShapeDtypeStruct((tokens, width), t) for t in (F32, BF, BF)]
         + [jax.ShapeDtypeStruct((8, width), F32)],
         compiler_params=params(),
         cost_estimate=cost(7, 38 << 20),
-    )(co, scale, hidden, mixed, middle, teacher, valid, *arrays_of(weight, recept))
+    )(co, scale, hidden, mixed, middle, *teachers, valid, *arrays_of(weight, recept))
 
 
 def grad_copies(co, whole, targets, n, sems, order, piece, merged=False):
@@ -626,9 +648,10 @@
     )(co, *models, *chans)
 
 
-def channel_back_kernel(co, dkv, mixed, hidden, active, *refs, layout, order):
-    arrays, (dkey, *refs) = take_refs(refs, layout)
-    targets, (whole, grads, sems_in, sems) = refs[:-4], refs[-4:]
+def channel_back_kernel(co, dkv, mixed, hidden, active, *refs, layout, part, order):
+    recept, refs = refs[: 2 * (1 - part)], refs[2 * (1 - part) :]
+    arrays, refs = take_refs(refs, layout)
+    dkey, *targets, whole, grads, narrow, sems_in, sems = refs
     j = pl.program_id(0)
     per_half = grads.shape[4] // WIDE
     columns = pl.ds(pl.multiple_of(lax.rem(j, per_half) * WIDE, WIDE), WIDE)
@@ -656,48 +679,53 @@
     dkey[...] = back
     keep(1, dot(mixed[...], back, TN))
 
-    if order is None:
-        wide = grads.shape[4]
-
-        def copies(turn, piece, size):
-            half = co[4] ^ turn
-            return [
-                pltpu.make_async_copy(
-                    grads.at[n, half, :, :, pl.ds(piece, size)],
-                    targets[0].at[:, half, :, pl.ds(n * wide + piece, size)],
-                    sems.at[n],
-                )
-                for n in (0, 1)
-            ]
-
-        for copy in copies(turn, pl.multiple_of(lax.rem(j, per_half) * WIDE, WIDE), WIDE):
-            copy.start()
-
-        @pl.when(j == pl.num_programs(0) - 1)
-        def _():
-            for which in (0, 1):
-                for copy in copies(which, 0, wide):
-                    copy.wait()
-
-        return
+    wide = grads.shape[4]
+
+    def narrow_copy(turn):
+        return pltpu.make_async_copy(
+            narrow.at[turn],
+            targets[0].at[:, co[4] ^ turn, :, pl.ds(2 * wide, narrow.shape[3])],
+            sems.at[2 + turn],
+        )
+
+    def block_copies(turn, piece, size):
+        half = co[4] ^ turn
+        return [
+            pltpu.make_async_copy(
+                grads.at[n, half, :, :, pl.ds(piece, size)],
+                targets[0].at[:, half, :, pl.ds(n * wide + piece, size)],
+                sems.at[n],
+            )
+            for n in (0, 1)
+        ]
 
     def slot_copies(which, piece):
         found = []
         for m, (array, index, rel) in enumerate(rel_slots(order)):
-            if rel["x"] != which:
-                continue
-            row, at = slot_place(co, rel)
-            for n in (0, 1):
-                found.append(
-                    pltpu.make_async_copy(
-                        grads.at[n, at, lax.div(row, SLOT), :, piece],
-                        targets[array].at[index + (n, slice(None), piece)],
-                        sems.at[n * 32 + m],
+            if rel["x"] == which:
+                row, at = slot_place(co, rel)
+                for n in (0, 1):
+                    found.append(
+                        pltpu.make_async_copy(
+                            grads.at[n, at, lax.div(row, SLOT), :, piece],
+                            targets[array].at[index + (n, slice(None), piece)],
+                            sems.at[32 * n + m],
+                        )
                     )
-                )
         return found
 
-    for which in (0, 1):
+    if part == 0:
+        for copy in block_copies(turn, pl.multiple_of(lax.rem(j, per_half) * WIDE, WIDE), WIDE):
+            copy.start()
+
+        @pl.when(lax.rem(j, per_half) == 0)
+        def _():
+            size = narrow.shape[3]
+            found = dot(recept[0][...], recept[1][:, pl.ds(pl.multiple_of(half * size, size), size)], TN)
+            narrow[turn] = found.astype(BF).reshape(16, SLOT, size)
+            narrow_copy(turn).start()
+
+    for which in range(2 * part):
 
         @pl.when(turn == which)
         def _(which=which):
@@ -707,44 +735,51 @@
     @pl.when(j == pl.num_programs(0) - 1)
     def _():
         for which in (0, 1):
-            for copy in slot_copies(which, slice(None)):
+            for copy in slot_copies(which, slice(None)) if part else block_copies(which, 0, wide):
                 copy.wait()
-
-
-def channel_back(co, dkv, mixed, hidden, active, weight, first, half, order):
+            if part == 0:
+                narrow_copy(which).wait()
+
+
+def channel_back(co, dkv, mixed, hidden, active, recept, weight, half, part, order):
     tokens, width = dkv.shape
     per_half = half // WIDE
-    skip, stride = first // WIDE, hidden.shape[1] // 2 // WIDE
+    skip, stride = part * per_half, hidden.shape[1] // 2 // WIDE
 
     def tile(j, co):
         return 0, (co[4] ^ lax.div(j, per_half)) * stride + skip + lax.rem(j, per_half)
 
     fixed = pl.BlockSpec((tokens, width), lambda j, co: (0, 0))
     block = pl.BlockSpec((tokens, WIDE), tile)
-    if order is None:
-        shapes = [jax.ShapeDtypeStruct((16, 2, SLOT, 2 * half), BF)]
-    else:
-        shapes = [jax.ShapeDtypeStruct((2, 2, 2, 2, SLOT, half), BF)] * 4
-    dkey, *slots = pl.pallas_call(
-        functools.partial(channel_back_kernel, layout=weight[0], order=order),
+    return pl.pallas_call(
+        functools.partial(channel_back_kernel, layout=weight[0], part=part, order=order),
         grid_spec=pltpu.PrefetchScalarGridSpec(
             num_scalar_prefetch=1,
             grid=(2 * per_half,),
-            in_specs=[fixed, fixed, block, block] + [anywhere()] * len(weight[1]),
+            in_specs=[fixed, fixed, block, block]
+            + [fixed] * len(recept)
+            + [anywhere()] * len(weight[1]),
             out_specs=[pl.BlockSpec((tokens, WIDE), column_tile(per_half))]
-            + [anywhere()] * len(shapes),
+            + [anywhere()] * (1 + 3 * part),
             scratch_shapes=[
                 pltpu.VMEM((2, width, half), BF),
                 pltpu.VMEM((2, 2, 16, SLOT, half), BF),
+                pltpu.VMEM((2, 16, SLOT, width // 2), BF),
                 pltpu.SemaphoreType.DMA((sem_count(weight),)),
                 pltpu.SemaphoreType.DMA((64,)),
             ],
         ),
-        out_shape=[jax.ShapeDtypeStruct((tokens, 2 * half), BF)] + shapes,
+        out_shape=[
+            jax.ShapeDtypeStruct((tokens, 2 * half), BF),
+            *(
+                [jax.ShapeDtypeStruct((2, 2, 2, 2, SLOT, half), BF)] * 4
+                if part
+                else [jax.ShapeDtypeStruct((16, 2, SLOT, 2 * half + width // 2), BF)]
+            ),
+        ],
         compiler_params=params(),
         cost_estimate=cost(half / 512 * 3.3, half / 512 * (14 << 20)),
-    )(co, dkv, mixed, hidden, active, *weight[1])
-    return dkey, slots
+    )(co, dkv, mixed, hidden, active, *recept, *weight[1])
 
 
 def middle_back_kernel(
@@ -765,16 +800,15 @@
         next_ref[...] = jnp.zeros_like(next_ref)
         for half in (0, 1):
             wait_half(recept, half)
-        for half in (0, 1):
             wait_half(copies, half)
 
     wide, narrow = dkey_a.shape[1] // 2, rw.shape[2]
+    gr_ref[...] = dot(drec[:, :narrow], rw[0], NT) + dot(drec[:, narrow:], rw[1], NT)
     gk_ref[...] = sum(
         dot(part[:, half * wide : (half + 1) * wide], ww[half, :, n * wide : (n + 1) * wide], NT)
         for n, part in enumerate((dkey_a, dkey_b))
         for half in (0, 1)
     )
-    gr_ref[...] = dot(drec[:, :narrow], rw[0], NT) + dot(drec[:, narrow:], rw[1], NT)
     steps = middle_ref.shape[0] // ROWS
     width = middle_ref.shape[1]
 
@@ -984,12 +1018,13 @@
             start_all(copies)
         sums_ref[...] = jnp.zeros_like(sums_ref)
         next_ref[...] = after_ref[...]
-        for copies in groups:
-            wait_half(copies, 0)
-            wait_half(copies, 1)
 
     half = kw.shape[2]
-    for grad, whole, out in ((dkey, kw, gk_ref), (dval, vw, gv_ref), (drec, rw, gr_ref)):
+    for copies, grad, whole, out in zip(
+        groups, (dkey, dval, drec), (kw, vw, rw), (gk_ref, gv_ref, gr_ref)
+    ):
+        wait_at_first(copies, 0)
+        wait_at_first(copies, 1)
         out[...] = dot(grad[:, :half], whole[0], NT) + dot(grad[:, half:], whole[1], NT)
     steps = x_ref.shape[0] // ROWS
     width = x_ref.shape[1]
@@ -1083,26 +1118,29 @@
 
 
 class Gather:
-    def __init__(self, shard, order):
+    def __init__(self, shard, order, first=None):
         self.order, self.state, self.done = order, (shard,), 0
+        if first is not None:
+            self.state, self.done = (shard, first), 1
 
     def step(self):
         n = self.done
         if n and n < 4:
             self.state = (jnp.stack(self.state),)
-        if n < 3:
+        if n < 4:
             self.state += (swap(self.state[0], self.order[n]),)
-        elif n == 3:
-            near = self.state[0]
-            self.state = (near, swap(near, self.order[3]), swap(near, "c"))
         else:
-            near, far, near_other = self.state
-            self.state = (near, far, near_other, swap(far, "c"))
+            near, far = self.state
+            self.state = (near, far, swap(near, "c"), swap(far, "c"))
         self.done += 1
 
     def part(self, first=0, skip=0, columns=None):
         assert self.done == 5
-        return ("rel", (self.order, skip), first, columns or self.state[0].shape[-1]), self.state
+        return ("rel", (self.order, skip, None), first, columns or self.state[0].shape[-1]), self.state
+
+    def part_with(self, others, base):
+        assert self.done == 4
+        return ("rel", (self.order, 0, base), 0, self.state[0].shape[-1]), (*self.state, others)
 
 
 def weight_of(*parts):
@@ -1338,43 +1376,41 @@
     own_vectors = jnp.concatenate([own_vectors, counts, jnp.zeros((4, piece), F32)])
     output_t, value_t = time_output.T, channel_value.T
 
-    def teacher_rows_of(mine, theirs):
-        return jnp.where(
-            side == 0,
-            jnp.concatenate([mine, theirs], axis=1),
-            jnp.concatenate([theirs, mine], axis=1),
-        )
-
     if sizes["x"] == 2:
         mine = lax.dynamic_slice_in_dim(teacher, side * tokens, tokens)
         theirs = lax.dynamic_slice_in_dim(teacher, (1 - side) * tokens, tokens)
+    else:
+        mine, theirs = jnp.split(teacher, 2, axis=1)
 
     key_order, val_order, rec_order = three_orders = ("wxuy", "wuyx", "wyxu")
     half = width // 2
     if fast:
         wide = channel_key.shape[1]
         split = wide // 2
-        keys = [Gather(channel_key[:, :split], "wuyx"), Gather(channel_key[:, split:], "wyux")]
-        first = pair_up(jnp.concatenate([time_key, time_value, time_recept, output_t], axis=1))
-        late = jnp.concatenate([value_t, channel_recept], axis=1)
-        first, late, own_vectors, masks_down, masks_up, mine, theirs = seal_all(
-            keys, first, late, own_vectors, masks_down, masks_up, mine, theirs
+        chains = keys_a, keys_b, late_b = [
+            Gather(channel_key[:, :split], "wuyx"),
+            Gather(channel_key[:, split:], "wxuy"),
+            Gather(value_t[:, split:], "wyxu"),
+        ]
+        first = jnp.concatenate([time_key, time_value, time_recept, output_t], axis=1)
+        late = jnp.concatenate([value_t[:, :split], channel_recept], axis=1)
+        first = lax.all_gather(first, EVERY)
+        theirs = swap(theirs, "x")
+        step_all(*chains)
+        (vectors,) = gather_vectors(own_vectors, 0, 4)
+        late, vectors, masks_down, masks_up, mine, theirs, carry, valid_rows, lead = seal_all(
+            chains, late, vectors, masks_down, masks_up, mine, theirs, carry, valid_rows, lead
         )
-        first = lax.all_gather(first, ("w", "u", "y", "c"))
-        step_all(*keys)
-        (vectors,) = gather_vectors(own_vectors, 0, 1)
-        late = pair_up(late)
-        late, vectors = seal_all(keys, late, vectors)
-        step_all(*keys)
-        (vectors,) = gather_vectors(vectors, 1, 3)
-        (vectors,) = seal_all(keys, vectors)
-        step_all(*keys)
-        (vectors,) = gather_vectors(vectors, 3, 5)
-        (vectors,) = seal_all(keys, vectors)
-        step_all(*keys)
+        step_all(*chains)
+        (vectors,) = gather_vectors(vectors, 4, 5)
+        (vectors,) = seal_all(chains, vectors)
+        step_all(*chains)
         mixed = first_mix(inputs, carry, vectors)
-        first, late, mixed, vectors = seal(first, late, mixed, vectors)
-        late = lax.all_gather(late, ("w", "u", "y", "c"))
+        (mixed,) = seal_all(chains, mixed)
+        step_all(*chains)
+        first, late, mixed = seal(first, late, mixed)
+        late = lax.all_gather(late, EVERY).reshape(16, 2, SLOT, -1)
+        first = first.reshape(16, 2, SLOT, -1)
         key_w, value_w, recept_w, output_w = (all_of(first, n * half, half) for n in range(4))
     else:
         early = gather_plain(channel_key)
@@ -1392,33 +1428,42 @@
 
     *saved, gated = time_forward(co, mixed, (key_w, value_w, recept_w), vectors, masks_down)
     if fast:
-        (gated, theirs) = seal_all(keys, gated, theirs)
-        step_all(*keys)
-    if sizes["x"] == 2:
+        (gated,) = seal_all((keys_a, keys_b), gated)
+        step_all(keys_a, keys_b)
+    if sizes["x"] == 2 and not fast:
         theirs = swap(theirs, "x")
     middle, mixed_k2, mixed_r2 = time_output_step(co, gated, inputs, carry, vectors, output_w)
     if fast:
-        middle, mixed_k2, mixed_r2 = seal_all(keys, middle, mixed_k2, mixed_r2)
-        ckey_w = weight_of(keys[0].part(), keys[1].part(split))
+        middle, mixed_k2, mixed_r2 = seal_all(chains, middle, mixed_k2, mixed_r2)
+        ckey_w = weight_of(keys_a.part(), keys_b.part(split))
+        late_b.step()
     hidden, active = hidden_step(co, mixed_k2, ckey_w)
     if fast:
-        hidden, theirs, late = seal(hidden, theirs, late)
-        cvalue_w = [all_of(late, skip, split) for skip in (0, split)]
-        crecept_w = all_of(late, wide, half)
-    teacher_rows = teacher_rows_of(mine, theirs) if sizes["x"] == 2 else teacher
+        hidden, late = seal_all((late_b,), hidden, late)
+        cvalue_w = [all_of(late, 0, split), weight_of(late_b.part())]
+        crecept_w = all_of(late, split, half)
     count = jnp.sum(vectors[11])
     scale = (float(tokens * devices) / count).reshape(1)
-    result, dres, dkv, drec2, loss_rows = result_step(
-        co, scale, hidden, mixed_r2, middle, teacher_rows, valid_rows, both_parts(cvalue_w, split), crecept_w
+    kept, arrived, dres, dkv, drec2, loss_rows = result_step(
+        co.at[4].set(side),
+        scale,
+        hidden,
+        mixed_r2,
+        middle,
+        (mine, theirs),
+        valid_rows,
+        both_parts(cvalue_w, split),
+        crecept_w,
     )
 
-    kept = lax.dynamic_slice_in_dim(result, side * half, half, axis=1)
-    arrived = lax.dynamic_slice_in_dim(result, (1 - side) * half, half, axis=1)
     if sizes["x"] == 2:
         arrived = swap(arrived, "x")
 
+    def outputs_of(kept, arrived):
+        return lax.dynamic_update_slice_in_dim(kept, arrived, (1 - side) * tokens, 0)
+
     back = functools.partial(channel_back, co)
-    order_b, order_c = "wyux", "wuxy"
+    order_b, order_c = "wuyx", "wuyx"
     edge = jnp.zeros((8, width), F32)
 
     def input_back_part(dmix, part, after, found):
@@ -1427,88 +1472,91 @@
         )
 
     if fast:
-        dkey_b, found = back(dkv, mixed_k2, hidden, active, cvalue_w[1], split, split, order_b)
+        dkey_1, *found = back(dkv, mixed_k2, hidden, active, (), cvalue_w[1], split, 1, order_b)
         group_b = Merged(found, order_b)
         (dkv,) = seal_all((group_b,), dkv)
         group_b.step()
-        dkey_a, (blocks,) = back(dkv, mixed_k2, hidden, active, cvalue_w[0], 0, split, None)
+        dkey_0, blocks = back(
+            dkv, mixed_k2, hidden, active, (mixed_r2, drec2), cvalue_w[0], split, 0, order_b
+        )
+        dkey_0, arrived, blocks = seal_all((group_b,), dkey_0, arrived, blocks)
         blocks = scatter_rows(blocks)
-        (dkey_a, arrived) = seal_all((group_b,), dkey_a, arrived)
         group_b.step()
+        outputs = outputs_of(kept, arrived)
         dmid, dtime, sums2 = middle_back(
-            co, (dkey_a, dkey_b), drec2, middle, dres, lead, vectors, ckey_w, crecept_w
+            co, (dkey_0, dkey_1), drec2, middle, dres, lead, vectors, ckey_w, crecept_w
         )
-        found = weight_grads(
-            co, ((mixed_r2, drec2, order_c), (dtime, gated, order_c)), merged=True
-        )
+        found = weight_grads(co, ((dtime, gated, order_c),), merged=True)
         group_c = Merged(found, order_c)
-        (dtime,) = seal_all((group_b, group_c), dtime)
+        dtime, outputs = seal_all((group_b, group_c), dtime, outputs)
         step_all(group_b, group_c)
         *dmix, sums_t = time_back(co, dtime, saved, vectors, masks_up, output_w)
-        (dmix, dmid) = seal_all((group_b, group_c), dmix, dmid)
-        step_all(group_b, group_c)
+        (dmix, dmid) = seal_all((group_c,), dmix, dmid)
+        group_c.step()
         found = weight_grads(co, [(m, d, order) for m, d, order in zip(mixed, dmix, three_orders)])
         group_t = Reduce(found, three_orders)
-        (dmix,) = seal_all((group_b, group_t), dmix)
-        step_all(group_b, group_t)
-        found, sums_l, edge = input_back_part(dmix, 0, edge, jnp.zeros_like(dmid))
+        (dmix,) = seal_all((group_b, group_c, group_t), dmix)
+        step_all(group_b, group_c, group_t)
+        found, sums_l, edge = input_back_part(dmix, 0, edge, dres)
         (dmix, edge, found) = seal_all((group_b, group_c, group_t), dmix, edge, found)
-        step_all(group_c, group_t)
+        step_all(group_b, group_c, group_t)
         input_grad, sums_u, _ = input_back_part(dmix, 1, edge, found)
     else:
-        dkey_b, found = back(dkv, mixed_k2, hidden, active, cvalue_w[1], split, split, order_b)
-        cv_b, ck_b = reduce_merged(found, order_b)
-        dkey_a, (blocks,) = back(dkv, mixed_k2, hidden, active, cvalue_w[0], 0, split, None)
-        cv_a, ck_a = (
+        dkey_1, *found = back(dkv, mixed_k2, hidden, active, (), cvalue_w[1], split, 1, order_b)
+        dkey_0, blocks = back(
+            dkv, mixed_k2, hidden, active, (mixed_r2, drec2), cvalue_w[0], split, 0, order_b
+        )
+        value_1, ckey_1 = reduce_merged(found, order_b)
+        value_0, ckey_0 = (
             reduce_blocks(blocks[..., n * split : (n + 1) * split]) for n in (0, 1)
         )
+        crecept_g = reduce_blocks(blocks[..., 2 * split :])
+        halves = 2 // sizes["x"]
+        cvalue_g, ckey_g = (
+            jnp.concatenate(
+                [v.reshape(-1, halves, split) for v in pair], axis=2
+            ).reshape(pair[0].shape[0], -1)
+            for pair in ((value_0, value_1), (ckey_0, ckey_1))
+        )
         dmid, dtime, sums2 = middle_back(
-            co, (dkey_a, dkey_b), drec2, middle, dres, lead, vectors, ckey_w, crecept_w
+            co, (dkey_0, dkey_1), drec2, middle, dres, lead, vectors, ckey_w, crecept_w
         )
-        found = weight_grads(
-            co, ((mixed_r2, drec2, order_c), (dtime, gated, order_c)), merged=True
-        )
-        crecept_g, output_g = reduce_merged(found, order_c)
+        found = weight_grads(co, ((dtime, gated, order_c),), merged=True)
+        (output_g,) = reduce_merged(found, order_c)
         *dmix, sums_t = time_back(co, dtime, saved, vectors, masks_up, output_w)
         found = weight_grads(co, [(m, d, order) for m, d, order in zip(mixed, dmix, three_orders)])
         key_g, val_g, rec_g = reduce_plain(found, three_orders)
-        found, sums_l, edge = input_back_part(dmix, 0, edge, jnp.zeros_like(dmid))
+        found, sums_l, edge = input_back_part(dmix, 0, edge, dres)
         input_grad, sums_u, _ = input_back_part(dmix, 1, edge, found)
 
     rows = jnp.concatenate([sums_l[:2] + sums_u[:2], sums_t, sums_l[2:] + sums_u[2:], sums2, loss_rows[None]])
     totals = jnp.sum(rows, axis=1)
     if fast:
-        (totals,) = seal_all((group_c, group_t), totals)
-        for axes in ("xc", "yu", "w"):
+        (totals,) = seal_all((group_b, group_c, group_t), totals)
+        for axes in ("wc", "xy", "u"):
             step_all(*[group for group in (group_c, group_t) if group.done < 5])
             for axis in axes:
                 totals = totals + swap(totals, axis)
-            (totals,) = seal_all((group_c, group_t), totals)
-        cv_b, ck_b = group_b.finish()
-        cv_a, ck_a = jnp.split(pair_sum(blocks), 2, axis=1)
-        crecept_g, output_g = group_c.finish()
+            totals, blocks = seal_all((group_c, group_t), totals, blocks)
+            if axes == "wc":
+                blocks = pair_sum(blocks)
+        cvalue_g, ckey_g = (
+            jnp.concatenate([blocks[:, n * split : (n + 1) * split], found], axis=1)
+            for n, found in enumerate(group_b.finish())
+        )
+        (output_g,) = group_c.finish()
+        crecept_g = blocks[:, 2 * split :]
         key_g, val_g, rec_g = group_t.finish()
     else:
         totals = lax.psum(totals, EVERY)
     loss = jnp.sum(totals[11]) / (2.0 * count * width)
     vector_g = lax.dynamic_slice_in_dim(totals, flat * piece, piece, axis=1)
-    if sizes["x"] == 2:
-        cvalue_g = jnp.concatenate([cv_a, cv_b], axis=1)
-        ckey_g = jnp.concatenate([ck_a, ck_b], axis=1)
-        outputs = jnp.where(
-            side == 0,
-            jnp.concatenate([kept, arrived], axis=0),
-            jnp.concatenate([arrived, kept], axis=0),
+    if not fast:
+        outputs = (
+            outputs_of(kept, arrived)
+            if sizes["x"] == 2
+            else jnp.concatenate([kept[:tokens], arrived], axis=1)
         )
-    else:
-        cvalue_g, ckey_g = (
-            jnp.concatenate([a.reshape(-1, 2, split), b.reshape(-1, 2, split)], axis=2).reshape(
-                a.shape[0], -1
-            )
-            for a, b in ((cv_a, cv_b), (ck_a, ck_b))
-        )
-        outputs = result
-
     return (
         outputs,
         loss,

time: 530 us -> 478 us (0.902)
  waiting for transfers between devices: 129 us -> 74.2 us
    ppermute x51 -> x55, waiting for transfers between devices: 122 us -> 64.7 us  [swap(): return lax.ppermute(values, axis, SWAP)]
    select_n x4 -> x0, other arithmetic: 8.44 us -> none  [the longest x1 3.46 us: on_device(): jnp.where(side == 0, jnp.concatenate([kept, arrived], axis=0), jnp.concat...]
    ppermute x51 -> x55, starting transfers between devices: 54.5 us -> 52.1 us  [swap(): return lax.ppermute(values, axis, SWAP)]
  transfers between devices with their start and end apart: 54 -> 58, of which waited for: 22 -> 20; matrix products, arithmetic and copies ran while one was open for 10% -> 13% of each run, Pallas kernels for 39% -> 43%
where the time goes in v4:
time: 478 us; the launch traced here: 472 us
  Pallas kernels  251 us (53%)
  waiting for transfers between devices  74.2 us (16%)
  starting transfers between devices  52.4 us (11%)
  other arithmetic  43.8 us (9%)
  local copies, waits for them, and re-layouts  32 us (7%)
  between operations  18.3 us (4%)
    ppermute x55, waiting for transfers between devices, swap(): return lax.ppermute(values, axis, SWAP)  64.7 us
    ppermute x55, starting transfers between devices, swap(): return lax.ppermute(values, axis, SWAP)  52.1 us
    pallas_call x2, Pallas kernels, channel_back(): pl.pallas_call(functools.partial(channel_back_kernel, layout=weight[0], p...  49.5 us
    pallas_call x2, Pallas kernels, input_back(): pl.pallas_call(functools.partial(input_back_kernel, layouts=[w[0] for w i...  32.5 us
    pallas_call x1, Pallas kernels, middle_back(): pl.pallas_call(functools.partial(middle_back_kernel, layouts=[weight[0],...  32.5 us
    pallas_call x1, Pallas kernels, time_forward(): pl.pallas_call(functools.partial(time_forward_kernel, layouts=[w[0] for w...  28.6 us
    pallas_call x1, Pallas kernels, result_step(): pl.pallas_call(functools.partial(result_kernel, layouts=[weight[0], recep...  24.7 us
    pallas_call x1, Pallas kernels, time_back(): pl.pallas_call(functools.partial(time_back_kernel, layout=weight[0]), gri...  23.4 us
  transfers between devices with their start and end apart: 58, of which 20 were waited for; matrix products, arithmetic and copies ran while one was open for 13% of the time, Pallas kernels for 43%

profile of v4, /device:TPU:0, one launch (start us, length us, event | category | flops | bytes accessed | tf_op | source)
XLA Modules:
  0.0 472.0 jit_solution(15684951756009521968)
XLA Ops:
  10.0 4.1 collective-permute-start
  15.1 2.9 collective-permute-start.2
  21.4 2.7 concatenate.133
  25.6 2.7 constant_dynamic-slice_fusion.1
  42.6 2.0 collective-permute-done.5
  46.3 2.8 collective-permute-done.6
  49.1 10.3 %collective-permute-done.7.theirs_ref = bf16[1024,512]{1,0:T(8,128)(2,1)S(1)} collective-permute-done((bf16[1024,512]{1,0:T(8,128)(2,1)S(1)}, bf16[1024,512]{1,0:T(8,128)(2,1)S(1)}, u32[]{:S(2)}, u32[]{:S(2)}) %collective-permute-start.7) | collective-permute-done | bytes 1048608 | tf_op jit(solution)/shard_map/ppermute | solution.py:1117
  59.5 1.9 broadcast_in_dim.137.masks
  61.4 2.2 broadcast_in_dim.145.masks
  70.5 6.5 %collective-permute-done.11 = f32[16,512]{1,0:T(8,128)S(1)} collective-permute-done((f32[16,512]{1,0:T(8,128)S(1)}, f32[16,512]{1,0:T(8,128)S(1)}, u32[]{:S(2)}, u32[]{:S(2)}) %collective-permute-start.11) | collective-permute-done | bytes 32800 | tf_op jit(solution)/shard_map/ppermute | solution.py:1117
  79.2 4.0 collective-permute-done.10
  83.3 1.8 collective-permute-start.12
  85.3 1.8 collective-permute-start.14
  87.1 8.3 %shard_map.364 = (bf16[1024,1024]{1,0:T(8,128)(2,1)}, bf16[1024,1024]{1,0:T(8,128)(2,1)}, bf16[1024,1024]{1,0:T(8,128)(2,1)}) custom-call(bf16[1024,1024]{1,0:T(8,128)(2,1)} %x_ref.7, f32[1024,128]{1,0:T(8,128)} %broadcast_in_dim.146.carry_ref, f32[16,1024]{1,0:T(8,128)} %maximum_select_fusion.1.vec_ref.vec), custom_call_target="tpu_custom_call" | custom-call | bytes 83886 | tf_op jit(solution)/shard_map/pallas_call | solution.py:228
  95.4 4.3 collective-permute-done.12
  101.0 9.0 %all-gather.5.cloned.1.call-done = bf16[2048,2048]{1,0:T(8,128)(2,1)} async-done(((bf16[64,2048]{1,0:T(8,128)(2,1)}), bf16[2048,2048]{1,0:T(8,128)(2,1)}) %all-gather.5.cloned.1.call-update) | async-done | bytes 8388624 | tf_op jit(solution)/shard_map/all_gather | solution.py:1397
  110.4 1.9 collective-permute-start.15
  116.1 1.7 collective-permute-start.21
  117.8 28.6 %shard_map.365 = (f32[1024,1024]{1,0:T(8,128)}, f32[1024,1024]{1,0:T(8,128)}, f32[1024,1024]{1,0:T(8,128)}, f32[1024,1024]{1,0:T(8,128)}, f32[1024,1024]{1,0:T(8,128)}, /*index=5*/bf16[1024,1024]{1,0:T(8,128)(2,1)}) custom-call(s32[5]{0:T(128)} %stack.159.co, bf16[1024,1024]{1,0:T(8,128)(2,1)} %get-tuple-element.258.mk.refs_0_, ...), custom_call_target="tpu_custom_call" | custom-call | flops 171798688 | bytes 356515 | tf_op jit(solution)/shard_map/pallas_call | solution.py:336
  147.5 13.5 %shard_map.366 = (f32[1024,1024]{1,0:T(8,128)}, bf16[1024,1024]{1,0:T(8,128)(2,1)}, bf16[1024,1024]{1,0:T(8,128)(2,1)}) custom-call(s32[5]{0:T(128)} %stack.159.co, bf16[1024,1024]{1,0:T(8,128)(2,1)} %get-tuple-element.270.gated.refs_1_, bf16[1024,1024]{1,0:T(8,128)(2,1)} %x_ref.7, f32[1024,128]{1,0:T(8,128)} %broadcast_in_dim.146.carry_ref, ...), custom_call_target="tpu_custom_call" | custom-call | flops 64424508 | bytes 146800 | tf_op jit(solution)/shard_map/pallas_call | solution.py:403
  164.5 18.6 %shard_map.367 = (bf16[1024,4096]{1,0:T(8,128)(2,1)}, bf16[1024,4096]{1,0:T(8,128)(2,1)}) custom-call(s32[5]{0:T(128)} %stack.159.co, bf16[1024,1024]{1,0:T(8,128)(2,1)} %get-tuple-element.276.mk.mixed, bf16[2,2,2,64,1024]{4,3,2,1,0:T(8,128)(2,1)} %copy-done.1, bf16[2,2,2,64,1024]{4,3,2,1,0:T(8,128)(2,1)} %collective-permute-done.15.refs_1_, ...), custom_call_target="tpu_custom_call" | custom-call | flops 96636768 | bytes 272629 | tf_op jit(solution)/shard_map/pallas_call | solution.py:461
  184.5 24.7 %shard_map.368 = (bf16[2048,512]{1,0:T(8,128)(2,1)}, bf16[1024,512]{1,0:T(8,128)(2,1)}, f32[1024,1024]{1,0:T(8,128)}, bf16[1024,1024]{1,0:T(8,128)(2,1)}, bf16[1024,1024]{1,0:T(8,128)(2,1)}, /*index=5*/f32[8,1024]{1,0:T(8,128)}) custom-call(s32[5]{0:T(128)} %copy-done.40, f32[1]{0:T(128)} %bitcast.38.scale, bf16[1024,4096]{1,0:T(8,128)(2,1)} %get-tuple-element.287.hidden, ...), custom_call_target="tpu_custom_call" | custom-call | flops 150323856 | bytes 398458 | tf_op jit(solution)/shard_map/pallas_call | solution.py:535
  209.2 23.3 %shard_map.369 = (bf16[1024,2048]{1,0:T(8,128)(2,1)}, bf16[2,2,2,2,64,1024]{5,4,3,2,1,0:T(8,128)(2,1)}, bf16[2,2,2,2,64,1024]{5,4,3,2,1,0:T(8,128)(2,1)}, bf16[2...) custom-call(s32[5]{0:T(128)} %stack.159.co, bf16[1024,1024]{1,0:T(8,128)(2,1)} %get-tuple-element.308.dkv, ...), custom_call_target="tpu_custom_call" | custom-call | flops 141733920 | bytes 293601 | tf_op jit(solution)/shard_map/pallas_call | solution.py:754
  234.2 26.2 %shard_map.370 = (bf16[1024,2048]{1,0:T(8,128)(2,1)}, bf16[16,2,64,2560]{3,2,1,0:T(8,128)(2,1)}) custom-call(s32[5]{0:T(128)} %stack.159.co, bf16[1024,1024]{1,0:T(8,128)(2,1)} %get-tuple-element.308.dkv, bf16[1024,1024]{1,0:T(8,128)(2,1)} %get-tuple-element.276.mk.mixed, bf16[1024,4096]{1,0:T(8,128)(2,1)} %get-tuple-element.287.hidden, ...), custom_call_target="tpu_custom_call" | custom-call | flops 141733920 | bytes 293601 | tf_op jit(solution)/shard_map/pallas_call | solution.py:754
  262.0 2.6 add.330
  265.4 32.5 %shard_map.371 = (f32[1024,1024]{1,0:T(8,128)}, bf16[1024,1024]{1,0:T(8,128)(2,1)}, f32[4,8,1024]{2,1,0:T(8,128)}) custom-call(s32[5]{0:T(128)} %stack.159.co, bf16[1024,2048]{1,0:T(8,128)(2,1)} %get-tuple-element.317.dkey_a, bf16[1024,2048]{1,0:T(8,128)(2,1)} %get-tuple-element.318.dkey_b, bf16[1024,1024]{1,0:T(8,128)(2,1)} %get-tuple-element.309.refs_1_.drec, ...), custom_call_target="tpu_custom_call" | custom-call | flops 171798688 | bytes 377487 | tf_op jit(solution)/shard_map/pallas_call | solution.py:858
  297.9 6.8 %shard_map.372 = (bf16[2,2,2,1,64,512]{5,4,3,2,1,0:T(8,128)(2,1)}, bf16[2,2,2,1,64,512]{5,4,3,2,1,0:T(8,128)(2,1)}, bf16[2,2,2,1,64,512]{5,4,3,2,1,0:T(8,128)(2,1)}, bf16[2,2,2,1,64,512]{5,4,3,2,1,0:T(8,128)(2,1)}) custom-call(s32[5]{0:T(128)} %stack.159.co, bf16[1024,1024]{1,0:T(8,128)(2,1)} %get-tuple-element.336.refs_0_.dtime, ...), custom_call_target="tpu_custom_call" | custom-call | flops 25769804 | bytes 62914 | tf_op jit(solution)/shard_map/pallas_call | solution.py:630
  305.8 6.2 %collective-permute-done.27 = bf16[2,2,2,2,64,1024]{5,4,3,2,1,0:T(8,128)(2,1)S(1)} collective-permute-done((bf16[2,2,2,2,64,1024]{5,4,3,2,1,0:T(8,128)(2,1)S(1)}, bf16[2,2,2,2,64,1024]{5,4,3,2,1,0:T(8,128)(2,1)S(1)}, u32[]{:S(2)}, u32[]{:S(2)}) %collective-permute-start.27) | collective-permute-done | bytes 2097184 | tf_op jit(solution)/shard_map/ppermute | solution.py:1117
  312.5 3.1 fusion.1
  315.9 23.4 %shard_map.373 = (bf16[1024,1024]{1,0:T(8,128)(2,1)}, bf16[1024,1024]{1,0:T(8,128)(2,1)}, bf16[1024,1024]{1,0:T(8,128)(2,1)}, f32[2,8,1024]{2,1,0:T(8,128)}) custom-call(s32[5]{0:T(128)} %stack.159.co, bf16[1024,1024]{1,0:T(8,128)(2,1)} %get-tuple-element.336.refs_0_.dtime, f32[1024,1024]{1,0:T(8,128)} %get-tuple-element.337.key_ref, ...), custom_call_target="tpu_custom_call" | custom-call | flops 193273536 | bytes 356515 | tf_op jit(solution)/shard_map/pallas_call | solution.py:975
  341.0 12.8 %shard_map.374 = (bf16[3,2,2,2,64,512]{5,4,3,2,1,0:T(8,128)(2,1)}, bf16[3,2,2,2,64,512]{5,4,3,2,1,0:T(8,128)(2,1)}, bf16[3,2,2,2,64,512]{5,4,3,2,1,0:T(8,128)(2,1)}, bf16[3,2,2,2,64,512]{5,4,3,2,1,0:T(8,128)(2,1)}) custom-call(s32[5]{0:T(128)} %stack.159.co, bf16[1024,1024]{1,0:T(8,128)(2,1)} %get-tuple-element.258.mk.refs_0_, ...), custom_call_target="tpu_custom_call" | custom-call | flops 77309408 | bytes 188743 | tf_op jit(solution)/shard_map/pallas_call | solution.py:630
  360.6 16.4 %shard_map.375 = (f32[1024,1024]{1,0:T(8,128)}, f32[5,8,1024]{2,1,0:T(8,128)}, f32[8,1024]{1,0:T(8,128)}) custom-call(s32[5]{0:T(128)} %stack.159.co, bf16[1024,1024]{1,0:T(8,128)(2,1)} %get-tuple-element.382.refs_3_.dkey, bf16[1024,1024]{1,0:T(8,128)(2,1)} %get-tuple-element.383.refs_4_.dval, ...), custom_call_target="tpu_custom_call", output_to_operand_aliasing={{0}: (9, {})} | custom-call | flops 85899344 | bytes 167772 | tf_op jit(solution)/shard_map/pallas_call | solution.py:1079
  377.2 5.8 %collective-permute-done.32 = bf16[2,2,64,1024]{3,2,1,0:T(8,128)(2,1)S(1)} collective-permute-done((bf16[2,2,64,1024]{3,2,1,0:T(8,128)(2,1)}, bf16[2,2,64,1024]{3,2,1,0:T(8,128)(2,1)S(1)}, u32[]{:S(2)}, u32[]{:S(2)}) %collective-permute-start.32) | collective-permute-done | bytes 524320 | tf_op jit(solution)/shard_map/ppermute | solution.py:1117
  386.6 2.6 add_bitcast_fusion
  389.2 1.9 collective-permute-start.38
  392.1 16.2 %shard_map.376 = (f32[1024,1024]{1,0:T(8,128)}, f32[5,8,1024]{2,1,0:T(8,128)}, f32[8,1024]{1,0:T(8,128)}) custom-call(s32[5]{0:T(128)} %stack.159.co, bf16[1024,1024]{1,0:T(8,128)(2,1)} %get-tuple-element.382.refs_3_.dkey, bf16[1024,1024]{1,0:T(8,128)(2,1)} %get-tuple-element.383.refs_4_.dval, ...), custom_call_target="tpu_custom_call", output_to_operand_aliasing={{0}: (9, {})} | custom-call | flops 85899344 | bytes 167772 | tf_op jit(solution)/shard_map/pallas_call | solution.py:1079
  416.3 3.0 collective-permute-start.41
  419.2 2.9 fusion.4
  422.5 2.0 collective-permute-start.44
  426.4 3.3 collective-permute-done.45
  433.0 1.9 collective-permute-start.50
  436.1 1.9 collective-permute-start.48
  438.0 2.6 collective-permute-done.50
  442.8 2.1 collective-permute-done.51
  445.0 1.9 collective-permute-done.52
  447.1 1.7 collective-permute-start.53
  449.8 3.4 collective-permute-done.54
  453.3 5.2 %collective-permute-done.53 = bf16[3,64,512]{2,1,0:T(8,128)(2,1)S(1)} collective-permute-done((bf16[3,64,512]{2,1,0:T(8,128)(2,1)S(1)}, bf16[3,64,512]{2,1,0:T(8,128)(2,1)S(1)}, u32[]{:S(2)}, u32[]{:S(2)}) %collective-permute-start.53) | collective-permute-done | bytes 196640 | tf_op jit(solution)/shard_map/ppermute | solution.py:1117
  (318 shorter events, 85.7 us)
Async XLA Ops:
  7.2 102.8 %all-gather.5.cloned.1.call-start = ((), (), s32[]{:S(2)}) async-start(), calls=%async_computation.2 | async-start | bytes 8650752 | tf_op jit(solution)/shard_map/all_gather | solution.py:1397
  8.9 174.7 %all-gather.7.cloned.1.call-start = ((), (), s32[]{:S(2)}) async-start(), calls=%async_computation.3 | async-start | bytes 6488064 | tf_op jit(solution)/shard_map/all_gather | solution.py:1412
  10.0 39.1 %collective-permute-start = (bf16[64,1024]{1,0:T(8,128)(2,1)S(1)}, bf16[64,1024]{1,0:T(8,128)(2,1)S(1)}, u32[]{:S(2)}, u32[]{:S(2)}) collective-permute-start(bf16[64,1024]{1,0:T(8,128)(2,1)S(1)} %get-tuple-element.232), channel_id=1, source_target_pairs={{0,16},{16,0},{1,17},{17,1},{2,18},{18,2},{3,19},{19,3},{4,20},{20... | collective-permute-start | bytes 393224 | tf_op jit(solution)/shard_map/ppermute | solution.py:1117
  14.1 35.0 %collective-permute-start.1 = (bf16[64,1024]{1,0:T(8,128)(2,1)S(1)}, bf16[64,1024]{1,0:T(8,128)(2,1)S(1)}, u32[]{:S(2)}, u32[]{:S(2)}) collective-permute-start(bf16[64,1024]{1,0:T(8,128)(2,1)S(1)} %get-tuple-element.234), channel_id=1, source_target_pairs={{0,16},{16,0},{1,17},{17,1},{2,18},{18,2},{3,19},{19,3},{4,20},{20... | collective-permute-start | bytes 393224 | tf_op jit(solution)/shard_map/ppermute | solution.py:1117
  15.1 34.0 %collective-permute-start.2 = (bf16[64,1024]{1,0:T(8,128)(2,1)S(1)}, bf16[64,1024]{1,0:T(8,128)(2,1)S(1)}, u32[]{:S(2)}, u32[]{:S(2)}) collective-permute-start(bf16[64,1024]{1,0:T(8,128)(2,1)S(1)} %get-tuple-element.236), channel_id=1, source_target_pairs={{0,16},{16,0},{1,17},{17,1},{2,18},{18,2},{3,19},{19,3},{4,20},{20... | collective-permute-start | bytes 393224 | tf_op jit(solution)/shard_map/ppermute | solution.py:1117
  24.1 14.7 %collective-permute-start.3 = (f32[16,32]{1,0:T(8,128)}, f32[16,32]{1,0:T(8,128)}, u32[]{:S(2)}, u32[]{:S(2)}) collective-permute-start(f32[16,32]{1,0:T(8,128)} %concatenate.133), channel_id=1, source_target_pairs={{0,1},{1,0},{2,3},{3,2},{4,5},{5,4},{6,7},{7,6},{8,9},{9,8},{10,11... | collective-permute-start | bytes 6152 | tf_op jit(solution)/shard_map/ppermute | solution.py:1117
  28.3 31.2 %collective-permute-start.7 = (bf16[1024,512]{1,0:T(8,128)(2,1)S(1)}, bf16[1024,512]{1,0:T(8,128)(2,1)S(1)}, u32[]{:S(2)}, u32[]{:S(2)}) collective-permute-start(bf16[1024,512]{1,0:T(8,128)(2,1)S(1)} %get-tuple-element.454), channel_id=1, source_target_pairs={{0,1},{1,0},{2,3},{3,2},{4,5},{5,4},{6,7},{7,6},{8,9},{9,8},{10,11... | collective-permute-start | bytes 3145736 | tf_op jit(solution)/shard_map/ppermute | solution.py:1117
  66.6 11.1 %collective-permute-start.8 = (bf16[2,64,1024]{2,1,0:T(8,128)(2,1)S(1)}, bf16[2,64,1024]{2,1,0:T(8,128)(2,1)S(1)}, u32[]{:S(2)}, u32[]{:S(2)}) collective-permute-start(bf16[2,64,1024]{2,1,0:T(8,128)(2,1)S(1)} %pad_maximum_fusion.7), channel_id=1, source_target_pairs={{0,8},{8,0},{1,9},{9,1},{2,10},{10,2},{3,11},{11,3},{4,12},{12,4},... | collective-permute-start | bytes 786440 | tf_op jit(solution)/shard_map/ppermute | solution.py:1117
  68.3 10.9 %collective-permute-start.9 = (bf16[2,64,1024]{2,1,0:T(8,128)(2,1)S(1)}, bf16[2,64,1024]{2,1,0:T(8,128)(2,1)S(1)}, u32[]{:S(2)}, u32[]{:S(2)}) collective-permute-start(bf16[2,64,1024]{2,1,0:T(8,128)(2,1)S(1)} %pad_maximum_fusion.8), channel_id=1, source_target_pairs={{0,1},{1,0},{2,3},{3,2},{4,5},{5,4},{6,7},{7,6},{8,9},{9,8},{10,11... | collective-permute-start | bytes 786440 | tf_op jit(solution)/shard_map/ppermute | solution.py:1117
  68.9 14.3 %collective-permute-start.10 = (bf16[2,64,1024]{2,1,0:T(8,128)(2,1)S(1)}, bf16[2,64,1024]{2,1,0:T(8,128)(2,1)S(1)}, u32[]{:S(2)}, u32[]{:S(2)}) collective-permute-start(bf16[2,64,1024]{2,1,0:T(8,128)(2,1)S(1)} %pad_maximum_fusion.9), channel_id=1, source_target_pairs={{0,4},{4,0},{1,5},{5,1},{2,6},{6,2},{3,7},{7,3},{8,12},{12,8},{9,1... | collective-permute-start | bytes 786440 | tf_op jit(solution)/shard_map/ppermute | solution.py:1117
  83.3 16.5 %collective-permute-start.12 = (bf16[2,2,64,1024]{3,2,1,0:T(8,128)(2,1)S(1)}, bf16[2,2,64,1024]{3,2,1,0:T(8,128)(2,1)S(1)}, u32[]{:S(2)}, u32[]{:S(2)}) collective-permute-start(bf16[2,2,64,1024]{3,2,1,0:T(8,128)(2,1)S(1)} %pad_maximum_fusion.3), channel_id=1, source_target_pairs={{0,4},{4,0},{1,5},{5,1},{2,6},{6,2},{3,7},{7,3},{8,12},{12,8},{9,1... | collective-permute-start | bytes 1572872 | tf_op jit(solution)/shard_map/ppermute | solution.py:1117
  85.1 14.6 %collective-permute-start.13 = (bf16[2,2,64,1024]{3,2,1,0:T(8,128)(2,1)S(1)}, bf16[2,2,64,1024]{3,2,1,0:T(8,128)(2,1)S(1)}, u32[]{:S(2)}, u32[]{:S(2)}) collective-permute-start(bf16[2,2,64,1024]{3,2,1,0:T(8,128)(2,1)S(1)} %pad_maximum_fusion.4), channel_id=1, source_target_pairs={{0,8},{8,0},{1,9},{9,1},{2,10},{10,2},{3,11},{11,3},{4,12},{12,4},... | collective-permute-start | bytes 1572872 | tf_op jit(solution)/shard_map/ppermute | solution.py:1117
  85.3 15.7 %collective-permute-start.14 = (bf16[2,2,64,1024]{3,2,1,0:T(8,128)(2,1)S(1)}, bf16[2,2,64,1024]{3,2,1,0:T(8,128)(2,1)}, u32[]{:S(2)}, u32[]{:S(2)}) collective-permute-start(bf16[2,2,64,1024]{3,2,1,0:T(8,128)(2,1)S(1)} %pad_maximum_fusion.5), channel_id=1, source_target_pairs={{0,1},{1,0},{2,3},{3,2},{4,5},{5,4},{6,7},{7,6},{8,9},{9,8},{10,11... | collective-permute-start | bytes 1572872 | tf_op jit(solution)/shard_map/ppermute | solution.py:1117
  110.0 321.6 %reduce-scatter.2.cloned.1.call-start = ((), (), s32[]{:S(2)}) async-start(), calls=%async_computation.1 | async-start | bytes 11141120 | tf_op jit(solution)/shard_map/reduce_scatter | solution.py:1259
  110.4 36.0 %collective-permute-start.15 = (bf16[2,2,2,64,1024]{4,3,2,1,0:T(8,128)(2,1)S(1)}, bf16[2,2,2,64,1024]{4,3,2,1,0:T(8,128)(2,1)}, u32[]{:S(2)}, u32[]{:S(2)}) collective-permute-start(bf16[2,2,2,64,1024]{4,3,2,1,0:T(8,128)(2,1)S(1)} %pad_maximum_fusion.refs_0_), channel_id=1, source_target_pairs={{0,1},{1,0},{2,3},{3,2},{4,5},{5,4},{6,7},{7,6},{8,9},{9,8},{10,11... | collective-permute-start | bytes 3145736 | tf_op jit(solution)/shard_map/ppermute | solution.py:1117
  113.4 33.0 %collective-permute-start.16 = (bf16[2,2,2,64,1024]{4,3,2,1,0:T(8,128)(2,1)S(1)}, bf16[2,2,2,64,1024]{4,3,2,1,0:T(8,128)(2,1)}, u32[]{:S(2)}, u32[]{:S(2)}) collective-permute-start(bf16[2,2,2,64,1024]{4,3,2,1,0:T(8,128)(2,1)S(1)} %pad_maximum_fusion.1.refs_4_), channel_id=1, source_target_pairs={{0,4},{4,0},{1,5},{5,1},{2,6},{6,2},{3,7},{7,3},{8,12},{12,8},{9,1... | collective-permute-start | bytes 3145736 | tf_op jit(solution)/shard_map/ppermute | solution.py:1117
  116.1 45.0 %collective-permute-start.21 = (bf16[2,2,2,64,1024]{4,3,2,1,0:T(8,128)(2,1)S(1)}, bf16[2,2,2,64,1024]{4,3,2,1,0:T(8,128)(2,1)}, u32[]{:S(2)}, u32[]{:S(2)}) collective-permute-start(bf16[2,2,2,64,1024]{4,3,2,1,0:T(8,128)(2,1)S(1)} %pad_maximum_fusion.2.refs_1_.refs_0_), channel_id=1, source_target_pairs={{0,8},{8,0},{1,9},{9,1},{2,10},{10,2},{3,11},{11,3},{4,12},{12,4},... | collective-permute-start | bytes 3145736 | tf_op jit(solution)/shard_map/ppermute | solution.py:1117
  146.5 14.6 %collective-permute-start.17 = (bf16[2,2,2,64,1024]{4,3,2,1,0:T(8,128)(2,1)S(1)}, bf16[2,2,2,64,1024]{4,3,2,1,0:T(8,128)(2,1)S(1)}, u32[]{:S(2)}, u32[]{:S(2)}) collective-permute-start(bf16[2,2,2,64,1024]{4,3,2,1,0:T(8,128)(2,1)S(1)} %pad_maximum_fusion.refs_0_), channel_id=1, source_target_pairs={{0,2},{2,0},{1,3},{3,1},{4,6},{6,4},{5,7},{7,5},{8,10},{10,8},{9,1... | collective-permute-start | bytes 3145736 | tf_op jit(solution)/shard_map/ppermute | solution.py:1117
  146.5 14.6 %collective-permute-start.18 = (bf16[2,2,2,64,1024]{4,3,2,1,0:T(8,128)(2,1)}, bf16[2,2,2,64,1024]{4,3,2,1,0:T(8,128)(2,1)S(1)}, u32[]{:S(2)}, u32[]{:S(2)}) collective-permute-start(bf16[2,2,2,64,1024]{4,3,2,1,0:T(8,128)(2,1)} %collective-permute-done.15.refs_1_), channel_id=1, source_target_pairs={{0,2},{2,0},{1,3},{3,1},{4,6},{6,4},{5,7},{7,5},{8,10},{10,8},{9,1... | collective-permute-start | bytes 3145736 | tf_op jit(solution)/shard_map/ppermute | solution.py:1117
  147.0 14.1 %collective-permute-start.19 = (bf16[2,2,2,64,1024]{4,3,2,1,0:T(8,128)(2,1)S(1)}, bf16[2,2,2,64,1024]{4,3,2,1,0:T(8,128)(2,1)}, u32[]{:S(2)}, u32[]{:S(2)}) collective-permute-start(bf16[2,2,2,64,1024]{4,3,2,1,0:T(8,128)(2,1)S(1)} %pad_maximum_fusion.1.refs_4_), channel_id=1, source_target_pairs={{0,2},{2,0},{1,3},{3,1},{4,6},{6,4},{5,7},{7,5},{8,10},{10,8},{9,1... | collective-permute-start | bytes 3145736 | tf_op jit(solution)/shard_map/ppermute | solution.py:1117
  147.1 14.0 %collective-permute-start.20 = (bf16[2,2,2,64,1024]{4,3,2,1,0:T(8,128)(2,1)}, bf16[2,2,2,64,1024]{4,3,2,1,0:T(8,128)(2,1)}, u32[]{:S(2)}, u32[]{:S(2)}) collective-permute-start(bf16[2,2,2,64,1024]{4,3,2,1,0:T(8,128)(2,1)} %collective-permute-done.16.refs_5_), channel_id=1, source_target_pairs={{0,2},{2,0},{1,3},{3,1},{4,6},{6,4},{5,7},{7,5},{8,10},{10,8},{9,1... | collective-permute-start | bytes 3145736 | tf_op jit(solution)/shard_map/ppermute | solution.py:1117
  161.2 22.0 %collective-permute-start.22 = (bf16[2,2,2,64,1024]{4,3,2,1,0:T(8,128)(2,1)S(1)}, bf16[2,2,2,64,1024]{4,3,2,1,0:T(8,128)(2,1)S(1)}, u32[]{:S(2)}, u32[]{:S(2)}) collective-permute-start(bf16[2,2,2,64,1024]{4,3,2,1,0:T(8,128)(2,1)S(1)} %pad_maximum_fusion.2.refs_1_.refs_0_), channel_id=1, source_target_pairs={{0,2},{2,0},{1,3},{3,1},{4,6},{6,4},{5,7},{7,5},{8,10},{10,8},{9,1... | collective-permute-start | bytes 3145736 | tf_op jit(solution)/shard_map/ppermute | solution.py:1117
  162.1 21.1 %collective-permute-start.23 = (bf16[2,2,2,64,1024]{4,3,2,1,0:T(8,128)(2,1)}, bf16[2,2,2,64,1024]{4,3,2,1,0:T(8,128)(2,1)S(1)}, u32[]{:S(2)}, u32[]{:S(2)}) collective-permute-start(bf16[2,2,2,64,1024]{4,3,2,1,0:T(8,128)(2,1)} %collective-permute-done.21.refs_2_.refs_1_), channel_id=1, source_target_pairs={{0,2},{2,0},{1,3},{3,1},{4,6},{6,4},{5,7},{7,5},{8,10},{10,8},{9,1... | collective-permute-start | bytes 3145736 | tf_op jit(solution)/shard_map/ppermute | solution.py:1117
  232.5 27.9 %collective-permute-start.24 = (bf16[2,2,2,2,64,1024]{5,4,3,2,1,0:T(8,128)(2,1)}, bf16[2,2,2,2,64,1024]{5,4,3,2,1,0:T(8,128)(2,1)}, u32[]{:S(2)}, u32[]{:S(2)}) collective-permute-start(bf16[2,2,2,2,64,1024]{5,4,3,2,1,0:T(8,128)(2,1)} %get-tuple-element.306), channel_id=1, source_target_pairs={{0,2},{2,0},{1,3},{3,1},{4,6},{6,4},{5,7},{7,5},{8,10},{10,8},{9,1... | collective-permute-start | bytes 6291464 | tf_op jit(solution)/shard_map/ppermute | solution.py:1117
  232.7 27.7 %collective-permute-start.25 = (bf16[2,2,2,2,64,1024]{5,4,3,2,1,0:T(8,128)(2,1)}, bf16[2,2,2,2,64,1024]{5,4,3,2,1,0:T(8,128)(2,1)}, u32[]{:S(2)}, u32[]{:S(2)}) collective-permute-start(bf16[2,2,2,2,64,1024]{5,4,3,2,1,0:T(8,128)(2,1)} %get-tuple-element.307), channel_id=1, source_target_pairs={{0,2},{2,0},{1,3},{3,1},{4,6},{6,4},{5,7},{7,5},{8,10},{10,8},{9,1... | collective-permute-start | bytes 6291464 | tf_op jit(solution)/shard_map/ppermute | solution.py:1117
  233.1 27.3 %collective-permute-start.26 = (bf16[1024,512]{1,0:T(8,128)(2,1)S(1)}, bf16[1024,512]{1,0:T(8,128)(2,1)S(1)}, u32[]{:S(2)}, u32[]{:S(2)}) collective-permute-start(bf16[1024,512]{1,0:T(8,128)(2,1)S(1)} %copy-done.41), channel_id=1, source_target_pairs={{0,1},{1,0},{2,3},{3,2},{4,5},{5,4},{6,7},{7,6},{8,9},{9,8},{10,11... | collective-permute-start | bytes 3145736 | tf_op jit(solution)/shard_map/ppermute | solution.py:1117
  264.5 47.5 %collective-permute-start.27 = (bf16[2,2,2,2,64,1024]{5,4,3,2,1,0:T(8,128)(2,1)S(1)}, bf16[2,2,2,2,64,1024]{5,4,3,2,1,0:T(8,128)(2,1)S(1)}, u32[]{:S(2)}, u32[]{:S(2)}) collective-permute-start(bf16[2,2,2,2,64,1024]{5,4,3,2,1,0:T(8,128)(2,1)S(1)} %add.330), channel_id=1, source_target_pairs={{0,1},{1,0},{2,3},{3,2},{4,5},{5,4},{6,7},{7,6},{8,9},{9,8},{10,11... | collective-permute-start | bytes 6291464 | tf_op jit(solution)/shard_map/ppermute | solution.py:1117
  312.0 27.3 %collective-permute-start.29 = (bf16[2,2,2,1,64,512]{5,4,3,2,1,0:T(8,128)(2,1)}, bf16[2,2,2,1,64,512]{5,4,3,2,1,0:T(8,128)(2,1)S(1)}, u32[]{:S(2)}, u32[]{:S(2)}) collective-permute-start(bf16[2,2,2,1,64,512]{5,4,3,2,1,0:T(8,128)(2,1)} %get-tuple-element.334), channel_id=1, source_target_pairs={{0,2},{2,0},{1,3},{3,1},{4,6},{6,4},{5,7},{7,5},{8,10},{10,8},{9,1... | collective-permute-start | bytes 1572872 | tf_op jit(solution)/shard_map/ppermute | solution.py:1117
  312.0 27.3 %collective-permute-start.30 = (bf16[2,2,2,1,64,512]{5,4,2,1,3,0:T(8,128)(2,1)}, bf16[2,2,2,1,64,512]{5,4,2,1,3,0:T(8,128)(2,1)S(1)}, u32[]{:S(2)}, u32[]{:S(2)}) collective-permute-start(bf16[2,2,2,1,64,512]{5,4,2,1,3,0:T(8,128)(2,1)} %bitcast.276), channel_id=1, source_target_pairs={{0,2},{2,0},{1,3},{3,1},{4,6},{6,4},{5,7},{7,5},{8,10},{10,8},{9,1... | collective-permute-start | bytes 1572872 | tf_op jit(solution)/shard_map/ppermute | solution.py:1117
  315.6 38.2 %collective-permute-start.28 = (bf16[2,2,2,64,1024]{4,3,2,1,0:T(8,128)(2,1)S(1)}, bf16[2,2,2,64,1024]{4,3,2,1,0:T(8,128)(2,1)S(1)}, u32[]{:S(2)}, u32[]{:S(2)}) collective-permute-start(bf16[2,2,2,64,1024]{4,3,2,1,0:T(8,128)(2,1)S(1)} %get-tuple-element.437), channel_id=1, source_target_pairs={{0,4},{4,0},{1,5},{5,1},{2,6},{6,2},{3,7},{7,3},{8,12},{12,8},{9,1... | collective-permute-start | bytes 3145736 | tf_op jit(solution)/shard_map/ppermute | solution.py:1117
  339.5 14.3 %collective-permute-start.31 = (bf16[2,2,2,1,64,512]{5,4,3,2,1,0:T(8,128)(2,1)S(1)}, bf16[2,2,2,1,64,512]{5,4,3,2,1,0:T(8,128)(2,1)S(1)}, u32[]{:S(2)}, u32[]{:S(2)}) collective-permute-start(bf16[2,2,2,1,64,512]{5,4,3,2,1,0:T(8,128)(2,1)S(1)} %add.335), channel_id=1, source_target_pairs={{0,1},{1,0},{2,3},{3,2},{4,5},{5,4},{6,7},{7,6},{8,9},{9,8},{10,11... | collective-permute-start | bytes 1572872 | tf_op jit(solution)/shard_map/ppermute | solution.py:1117
  354.6 28.3 %collective-permute-start.34 = (bf16[3,2,2,2,64,512]{5,4,3,2,1,0:T(8,128)(2,1)}, bf16[3,2,2,2,64,512]{5,4,3,2,1,0:T(8,128)(2,1)}, u32[]{:S(2)}, u32[]{:S(2)}) collective-permute-start(bf16[3,2,2,2,64,512]{5,4,3,2,1,0:T(8,128)(2,1)} %get-tuple-element.365), channel_id=1, source_target_pairs={{0,2},{2,0},{1,3},{3,1},{4,6},{6,4},{5,7},{7,5},{8,10},{10,8},{9,1... | collective-permute-start | bytes 4718600 | tf_op jit(solution)/shard_map/ppermute | solution.py:1117
  354.6 28.3 %collective-permute-start.35 = (bf16[3,2,2,2,64,512]{5,4,3,2,1,0:T(8,128)(2,1)}, bf16[3,2,2,2,64,512]{5,4,3,2,1,0:T(8,128)(2,1)S(1)}, u32[]{:S(2)}, u32[]{:S(2)}) collective-permute-start(bf16[3,2,2,2,64,512]{5,4,3,2,1,0:T(8,128)(2,1)} %get-tuple-element.366), channel_id=1, source_target_pairs={{0,2},{2,0},{1,3},{3,1},{4,6},{6,4},{5,7},{7,5},{8,10},{10,8},{9,1... | collective-permute-start | bytes 4718600 | tf_op jit(solution)/shard_map/ppermute | solution.py:1117
  356.3 26.6 %collective-permute-start.32 = (bf16[2,2,64,1024]{3,2,1,0:T(8,128)(2,1)}, bf16[2,2,64,1024]{3,2,1,0:T(8,128)(2,1)S(1)}, u32[]{:S(2)}, u32[]{:S(2)}) collective-permute-start(bf16[2,2,64,1024]{3,2,1,0:T(8,128)(2,1)} %get-tuple-element.452), channel_id=1, source_target_pairs={{0,8},{8,0},{1,9},{9,1},{2,10},{10,2},{3,11},{11,3},{4,12},{12,4},... | collective-permute-start | bytes 1572872 | tf_op jit(solution)/shard_map/ppermute | solution.py:1117
  358.7 18.4 %collective-permute-start.33 = (bf16[2,2,1,64,512]{4,3,1,0,2:T(8,128)(2,1)}, bf16[2,2,1,64,512]{4,3,1,0,2:T(8,128)(2,1)}, u32[]{:S(2)}, u32[]{:S(2)}) collective-permute-start(bf16[2,2,1,64,512]{4,3,1,0,2:T(8,128)(2,1)} %fusion.14), channel_id=1, source_target_pairs={{0,4},{4,0},{1,5},{5,1},{2,6},{6,2},{3,7},{7,3},{8,12},{12,8},{9,1... | collective-permute-start | bytes 786440 | tf_op jit(solution)/shard_map/ppermute | solution.py:1117
  383.9 31.4 %collective-permute-start.36 = (bf16[2,64,1024]{2,1,0:T(8,128)(2,1)}, bf16[2,64,1024]{2,1,0:T(8,128)(2,1)}, u32[]{:S(2)}, u32[]{:S(2)}) collective-permute-start(bf16[2,64,1024]{2,1,0:T(8,128)(2,1)} %get-tuple-element.456), channel_id=1, source_target_pairs={{0,16},{16,0},{1,17},{17,1},{2,18},{18,2},{3,19},{19,3},{4,20},{20... | collective-permute-start | bytes 786440 | tf_op jit(solution)/shard_map/ppermute | solution.py:1117
  385.5 29.8 %collective-permute-start.37 = (bf16[2,1,64,512]{3,2,0,1:T(8,128)(2,1)}, bf16[2,1,64,512]{3,2,0,1:T(8,128)(2,1)}, u32[]{:S(2)}, u32[]{:S(2)}) collective-permute-start(bf16[2,1,64,512]{3,2,0,1:T(8,128)(2,1)} %fusion.23), channel_id=1, source_target_pairs={{0,8},{8,0},{1,9},{9,1},{2,10},{10,2},{3,11},{11,3},{4,12},{12,4},... | collective-permute-start | bytes 393224 | tf_op jit(solution)/shard_map/ppermute | solution.py:1117
  389.2 26.2 %collective-permute-start.38 = (bf16[2,2,2,64,512]{4,3,2,1,0:T(8,128)(2,1)}, bf16[2,2,2,64,512]{4,3,2,1,0:T(8,128)(2,1)}, u32[]{:S(2)}, u32[]{:S(2)}) collective-permute-start(bf16[2,2,2,64,512]{4,3,2,1,0:T(8,128)(2,1)} %get-tuple-element.451), channel_id=1, source_target_pairs={{0,4},{4,0},{1,5},{5,1},{2,6},{6,2},{3,7},{7,3},{8,12},{12,8},{9,1... | collective-permute-start | bytes 1572872 | tf_op jit(solution)/shard_map/ppermute | solution.py:1117
  391.1 24.3 %collective-permute-start.39 = (bf16[2,2,2,64,512]{4,3,2,1,0:T(8,128)(2,1)}, bf16[2,2,2,64,512]{4,3,2,1,0:T(8,128)(2,1)}, u32[]{:S(2)}, u32[]{:S(2)}) collective-permute-start(bf16[2,2,2,64,512]{4,3,2,1,0:T(8,128)(2,1)} %get-tuple-element.450), channel_id=1, source_target_pairs={{0,1},{1,0},{2,3},{3,2},{4,5},{5,4},{6,7},{7,6},{8,9},{9,8},{10,11... | collective-permute-start | bytes 1572872 | tf_op jit(solution)/shard_map/ppermute | solution.py:1117
  391.1 24.2 %collective-permute-start.40 = (bf16[2,2,2,64,512]{4,3,2,1,0:T(8,128)(2,1)}, bf16[2,2,2,64,512]{4,3,2,1,0:T(8,128)(2,1)}, u32[]{:S(2)}, u32[]{:S(2)}) collective-permute-start(bf16[2,2,2,64,512]{4,3,2,1,0:T(8,128)(2,1)} %get-tuple-element.449), channel_id=1, source_target_pairs={{0,8},{8,0},{1,9},{9,1},{2,10},{10,2},{3,11},{11,3},{4,12},{12,4},... | collective-permute-start | bytes 1572872 | tf_op jit(solution)/shard_map/ppermute | solution.py:1117
  416.3 14.8 %collective-permute-start.41 = (bf16[1,64,512]{2,1,0:T(8,128)(2,1)S(1)}, bf16[1,64,512]{2,1,0:T(8,128)(2,1)S(1)}, u32[]{:S(2)}, u32[]{:S(2)}) collective-permute-start(bf16[1,64,512]{2,1,0:T(8,128)(2,1)S(1)} %fusion.29), channel_id=1, source_target_pairs={{0,16},{16,0},{1,17},{17,1},{2,18},{18,2},{3,19},{19,3},{4,20},{20... | collective-permute-start | bytes 196616 | tf_op jit(solution)/shard_map/ppermute | solution.py:1117
  422.2 8.9 %collective-permute-start.42 = (bf16[2,2,64,512]{3,2,1,0:T(8,128)(2,1)S(1)}, bf16[2,2,64,512]{3,2,1,0:T(8,128)(2,1)S(1)}, u32[]{:S(2)}, u32[]{:S(2)}) collective-permute-start(bf16[2,2,64,512]{3,2,1,0:T(8,128)(2,1)S(1)} %get-tuple-element.448), channel_id=1, source_target_pairs={{0,8},{8,0},{1,9},{9,1},{2,10},{10,2},{3,11},{11,3},{4,12},{12,4},... | collective-permute-start | bytes 786440 | tf_op jit(solution)/shard_map/ppermute | solution.py:1117
  422.3 8.7 %collective-permute-start.43 = (bf16[2,2,64,512]{3,2,1,0:T(8,128)(2,1)S(1)}, bf16[2,2,64,512]{3,2,1,0:T(8,128)(2,1)S(1)}, u32[]{:S(2)}, u32[]{:S(2)}) collective-permute-start(bf16[2,2,64,512]{3,2,1,0:T(8,128)(2,1)S(1)} %get-tuple-element.446), channel_id=1, source_target_pairs={{0,4},{4,0},{1,5},{5,1},{2,6},{6,2},{3,7},{7,3},{8,12},{12,8},{9,1... | collective-permute-start | bytes 786440 | tf_op jit(solution)/shard_map/ppermute | solution.py:1117
  422.5 9.2 %collective-permute-start.44 = (bf16[2,2,64,512]{3,2,1,0:T(8,128)(2,1)S(1)}, bf16[2,2,64,512]{3,2,1,0:T(8,128)(2,1)S(1)}, u32[]{:S(2)}, u32[]{:S(2)}) collective-permute-start(bf16[2,2,64,512]{3,2,1,0:T(8,128)(2,1)S(1)} %get-tuple-element.439), channel_id=1, source_target_pairs={{0,1},{1,0},{2,3},{3,2},{4,5},{5,4},{6,7},{7,6},{8,9},{9,8},{10,11... | collective-permute-start | bytes 786440 | tf_op jit(solution)/shard_map/ppermute | solution.py:1117
  432.8 14.1 %collective-permute-start.47 = (bf16[2,64,512]{2,1,0:T(8,128)(2,1)S(1)}, bf16[2,64,512]{2,1,0:T(8,128)(2,1)S(1)}, u32[]{:S(2)}, u32[]{:S(2)}) collective-permute-start(bf16[2,64,512]{2,1,0:T(8,128)(2,1)S(1)} %get-tuple-element.466), channel_id=1, source_target_pairs={{0,1},{1,0},{2,3},{3,2},{4,5},{5,4},{6,7},{7,6},{8,9},{9,8},{10,11... | collective-permute-start | bytes 393224 | tf_op jit(solution)/shard_map/ppermute | solution.py:1117
  435.9 11.0 %collective-permute-start.52 = (bf16[64,2560]{1,0:T(8,128)(2,1)S(1)}, bf16[64,2560]{1,0:T(8,128)(2,1)S(1)}, u32[]{:S(2)}, u32[]{:S(2)}) collective-permute-start(bf16[64,2560]{1,0:T(8,128)(2,1)S(1)} %dynamic-slice_bitcast_fusion), channel_id=1, source_target_pairs={{0,1},{1,0},{2,3},{3,2},{4,5},{5,4},{6,7},{7,6},{8,9},{9,8},{10,11... | collective-permute-start | bytes 983048 | tf_op jit(solution)/shard_map/ppermute | solution.py:1117
  436.1 10.8 %collective-permute-start.48 = (bf16[2,64,512]{2,1,0:T(8,128)(2,1)S(1)}, bf16[2,64,512]{2,1,0:T(8,128)(2,1)S(1)}, u32[]{:S(2)}, u32[]{:S(2)}) collective-permute-start(bf16[2,64,512]{2,1,0:T(8,128)(2,1)S(1)} %get-tuple-element.464), channel_id=1, source_target_pairs={{0,8},{8,0},{1,9},{9,1},{2,10},{10,2},{3,11},{11,3},{4,12},{12,4},... | collective-permute-start | bytes 393224 | tf_op jit(solution)/shard_map/ppermute | solution.py:1117
  447.1 11.4 %collective-permute-start.53 = (bf16[3,64,512]{2,1,0:T(8,128)(2,1)S(1)}, bf16[3,64,512]{2,1,0:T(8,128)(2,1)S(1)}, u32[]{:S(2)}, u32[]{:S(2)}) collective-permute-start(bf16[3,64,512]{2,1,0:T(8,128)(2,1)S(1)} %pad_maximum_fusion.12), channel_id=1, source_target_pairs={{0,16},{16,0},{1,17},{17,1},{2,18},{18,2},{3,19},{19,3},{4,20},{20... | collective-permute-start | bytes 589832 | tf_op jit(solution)/shard_map/ppermute | solution.py:1117
  (52 other events, 578.1 us)
Sparse Core Ops, SparseCore 0:
  11.0 98.9 all-gather.4
  112.9 70.6 all-gather.6
  260.5 139.7 reduce-scatter.1

commit v5 on v4

--- a/solution.py
+++ b/solution.py
@@ -40,14 +40,17 @@
 
 def slot_place(co, rel):
     at = {axis: co[n] ^ rel[axis] for n, axis in enumerate(EVERY)}
-    block = at["w"] * 8 + at["u"] * 4 + at["y"] * 2 + at["c"]
-    return pl.multiple_of(block * SLOT, SLOT), at["x"]
-
-
-def weight_copies(co, refs, whole, sems, layout):
-    copies = []
+    return at["w"] * 8 + at["u"] * 4 + at["y"] * 2 + at["c"], at["x"]
+
+
+def rows_of(whole, half, columns=slice(None)):
+    found = whole[half, :, :, columns]
+    return found.reshape(found.shape[0] * found.shape[1], found.shape[2])
+
+
+def start_weight(co, refs, whole, sems, layout, halves=(0, 1)):
     refs = list(refs)
-    for kind, order, first, columns in layout:
+    for n, (kind, order, first, columns) in enumerate(layout):
         target = pl.ds(first, columns)
         if kind == "rel":
             order, skip, base = order
@@ -55,34 +58,29 @@
                 arrays, refs = refs[:4], refs[4:]
             else:
                 arrays, refs = [*refs[:2], refs[2].at[base], refs[2].at[base + 1]], refs[3:]
-            for which, index, rel in rel_slots(order):
-                row, half = slot_place(co, rel)
-                copies.append(
-                    (
-                        rel["x"],
-                        pltpu.make_async_copy(
-                            arrays[which].at[index + (slice(None), pl.ds(skip, columns))],
-                            whole.at[half, pl.ds(row, SLOT), target],
-                            sems.at[len(copies)],
-                        ),
-                    )
-                )
+            for which, index, rel in sorted(rel_slots(order), key=lambda slot: slot[2]["x"]):
+                if rel["x"] in halves:
+                    block, half = slot_place(co, rel)
+                    pltpu.make_async_copy(
+                        arrays[which].at[index + (slice(None), pl.ds(skip, columns))],
+                        whole.at[half, block, :, target],
+                        sems.at[2 * n + rel["x"]],
+                    ).start()
         else:
             array, refs = refs[0], refs[1:]
-            for rel_x in (0, 1):
+            for rel_x in halves:
                 half = co[4] ^ rel_x
-                for block in range(16):
-                    copies.append(
-                        (
-                            rel_x,
-                            pltpu.make_async_copy(
-                                array.at[block, half, :, pl.ds(order, columns)],
-                                whole.at[half, pl.ds(block * SLOT, SLOT), target],
-                                sems.at[len(copies)],
-                            ),
-                        )
-                    )
-    return copies
+                pltpu.make_async_copy(
+                    array.at[:, half, :, pl.ds(order, columns)],
+                    whole.at[half, :, :, target],
+                    sems.at[2 * n + rel_x],
+                ).start()
+
+
+def wait_weight(co, whole, sems, layout, rel_x):
+    for n, (_, _, first, columns) in enumerate(layout):
+        held = whole.at[co[4] ^ rel_x, :, :, pl.ds(first, columns)]
+        pltpu.make_async_copy(held, held, sems.at[2 * n + rel_x]).wait()
 
 
 def take_refs(refs, layout):
@@ -106,19 +104,10 @@
     return sum(part[3] for part in weight[0])
 
 
-def sem_count(weight):
-    return 32 * len(weight[0])
-
-
-def start_all(copies):
-    for _, copy in copies:
-        copy.start()
-
-
-def wait_half(copies, half):
-    for which, copy in copies:
-        if which == half:
-            copy.wait()
+def weight_scratch(*weights):
+    return [pltpu.VMEM((2, 16, SLOT, weight_width(w)), BF) for w in weights] + [
+        pltpu.SemaphoreType.DMA((2 * len(w[0]),)) for w in weights
+    ]
 
 
 ROWS = 32
@@ -139,12 +128,6 @@
 
 def spread_mean(total, width):
     return jnp.broadcast_to(jnp.sum(total, axis=1, keepdims=True) * (1.0 / width), total.shape)
-
-
-def wait_at_first(copies, half):
-    @pl.when(pl.program_id(0) == 0)
-    def _():
-        wait_half(copies, half)
 
 
 def norm_stats(load, width):
@@ -216,7 +199,7 @@
     def _():
         last[...] = jnp.zeros_like(last)
 
-    lasts = lax.fori_loop(0, x_ref.shape[0] // ROWS, step, row_parts(last), unroll=2)
+    lasts = lax.fori_loop(0, x_ref.shape[0] // ROWS, step, row_parts(last), unroll=4)
     for strip, value in zip(strips(width), lasts):
         last[0:1, strip] = value
 
@@ -241,6 +224,7 @@
     )(x, carry, vectors)
 
 
+FORWARD_TILE = 512
 TILE = 256
 
 
@@ -249,8 +233,8 @@
     return [jnp.exp(-float(n) * speed) for n in (1, 2, 4, 8)]
 
 
-def twice(values):
-    return jnp.concatenate([values] * (TILE // 128), axis=1)
+def repeated(values, size):
+    return jnp.concatenate([values] * (size // LANES), axis=1)
 
 
 def time_forward_kernel(
@@ -259,33 +243,29 @@
     key_w, refs = take_refs(refs, layouts[0])
     val_w, refs = take_refs(refs, layouts[1])
     rec_w, refs = take_refs(refs, layouts[2])
-    key_ref, val_ref, rec_ref, pa_ref, pb_ref, gated_ref, kw, vw, rw, sems = refs
+    key_ref, val_ref, rec_ref, pa_ref, pb_ref, gated_ref, *scratch = refs
+    wholes, sems = scratch[:3], scratch[3:]
     j = pl.program_id(0)
-    per_half = kw.shape[2] // TILE
-    groups = [
-        weight_copies(co, arrays, whole, sems.at[n], layout)
-        for n, (arrays, whole, layout) in enumerate(zip((key_w, val_w, rec_w), (kw, vw, rw), layouts))
-    ]
+    per_half = wholes[0].shape[3] // FORWARD_TILE
 
     @pl.when(j == 0)
     def _():
-        for copies in groups:
-            start_all(copies)
-        for copies in groups:
-            wait_half(copies, 0)
-
-    @pl.when(j == per_half)
-    def _():
-        for copies in groups:
-            wait_half(copies, 1)
+        for arrays, whole, sem, layout in zip((key_w, val_w, rec_w), wholes, sems, layouts):
+            start_weight(co, arrays, whole, sem, layout)
+
+    for which in (0, 1):
+
+        @pl.when(j == which * per_half)
+        def _(which=which):
+            for whole, sem, layout in zip(wholes, sems, layouts):
+                wait_weight(co, whole, sem, layout, which)
 
     half = co[4] ^ lax.div(j, per_half)
-    columns = pl.ds(pl.multiple_of(lax.rem(j, per_half) * TILE, TILE), TILE)
-    key_ref[...] = dot(mk[...], kw[half, :, columns], NN)
-    val_ref[...] = dot(mv[...], vw[half, :, columns], NN)
-    rec_ref[...] = dot(mr[...], rw[half, :, columns], NN)
-
-    spread = (8, TILE)
+    columns = pl.ds(pl.multiple_of(lax.rem(j, per_half) * FORWARD_TILE, FORWARD_TILE), FORWARD_TILE)
+    for mixed, whole, out in zip((mk, mv, mr), wholes, (key_ref, val_ref, rec_ref)):
+        out[...] = dot(mixed[...], rows_of(whole, half, columns), NN)
+
+    spread = (8, FORWARD_TILE)
     decay = jnp.broadcast_to(vec[2:3, :], spread)
     first = jnp.broadcast_to(vec[3:4, :], spread)
     r1, r2, r4, r8 = scan_rates(decay)
@@ -294,7 +274,7 @@
     def group(start, state):
         rows = pl.ds(start, 8)
         key, val, pre = key_ref[rows, :], val_ref[rows, :], rec_ref[rows, :]
-        m1, m2, m4, mf, ml = (twice(masks[n, rows, :]) for n in range(5))
+        m1, m2, m4, mf, ml = (repeated(masks[n, rows, :], FORWARD_TILE) for n in range(5))
         rec = 1.0 / (1.0 + jnp.exp(-pre))
         power = jnp.exp(key)
         bonus = jnp.exp(first + key)
@@ -320,33 +300,32 @@
         return state
 
     zero = jnp.zeros(spread, F32)
-    lax.fori_loop(0, key_ref.shape[0] // CHUNK, step, (zero, zero), unroll=2)
+    lax.fori_loop(0, key_ref.shape[0] // CHUNK, step, (zero, zero), unroll=4)
 
 
 def time_forward(co, mixed, weights, vectors, masks):
     tokens, width = mixed[0].shape
     half = width // 2
-    per_half = half // TILE
+    per_half = half // FORWARD_TILE
 
     def tile(j, co):
         return 0, (co[4] ^ lax.div(j, per_half)) * per_half + lax.rem(j, per_half)
 
     fixed = pl.BlockSpec((tokens, width), lambda j, co: (0, 0))
-    block = pl.BlockSpec((tokens, TILE), tile)
+    block = pl.BlockSpec((tokens, FORWARD_TILE), tile)
     return pl.pallas_call(
         functools.partial(time_forward_kernel, layouts=[w[0] for w in weights]),
         grid_spec=pltpu.PrefetchScalarGridSpec(
             num_scalar_prefetch=1,
-            grid=(width // TILE,),
+            grid=(width // FORWARD_TILE,),
             in_specs=[fixed] * 3
             + [
-                pl.BlockSpec((vectors.shape[0], TILE), tile),
+                pl.BlockSpec((vectors.shape[0], FORWARD_TILE), tile),
                 pl.BlockSpec(masks.shape, lambda j, co: (0, 0, 0)),
             ]
             + [anywhere()] * len(arrays_of(*weights)),
             out_specs=[block] * 6,
-            scratch_shapes=[pltpu.VMEM((2, width, half), BF)] * 3
-            + [pltpu.SemaphoreType.DMA((3, 32))],
+            scratch_shapes=weight_scratch(*weights),
         ),
         out_shape=[jax.ShapeDtypeStruct((tokens, width), F32)] * 5
         + [jax.ShapeDtypeStruct((tokens, width), BF)],
@@ -359,19 +338,20 @@
     co, gated, x_ref, carry_ref, vec_ref, *refs, layout
 ):
     arrays, refs = take_refs(refs, layout)
-    middle_ref, mk_ref, mr_ref, ow, last, sems = refs
+    middle_ref, mk_ref, mr_ref, last, ow, sems = refs
     i = pl.program_id(0)
-    copies = weight_copies(co, arrays, ow, sems, layout)
 
     @pl.when(i == 0)
     def _():
-        start_all(copies)
+        start_weight(co, arrays, ow, sems, layout)
         last[...] = jnp.zeros_like(last)
-        wait_half(copies, 0)
-        wait_half(copies, 1)
-
-    half = ow.shape[2]
-    middle_ref[...] = dot(gated[:, :half], ow[0], NT) + dot(gated[:, half:], ow[1], NT)
+        for half in (0, 1):
+            wait_weight(co, ow, sems, layout, half)
+
+    half = ow.shape[3]
+    middle_ref[...] = dot(gated[:, :half], rows_of(ow, 0), NT) + dot(
+        gated[:, half:], rows_of(ow, 1), NT
+    )
     width = x_ref.shape[1]
 
     def step(n, before):
@@ -391,7 +371,7 @@
             lasts.append(normed[ROWS - 1 :, :])
         return tuple(lasts)
 
-    lasts = lax.fori_loop(0, x_ref.shape[0] // ROWS, step, row_parts(last), unroll=2)
+    lasts = lax.fori_loop(0, x_ref.shape[0] // ROWS, step, row_parts(last), unroll=4)
     for strip, value in zip(strips(width), lasts):
         last[0:1, strip] = value
 
@@ -413,11 +393,7 @@
             ]
             + [anywhere()] * len(weight[1]),
             out_specs=[tall] * 3,
-            scratch_shapes=[
-                pltpu.VMEM((2, width, width // 2), BF),
-                pltpu.VMEM((8, width), F32),
-                pltpu.SemaphoreType.DMA((32,)),
-            ],
+            scratch_shapes=[pltpu.VMEM((8, width), F32)] + weight_scratch(weight),
         ),
         out_shape=[jax.ShapeDtypeStruct((tokens, width), t) for t in (F32, BF, BF)],
         compiler_params=params(),
@@ -431,21 +407,21 @@
 def hidden_kernel(co, mk, *refs, layout):
     arrays, (hidden_ref, active_ref, whole, sems) = take_refs(refs, layout)
     j = pl.program_id(0)
-    per_half = whole.shape[2] // WIDE
-    copies = weight_copies(co, arrays, whole, sems, layout)
+    per_half = whole.shape[3] // WIDE
 
     @pl.when(j == 0)
     def _():
-        start_all(copies)
-        wait_half(copies, 0)
-
-    @pl.when(j == per_half)
-    def _():
-        wait_half(copies, 1)
+        start_weight(co, arrays, whole, sems, layout)
+
+    for which in (0, 1):
+
+        @pl.when(j == which * per_half)
+        def _(which=which):
+            wait_weight(co, whole, sems, layout, which)
 
     half = co[4] ^ lax.div(j, per_half)
     columns = pl.ds(pl.multiple_of(lax.rem(j, per_half) * WIDE, WIDE), WIDE)
-    active = jnp.maximum(dot(mk[...], whole[half, :, columns], NN), 0.0)
+    active = jnp.maximum(dot(mk[...], rows_of(whole, half, columns), NN), 0.0)
     active_ref[...] = active.astype(BF)
     hidden_ref[...] = (active * active).astype(BF)
 
@@ -466,10 +442,7 @@
             in_specs=[pl.BlockSpec((tokens, width), lambda j, co: (0, 0))]
             + [anywhere()] * len(weight[1]),
             out_specs=[block] * 2,
-            scratch_shapes=[
-                pltpu.VMEM((2, width, half), BF),
-                pltpu.SemaphoreType.DMA((sem_count(weight),)),
-            ],
+            scratch_shapes=weight_scratch(weight),
         ),
         out_shape=[jax.ShapeDtypeStruct((tokens, 2 * half), BF)] * 2,
         compiler_params=params(),
@@ -482,24 +455,24 @@
 ):
     value_w, refs = take_refs(refs, layouts[0])
     recept_w, refs = take_refs(refs, layouts[1])
-    *outs, dres_ref, dkv_ref, drec_ref, loss_ref, ww, rw, kv_ref, pre_ref, sems, sems_r = refs
+    *outs, dres_ref, dkv_ref, drec_ref, loss_ref, kv_ref, pre_ref, ww, rw, sems, sems_r = refs
     i = pl.program_id(0)
-    copies = weight_copies(co, value_w, ww, sems, layouts[0])
-    recept = weight_copies(co, recept_w, rw, sems_r, layouts[1])
 
     @pl.when(i == 0)
     def _():
-        start_all(recept)
-        start_all(copies)
+        start_weight(co, recept_w, rw, sems_r, layouts[1])
+        start_weight(co, value_w, ww, sems, layouts[0])
         loss_ref[...] = jnp.zeros_like(loss_ref)
         for half in (0, 1):
-            wait_half(recept, half)
-            wait_half(copies, half)
-
-    wide, narrow = ww.shape[2], rw.shape[2]
-    pre_ref[:, :narrow] = dot(mr[...], rw[0], NN)
-    pre_ref[:, narrow:] = dot(mr[...], rw[1], NN)
-    kv_ref[...] = dot(hidden[:, :wide], ww[0], NT) + dot(hidden[:, wide:], ww[1], NT)
+            wait_weight(co, rw, sems_r, layouts[1], half)
+            wait_weight(co, ww, sems, layouts[0], half)
+
+    wide, narrow = ww.shape[3], rw.shape[3]
+    pre_ref[:, :narrow] = dot(mr[...], rows_of(rw, 0), NN)
+    pre_ref[:, narrow:] = dot(mr[...], rows_of(rw, 1), NN)
+    kv_ref[...] = dot(hidden[:, :wide], rows_of(ww, 0), NT) + dot(
+        hidden[:, wide:], rows_of(ww, 1), NT
+    )
     factor = scale[0]
 
     def step(n, _):
@@ -523,7 +496,7 @@
             loss_ref[:, strip] += fold_rows(error * error)
         return 0
 
-    lax.fori_loop(0, kv_ref.shape[0] // ROWS, step, 0)
+    lax.fori_loop(0, kv_ref.shape[0] // ROWS, step, 0, unroll=2)
 
 
 def result_step(co, scale, hidden, mixed, middle, teachers, valid, weight, recept):
@@ -549,14 +522,7 @@
             out_specs=[pl.BlockSpec((rows, width // 2), lambda i, co, s: (co[4] * 4 + i, 0)), thin]
             + [tall] * 3
             + [pl.BlockSpec((8, width), lambda i, co, s: (0, 0))],
-            scratch_shapes=[
-                pltpu.VMEM((2, width, wide), BF),
-                pltpu.VMEM((2, width, width // 2), BF),
-                pltpu.VMEM((rows, width), F32),
-                pltpu.VMEM((rows, width), F32),
-                pltpu.SemaphoreType.DMA((sem_count(weight),)),
-                pltpu.SemaphoreType.DMA((sem_count(recept),)),
-            ],
+            scratch_shapes=[pltpu.VMEM((rows, width), F32)] * 2 + weight_scratch(weight, recept),
         ),
         out_shape=[jax.ShapeDtypeStruct((n * tokens, width // 2), BF) for n in (2, 1)]
         + [jax.ShapeDtypeStruct((tokens, width), t) for t in (F32, BF, BF)]
@@ -566,27 +532,26 @@
     )(co, scale, hidden, mixed, middle, *teachers, valid, *arrays_of(weight, recept))
 
 
-def grad_copies(co, whole, targets, n, sems, order, piece, merged=False):
-    found = ([], [])
-    for m, (which, index, rel) in enumerate(rel_slots(order)):
-        row, half = slot_place(co, rel)
-        found[rel["x"]].append(
+def start_grads(co, whole, targets, n, sem, order, which, merged):
+    for array, index, rel in rel_slots(order):
+        if rel["x"] == which:
+            block, half = slot_place(co, rel)
             pltpu.make_async_copy(
-                whole.at[half, pl.ds(row, SLOT), piece],
-                targets[which].at[
-                    (index + (n,) if merged else (n,) + index) + (slice(None), piece)
-                ],
-                sems.at[m],
-            )
-        )
-    return found
+                whole.at[half, block],
+                targets[array].at[index + (n,) if merged else (n,) + index],
+                sem,
+            ).start()
+
+
+def wait_bytes(held, sem):
+    pltpu.make_async_copy(held, held, sem).wait()
 
 
 def weight_grads_kernel(co, *refs, orders, merged):
     count = len(orders)
     models, chans, refs = refs[:count], refs[count : 2 * count], refs[2 * count :]
     targets, (held, given, whole, sems_in, sems_out) = refs[:4], refs[4:]
-    half = whole.shape[3]
+    half = whole.shape[4]
     loads = []
     for n in range(count):
         for m, (source, place) in enumerate(((models[n], held), (chans[n], given))):
@@ -599,26 +564,19 @@
         def step(turn, _, n=n, order=order):
             at = co[4] ^ turn
             columns = pl.ds(pl.multiple_of(at * half, half), half)
-            whole[n, at] = dot(held[n], given[n, :, columns], TN).astype(BF)
+            found = dot(held[n], given[n, :, columns], TN).astype(BF)
+            whole[n, at] = found.reshape(16, SLOT, half)
             for which in (0, 1):
 
                 @pl.when(turn == which)
                 def _(which=which):
-                    copies = grad_copies(
-                        co, whole.at[n], targets, n, sems_out.at[n], order, slice(None), merged
-                    )
-                    for copy in copies[which]:
-                        copy.start()
+                    start_grads(co, whole.at[n], targets, n, sems_out.at[n], order, which, merged)
 
             return 0
 
         lax.fori_loop(0, 2, step, 0)
-    for n, order in enumerate(orders):
-        for copies in grad_copies(
-            co, whole.at[n], targets, n, sems_out.at[n], order, slice(None), merged
-        ):
-            for copy in copies:
-                copy.wait()
+    for n in range(count):
+        wait_bytes(whole.at[n], sems_out.at[n])
 
 
 def weight_grads(co, pairs, merged=False):
@@ -637,9 +595,9 @@
             scratch_shapes=[
                 pltpu.VMEM((count, tokens, width), BF),
                 pltpu.VMEM((count, tokens, width), BF),
-                pltpu.VMEM((count, 2, width, half), BF),
+                pltpu.VMEM((count, 2, 16, SLOT, half), BF),
                 pltpu.SemaphoreType.DMA((2 * count,)),
-                pltpu.SemaphoreType.DMA((count, 32)),
+                pltpu.SemaphoreType.DMA((count,)),
             ],
         ),
         out_shape=[jax.ShapeDtypeStruct(dims + (SLOT, half), BF)] * 4,
@@ -651,17 +609,16 @@
 def channel_back_kernel(co, dkv, mixed, hidden, active, *refs, layout, part, order):
     recept, refs = refs[: 2 * (1 - part)], refs[2 * (1 - part) :]
     arrays, refs = take_refs(refs, layout)
-    dkey, *targets, whole, grads, narrow, sems_in, sems = refs
+    dkey, *targets, grads, narrow, sems, whole, sems_in = refs
     j = pl.program_id(0)
     per_half = grads.shape[4] // WIDE
     columns = pl.ds(pl.multiple_of(lax.rem(j, per_half) * WIDE, WIDE), WIDE)
     turn = lax.div(j, per_half)
     half = co[4] ^ turn
-    loads = weight_copies(co, arrays, whole, sems_in, layout)
 
     @pl.when(j == 0)
     def _():
-        start_all(loads)
+        start_weight(co, arrays, whole, sems_in, layout)
 
     def keep(n, values):
         grads[n, half, :, :, columns] = values.astype(BF).reshape(16, SLOT, WIDE)
@@ -672,9 +629,9 @@
 
         @pl.when(j == which * per_half)
         def _(which=which):
-            wait_half(loads, which)
-
-    back = dot(dkv[...], whole[half, :, columns], NN)
+            wait_weight(co, whole, sems_in, layout, which)
+
+    back = dot(dkv[...], rows_of(whole, half, columns), NN)
     back = (2.0 * active[...].astype(F32) * back).astype(BF)
     dkey[...] = back
     keep(1, dot(mixed[...], back, TN))
@@ -688,35 +645,13 @@
             sems.at[2 + turn],
         )
 
-    def block_copies(turn, piece, size):
-        half = co[4] ^ turn
-        return [
+    if part == 0:
+        for n in (0, 1):
             pltpu.make_async_copy(
-                grads.at[n, half, :, :, pl.ds(piece, size)],
-                targets[0].at[:, half, :, pl.ds(n * wide + piece, size)],
+                grads.at[n, half, :, :, columns],
+                targets[0].at[:, half, :, pl.ds(pl.multiple_of(n * wide + columns.start, WIDE), WIDE)],
                 sems.at[n],
-            )
-            for n in (0, 1)
-        ]
-
-    def slot_copies(which, piece):
-        found = []
-        for m, (array, index, rel) in enumerate(rel_slots(order)):
-            if rel["x"] == which:
-                row, at = slot_place(co, rel)
-                for n in (0, 1):
-                    found.append(
-                        pltpu.make_async_copy(
-                            grads.at[n, at, lax.div(row, SLOT), :, piece],
-                            targets[array].at[index + (n, slice(None), piece)],
-                            sems.at[32 * n + m],
-                        )
-                    )
-        return found
-
-    if part == 0:
-        for copy in block_copies(turn, pl.multiple_of(lax.rem(j, per_half) * WIDE, WIDE), WIDE):
-            copy.start()
+            ).start()
 
         @pl.when(lax.rem(j, per_half) == 0)
         def _():
@@ -729,16 +664,22 @@
 
         @pl.when(turn == which)
         def _(which=which):
-            for copy in slot_copies(which, columns):
-                copy.start()
+            for array, index, rel in rel_slots(order):
+                if rel["x"] == which:
+                    block, at = slot_place(co, rel)
+                    for n in (0, 1):
+                        pltpu.make_async_copy(
+                            grads.at[n, at, block, :, columns],
+                            targets[array].at[index + (n, slice(None), columns)],
+                            sems.at[n],
+                        ).start()
 
     @pl.when(j == pl.num_programs(0) - 1)
     def _():
-        for which in (0, 1):
-            for copy in slot_copies(which, slice(None)) if part else block_copies(which, 0, wide):
-                copy.wait()
+        for n in (0, 1):
+            wait_bytes(grads.at[n], sems.at[n])
             if part == 0:
-                narrow_copy(which).wait()
+                narrow_copy(n).wait()
 
 
 def channel_back(co, dkv, mixed, hidden, active, recept, weight, half, part, order):
@@ -762,12 +703,11 @@
             out_specs=[pl.BlockSpec((tokens, WIDE), column_tile(per_half))]
             + [anywhere()] * (1 + 3 * part),
             scratch_shapes=[
-                pltpu.VMEM((2, width, half), BF),
                 pltpu.VMEM((2, 2, 16, SLOT, half), BF),
                 pltpu.VMEM((2, 16, SLOT, width // 2), BF),
-                pltpu.SemaphoreType.DMA((sem_count(weight),)),
-                pltpu.SemaphoreType.DMA((64,)),
-            ],
+                pltpu.SemaphoreType.DMA((4,)),
+            ]
+            + weight_scratch(weight),
         ),
         out_shape=[
             jax.ShapeDtypeStruct((tokens, 2 * half), BF),
@@ -787,25 +727,29 @@
 ):
     key_w, refs = take_refs(refs, layouts[0])
     recept_w, refs = take_refs(refs, layouts[1])
-    dmid_ref, dtime_ref, sums_ref, ww, rw, gk_ref, gr_ref, next_ref, sems, sems_r = refs
+    dmid_ref, dtime_ref, sums_ref, gk_ref, gr_ref, next_ref, ww, rw, sems, sems_r = refs
     i = pl.program_id(0)
-    copies = weight_copies(co, key_w, ww, sems, layouts[0])
-    recept = weight_copies(co, recept_w, rw, sems_r, layouts[1])
 
     @pl.when(i == 0)
     def _():
-        start_all(recept)
-        start_all(copies)
+        start_weight(co, recept_w, rw, sems_r, layouts[1])
+        start_weight(co, key_w, ww, sems, layouts[0])
         sums_ref[...] = jnp.zeros_like(sums_ref)
         next_ref[...] = jnp.zeros_like(next_ref)
         for half in (0, 1):
-            wait_half(recept, half)
-            wait_half(copies, half)
-
-    wide, narrow = dkey_a.shape[1] // 2, rw.shape[2]
-    gr_ref[...] = dot(drec[:, :narrow], rw[0], NT) + dot(drec[:, narrow:], rw[1], NT)
+            wait_weight(co, rw, sems_r, layouts[1], half)
+            wait_weight(co, ww, sems, layouts[0], half)
+
+    wide, narrow = dkey_a.shape[1] // 2, rw.shape[3]
+    gr_ref[...] = dot(drec[:, :narrow], rows_of(rw, 0), NT) + dot(
+        drec[:, narrow:], rows_of(rw, 1), NT
+    )
     gk_ref[...] = sum(
-        dot(part[:, half * wide : (half + 1) * wide], ww[half, :, n * wide : (n + 1) * wide], NT)
+        dot(
+            part[:, half * wide : (half + 1) * wide],
+            rows_of(ww, half, slice(n * wide, (n + 1) * wide)),
+            NT,
+        )
         for n, part in enumerate((dkey_a, dkey_b))
         for half in (0, 1)
     )
@@ -844,7 +788,7 @@
             dtime_ref[rows, strip] = dmid.astype(BF)
         return tuple(tuple(f) for f in firsts)
 
-    after = lax.fori_loop(0, steps, step, tuple(row_parts(next_ref, m) for m in (0, 1)), unroll=2)
+    after = lax.fori_loop(0, steps, step, tuple(row_parts(next_ref, m) for m in (0, 1)), unroll=4)
     for m, values in enumerate(after):
         for strip, value in zip(strips(width), values):
             next_ref[m : m + 1, strip] = value
@@ -871,15 +815,9 @@
             ]
             + [anywhere()] * len(arrays_of(weight, recept)),
             out_specs=[tall] * 2 + [pl.BlockSpec((4, 8, width), lambda i, co: (0, 0, 0))],
-            scratch_shapes=[
-                pltpu.VMEM((2, width, wide), BF),
-                pltpu.VMEM((2, width, width // 2), BF),
-                pltpu.VMEM((rows, width), F32),
-                pltpu.VMEM((rows, width), F32),
-                pltpu.VMEM((8, width), F32),
-                pltpu.SemaphoreType.DMA((sem_count(weight),)),
-                pltpu.SemaphoreType.DMA((sem_count(recept),)),
-            ],
+            scratch_shapes=[pltpu.VMEM((rows, width), F32)] * 2
+            + [pltpu.VMEM((8, width), F32)]
+            + weight_scratch(weight, recept),
         ),
         out_shape=[
             jax.ShapeDtypeStruct((tokens, width), F32),
@@ -895,23 +833,23 @@
     co, dtime, key_ref, val_ref, rec_ref, pa_ref, pb_ref, vec, masks, *refs, layout,
 ):
     arrays, refs = take_refs(refs, layout)
-    dkey_ref, dval_ref, drec_ref, sums_ref, ow, dg_ref, sems = refs
+    dkey_ref, dval_ref, drec_ref, sums_ref, dg_ref, ow, sems = refs
     j = pl.program_id(0)
-    per_half = ow.shape[2] // TILE
-    copies = weight_copies(co, arrays, ow, sems, layout)
+    per_half = ow.shape[3] // TILE
 
     @pl.when(j == 0)
     def _():
-        start_all(copies)
-        wait_half(copies, 0)
-
-    @pl.when(j == per_half)
-    def _():
-        wait_half(copies, 1)
+        start_weight(co, arrays, ow, sems, layout)
+
+    for which in (0, 1):
+
+        @pl.when(j == which * per_half)
+        def _(which=which):
+            wait_weight(co, ow, sems, layout, which)
 
     half = co[4] ^ lax.div(j, per_half)
     columns = pl.ds(pl.multiple_of(lax.rem(j, per_half) * TILE, TILE), TILE)
-    dg_ref[...] = dot(dtime[...], ow[half, :, columns], NN)
+    dg_ref[...] = dot(dtime[...], rows_of(ow, half, columns), NN)
 
     spread = (8, TILE)
     decay = jnp.broadcast_to(vec[2:3, :], spread)
@@ -922,7 +860,7 @@
 
     def group(start, state):
         rows = pl.ds(start, 8)
-        n1, n2, n4, nf, c0, ml = (twice(masks[n, rows, :]) for n in (0, 1, 2, 3, 4, 5))
+        n1, n2, n4, nf, c0, ml = (repeated(masks[n, rows, :], TILE) for n in (0, 1, 2, 3, 4, 5))
         key, val, rec, dg = key_ref[rows, :], val_ref[rows, :], rec_ref[rows, :], dg_ref[rows, :]
         pa, pb = pa_ref[rows, :], pb_ref[rows, :]
         power = jnp.exp(key)
@@ -962,7 +900,7 @@
         return state
 
     zero = jnp.zeros(spread, F32)
-    _, _, first_sum, decay_sum = lax.fori_loop(0, steps, step, (zero,) * 4, unroll=2)
+    _, _, first_sum, decay_sum = lax.fori_loop(0, steps, step, (zero,) * 4, unroll=4)
     sums_ref[0] = -r1 * jnp.exp(decay) * decay_sum
     sums_ref[1] = first_sum
 
@@ -986,11 +924,7 @@
             + [anywhere()] * len(weight[1]),
             out_specs=[block] * 3
             + [pl.BlockSpec((2, 8, TILE), lambda j, co: (0,) + tile(j, co))],
-            scratch_shapes=[
-                pltpu.VMEM((2, width, half), BF),
-                pltpu.VMEM((tokens, TILE), F32),
-                pltpu.SemaphoreType.DMA((32,)),
-            ],
+            scratch_shapes=[pltpu.VMEM((tokens, TILE), F32)] + weight_scratch(weight),
         ),
         out_shape=[jax.ShapeDtypeStruct((tokens, width), BF)] * 3
         + [jax.ShapeDtypeStruct((2, 8, width), F32)],
@@ -1000,32 +934,35 @@
 
 
 def input_back_kernel(
-    co, dkey, dval, drec, x_ref, dmid_ref, lead_ref, vec_ref, after_ref, _, *refs, layouts,
+    co, dkey, dval, drec, x_ref, dmid_ref, lead_ref, vec_ref, after_ref, *refs, layouts, part,
 ):
+    count = 1 if part else 3
+    before, refs = refs[:count], refs[count + 1 :]
     key_w, refs = take_refs(refs, layouts[0])
     val_w, refs = take_refs(refs, layouts[1])
     rec_w, refs = take_refs(refs, layouts[2])
-    out_ref, sums_ref, next_ref, kw, vw, rw, gk_ref, gv_ref, gr_ref, sems = refs
+    out_ref, totals_ref, next_ref, sums_ref, gk_ref, gv_ref, gr_ref, *scratch = refs
+    wholes, sems = scratch[:3], scratch[3:]
     i = pl.program_id(0)
-    groups = [
-        weight_copies(co, arrays, whole, sems.at[n], layout)
-        for n, (arrays, whole, layout) in enumerate(zip((key_w, val_w, rec_w), (kw, vw, rw), layouts))
-    ]
 
     @pl.when(i == 0)
     def _():
-        for copies in groups:
-            start_all(copies)
+        for arrays, whole, sem, layout in zip((key_w, val_w, rec_w), wholes, sems, layouts):
+            start_weight(co, arrays, whole, sem, layout)
         sums_ref[...] = jnp.zeros_like(sums_ref)
         next_ref[...] = after_ref[...]
 
-    half = kw.shape[2]
-    for copies, grad, whole, out in zip(
-        groups, (dkey, dval, drec), (kw, vw, rw), (gk_ref, gv_ref, gr_ref)
-    ):
-        wait_at_first(copies, 0)
-        wait_at_first(copies, 1)
-        out[...] = dot(grad[:, :half], whole[0], NT) + dot(grad[:, half:], whole[1], NT)
+    half = wholes[0].shape[3]
+    for n, (grad, out) in enumerate(((dkey, gk_ref), (dval, gv_ref), (drec, gr_ref))):
+
+        @pl.when(i == 0)
+        def _(n=n):
+            for which in (0, 1):
+                wait_weight(co, wholes[n], sems[n], layouts[n], which)
+
+        out[...] = dot(grad[:, :half], rows_of(wholes[n], 0), NT) + dot(
+            grad[:, half:], rows_of(wholes[n], 1), NT
+        )
     steps = x_ref.shape[0] // ROWS
     width = x_ref.shape[1]
 
@@ -1061,13 +998,28 @@
             )
         return tuple(tuple(f) for f in firsts)
 
-    after = lax.fori_loop(0, steps, step, tuple(row_parts(next_ref, m) for m in range(3)), unroll=2)
+    after = lax.fori_loop(0, steps, step, tuple(row_parts(next_ref, m) for m in range(3)), unroll=4)
     for m, values in enumerate(after):
         for strip, value in zip(strips(width), values):
             next_ref[m : m + 1, strip] = value
 
-
-def input_back(co, grads, x, dmid, lead, vectors, weights, part, after, found):
+    @pl.when(i == pl.num_programs(0) - 1)
+    def _():
+        if part:
+            totals_ref[...] = before[0][...]
+        else:
+            time_sums, channel_sums, loss_sums = before
+            totals_ref[...] = jnp.zeros_like(totals_ref)
+            for n in range(2):
+                totals_ref[2 + n : 3 + n, :] = jnp.sum(time_sums[n], axis=0, keepdims=True)
+            for n in range(4):
+                totals_ref[7 + n : 8 + n, :] = jnp.sum(channel_sums[n], axis=0, keepdims=True)
+            totals_ref[11:12, :] = jnp.sum(loss_sums[...], axis=0, keepdims=True)
+        for n, row in enumerate((0, 1, 4, 5, 6)):
+            totals_ref[row : row + 1, :] += jnp.sum(sums_ref[n], axis=0, keepdims=True)
+
+
+def input_back(co, grads, x, dmid, lead, vectors, weights, part, after, before, found):
     tokens, width = x.shape
     rows = tokens // 4
 
@@ -1077,7 +1029,7 @@
     tall = pl.BlockSpec((rows, width), at)
     edge = pl.BlockSpec((8, width), lambda i, co: (0, 0))
     return pl.pallas_call(
-        functools.partial(input_back_kernel, layouts=[w[0] for w in weights]),
+        functools.partial(input_back_kernel, layouts=[w[0] for w in weights], part=part),
         grid_spec=pltpu.PrefetchScalarGridSpec(
             num_scalar_prefetch=1,
             grid=(2,),
@@ -1086,27 +1038,26 @@
                 pl.BlockSpec((rows, LANES), at),
                 pl.BlockSpec(vectors.shape, lambda i, co: (0, 0)),
                 edge,
+                *(
+                    pl.BlockSpec(sums.shape, lambda i, co, dims=sums.ndim: (0,) * dims)
+                    for sums in before
+                ),
                 anywhere(),
             ]
             + [anywhere()] * len(arrays_of(*weights)),
-            out_specs=[
-                tall,
-                pl.BlockSpec((5, 8, width), lambda i, co: (0, 0, 0)),
-                edge,
-            ],
-            scratch_shapes=[pltpu.VMEM((2, width, width // 2), BF)] * 3
-            + [pltpu.VMEM((rows, width), F32)] * 3
-            + [pltpu.SemaphoreType.DMA((3, 32))],
+            out_specs=[tall, pl.BlockSpec((12, width), lambda i, co: (0, 0)), edge],
+            scratch_shapes=[pltpu.VMEM((5, 8, width), F32)]
+            + [pltpu.VMEM((rows, width), F32)] * 3 + weight_scratch(*weights),
         ),
         out_shape=[
             jax.ShapeDtypeStruct((tokens, width), F32),
-            jax.ShapeDtypeStruct((5, 8, width), F32),
+            jax.ShapeDtypeStruct((12, width), F32),
             jax.ShapeDtypeStruct((8, width), F32),
         ],
-        input_output_aliases={9: 0},
+        input_output_aliases={9 + len(before): 0},
         compiler_params=params(),
         cost_estimate=cost(4, 16 << 20),
-    )(co, *grads, x, dmid, lead, vectors, after, found, *arrays_of(*weights))
+    )(co, *grads, x, dmid, lead, vectors, after, *before, found, *arrays_of(*weights))
 
 
 def seal(*values):
@@ -1466,9 +1417,9 @@
     order_b, order_c = "wuyx", "wuyx"
     edge = jnp.zeros((8, width), F32)
 
-    def input_back_part(dmix, part, after, found):
+    def input_back_part(dmix, part, after, before, found):
         return input_back(
-            co, dmix, inputs, dmid, lead, vectors, (key_w, value_w, recept_w), part, after, found
+            co, dmix, inputs, dmid, lead, vectors, (key_w, value_w, recept_w), part, after, before, found
         )
 
     if fast:
@@ -1497,10 +1448,10 @@
         group_t = Reduce(found, three_orders)
         (dmix,) = seal_all((group_b, group_c, group_t), dmix)
         step_all(group_b, group_c, group_t)
-        found, sums_l, edge = input_back_part(dmix, 0, edge, dres)
-        (dmix, edge, found) = seal_all((group_b, group_c, group_t), dmix, edge, found)
-        step_all(group_b, group_c, group_t)
-        input_grad, sums_u, _ = input_back_part(dmix, 1, edge, found)
+        found, totals, edge = input_back_part(dmix, 0, edge, (sums_t, sums2, loss_rows), dres)
+        (dmix, edge, found) = seal_all((group_c, group_t), dmix, edge, found)
+        step_all(group_c, group_t)
+        input_grad, totals, _ = input_back_part(dmix, 1, edge, (totals,), found)
     else:
         dkey_1, *found = back(dkv, mixed_k2, hidden, active, (), cvalue_w[1], split, 1, order_b)
         dkey_0, blocks = back(
@@ -1526,24 +1477,27 @@
         *dmix, sums_t = time_back(co, dtime, saved, vectors, masks_up, output_w)
         found = weight_grads(co, [(m, d, order) for m, d, order in zip(mixed, dmix, three_orders)])
         key_g, val_g, rec_g = reduce_plain(found, three_orders)
-        found, sums_l, edge = input_back_part(dmix, 0, edge, dres)
-        input_grad, sums_u, _ = input_back_part(dmix, 1, edge, found)
-
-    rows = jnp.concatenate([sums_l[:2] + sums_u[:2], sums_t, sums_l[2:] + sums_u[2:], sums2, loss_rows[None]])
-    totals = jnp.sum(rows, axis=1)
+        found, totals, edge = input_back_part(dmix, 0, edge, (sums_t, sums2, loss_rows), dres)
+        input_grad, totals, _ = input_back_part(dmix, 1, edge, (totals,), found)
+
     if fast:
         (totals,) = seal_all((group_b, group_c, group_t), totals)
-        for axes in ("wc", "xy", "u"):
-            step_all(*[group for group in (group_c, group_t) if group.done < 5])
+        for axes in ("wc", "y", "xu"):
+            step_all(*[group for group in (group_t, group_c, group_b) if group.done < 5])
             for axis in axes:
                 totals = totals + swap(totals, axis)
-            totals, blocks = seal_all((group_c, group_t), totals, blocks)
-            if axes == "wc":
+            if axes == "y":
                 blocks = pair_sum(blocks)
-        cvalue_g, ckey_g = (
-            jnp.concatenate([blocks[:, n * split : (n + 1) * split], found], axis=1)
-            for n, found in enumerate(group_b.finish())
-        )
+                totals, blocks = seal_all((group_b, group_c, group_t), totals, blocks)
+                cvalue_g, ckey_g = (
+                    jnp.concatenate([blocks[:, n * split : (n + 1) * split], found], axis=1)
+                    for n, found in enumerate(group_b.finish())
+                )
+                cvalue_g = cvalue_g.T
+            elif axes == "wc":
+                totals, blocks = seal_all((group_c, group_t), totals, blocks)
+        totals, cvalue_g, ckey_g = seal_all((group_t,), totals, cvalue_g, ckey_g)
+        cvalue_g = cvalue_g.T
         (output_g,) = group_c.finish()
         crecept_g = blocks[:, 2 * split :]
         key_g, val_g, rec_g = group_t.finish()

time: 478 us -> 463 us (0.969)
  Pallas kernels: 251 us -> 237 us
  other arithmetic: 43.8 us -> 37.8 us
  waiting for transfers between devices: 74.2 us -> 79.3 us
  transfers between devices with their start and end apart: 58 -> 58, of which waited for: 20 -> 22; matrix products, arithmetic and copies ran while one was open for 13% -> 13% of each run, Pallas kernels for 43% -> 42%
where the time goes in v5:
time: 463 us; the launch traced here: 458 us
  Pallas kernels  237 us (51%)
  waiting for transfers between devices  79.3 us (17%)
  starting transfers between devices  55.6 us (12%)
  other arithmetic  37.8 us (8%)
  local copies, waits for them, and re-layouts  29.4 us (6%)
  between operations  18.2 us (4%)
    ppermute x55, waiting for transfers between devices, swap(): return lax.ppermute(values, axis, SWAP)  65 us
    ppermute x55, starting transfers between devices, swap(): return lax.ppermute(values, axis, SWAP)  55.3 us
    pallas_call x2, Pallas kernels, channel_back(): pl.pallas_call(functools.partial(channel_back_kernel, layout=weight[0], p...  46.9 us
    pallas_call x1, Pallas kernels, middle_back(): pl.pallas_call(functools.partial(middle_back_kernel, layouts=[weight[0],...  30.9 us
    pallas_call x2, Pallas kernels, input_back(): pl.pallas_call(functools.partial(input_back_kernel, layouts=[w[0] for w i...  30.5 us
    pallas_call x1, Pallas kernels, time_forward(): pl.pallas_call(functools.partial(time_forward_kernel, layouts=[w[0] for w...  26.2 us
    pallas_call x1, Pallas kernels, result_step(): pl.pallas_call(functools.partial(result_kernel, layouts=[weight[0], recep...  23.6 us
    pallas_call x1, Pallas kernels, time_back(): pl.pallas_call(functools.partial(time_back_kernel, layout=weight[0]), gri...  23.4 us
  transfers between devices with their start and end apart: 58, of which 22 were waited for; matrix products, arithmetic and copies ran while one was open for 13% of the time, Pallas kernels for 42%

profile of v5, /device:TPU:0, one launch (start us, length us, event | category | flops | bytes accessed | tf_op | source)
XLA Modules:
  0.0 457.5 jit_solution(15576838582818436443)
XLA Ops:
  7.2 1.7 pad_maximum_fusion.10
  10.0 4.1 collective-permute-start
  15.2 2.9 collective-permute-start.2
  21.4 2.7 concatenate.130
  25.6 2.6 constant_dynamic-slice_fusion.1
  42.6 2.0 collective-permute-done.5
  46.3 2.8 collective-permute-done.6
  49.1 10.3 %collective-permute-done.7.theirs_ref = bf16[1024,512]{1,0:T(8,128)(2,1)S(1)} collective-permute-done((bf16[1024,512]{1,0:T(8,128)(2,1)S(1)}, bf16[1024,512]{1,0:T(8,128)(2,1)S(1)}, u32[]{:S(2)}, u32[]{:S(2)}) %collective-permute-start.7) | collective-permute-done | bytes 1048608 | tf_op jit(solution)/shard_map/ppermute | solution.py:1068
  59.5 1.9 broadcast_in_dim.134.masks
  61.4 2.2 broadcast_in_dim.142.masks
  66.6 1.6 collective-permute-start.8
  70.5 6.6 %collective-permute-done.11 = f32[16,512]{1,0:T(8,128)S(1)} collective-permute-done((f32[16,512]{1,0:T(8,128)S(1)}, f32[16,512]{1,0:T(8,128)S(1)}, u32[]{:S(2)}, u32[]{:S(2)}) %collective-permute-start.11) | collective-permute-done | bytes 32800 | tf_op jit(solution)/shard_map/ppermute | solution.py:1068
  79.2 4.0 collective-permute-done.10
  83.3 1.8 collective-permute-start.12
  85.3 1.8 collective-permute-start.14
  87.1 7.4 %shard_map.364 = (bf16[1024,1024]{1,0:T(8,128)(2,1)}, bf16[1024,1024]{1,0:T(8,128)(2,1)}, bf16[1024,1024]{1,0:T(8,128)(2,1)}) custom-call(bf16[1024,1024]{1,0:T(8,128)(2,1)} %x_ref.7, f32[1024,128]{1,0:T(8,128)} %broadcast_in_dim.143.carry_ref, f32[16,1024]{1,0:T(8,128)} %maximum_select_fusion.1.vec_ref.vec), custom_call_target="tpu_custom_call" | custom-call | bytes 83886 | tf_op jit(solution)/shard_map/pallas_call | solution.py:211
  94.5 5.2 %collective-permute-done.12 = bf16[2,2,64,1024]{3,2,1,0:T(8,128)(2,1)S(1)} collective-permute-done((bf16[2,2,64,1024]{3,2,1,0:T(8,128)(2,1)S(1)}, bf16[2,2,64,1024]{3,2,1,0:T(8,128)(2,1)S(1)}, u32[]{:S(2)}, u32[]{:S(2)}) %collective-permute-start.12) | collective-permute-done | bytes 524320 | tf_op jit(solution)/shard_map/ppermute | solution.py:1068
  100.9 9.1 %all-gather.5.cloned.1.call-done = bf16[2048,2048]{1,0:T(8,128)(2,1)} async-done(((bf16[64,2048]{1,0:T(8,128)(2,1)}), bf16[2048,2048]{1,0:T(8,128)(2,1)}) %all-gather.5.cloned.1.call-update) | async-done | bytes 8388624 | tf_op jit(solution)/shard_map/all_gather | solution.py:1348
  110.4 1.9 collective-permute-start.15
  116.1 1.7 collective-permute-start.21
  117.8 26.2 %shard_map.365 = (f32[1024,1024]{1,0:T(8,128)}, f32[1024,1024]{1,0:T(8,128)}, f32[1024,1024]{1,0:T(8,128)}, f32[1024,1024]{1,0:T(8,128)}, f32[1024,1024]{1,0:T(8,128)}, /*index=5*/bf16[1024,1024]{1,0:T(8,128)(2,1)}) custom-call(s32[5]{0:T(128)} %stack.159.co, bf16[1024,1024]{1,0:T(8,128)(2,1)} %get-tuple-element.257.mk.refs_0_, ...), custom_call_target="tpu_custom_call" | custom-call | flops 171798688 | bytes 356515 | tf_op jit(solution)/shard_map/pallas_call | solution.py:316
  145.2 12.4 %shard_map.366 = (f32[1024,1024]{1,0:T(8,128)}, bf16[1024,1024]{1,0:T(8,128)(2,1)}, bf16[1024,1024]{1,0:T(8,128)(2,1)}) custom-call(s32[5]{0:T(128)} %stack.159.co, bf16[1024,1024]{1,0:T(8,128)(2,1)} %get-tuple-element.269.gated.refs_1_, bf16[1024,1024]{1,0:T(8,128)(2,1)} %x_ref.7, f32[1024,128]{1,0:T(8,128)} %broadcast_in_dim.143.carry_ref, ...), custom_call_target="tpu_custom_call" | custom-call | flops 64424508 | bytes 146800 | tf_op jit(solution)/shard_map/pallas_call | solution.py:383
  161.0 17.4 %shard_map.367 = (bf16[1024,4096]{1,0:T(8,128)(2,1)}, bf16[1024,4096]{1,0:T(8,128)(2,1)}) custom-call(s32[5]{0:T(128)} %stack.159.co, bf16[1024,1024]{1,0:T(8,128)(2,1)} %get-tuple-element.275.mk.mixed, bf16[2,2,2,64,1024]{4,3,2,1,0:T(8,128)(2,1)} %copy-done.1, bf16[2,2,2,64,1024]{4,3,2,1,0:T(8,128)(2,1)} %collective-permute-done.15.refs_1_, ...), custom_call_target="tpu_custom_call" | custom-call | flops 96636768 | bytes 272629 | tf_op jit(solution)/shard_map/pallas_call | solution.py:437
  178.4 5.2 %all-gather.7.cloned.1.call-done = bf16[2048,1536]{1,0:T(8,128)(2,1)} async-done(((bf16[64,1536]{1,0:T(8,128)(2,1)}), bf16[2048,1536]{1,0:T(8,128)(2,1)}) %all-gather.7.cloned.1.call-update) | async-done | bytes 6291472 | tf_op jit(solution)/shard_map/all_gather | solution.py:1363
  183.6 23.6 %shard_map.368 = (bf16[2048,512]{1,0:T(8,128)(2,1)}, bf16[1024,512]{1,0:T(8,128)(2,1)}, f32[1024,1024]{1,0:T(8,128)}, bf16[1024,1024]{1,0:T(8,128)(2,1)}, bf16[1024,1024]{1,0:T(8,128)(2,1)}, /*index=5*/f32[8,1024]{1,0:T(8,128)}) custom-call(s32[5]{0:T(128)} %copy-done.34, f32[1]{0:T(128)} %bitcast.38.scale, bf16[1024,4096]{1,0:T(8,128)(2,1)} %get-tuple-element.286.hidden, ...), custom_call_target="tpu_custom_call" | custom-call | flops 150323856 | bytes 398458 | tf_op jit(solution)/shard_map/pallas_call | solution.py:508
  207.2 21.5 %shard_map.369 = (bf16[1024,2048]{1,0:T(8,128)(2,1)}, bf16[2,2,2,2,64,1024]{5,4,3,2,1,0:T(8,128)(2,1)}, bf16[2,2,2,2,64,1024]{5,4,3,2,1,0:T(8,128)(2,1)}, bf16[2...) custom-call(s32[5]{0:T(128)} %stack.159.co, bf16[1024,1024]{1,0:T(8,128)(2,1)} %get-tuple-element.307.dkv, ...), custom_call_target="tpu_custom_call" | custom-call | flops 141733920 | bytes 293601 | tf_op jit(solution)/shard_map/pallas_call | solution.py:695
  230.8 25.4 %shard_map.370 = (bf16[1024,2048]{1,0:T(8,128)(2,1)}, bf16[16,2,64,2560]{3,2,1,0:T(8,128)(2,1)}) custom-call(s32[5]{0:T(128)} %stack.159.co, bf16[1024,1024]{1,0:T(8,128)(2,1)} %get-tuple-element.307.dkv, bf16[1024,1024]{1,0:T(8,128)(2,1)} %get-tuple-element.275.mk.mixed, bf16[1024,4096]{1,0:T(8,128)(2,1)} %get-tuple-element.286.hidden, ...), custom_call_target="tpu_custom_call" | custom-call | flops 141733920 | bytes 293601 | tf_op jit(solution)/shard_map/pallas_call | solution.py:695
  257.8 2.6 add.324
  261.0 30.9 %shard_map.371 = (f32[1024,1024]{1,0:T(8,128)}, bf16[1024,1024]{1,0:T(8,128)(2,1)}, f32[4,8,1024]{2,1,0:T(8,128)}) custom-call(s32[5]{0:T(128)} %stack.159.co, bf16[1024,2048]{1,0:T(8,128)(2,1)} %get-tuple-element.316.dkey_a, bf16[1024,2048]{1,0:T(8,128)(2,1)} %get-tuple-element.317.dkey_b, bf16[1024,1024]{1,0:T(8,128)(2,1)} %get-tuple-element.308.refs_1_.drec, ...), custom_call_target="tpu_custom_call" | custom-call | flops 171798688 | bytes 377487 | tf_op jit(solution)/shard_map/pallas_call | solution.py:802
  291.9 6.5 %shard_map.372 = (bf16[2,2,2,1,64,512]{5,4,3,2,1,0:T(8,128)(2,1)}, bf16[2,2,2,1,64,512]{5,4,3,2,1,0:T(8,128)(2,1)}, bf16[2,2,2,1,64,512]{5,4,3,2,1,0:T(8,128)(2,1)}, bf16[2,2,2,1,64,512]{5,4,3,2,1,0:T(8,128)(2,1)}) custom-call(s32[5]{0:T(128)} %stack.159.co, bf16[1024,1024]{1,0:T(8,128)(2,1)} %get-tuple-element.335.refs_0_.dtime, ...), custom_call_target="tpu_custom_call" | custom-call | flops 25769804 | bytes 62914 | tf_op jit(solution)/shard_map/pallas_call | solution.py:588
  299.5 8.5 %collective-permute-done.27 = bf16[2,2,2,2,64,1024]{5,4,3,2,1,0:T(8,128)(2,1)S(1)} collective-permute-done((bf16[2,2,2,2,64,1024]{5,4,3,2,1,0:T(8,128)(2,1)S(1)}, bf16[2,2,2,2,64,1024]{5,4,3,2,1,0:T(8,128)(2,1)S(1)}, u32[]{:S(2)}, u32[]{:S(2)}) %collective-permute-start.27) | collective-permute-done | bytes 2097184 | tf_op jit(solution)/shard_map/ppermute | solution.py:1068
  308.5 3.0 fusion.1
  312.1 23.4 %shard_map.373 = (bf16[1024,1024]{1,0:T(8,128)(2,1)}, bf16[1024,1024]{1,0:T(8,128)(2,1)}, bf16[1024,1024]{1,0:T(8,128)(2,1)}, f32[2,8,1024]{2,1,0:T(8,128)}) custom-call(s32[5]{0:T(128)} %stack.159.co, bf16[1024,1024]{1,0:T(8,128)(2,1)} %get-tuple-element.335.refs_0_.dtime, f32[1024,1024]{1,0:T(8,128)} %get-tuple-element.336.key_ref, ...), custom_call_target="tpu_custom_call" | custom-call | flops 193273536 | bytes 356515 | tf_op jit(solution)/shard_map/pallas_call | solution.py:913
  338.3 11.9 %shard_map.374 = (bf16[3,2,2,2,64,512]{5,4,3,2,1,0:T(8,128)(2,1)}, bf16[3,2,2,2,64,512]{5,4,3,2,1,0:T(8,128)(2,1)}, bf16[3,2,2,2,64,512]{5,4,3,2,1,0:T(8,128)(2,1)}, bf16[3,2,2,2,64,512]{5,4,3,2,1,0:T(8,128)(2,1)}) custom-call(s32[5]{0:T(128)} %stack.159.co, bf16[1024,1024]{1,0:T(8,128)(2,1)} %get-tuple-element.257.mk.refs_0_, ...), custom_call_target="tpu_custom_call" | custom-call | flops 77309408 | bytes 188743 | tf_op jit(solution)/shard_map/pallas_call | solution.py:588
  356.8 15.3 %shard_map.375 = (f32[1024,1024]{1,0:T(8,128)}, f32[12,1024]{1,0:T(8,128)}, f32[8,1024]{1,0:T(8,128)}) custom-call(s32[5]{0:T(128)} %stack.159.co, bf16[1024,1024]{1,0:T(8,128)(2,1)} %get-tuple-element.381.refs_3_.dkey, bf16[1024,1024]{1,0:T(8,128)(2,1)} %get-tuple-element.382.refs_4_.dval, ...), custom_call_target="tpu_custom_call", output_to_operand_aliasing={{0}: (12, {})} | custom-call | flops 85899344 | bytes 167772 | tf_op jit(solution)/shard_map/pallas_call | solution.py:1031
  373.3 2.6 add_bitcast_fusion
  380.1 1.8 collective-permute-start.36
  381.9 15.2 %shard_map.376 = (f32[1024,1024]{1,0:T(8,128)}, f32[12,1024]{1,0:T(8,128)}, f32[8,1024]{1,0:T(8,128)}) custom-call(s32[5]{0:T(128)} %stack.159.co, bf16[1024,1024]{1,0:T(8,128)(2,1)} %get-tuple-element.381.refs_3_.dkey, bf16[1024,1024]{1,0:T(8,128)(2,1)} %get-tuple-element.382.refs_4_.dval, ...), custom_call_target="tpu_custom_call", output_to_operand_aliasing={{0}: (10, {})} | custom-call | flops 85899344 | bytes 167772 | tf_op jit(solution)/shard_map/pallas_call | solution.py:1031
  397.2 6.4 %collective-permute-done.36 = bf16[2,1,64,512]{3,2,0,1:T(8,128)(2,1)S(1)} collective-permute-done((bf16[2,1,64,512]{3,2,0,1:T(8,128)(2,1)S(1)}, bf16[2,1,64,512]{3,2,0,1:T(8,128)(2,1)S(1)}, u32[]{:S(2)}, u32[]{:S(2)}) %collective-permute-start.36) | collective-permute-done | bytes 131104 | tf_op jit(solution)/shard_map/ppermute | solution.py:1068
  404.4 1.8 collective-permute-start.41
  406.2 2.2 fusion.4
  411.1 2.0 collective-permute-start.45
  414.1 2.3 collective-permute-done.45
  417.7 2.1 collective-permute-start.40
  427.4 3.3 collective-permute-done.50
  431.6 2.5 collective-permute-done.51
  435.8 2.2 collective-permute-start.52
  444.0 3.0 collective-permute-done.54
  (300 shorter events, 83.7 us)
Async XLA Ops:
  7.2 102.8 %all-gather.5.cloned.1.call-start = ((), (), s32[]{:S(2)}) async-start(), calls=%async_computation.2 | async-start | bytes 8650752 | tf_op jit(solution)/shard_map/all_gather | solution.py:1348
  8.9 174.6 %all-gather.7.cloned.1.call-start = ((), (), s32[]{:S(2)}) async-start(), calls=%async_computation.3 | async-start | bytes 6488064 | tf_op jit(solution)/shard_map/all_gather | solution.py:1363
  10.0 39.1 %collective-permute-start = (bf16[64,1024]{1,0:T(8,128)(2,1)S(1)}, bf16[64,1024]{1,0:T(8,128)(2,1)S(1)}, u32[]{:S(2)}, u32[]{:S(2)}) collective-permute-start(bf16[64,1024]{1,0:T(8,128)(2,1)S(1)} %get-tuple-element.231), channel_id=1, source_target_pairs={{0,16},{16,0},{1,17},{17,1},{2,18},{18,2},{3,19},{19,3},{4,20},{20... | collective-permute-start | bytes 393224 | tf_op jit(solution)/shard_map/ppermute | solution.py:1068
  14.1 35.0 %collective-permute-start.1 = (bf16[64,1024]{1,0:T(8,128)(2,1)S(1)}, bf16[64,1024]{1,0:T(8,128)(2,1)S(1)}, u32[]{:S(2)}, u32[]{:S(2)}) collective-permute-start(bf16[64,1024]{1,0:T(8,128)(2,1)S(1)} %get-tuple-element.233), channel_id=1, source_target_pairs={{0,16},{16,0},{1,17},{17,1},{2,18},{18,2},{3,19},{19,3},{4,20},{20... | collective-permute-start | bytes 393224 | tf_op jit(solution)/shard_map/ppermute | solution.py:1068
  15.2 34.0 %collective-permute-start.2 = (bf16[64,1024]{1,0:T(8,128)(2,1)S(1)}, bf16[64,1024]{1,0:T(8,128)(2,1)S(1)}, u32[]{:S(2)}, u32[]{:S(2)}) collective-permute-start(bf16[64,1024]{1,0:T(8,128)(2,1)S(1)} %get-tuple-element.235), channel_id=1, source_target_pairs={{0,16},{16,0},{1,17},{17,1},{2,18},{18,2},{3,19},{19,3},{4,20},{20... | collective-permute-start | bytes 393224 | tf_op jit(solution)/shard_map/ppermute | solution.py:1068
  24.1 14.7 %collective-permute-start.3 = (f32[16,32]{1,0:T(8,128)}, f32[16,32]{1,0:T(8,128)}, u32[]{:S(2)}, u32[]{:S(2)}) collective-permute-start(f32[16,32]{1,0:T(8,128)} %concatenate.130), channel_id=1, source_target_pairs={{0,1},{1,0},{2,3},{3,2},{4,5},{5,4},{6,7},{7,6},{8,9},{9,8},{10,11... | collective-permute-start | bytes 6152 | tf_op jit(solution)/shard_map/ppermute | solution.py:1068
  28.2 31.2 %collective-permute-start.7 = (bf16[1024,512]{1,0:T(8,128)(2,1)S(1)}, bf16[1024,512]{1,0:T(8,128)(2,1)S(1)}, u32[]{:S(2)}, u32[]{:S(2)}) collective-permute-start(bf16[1024,512]{1,0:T(8,128)(2,1)S(1)} %get-tuple-element.452), channel_id=1, source_target_pairs={{0,1},{1,0},{2,3},{3,2},{4,5},{5,4},{6,7},{7,6},{8,9},{9,8},{10,11... | collective-permute-start | bytes 3145736 | tf_op jit(solution)/shard_map/ppermute | solution.py:1068
  66.6 11.1 %collective-permute-start.8 = (bf16[2,64,1024]{2,1,0:T(8,128)(2,1)S(1)}, bf16[2,64,1024]{2,1,0:T(8,128)(2,1)S(1)}, u32[]{:S(2)}, u32[]{:S(2)}) collective-permute-start(bf16[2,64,1024]{2,1,0:T(8,128)(2,1)S(1)} %pad_maximum_fusion.7), channel_id=1, source_target_pairs={{0,8},{8,0},{1,9},{9,1},{2,10},{10,2},{3,11},{11,3},{4,12},{12,4},... | collective-permute-start | bytes 786440 | tf_op jit(solution)/shard_map/ppermute | solution.py:1068
  68.3 10.9 %collective-permute-start.9 = (bf16[2,64,1024]{2,1,0:T(8,128)(2,1)S(1)}, bf16[2,64,1024]{2,1,0:T(8,128)(2,1)S(1)}, u32[]{:S(2)}, u32[]{:S(2)}) collective-permute-start(bf16[2,64,1024]{2,1,0:T(8,128)(2,1)S(1)} %pad_maximum_fusion.8), channel_id=1, source_target_pairs={{0,1},{1,0},{2,3},{3,2},{4,5},{5,4},{6,7},{7,6},{8,9},{9,8},{10,11... | collective-permute-start | bytes 786440 | tf_op jit(solution)/shard_map/ppermute | solution.py:1068
  68.9 14.3 %collective-permute-start.10 = (bf16[2,64,1024]{2,1,0:T(8,128)(2,1)S(1)}, bf16[2,64,1024]{2,1,0:T(8,128)(2,1)S(1)}, u32[]{:S(2)}, u32[]{:S(2)}) collective-permute-start(bf16[2,64,1024]{2,1,0:T(8,128)(2,1)S(1)} %pad_maximum_fusion.9), channel_id=1, source_target_pairs={{0,4},{4,0},{1,5},{5,1},{2,6},{6,2},{3,7},{7,3},{8,12},{12,8},{9,1... | collective-permute-start | bytes 786440 | tf_op jit(solution)/shard_map/ppermute | solution.py:1068
  83.3 16.4 %collective-permute-start.12 = (bf16[2,2,64,1024]{3,2,1,0:T(8,128)(2,1)S(1)}, bf16[2,2,64,1024]{3,2,1,0:T(8,128)(2,1)S(1)}, u32[]{:S(2)}, u32[]{:S(2)}) collective-permute-start(bf16[2,2,64,1024]{3,2,1,0:T(8,128)(2,1)S(1)} %pad_maximum_fusion.3), channel_id=1, source_target_pairs={{0,4},{4,0},{1,5},{5,1},{2,6},{6,2},{3,7},{7,3},{8,12},{12,8},{9,1... | collective-permute-start | bytes 1572872 | tf_op jit(solution)/shard_map/ppermute | solution.py:1068
  85.1 14.6 %collective-permute-start.13 = (bf16[2,2,64,1024]{3,2,1,0:T(8,128)(2,1)S(1)}, bf16[2,2,64,1024]{3,2,1,0:T(8,128)(2,1)S(1)}, u32[]{:S(2)}, u32[]{:S(2)}) collective-permute-start(bf16[2,2,64,1024]{3,2,1,0:T(8,128)(2,1)S(1)} %pad_maximum_fusion.4), channel_id=1, source_target_pairs={{0,8},{8,0},{1,9},{9,1},{2,10},{10,2},{3,11},{11,3},{4,12},{12,4},... | collective-permute-start | bytes 1572872 | tf_op jit(solution)/shard_map/ppermute | solution.py:1068
  85.3 15.6 %collective-permute-start.14 = (bf16[2,2,64,1024]{3,2,1,0:T(8,128)(2,1)S(1)}, bf16[2,2,64,1024]{3,2,1,0:T(8,128)(2,1)S(1)}, u32[]{:S(2)}, u32[]{:S(2)}) collective-permute-start(bf16[2,2,64,1024]{3,2,1,0:T(8,128)(2,1)S(1)} %pad_maximum_fusion.5), channel_id=1, source_target_pairs={{0,1},{1,0},{2,3},{3,2},{4,5},{5,4},{6,7},{7,6},{8,9},{9,8},{10,11... | collective-permute-start | bytes 1572872 | tf_op jit(solution)/shard_map/ppermute | solution.py:1068
  110.0 310.5 %reduce-scatter.2.cloned.1.call-start = ((), (), s32[]{:S(2)}) async-start(), calls=%async_computation.1 | async-start | bytes 11141120 | tf_op jit(solution)/shard_map/reduce_scatter | solution.py:1210
  110.4 33.6 %collective-permute-start.15 = (bf16[2,2,2,64,1024]{4,3,2,1,0:T(8,128)(2,1)S(1)}, bf16[2,2,2,64,1024]{4,3,2,1,0:T(8,128)(2,1)}, u32[]{:S(2)}, u32[]{:S(2)}) collective-permute-start(bf16[2,2,2,64,1024]{4,3,2,1,0:T(8,128)(2,1)S(1)} %pad_maximum_fusion.refs_0_), channel_id=1, source_target_pairs={{0,1},{1,0},{2,3},{3,2},{4,5},{5,4},{6,7},{7,6},{8,9},{9,8},{10,11... | collective-permute-start | bytes 3145736 | tf_op jit(solution)/shard_map/ppermute | solution.py:1068
  113.4 30.6 %collective-permute-start.16 = (bf16[2,2,2,64,1024]{4,3,2,1,0:T(8,128)(2,1)S(1)}, bf16[2,2,2,64,1024]{4,3,2,1,0:T(8,128)(2,1)}, u32[]{:S(2)}, u32[]{:S(2)}) collective-permute-start(bf16[2,2,2,64,1024]{4,3,2,1,0:T(8,128)(2,1)S(1)} %pad_maximum_fusion.1.refs_4_), channel_id=1, source_target_pairs={{0,4},{4,0},{1,5},{5,1},{2,6},{6,2},{3,7},{7,3},{8,12},{12,8},{9,1... | collective-permute-start | bytes 3145736 | tf_op jit(solution)/shard_map/ppermute | solution.py:1068
  116.1 41.4 %collective-permute-start.21 = (bf16[2,2,2,64,1024]{4,3,2,1,0:T(8,128)(2,1)S(1)}, bf16[2,2,2,64,1024]{4,3,2,1,0:T(8,128)(2,1)}, u32[]{:S(2)}, u32[]{:S(2)}) collective-permute-start(bf16[2,2,2,64,1024]{4,3,2,1,0:T(8,128)(2,1)S(1)} %pad_maximum_fusion.2.refs_1_.refs_0_), channel_id=1, source_target_pairs={{0,8},{8,0},{1,9},{9,1},{2,10},{10,2},{3,11},{11,3},{4,12},{12,4},... | collective-permute-start | bytes 3145736 | tf_op jit(solution)/shard_map/ppermute | solution.py:1068
  144.1 13.5 %collective-permute-start.17 = (bf16[2,2,2,64,1024]{4,3,2,1,0:T(8,128)(2,1)S(1)}, bf16[2,2,2,64,1024]{4,3,2,1,0:T(8,128)(2,1)S(1)}, u32[]{:S(2)}, u32[]{:S(2)}) collective-permute-start(bf16[2,2,2,64,1024]{4,3,2,1,0:T(8,128)(2,1)S(1)} %pad_maximum_fusion.refs_0_), channel_id=1, source_target_pairs={{0,2},{2,0},{1,3},{3,1},{4,6},{6,4},{5,7},{7,5},{8,10},{10,8},{9,1... | collective-permute-start | bytes 3145736 | tf_op jit(solution)/shard_map/ppermute | solution.py:1068
  144.2 13.4 %collective-permute-start.18 = (bf16[2,2,2,64,1024]{4,3,2,1,0:T(8,128)(2,1)}, bf16[2,2,2,64,1024]{4,3,2,1,0:T(8,128)(2,1)S(1)}, u32[]{:S(2)}, u32[]{:S(2)}) collective-permute-start(bf16[2,2,2,64,1024]{4,3,2,1,0:T(8,128)(2,1)} %collective-permute-done.15.refs_1_), channel_id=1, source_target_pairs={{0,2},{2,0},{1,3},{3,1},{4,6},{6,4},{5,7},{7,5},{8,10},{10,8},{9,1... | collective-permute-start | bytes 3145736 | tf_op jit(solution)/shard_map/ppermute | solution.py:1068
  144.7 13.0 %collective-permute-start.19 = (bf16[2,2,2,64,1024]{4,3,2,1,0:T(8,128)(2,1)S(1)}, bf16[2,2,2,64,1024]{4,3,2,1,0:T(8,128)(2,1)}, u32[]{:S(2)}, u32[]{:S(2)}) collective-permute-start(bf16[2,2,2,64,1024]{4,3,2,1,0:T(8,128)(2,1)S(1)} %pad_maximum_fusion.1.refs_4_), channel_id=1, source_target_pairs={{0,2},{2,0},{1,3},{3,1},{4,6},{6,4},{5,7},{7,5},{8,10},{10,8},{9,1... | collective-permute-start | bytes 3145736 | tf_op jit(solution)/shard_map/ppermute | solution.py:1068
  144.7 12.9 %collective-permute-start.20 = (bf16[2,2,2,64,1024]{4,3,2,1,0:T(8,128)(2,1)}, bf16[2,2,2,64,1024]{4,3,2,1,0:T(8,128)(2,1)}, u32[]{:S(2)}, u32[]{:S(2)}) collective-permute-start(bf16[2,2,2,64,1024]{4,3,2,1,0:T(8,128)(2,1)} %collective-permute-done.16.refs_5_), channel_id=1, source_target_pairs={{0,2},{2,0},{1,3},{3,1},{4,6},{6,4},{5,7},{7,5},{8,10},{10,8},{9,1... | collective-permute-start | bytes 3145736 | tf_op jit(solution)/shard_map/ppermute | solution.py:1068
  157.6 20.7 %collective-permute-start.22 = (bf16[2,2,2,64,1024]{4,3,2,1,0:T(8,128)(2,1)S(1)}, bf16[2,2,2,64,1024]{4,3,2,1,0:T(8,128)(2,1)S(1)}, u32[]{:S(2)}, u32[]{:S(2)}) collective-permute-start(bf16[2,2,2,64,1024]{4,3,2,1,0:T(8,128)(2,1)S(1)} %pad_maximum_fusion.2.refs_1_.refs_0_), channel_id=1, source_target_pairs={{0,2},{2,0},{1,3},{3,1},{4,6},{6,4},{5,7},{7,5},{8,10},{10,8},{9,1... | collective-permute-start | bytes 3145736 | tf_op jit(solution)/shard_map/ppermute | solution.py:1068
  158.6 19.8 %collective-permute-start.23 = (bf16[2,2,2,64,1024]{4,3,2,1,0:T(8,128)(2,1)}, bf16[2,2,2,64,1024]{4,3,2,1,0:T(8,128)(2,1)S(1)}, u32[]{:S(2)}, u32[]{:S(2)}) collective-permute-start(bf16[2,2,2,64,1024]{4,3,2,1,0:T(8,128)(2,1)} %collective-permute-done.21.refs_2_.refs_1_), channel_id=1, source_target_pairs={{0,2},{2,0},{1,3},{3,1},{4,6},{6,4},{5,7},{7,5},{8,10},{10,8},{9,1... | collective-permute-start | bytes 3145736 | tf_op jit(solution)/shard_map/ppermute | solution.py:1068
  228.8 27.4 %collective-permute-start.24 = (bf16[2,2,2,2,64,1024]{5,4,3,2,1,0:T(8,128)(2,1)}, bf16[2,2,2,2,64,1024]{5,4,3,2,1,0:T(8,128)(2,1)}, u32[]{:S(2)}, u32[]{:S(2)}) collective-permute-start(bf16[2,2,2,2,64,1024]{5,4,3,2,1,0:T(8,128)(2,1)} %get-tuple-element.305), channel_id=1, source_target_pairs={{0,2},{2,0},{1,3},{3,1},{4,6},{6,4},{5,7},{7,5},{8,10},{10,8},{9,1... | collective-permute-start | bytes 6291464 | tf_op jit(solution)/shard_map/ppermute | solution.py:1068
  229.1 27.1 %collective-permute-start.25 = (bf16[2,2,2,2,64,1024]{5,4,3,2,1,0:T(8,128)(2,1)}, bf16[2,2,2,2,64,1024]{5,4,3,2,1,0:T(8,128)(2,1)}, u32[]{:S(2)}, u32[]{:S(2)}) collective-permute-start(bf16[2,2,2,2,64,1024]{5,4,3,2,1,0:T(8,128)(2,1)} %get-tuple-element.306), channel_id=1, source_target_pairs={{0,2},{2,0},{1,3},{3,1},{4,6},{6,4},{5,7},{7,5},{8,10},{10,8},{9,1... | collective-permute-start | bytes 6291464 | tf_op jit(solution)/shard_map/ppermute | solution.py:1068
  229.3 26.8 %collective-permute-start.26 = (bf16[1024,512]{1,0:T(8,128)(2,1)S(1)}, bf16[1024,512]{1,0:T(8,128)(2,1)S(1)}, u32[]{:S(2)}, u32[]{:S(2)}) collective-permute-start(bf16[1024,512]{1,0:T(8,128)(2,1)S(1)} %copy-done.35), channel_id=1, source_target_pairs={{0,1},{1,0},{2,3},{3,2},{4,5},{5,4},{6,7},{7,6},{8,9},{9,8},{10,11... | collective-permute-start | bytes 3145736 | tf_op jit(solution)/shard_map/ppermute | solution.py:1068
  260.4 47.6 %collective-permute-start.27 = (bf16[2,2,2,2,64,1024]{5,4,3,2,1,0:T(8,128)(2,1)S(1)}, bf16[2,2,2,2,64,1024]{5,4,3,2,1,0:T(8,128)(2,1)S(1)}, u32[]{:S(2)}, u32[]{:S(2)}) collective-permute-start(bf16[2,2,2,2,64,1024]{5,4,3,2,1,0:T(8,128)(2,1)S(1)} %add.324), channel_id=1, source_target_pairs={{0,1},{1,0},{2,3},{3,2},{4,5},{5,4},{6,7},{7,6},{8,9},{9,8},{10,11... | collective-permute-start | bytes 6291464 | tf_op jit(solution)/shard_map/ppermute | solution.py:1068
  307.9 27.6 %collective-permute-start.29 = (bf16[2,2,2,1,64,512]{5,4,3,2,1,0:T(8,128)(2,1)}, bf16[2,2,2,1,64,512]{5,4,3,2,1,0:T(8,128)(2,1)}, u32[]{:S(2)}, u32[]{:S(2)}) collective-permute-start(bf16[2,2,2,1,64,512]{5,4,3,2,1,0:T(8,128)(2,1)} %get-tuple-element.333), channel_id=1, source_target_pairs={{0,2},{2,0},{1,3},{3,1},{4,6},{6,4},{5,7},{7,5},{8,10},{10,8},{9,1... | collective-permute-start | bytes 1572872 | tf_op jit(solution)/shard_map/ppermute | solution.py:1068
  307.9 27.6 %collective-permute-start.30 = (bf16[2,2,2,1,64,512]{5,4,2,1,3,0:T(8,128)(2,1)}, bf16[2,2,2,1,64,512]{5,4,2,1,3,0:T(8,128)(2,1)}, u32[]{:S(2)}, u32[]{:S(2)}) collective-permute-start(bf16[2,2,2,1,64,512]{5,4,2,1,3,0:T(8,128)(2,1)} %bitcast.277), channel_id=1, source_target_pairs={{0,2},{2,0},{1,3},{3,1},{4,6},{6,4},{5,7},{7,5},{8,10},{10,8},{9,1... | collective-permute-start | bytes 1572872 | tf_op jit(solution)/shard_map/ppermute | solution.py:1068
  311.5 38.8 %collective-permute-start.28 = (bf16[2,2,2,64,1024]{4,3,2,1,0:T(8,128)(2,1)S(1)}, bf16[2,2,2,64,1024]{4,3,2,1,0:T(8,128)(2,1)S(1)}, u32[]{:S(2)}, u32[]{:S(2)}) collective-permute-start(bf16[2,2,2,64,1024]{4,3,2,1,0:T(8,128)(2,1)S(1)} %get-tuple-element.435), channel_id=1, source_target_pairs={{0,4},{4,0},{1,5},{5,1},{2,6},{6,2},{3,7},{7,3},{8,12},{12,8},{9,1... | collective-permute-start | bytes 3145736 | tf_op jit(solution)/shard_map/ppermute | solution.py:1068
  336.8 13.6 %collective-permute-start.31 = (bf16[2,2,2,1,64,512]{5,4,3,2,1,0:T(8,128)(2,1)S(1)}, bf16[2,2,2,1,64,512]{5,4,3,2,1,0:T(8,128)(2,1)S(1)}, u32[]{:S(2)}, u32[]{:S(2)}) collective-permute-start(bf16[2,2,2,1,64,512]{5,4,3,2,1,0:T(8,128)(2,1)S(1)} %add.329), channel_id=1, source_target_pairs={{0,1},{1,0},{2,3},{3,2},{4,5},{5,4},{6,7},{7,6},{8,9},{9,8},{10,11... | collective-permute-start | bytes 1572872 | tf_op jit(solution)/shard_map/ppermute | solution.py:1068
  350.4 22.9 %collective-permute-start.34 = (bf16[3,2,2,2,64,512]{5,4,3,2,1,0:T(8,128)(2,1)}, bf16[3,2,2,2,64,512]{5,4,3,2,1,0:T(8,128)(2,1)}, u32[]{:S(2)}, u32[]{:S(2)}) collective-permute-start(bf16[3,2,2,2,64,512]{5,4,3,2,1,0:T(8,128)(2,1)} %get-tuple-element.364), channel_id=1, source_target_pairs={{0,2},{2,0},{1,3},{3,1},{4,6},{6,4},{5,7},{7,5},{8,10},{10,8},{9,1... | collective-permute-start | bytes 4718600 | tf_op jit(solution)/shard_map/ppermute | solution.py:1068
  350.4 22.9 %collective-permute-start.35 = (bf16[3,2,2,2,64,512]{5,4,3,2,1,0:T(8,128)(2,1)}, bf16[3,2,2,2,64,512]{5,4,3,2,1,0:T(8,128)(2,1)S(1)}, u32[]{:S(2)}, u32[]{:S(2)}) collective-permute-start(bf16[3,2,2,2,64,512]{5,4,3,2,1,0:T(8,128)(2,1)} %get-tuple-element.365), channel_id=1, source_target_pairs={{0,2},{2,0},{1,3},{3,1},{4,6},{6,4},{5,7},{7,5},{8,10},{10,8},{9,1... | collective-permute-start | bytes 4718600 | tf_op jit(solution)/shard_map/ppermute | solution.py:1068
  352.0 21.3 %collective-permute-start.33 = (bf16[2,2,1,64,512]{4,3,1,0,2:T(8,128)(2,1)S(1)}, bf16[2,2,1,64,512]{4,3,1,0,2:T(8,128)(2,1)S(1)}, u32[]{:S(2)}, u32[]{:S(2)}) collective-permute-start(bf16[2,2,1,64,512]{4,3,1,0,2:T(8,128)(2,1)S(1)} %fusion.14), channel_id=1, source_target_pairs={{0,4},{4,0},{1,5},{5,1},{2,6},{6,2},{3,7},{7,3},{8,12},{12,8},{9,1... | collective-permute-start | bytes 786440 | tf_op jit(solution)/shard_map/ppermute | solution.py:1068
  354.7 42.5 %collective-permute-start.32 = (bf16[2,2,64,1024]{3,2,1,0:T(8,128)(2,1)}, bf16[2,2,64,1024]{3,2,1,0:T(8,128)(2,1)S(1)}, u32[]{:S(2)}, u32[]{:S(2)}) collective-permute-start(bf16[2,2,64,1024]{3,2,1,0:T(8,128)(2,1)} %get-tuple-element.450), channel_id=1, source_target_pairs={{0,8},{8,0},{1,9},{9,1},{2,10},{10,2},{3,11},{11,3},{4,12},{12,4},... | collective-permute-start | bytes 1572872 | tf_op jit(solution)/shard_map/ppermute | solution.py:1068
  375.9 27.7 %collective-permute-start.37 = (bf16[2,2,2,64,512]{4,3,2,1,0:T(8,128)(2,1)}, bf16[2,2,2,64,512]{4,3,2,1,0:T(8,128)(2,1)S(1)}, u32[]{:S(2)}, u32[]{:S(2)}) collective-permute-start(bf16[2,2,2,64,512]{4,3,2,1,0:T(8,128)(2,1)} %get-tuple-element.449), channel_id=1, source_target_pairs={{0,4},{4,0},{1,5},{5,1},{2,6},{6,2},{3,7},{7,3},{8,12},{12,8},{9,1... | collective-permute-start | bytes 1572872 | tf_op jit(solution)/shard_map/ppermute | solution.py:1068
  376.7 26.9 %collective-permute-start.38 = (bf16[2,2,2,64,512]{4,3,2,1,0:T(8,128)(2,1)}, bf16[2,2,2,64,512]{4,3,2,1,0:T(8,128)(2,1)}, u32[]{:S(2)}, u32[]{:S(2)}) collective-permute-start(bf16[2,2,2,64,512]{4,3,2,1,0:T(8,128)(2,1)} %get-tuple-element.448), channel_id=1, source_target_pairs={{0,1},{1,0},{2,3},{3,2},{4,5},{5,4},{6,7},{7,6},{8,9},{9,8},{10,11... | collective-permute-start | bytes 1572872 | tf_op jit(solution)/shard_map/ppermute | solution.py:1068
  378.2 25.4 %collective-permute-start.39 = (bf16[2,2,2,64,512]{4,3,2,1,0:T(8,128)(2,1)}, bf16[2,2,2,64,512]{4,3,2,1,0:T(8,128)(2,1)}, u32[]{:S(2)}, u32[]{:S(2)}) collective-permute-start(bf16[2,2,2,64,512]{4,3,2,1,0:T(8,128)(2,1)} %get-tuple-element.447), channel_id=1, source_target_pairs={{0,8},{8,0},{1,9},{9,1},{2,10},{10,2},{3,11},{11,3},{4,12},{12,4},... | collective-permute-start | bytes 1572872 | tf_op jit(solution)/shard_map/ppermute | solution.py:1068
  380.1 23.5 %collective-permute-start.36 = (bf16[2,1,64,512]{3,2,0,1:T(8,128)(2,1)S(1)}, bf16[2,1,64,512]{3,2,0,1:T(8,128)(2,1)S(1)}, u32[]{:S(2)}, u32[]{:S(2)}) collective-permute-start(bf16[2,1,64,512]{3,2,0,1:T(8,128)(2,1)S(1)} %fusion.23), channel_id=1, source_target_pairs={{0,8},{8,0},{1,9},{9,1},{2,10},{10,2},{3,11},{11,3},{4,12},{12,4},... | collective-permute-start | bytes 393224 | tf_op jit(solution)/shard_map/ppermute | solution.py:1068
  404.4 15.4 %collective-permute-start.41 = (bf16[1,64,512]{2,1,0:T(8,128)(2,1)S(1)}, bf16[1,64,512]{2,1,0:T(8,128)(2,1)S(1)}, u32[]{:S(2)}, u32[]{:S(2)}) collective-permute-start(bf16[1,64,512]{2,1,0:T(8,128)(2,1)S(1)} %fusion.29), channel_id=1, source_target_pairs={{0,16},{16,0},{1,17},{17,1},{2,18},{18,2},{3,19},{19,3},{4,20},{20... | collective-permute-start | bytes 196616 | tf_op jit(solution)/shard_map/ppermute | solution.py:1068
  408.4 11.5 %collective-permute-start.42 = (bf16[2,2,64,512]{3,2,1,0:T(8,128)(2,1)S(1)}, bf16[2,2,64,512]{3,2,1,0:T(8,128)(2,1)S(1)}, u32[]{:S(2)}, u32[]{:S(2)}) collective-permute-start(bf16[2,2,64,512]{3,2,1,0:T(8,128)(2,1)S(1)} %get-tuple-element.446), channel_id=1, source_target_pairs={{0,8},{8,0},{1,9},{9,1},{2,10},{10,2},{3,11},{11,3},{4,12},{12,4},... | collective-permute-start | bytes 786440 | tf_op jit(solution)/shard_map/ppermute | solution.py:1068
  409.0 10.8 %collective-permute-start.43 = (bf16[2,2,64,512]{3,2,1,0:T(8,128)(2,1)S(1)}, bf16[2,2,64,512]{3,2,1,0:T(8,128)(2,1)S(1)}, u32[]{:S(2)}, u32[]{:S(2)}) collective-permute-start(bf16[2,2,64,512]{3,2,1,0:T(8,128)(2,1)S(1)} %get-tuple-element.444), channel_id=1, source_target_pairs={{0,4},{4,0},{1,5},{5,1},{2,6},{6,2},{3,7},{7,3},{8,12},{12,8},{9,1... | collective-permute-start | bytes 786440 | tf_op jit(solution)/shard_map/ppermute | solution.py:1068
  409.7 10.2 %collective-permute-start.44 = (bf16[2,2,64,512]{3,2,1,0:T(8,128)(2,1)S(1)}, bf16[2,2,64,512]{3,2,1,0:T(8,128)(2,1)S(1)}, u32[]{:S(2)}, u32[]{:S(2)}) collective-permute-start(bf16[2,2,64,512]{3,2,1,0:T(8,128)(2,1)S(1)} %get-tuple-element.437), channel_id=1, source_target_pairs={{0,1},{1,0},{2,3},{3,2},{4,5},{5,4},{6,7},{7,6},{8,9},{9,8},{10,11... | collective-permute-start | bytes 786440 | tf_op jit(solution)/shard_map/ppermute | solution.py:1068
  417.7 16.4 %collective-permute-start.40 = (bf16[2,64,1024]{2,1,0:T(8,128)(2,1)}, bf16[2,64,1024]{2,1,0:T(8,128)(2,1)S(1)}, u32[]{:S(2)}, u32[]{:S(2)}) collective-permute-start(bf16[2,64,1024]{2,1,0:T(8,128)(2,1)} %get-tuple-element.454), channel_id=1, source_target_pairs={{0,16},{16,0},{1,17},{17,1},{2,18},{18,2},{3,19},{19,3},{4,20},{20... | collective-permute-start | bytes 786440 | tf_op jit(solution)/shard_map/ppermute | solution.py:1068
  421.7 12.5 %collective-permute-start.47 = (bf16[2,64,512]{2,1,0:T(8,128)(2,1)S(1)}, bf16[2,64,512]{2,1,0:T(8,128)(2,1)S(1)}, u32[]{:S(2)}, u32[]{:S(2)}) collective-permute-start(bf16[2,64,512]{2,1,0:T(8,128)(2,1)S(1)} %get-tuple-element.464), channel_id=1, source_target_pairs={{0,1},{1,0},{2,3},{3,2},{4,5},{5,4},{6,7},{7,6},{8,9},{9,8},{10,11... | collective-permute-start | bytes 393224 | tf_op jit(solution)/shard_map/ppermute | solution.py:1068
  423.8 10.3 %collective-permute-start.51 = (bf16[64,2560]{1,0:T(8,128)(2,1)S(1)}, bf16[64,2560]{1,0:T(8,128)(2,1)S(1)}, u32[]{:S(2)}, u32[]{:S(2)}) collective-permute-start(bf16[64,2560]{1,0:T(8,128)(2,1)S(1)} %dynamic-slice_bitcast_fusion), channel_id=1, source_target_pairs={{0,1},{1,0},{2,3},{3,2},{4,5},{5,4},{6,7},{7,6},{8,9},{9,8},{10,11... | collective-permute-start | bytes 983048 | tf_op jit(solution)/shard_map/ppermute | solution.py:1068
  425.9 9.1 %collective-permute-start.48 = (bf16[2,64,512]{2,1,0:T(8,128)(2,1)S(1)}, bf16[2,64,512]{2,1,0:T(8,128)(2,1)S(1)}, u32[]{:S(2)}, u32[]{:S(2)}) collective-permute-start(bf16[2,64,512]{2,1,0:T(8,128)(2,1)S(1)} %get-tuple-element.462), channel_id=1, source_target_pairs={{0,8},{8,0},{1,9},{9,1},{2,10},{10,2},{3,11},{11,3},{4,12},{12,4},... | collective-permute-start | bytes 393224 | tf_op jit(solution)/shard_map/ppermute | solution.py:1068
  435.8 11.2 %collective-permute-start.52 = (bf16[3,64,512]{2,1,0:T(8,128)(2,1)S(1)}, bf16[3,64,512]{2,1,0:T(8,128)(2,1)S(1)}, u32[]{:S(2)}, u32[]{:S(2)}) collective-permute-start(bf16[3,64,512]{2,1,0:T(8,128)(2,1)S(1)} %pad_maximum_fusion.12), channel_id=1, source_target_pairs={{0,16},{16,0},{1,17},{17,1},{2,18},{18,2},{3,19},{19,3},{4,20},{20... | collective-permute-start | bytes 589832 | tf_op jit(solution)/shard_map/ppermute | solution.py:1068
  (46 other events, 467.0 us)
Sparse Core Ops, SparseCore 0:
  11.0 98.9 all-gather.4
  112.9 70.6 all-gather.6
  256.4 143.5 reduce-scatter.1

commit v6 on v5

--- a/solution.py
+++ b/solution.py
@@ -1414,7 +1414,7 @@
         return lax.dynamic_update_slice_in_dim(kept, arrived, (1 - side) * tokens, 0)
 
     back = functools.partial(channel_back, co)
-    order_b, order_c = "wuyx", "wuyx"
+    order_b, order_c = "wuyx", "wuxy"
     edge = jnp.zeros((8, width), F32)
 
     def input_back_part(dmix, part, after, before, found):
@@ -1423,24 +1423,25 @@
         )
 
     if fast:
-        dkey_1, *found = back(dkv, mixed_k2, hidden, active, (), cvalue_w[1], split, 1, order_b)
-        group_b = Merged(found, order_b)
-        (dkv,) = seal_all((group_b,), dkv)
-        group_b.step()
         dkey_0, blocks = back(
             dkv, mixed_k2, hidden, active, (mixed_r2, drec2), cvalue_w[0], split, 0, order_b
         )
-        dkey_0, arrived, blocks = seal_all((group_b,), dkey_0, arrived, blocks)
+        dkv, arrived, blocks = seal(dkv, arrived, blocks)
         blocks = scatter_rows(blocks)
+        dkey_1, *found = back(dkv, mixed_k2, hidden, active, (), cvalue_w[1], split, 1, order_b)
+        group_b = Merged(found, order_b)
+        (dkey_1,) = seal_all((group_b,), dkey_1)
         group_b.step()
         outputs = outputs_of(kept, arrived)
         dmid, dtime, sums2 = middle_back(
             co, (dkey_0, dkey_1), drec2, middle, dres, lead, vectors, ckey_w, crecept_w
         )
+        (dtime,) = seal_all((group_b,), dtime)
+        group_b.step()
         found = weight_grads(co, ((dtime, gated, order_c),), merged=True)
         group_c = Merged(found, order_c)
-        dtime, outputs = seal_all((group_b, group_c), dtime, outputs)
-        step_all(group_b, group_c)
+        dtime, outputs = seal_all((group_c,), dtime, outputs)
+        group_c.step()
         *dmix, sums_t = time_back(co, dtime, saved, vectors, masks_up, output_w)
         (dmix, dmid) = seal_all((group_c,), dmix, dmid)
         group_c.step()

time: 463 us -> 459 us (level)
    ppermute x55, waiting for transfers between devices: 65 us -> 54.3 us  [swap(): return lax.ppermute(values, axis, SWAP)]
    all_gather x1, waiting for transfers between devices: 9.13 us -> 18.2 us  [on_device(): first = lax.all_gather(first, EVERY)]
  transfers between devices with their start and end apart: 58 -> 58, of which waited for: 22 -> 18; matrix products, arithmetic and copies ran while one was open for 13% -> 12% of each run, Pallas kernels for 42% -> 47%
where the time goes in v6:
time: 459 us; the launch traced here: 452 us
  Pallas kernels  235 us (51%)
  waiting for transfers between devices  79.5 us (17%)
  starting transfers between devices  55 us (12%)
  other arithmetic  38.3 us (8%)
  local copies, waits for them, and re-layouts  26.1 us (6%)
  between operations  18.3 us (4%)
    ppermute x55, starting transfers between devices, swap(): return lax.ppermute(values, axis, SWAP)  54.8 us
    ppermute x55, waiting for transfers between devices, swap(): return lax.ppermute(values, axis, SWAP)  54.3 us
    pallas_call x2, Pallas kernels, channel_back(): pl.pallas_call(functools.partial(channel_back_kernel, layout=weight[0], p...  46.7 us
    pallas_call x2, Pallas kernels, input_back(): pl.pallas_call(functools.partial(input_back_kernel, layouts=[w[0] for w i...  30.3 us
    pallas_call x1, Pallas kernels, middle_back(): pl.pallas_call(functools.partial(middle_back_kernel, layouts=[weight[0],...  28.8 us
    pallas_call x1, Pallas kernels, time_forward(): pl.pallas_call(functools.partial(time_forward_kernel, layouts=[w[0] for w...  26.1 us
    pallas_call x1, Pallas kernels, result_step(): pl.pallas_call(functools.partial(result_kernel, layouts=[weight[0], recep...  23.7 us
    pallas_call x1, Pallas kernels, time_back(): pl.pallas_call(functools.partial(time_back_kernel, layout=weight[0]), gri...  23.1 us
  transfers between devices with their start and end apart: 58, of which 18 were waited for; matrix products, arithmetic and copies ran while one was open for 12% of the time, Pallas kernels for 47%

profile of v6, /device:TPU:0, one launch (start us, length us, event | category | flops | bytes accessed | tf_op | source)
XLA Modules:
  0.0 452.2 jit_solution(9254497503271076790)
XLA Ops:
  7.2 1.6 pad_maximum_fusion.10
  13.7 3.0 collective-permute-start.3
  16.7 2.7 constant_dynamic-slice_fusion.1
  19.5 3.1 collective-permute-start
  22.8 2.9 collective-permute-start.2
  35.8 1.6 pad_maximum_fusion.11
  41.7 2.0 collective-permute-done.5
  43.8 1.6 collective-permute-start.6
  45.4 2.1 collective-permute-done.6
  47.6 2.2 broadcast_in_dim.142.masks
  49.8 1.9 broadcast_in_dim.134.masks
  55.6 1.6 collective-permute-start.10
  57.2 1.6 collective-permute-start.9
  58.8 1.6 collective-permute-start.8
  61.2 7.0 %collective-permute-done.11 = f32[16,512]{1,0:T(8,128)S(1)} collective-permute-done((f32[16,512]{1,0:T(8,128)S(1)}, f32[16,512]{1,0:T(8,128)S(1)}, u32[]{:S(2)}, u32[]{:S(2)}) %collective-permute-start.11) | collective-permute-done | bytes 32800 | tf_op jit(solution)/shard_map/ppermute | solution.py:1068
  68.8 1.8 collective-permute-done.8
  70.7 3.2 collective-permute-start.14
  76.0 7.4 %shard_map.364 = (bf16[1024,1024]{1,0:T(8,128)(2,1)}, bf16[1024,1024]{1,0:T(8,128)(2,1)}, bf16[1024,1024]{1,0:T(8,128)(2,1)}) custom-call(bf16[1024,1024]{1,0:T(8,128)(2,1)} %x_ref.7, f32[1024,128]{1,0:T(8,128)} %broadcast_in_dim.143.carry_ref, f32[16,1024]{1,0:T(8,128)} %maximum_select_fusion.1.vec_ref.vec), custom_call_target="tpu_custom_call" | custom-call | bytes 83886 | tf_op jit(solution)/shard_map/pallas_call | solution.py:211
  83.4 7.4 %collective-permute-done.14 = bf16[2,2,64,1024]{3,2,1,0:T(8,128)(2,1)} collective-permute-done((bf16[2,2,64,1024]{3,2,1,0:T(8,128)(2,1)S(1)}, bf16[2,2,64,1024]{3,2,1,0:T(8,128)(2,1)}, u32[]{:S(2)}, u32[]{:S(2)}) %collective-permute-start.14) | collective-permute-done | bytes 524320 | tf_op jit(solution)/shard_map/ppermute | solution.py:1068
  90.8 7.1 %collective-permute-done.13 = bf16[2,2,64,1024]{3,2,1,0:T(8,128)(2,1)S(1)} collective-permute-done((bf16[2,2,64,1024]{3,2,1,0:T(8,128)(2,1)S(1)}, bf16[2,2,64,1024]{3,2,1,0:T(8,128)(2,1)S(1)}, u32[]{:S(2)}, u32[]{:S(2)}) %collective-permute-start.13) | collective-permute-done | bytes 524320 | tf_op jit(solution)/shard_map/ppermute | solution.py:1068
  97.9 18.2 %all-gather.5.cloned.1.call-done = bf16[2048,2048]{1,0:T(8,128)(2,1)} async-done(((bf16[64,2048]{1,0:T(8,128)(2,1)}), bf16[2048,2048]{1,0:T(8,128)(2,1)}) %all-gather.5.cloned.1.call-update) | async-done | bytes 8388624 | tf_op jit(solution)/shard_map/all_gather | solution.py:1348
  120.3 26.1 %shard_map.365 = (f32[1024,1024]{1,0:T(8,128)}, f32[1024,1024]{1,0:T(8,128)}, f32[1024,1024]{1,0:T(8,128)}, f32[1024,1024]{1,0:T(8,128)}, f32[1024,1024]{1,0:T(8,128)}, /*index=5*/bf16[1024,1024]{1,0:T(8,128)(2,1)}) custom-call(s32[5]{0:T(128)} %stack.159.co, bf16[1024,1024]{1,0:T(8,128)(2,1)} %get-tuple-element.256.mk.refs_0_, ...), custom_call_target="tpu_custom_call" | custom-call | flops 171798688 | bytes 356515 | tf_op jit(solution)/shard_map/pallas_call | solution.py:316
  147.6 12.3 %shard_map.366 = (f32[1024,1024]{1,0:T(8,128)}, bf16[1024,1024]{1,0:T(8,128)(2,1)}, bf16[1024,1024]{1,0:T(8,128)(2,1)}) custom-call(s32[5]{0:T(128)} %stack.159.co, bf16[1024,1024]{1,0:T(8,128)(2,1)} %get-tuple-element.268.gated.refs_1_, bf16[1024,1024]{1,0:T(8,128)(2,1)} %x_ref.7, f32[1024,128]{1,0:T(8,128)} %broadcast_in_dim.143.carry_ref, ...), custom_call_target="tpu_custom_call" | custom-call | flops 64424508 | bytes 146800 | tf_op jit(solution)/shard_map/pallas_call | solution.py:383
  163.4 17.3 %shard_map.367 = (bf16[1024,4096]{1,0:T(8,128)(2,1)}, bf16[1024,4096]{1,0:T(8,128)(2,1)}) custom-call(s32[5]{0:T(128)} %stack.159.co, bf16[1024,1024]{1,0:T(8,128)(2,1)} %get-tuple-element.274.mk.mixed, bf16[2,2,2,64,1024]{4,3,2,1,0:T(8,128)(2,1)} %copy-done.2, bf16[2,2,2,64,1024]{4,3,2,1,0:T(8,128)(2,1)} %collective-permute-done.15.refs_1_, ...), custom_call_target="tpu_custom_call" | custom-call | flops 96636768 | bytes 272629 | tf_op jit(solution)/shard_map/pallas_call | solution.py:437
  180.8 7.0 %all-gather.7.cloned.1.call-done = bf16[2048,1536]{1,0:T(8,128)(2,1)} async-done(((bf16[64,1536]{1,0:T(8,128)(2,1)}), bf16[2048,1536]{1,0:T(8,128)(2,1)}) %all-gather.7.cloned.1.call-update) | async-done | bytes 6291472 | tf_op jit(solution)/shard_map/all_gather | solution.py:1363
  187.8 23.7 %shard_map.368 = (bf16[2048,512]{1,0:T(8,128)(2,1)}, bf16[1024,512]{1,0:T(8,128)(2,1)}, f32[1024,1024]{1,0:T(8,128)}, bf16[1024,1024]{1,0:T(8,128)(2,1)}, bf16[1024,1024]{1,0:T(8,128)(2,1)}, /*index=5*/f32[8,1024]{1,0:T(8,128)}) custom-call(s32[5]{0:T(128)} %copy-done.33, f32[1]{0:T(128)} %bitcast.38.scale, bf16[1024,4096]{1,0:T(8,128)(2,1)} %get-tuple-element.285.hidden, ...), custom_call_target="tpu_custom_call" | custom-call | flops 150323856 | bytes 398458 | tf_op jit(solution)/shard_map/pallas_call | solution.py:508
  212.9 25.1 %shard_map.369 = (bf16[1024,2048]{1,0:T(8,128)(2,1)}, bf16[16,2,64,2560]{3,2,1,0:T(8,128)(2,1)}) custom-call(s32[5]{0:T(128)} %stack.159.co, bf16[1024,1024]{1,0:T(8,128)(2,1)} %get-tuple-element.301.dkv, bf16[1024,1024]{1,0:T(8,128)(2,1)} %get-tuple-element.274.mk.mixed, bf16[1024,4096]{1,0:T(8,128)(2,1)} %get-tuple-element.285.hidden, ...), custom_call_target="tpu_custom_call" | custom-call | flops 141733920 | bytes 293601 | tf_op jit(solution)/shard_map/pallas_call | solution.py:695
  238.1 21.6 %shard_map.370 = (bf16[1024,2048]{1,0:T(8,128)(2,1)}, bf16[2,2,2,2,64,1024]{5,4,3,2,1,0:T(8,128)(2,1)}, bf16[2,2,2,2,64,1024]{5,4,3,2,1,0:T(8,128)(2,1)}, bf16[2...) custom-call(s32[5]{0:T(128)} %stack.159.co, bf16[1024,1024]{1,0:T(8,128)(2,1)} %get-tuple-element.301.dkv, ...), custom_call_target="tpu_custom_call" | custom-call | flops 141733920 | bytes 293601 | tf_op jit(solution)/shard_map/pallas_call | solution.py:695
  260.3 28.8 %shard_map.371 = (f32[1024,1024]{1,0:T(8,128)}, bf16[1024,1024]{1,0:T(8,128)(2,1)}, f32[4,8,1024]{2,1,0:T(8,128)}) custom-call(s32[5]{0:T(128)} %stack.159.co, bf16[1024,2048]{1,0:T(8,128)(2,1)} %get-tuple-element.311.dkey_a, bf16[1024,2048]{1,0:T(8,128)(2,1)} %get-tuple-element.312.dkey_b, bf16[1024,1024]{1,0:T(8,128)(2,1)} %get-tuple-element.299.refs_1_.drec, ...), custom_call_target="tpu_custom_call" | custom-call | flops 171798688 | bytes 377487 | tf_op jit(solution)/shard_map/pallas_call | solution.py:802
  290.4 2.6 add.324
  294.8 6.6 %shard_map.372 = (bf16[2,2,2,1,64,512]{5,4,3,2,1,0:T(8,128)(2,1)}, bf16[2,2,2,1,64,512]{5,4,3,2,1,0:T(8,128)(2,1)}, bf16[2,2,2,1,64,512]{5,4,3,2,1,0:T(8,128)(2,1)}, bf16[2,2,2,1,64,512]{5,4,3,2,1,0:T(8,128)(2,1)}) custom-call(s32[5]{0:T(128)} %stack.159.co, bf16[1024,1024]{1,0:T(8,128)(2,1)} %get-tuple-element.332.refs_0_.dtime, ...), custom_call_target="tpu_custom_call" | custom-call | flops 25769804 | bytes 62914 | tf_op jit(solution)/shard_map/pallas_call | solution.py:588
  302.0 23.1 %shard_map.373 = (bf16[1024,1024]{1,0:T(8,128)(2,1)}, bf16[1024,1024]{1,0:T(8,128)(2,1)}, bf16[1024,1024]{1,0:T(8,128)(2,1)}, f32[2,8,1024]{2,1,0:T(8,128)}) custom-call(s32[5]{0:T(128)} %stack.159.co, bf16[1024,1024]{1,0:T(8,128)(2,1)} %get-tuple-element.332.refs_0_.dtime, f32[1024,1024]{1,0:T(8,128)} %get-tuple-element.333.key_ref, ...), custom_call_target="tpu_custom_call" | custom-call | flops 193273536 | bytes 356515 | tf_op jit(solution)/shard_map/pallas_call | solution.py:913
  327.6 12.6 %shard_map.374 = (bf16[3,2,2,2,64,512]{5,4,3,2,1,0:T(8,128)(2,1)}, bf16[3,2,2,2,64,512]{5,4,3,2,1,0:T(8,128)(2,1)}, bf16[3,2,2,2,64,512]{5,4,3,2,1,0:T(8,128)(2,1)}, bf16[3,2,2,2,64,512]{5,4,3,2,1,0:T(8,128)(2,1)}) custom-call(s32[5]{0:T(128)} %stack.159.co, bf16[1024,1024]{1,0:T(8,128)(2,1)} %get-tuple-element.256.mk.refs_0_, ...), custom_call_target="tpu_custom_call" | custom-call | flops 77309408 | bytes 188743 | tf_op jit(solution)/shard_map/pallas_call | solution.py:588
  340.2 2.8 collective-permute-done.30
  343.5 1.8 fusion.13
  346.5 4.6 %fusion.1 = (bf16[2,2,2,64,1024]{4,3,2,1,0:T(8,128)(2,1)}, bf16[2,2,2,64,1024]{4,3,2,1,0:T(8,128)(2,1)S(1)}) fusion(bf16[2,2,2,2,64,1024]{5,4,3,2,1,0:T(8,128)(2,1)} %collective-permute-done.27, bf16[2,2,2,2,64,1024]{5,4,3,2,1,0:T(8,128)(2,1)} %collective-permute-done.26, bf16[2,2,2,2,64,1024]{5,4,3,2,1,0:T(8,128)(2,1)S(1)} %copy-done.10), kind=kLoop, calls=%fused_computation.3 | loop fusion | flops 6291456 | bytes 8388608 | tf_op jit(solution)/shard_map/convert_element_type | solution.py:1116
  353.1 15.1 %shard_map.375 = (f32[1024,1024]{1,0:T(8,128)}, f32[12,1024]{1,0:T(8,128)}, f32[8,1024]{1,0:T(8,128)}) custom-call(s32[5]{0:T(128)} %stack.159.co, bf16[1024,1024]{1,0:T(8,128)(2,1)} %get-tuple-element.379.refs_3_.dkey, bf16[1024,1024]{1,0:T(8,128)(2,1)} %get-tuple-element.380.refs_4_.dval, ...), custom_call_target="tpu_custom_call", output_to_operand_aliasing={{0}: (12, {})} | custom-call | flops 85899344 | bytes 167772 | tf_op jit(solution)/shard_map/pallas_call | solution.py:1031
  370.0 2.5 add_bitcast_fusion
  378.3 15.2 %shard_map.376 = (f32[1024,1024]{1,0:T(8,128)}, f32[12,1024]{1,0:T(8,128)}, f32[8,1024]{1,0:T(8,128)}) custom-call(s32[5]{0:T(128)} %stack.159.co, bf16[1024,1024]{1,0:T(8,128)(2,1)} %get-tuple-element.379.refs_3_.dkey, bf16[1024,1024]{1,0:T(8,128)(2,1)} %get-tuple-element.380.refs_4_.dval, ...), custom_call_target="tpu_custom_call", output_to_operand_aliasing={{0}: (10, {})} | custom-call | flops 85899344 | bytes 167772 | tf_op jit(solution)/shard_map/pallas_call | solution.py:1031
  394.6 1.6 add_convert_fusion.3
  397.4 1.8 collective-permute-start.42
  399.2 2.0 collective-permute-start.43
  402.6 1.9 collective-permute-start.41
  404.5 8.0 %collective-permute-done.39 = bf16[2,2,64,1024]{3,2,1,0:T(8,128)(2,1)S(1)} collective-permute-done((bf16[2,2,64,1024]{3,2,1,0:T(8,128)(2,1)S(1)}, bf16[2,2,64,1024]{3,2,1,0:T(8,128)(2,1)S(1)}, u32[]{:S(2)}, u32[]{:S(2)}) %collective-permute-start.39) | collective-permute-done | bytes 524320 | tf_op jit(solution)/shard_map/ppermute | solution.py:1068
  412.7 3.4 collective-permute-start.40
  416.1 3.4 collective-permute-done.42
  427.0 2.7 collective-permute-done.51
  437.7 4.0 collective-permute-done.54
  (296 shorter events, 74.8 us)
Async XLA Ops:
  7.2 108.8 %all-gather.5.cloned.1.call-start = ((), (), s32[]{:S(2)}) async-start(), calls=%async_computation.2 | async-start | bytes 8650752 | tf_op jit(solution)/shard_map/all_gather | solution.py:1348
  8.9 178.9 %all-gather.7.cloned.1.call-start = ((), (), s32[]{:S(2)}) async-start(), calls=%async_computation.3 | async-start | bytes 6488064 | tf_op jit(solution)/shard_map/all_gather | solution.py:1363
  13.7 24.3 %collective-permute-start.3 = (f32[16,32]{1,0:T(8,128)S(1)}, f32[16,32]{1,0:T(8,128)}, u32[]{:S(2)}, u32[]{:S(2)}) collective-permute-start(f32[16,32]{1,0:T(8,128)S(1)} %concatenate.130), channel_id=1, source_target_pairs={{0,1},{1,0},{2,3},{3,2},{4,5},{5,4},{6,7},{7,6},{8,9},{9,8},{10,11... | collective-permute-start | bytes 6152 | tf_op jit(solution)/shard_map/ppermute | solution.py:1068
  19.4 28.1 %collective-permute-start.7 = (bf16[1024,512]{1,0:T(8,128)(2,1)S(1)}, bf16[1024,512]{1,0:T(8,128)(2,1)S(1)}, u32[]{:S(2)}, u32[]{:S(2)}) collective-permute-start(bf16[1024,512]{1,0:T(8,128)(2,1)S(1)} %get-tuple-element.450), channel_id=1, source_target_pairs={{0,1},{1,0},{2,3},{3,2},{4,5},{5,4},{6,7},{7,6},{8,9},{9,8},{10,11... | collective-permute-start | bytes 3145736 | tf_op jit(solution)/shard_map/ppermute | solution.py:1068
  19.5 28.0 %collective-permute-start = (bf16[64,1024]{1,0:T(8,128)(2,1)S(1)}, bf16[64,1024]{1,0:T(8,128)(2,1)S(1)}, u32[]{:S(2)}, u32[]{:S(2)}) collective-permute-start(bf16[64,1024]{1,0:T(8,128)(2,1)S(1)} %get-tuple-element.230), channel_id=1, source_target_pairs={{0,16},{16,0},{1,17},{17,1},{2,18},{18,2},{3,19},{19,3},{4,20},{20... | collective-permute-start | bytes 393224 | tf_op jit(solution)/shard_map/ppermute | solution.py:1068
  22.7 24.9 %collective-permute-start.1 = (bf16[64,1024]{1,0:T(8,128)(2,1)S(1)}, bf16[64,1024]{1,0:T(8,128)(2,1)S(1)}, u32[]{:S(2)}, u32[]{:S(2)}) collective-permute-start(bf16[64,1024]{1,0:T(8,128)(2,1)S(1)} %get-tuple-element.232), channel_id=1, source_target_pairs={{0,16},{16,0},{1,17},{17,1},{2,18},{18,2},{3,19},{19,3},{4,20},{20... | collective-permute-start | bytes 393224 | tf_op jit(solution)/shard_map/ppermute | solution.py:1068
  22.8 24.8 %collective-permute-start.2 = (bf16[64,1024]{1,0:T(8,128)(2,1)S(1)}, bf16[64,1024]{1,0:T(8,128)(2,1)}, u32[]{:S(2)}, u32[]{:S(2)}) collective-permute-start(bf16[64,1024]{1,0:T(8,128)(2,1)S(1)} %get-tuple-element.234), channel_id=1, source_target_pairs={{0,16},{16,0},{1,17},{17,1},{2,18},{18,2},{3,19},{19,3},{4,20},{20... | collective-permute-start | bytes 393224 | tf_op jit(solution)/shard_map/ppermute | solution.py:1068
  55.6 13.2 %collective-permute-start.10 = (bf16[2,64,1024]{2,1,0:T(8,128)(2,1)S(1)}, bf16[2,64,1024]{2,1,0:T(8,128)(2,1)S(1)}, u32[]{:S(2)}, u32[]{:S(2)}) collective-permute-start(bf16[2,64,1024]{2,1,0:T(8,128)(2,1)S(1)} %pad_maximum_fusion.9), channel_id=1, source_target_pairs={{0,4},{4,0},{1,5},{5,1},{2,6},{6,2},{3,7},{7,3},{8,12},{12,8},{9,1... | collective-permute-start | bytes 786440 | tf_op jit(solution)/shard_map/ppermute | solution.py:1068
  57.2 11.6 %collective-permute-start.9 = (bf16[2,64,1024]{2,1,0:T(8,128)(2,1)S(1)}, bf16[2,64,1024]{2,1,0:T(8,128)(2,1)S(1)}, u32[]{:S(2)}, u32[]{:S(2)}) collective-permute-start(bf16[2,64,1024]{2,1,0:T(8,128)(2,1)S(1)} %pad_maximum_fusion.8), channel_id=1, source_target_pairs={{0,1},{1,0},{2,3},{3,2},{4,5},{5,4},{6,7},{7,6},{8,9},{9,8},{10,11... | collective-permute-start | bytes 786440 | tf_op jit(solution)/shard_map/ppermute | solution.py:1068
  58.8 11.9 %collective-permute-start.8 = (bf16[2,64,1024]{2,1,0:T(8,128)(2,1)S(1)}, bf16[2,64,1024]{2,1,0:T(8,128)(2,1)S(1)}, u32[]{:S(2)}, u32[]{:S(2)}) collective-permute-start(bf16[2,64,1024]{2,1,0:T(8,128)(2,1)S(1)} %pad_maximum_fusion.7), channel_id=1, source_target_pairs={{0,8},{8,0},{1,9},{9,1},{2,10},{10,2},{3,11},{11,3},{4,12},{12,4},... | collective-permute-start | bytes 786440 | tf_op jit(solution)/shard_map/ppermute | solution.py:1068
  60.4 7.8 %collective-permute-start.11 = (f32[16,512]{1,0:T(8,128)S(1)}, f32[16,512]{1,0:T(8,128)S(1)}, u32[]{:S(2)}, u32[]{:S(2)}) collective-permute-start(f32[16,512]{1,0:T(8,128)S(1)} %maximum_select_fusion.2), channel_id=1, source_target_pairs={{0,16},{16,0},{1,17},{17,1},{2,18},{18,2},{3,19},{19,3},{4,20},{20... | collective-permute-start | bytes 98312 | tf_op jit(solution)/shard_map/ppermute | solution.py:1068
  70.7 20.1 %collective-permute-start.14 = (bf16[2,2,64,1024]{3,2,1,0:T(8,128)(2,1)S(1)}, bf16[2,2,64,1024]{3,2,1,0:T(8,128)(2,1)}, u32[]{:S(2)}, u32[]{:S(2)}) collective-permute-start(bf16[2,2,64,1024]{3,2,1,0:T(8,128)(2,1)S(1)} %pad_maximum_fusion.5), channel_id=1, source_target_pairs={{0,1},{1,0},{2,3},{3,2},{4,5},{5,4},{6,7},{7,6},{8,9},{9,8},{10,11... | collective-permute-start | bytes 1572872 | tf_op jit(solution)/shard_map/ppermute | solution.py:1068
  74.0 23.9 %collective-permute-start.13 = (bf16[2,2,64,1024]{3,2,1,0:T(8,128)(2,1)S(1)}, bf16[2,2,64,1024]{3,2,1,0:T(8,128)(2,1)S(1)}, u32[]{:S(2)}, u32[]{:S(2)}) collective-permute-start(bf16[2,2,64,1024]{3,2,1,0:T(8,128)(2,1)S(1)} %pad_maximum_fusion.4), channel_id=1, source_target_pairs={{0,8},{8,0},{1,9},{9,1},{2,10},{10,2},{3,11},{11,3},{4,12},{12,4},... | collective-permute-start | bytes 1572872 | tf_op jit(solution)/shard_map/ppermute | solution.py:1068
  75.4 22.5 %collective-permute-start.12 = (bf16[2,2,64,1024]{3,2,1,0:T(8,128)(2,1)S(1)}, bf16[2,2,64,1024]{3,2,1,0:T(8,128)(2,1)S(1)}, u32[]{:S(2)}, u32[]{:S(2)}) collective-permute-start(bf16[2,2,64,1024]{3,2,1,0:T(8,128)(2,1)S(1)} %pad_maximum_fusion.3), channel_id=1, source_target_pairs={{0,4},{4,0},{1,5},{5,1},{2,6},{6,2},{3,7},{7,3},{8,12},{12,8},{9,1... | collective-permute-start | bytes 1572872 | tf_op jit(solution)/shard_map/ppermute | solution.py:1068
  116.1 303.5 %reduce-scatter.2.cloned.1.call-start = ((), (), s32[]{:S(2)}) async-start(), calls=%async_computation.1 | async-start | bytes 11141120 | tf_op jit(solution)/shard_map/reduce_scatter | solution.py:1210
  116.4 30.1 %collective-permute-start.16 = (bf16[2,2,2,64,1024]{4,3,2,1,0:T(8,128)(2,1)S(1)}, bf16[2,2,2,64,1024]{4,3,2,1,0:T(8,128)(2,1)}, u32[]{:S(2)}, u32[]{:S(2)}) collective-permute-start(bf16[2,2,2,64,1024]{4,3,2,1,0:T(8,128)(2,1)S(1)} %pad_maximum_fusion.1.refs_4_), channel_id=1, source_target_pairs={{0,4},{4,0},{1,5},{5,1},{2,6},{6,2},{3,7},{7,3},{8,12},{12,8},{9,1... | collective-permute-start | bytes 3145736 | tf_op jit(solution)/shard_map/ppermute | solution.py:1068
  117.9 28.6 %collective-permute-start.15 = (bf16[2,2,2,64,1024]{4,3,2,1,0:T(8,128)(2,1)S(1)}, bf16[2,2,2,64,1024]{4,3,2,1,0:T(8,128)(2,1)}, u32[]{:S(2)}, u32[]{:S(2)}) collective-permute-start(bf16[2,2,2,64,1024]{4,3,2,1,0:T(8,128)(2,1)S(1)} %pad_maximum_fusion.refs_0_), channel_id=1, source_target_pairs={{0,1},{1,0},{2,3},{3,2},{4,5},{5,4},{6,7},{7,6},{8,9},{9,8},{10,11... | collective-permute-start | bytes 3145736 | tf_op jit(solution)/shard_map/ppermute | solution.py:1068
  120.2 39.8 %collective-permute-start.21 = (bf16[2,2,2,64,1024]{4,3,2,1,0:T(8,128)(2,1)S(1)}, bf16[2,2,2,64,1024]{4,3,2,1,0:T(8,128)(2,1)}, u32[]{:S(2)}, u32[]{:S(2)}) collective-permute-start(bf16[2,2,2,64,1024]{4,3,2,1,0:T(8,128)(2,1)S(1)} %pad_maximum_fusion.2.refs_1_.refs_0_), channel_id=1, source_target_pairs={{0,8},{8,0},{1,9},{9,1},{2,10},{10,2},{3,11},{11,3},{4,12},{12,4},... | collective-permute-start | bytes 3145736 | tf_op jit(solution)/shard_map/ppermute | solution.py:1068
  146.5 13.4 %collective-permute-start.17 = (bf16[2,2,2,64,1024]{4,3,2,1,0:T(8,128)(2,1)S(1)}, bf16[2,2,2,64,1024]{4,3,2,1,0:T(8,128)(2,1)S(1)}, u32[]{:S(2)}, u32[]{:S(2)}) collective-permute-start(bf16[2,2,2,64,1024]{4,3,2,1,0:T(8,128)(2,1)S(1)} %pad_maximum_fusion.refs_0_), channel_id=1, source_target_pairs={{0,2},{2,0},{1,3},{3,1},{4,6},{6,4},{5,7},{7,5},{8,10},{10,8},{9,1... | collective-permute-start | bytes 3145736 | tf_op jit(solution)/shard_map/ppermute | solution.py:1068
  146.7 13.3 %collective-permute-start.18 = (bf16[2,2,2,64,1024]{4,3,2,1,0:T(8,128)(2,1)}, bf16[2,2,2,64,1024]{4,3,2,1,0:T(8,128)(2,1)S(1)}, u32[]{:S(2)}, u32[]{:S(2)}) collective-permute-start(bf16[2,2,2,64,1024]{4,3,2,1,0:T(8,128)(2,1)} %collective-permute-done.15.refs_1_), channel_id=1, source_target_pairs={{0,2},{2,0},{1,3},{3,1},{4,6},{6,4},{5,7},{7,5},{8,10},{10,8},{9,1... | collective-permute-start | bytes 3145736 | tf_op jit(solution)/shard_map/ppermute | solution.py:1068
  147.1 12.9 %collective-permute-start.19 = (bf16[2,2,2,64,1024]{4,3,2,1,0:T(8,128)(2,1)S(1)}, bf16[2,2,2,64,1024]{4,3,2,1,0:T(8,128)(2,1)}, u32[]{:S(2)}, u32[]{:S(2)}) collective-permute-start(bf16[2,2,2,64,1024]{4,3,2,1,0:T(8,128)(2,1)S(1)} %pad_maximum_fusion.1.refs_4_), channel_id=1, source_target_pairs={{0,2},{2,0},{1,3},{3,1},{4,6},{6,4},{5,7},{7,5},{8,10},{10,8},{9,1... | collective-permute-start | bytes 3145736 | tf_op jit(solution)/shard_map/ppermute | solution.py:1068
  147.2 12.8 %collective-permute-start.20 = (bf16[2,2,2,64,1024]{4,3,2,1,0:T(8,128)(2,1)}, bf16[2,2,2,64,1024]{4,3,2,1,0:T(8,128)(2,1)}, u32[]{:S(2)}, u32[]{:S(2)}) collective-permute-start(bf16[2,2,2,64,1024]{4,3,2,1,0:T(8,128)(2,1)} %collective-permute-done.16.refs_5_), channel_id=1, source_target_pairs={{0,2},{2,0},{1,3},{3,1},{4,6},{6,4},{5,7},{7,5},{8,10},{10,8},{9,1... | collective-permute-start | bytes 3145736 | tf_op jit(solution)/shard_map/ppermute | solution.py:1068
  160.0 20.7 %collective-permute-start.22 = (bf16[2,2,2,64,1024]{4,3,2,1,0:T(8,128)(2,1)S(1)}, bf16[2,2,2,64,1024]{4,3,2,1,0:T(8,128)(2,1)S(1)}, u32[]{:S(2)}, u32[]{:S(2)}) collective-permute-start(bf16[2,2,2,64,1024]{4,3,2,1,0:T(8,128)(2,1)S(1)} %pad_maximum_fusion.2.refs_1_.refs_0_), channel_id=1, source_target_pairs={{0,2},{2,0},{1,3},{3,1},{4,6},{6,4},{5,7},{7,5},{8,10},{10,8},{9,1... | collective-permute-start | bytes 3145736 | tf_op jit(solution)/shard_map/ppermute | solution.py:1068
  161.0 19.8 %collective-permute-start.23 = (bf16[2,2,2,64,1024]{4,3,2,1,0:T(8,128)(2,1)}, bf16[2,2,2,64,1024]{4,3,2,1,0:T(8,128)(2,1)S(1)}, u32[]{:S(2)}, u32[]{:S(2)}) collective-permute-start(bf16[2,2,2,64,1024]{4,3,2,1,0:T(8,128)(2,1)} %collective-permute-done.21.refs_2_.refs_1_), channel_id=1, source_target_pairs={{0,2},{2,0},{1,3},{3,1},{4,6},{6,4},{5,7},{7,5},{8,10},{10,8},{9,1... | collective-permute-start | bytes 3145736 | tf_op jit(solution)/shard_map/ppermute | solution.py:1068
  211.4 26.6 %collective-permute-start.24 = (bf16[1024,512]{1,0:T(8,128)(2,1)}, bf16[1024,512]{1,0:T(8,128)(2,1)S(1)}, u32[]{:S(2)}, u32[]{:S(2)}) collective-permute-start(bf16[1024,512]{1,0:T(8,128)(2,1)} %get-tuple-element.297), channel_id=1, source_target_pairs={{0,1},{1,0},{2,3},{3,2},{4,5},{5,4},{6,7},{7,6},{8,9},{9,8},{10,11... | collective-permute-start | bytes 3145736 | tf_op jit(solution)/shard_map/ppermute | solution.py:1068
  259.7 29.4 %collective-permute-start.25 = (bf16[2,2,2,2,64,1024]{5,4,3,2,1,0:T(8,128)(2,1)}, bf16[2,2,2,2,64,1024]{5,4,3,2,1,0:T(8,128)(2,1)S(1)}, u32[]{:S(2)}, u32[]{:S(2)}) collective-permute-start(bf16[2,2,2,2,64,1024]{5,4,3,2,1,0:T(8,128)(2,1)} %get-tuple-element.309), channel_id=1, source_target_pairs={{0,2},{2,0},{1,3},{3,1},{4,6},{6,4},{5,7},{7,5},{8,10},{10,8},{9,1... | collective-permute-start | bytes 6291464 | tf_op jit(solution)/shard_map/ppermute | solution.py:1068
  259.8 29.3 %collective-permute-start.26 = (bf16[2,2,2,2,64,1024]{5,4,3,2,1,0:T(8,128)(2,1)}, bf16[2,2,2,2,64,1024]{5,4,3,2,1,0:T(8,128)(2,1)}, u32[]{:S(2)}, u32[]{:S(2)}) collective-permute-start(bf16[2,2,2,2,64,1024]{5,4,3,2,1,0:T(8,128)(2,1)} %get-tuple-element.310), channel_id=1, source_target_pairs={{0,2},{2,0},{1,3},{3,1},{4,6},{6,4},{5,7},{7,5},{8,10},{10,8},{9,1... | collective-permute-start | bytes 6291464 | tf_op jit(solution)/shard_map/ppermute | solution.py:1068
  293.0 49.9 %collective-permute-start.27 = (bf16[2,2,2,2,64,1024]{5,4,3,2,1,0:T(8,128)(2,1)S(1)}, bf16[2,2,2,2,64,1024]{5,4,3,2,1,0:T(8,128)(2,1)}, u32[]{:S(2)}, u32[]{:S(2)}) collective-permute-start(bf16[2,2,2,2,64,1024]{5,4,3,2,1,0:T(8,128)(2,1)S(1)} %add.324), channel_id=1, source_target_pairs={{0,1},{1,0},{2,3},{3,2},{4,5},{5,4},{6,7},{7,6},{8,9},{9,8},{10,11... | collective-permute-start | bytes 6291464 | tf_op jit(solution)/shard_map/ppermute | solution.py:1068
  301.4 23.7 %collective-permute-start.28 = (bf16[2,2,2,1,64,512]{5,4,3,2,1,0:T(8,128)(2,1)}, bf16[2,2,2,1,64,512]{5,4,3,2,1,0:T(8,128)(2,1)S(1)}, u32[]{:S(2)}, u32[]{:S(2)}) collective-permute-start(bf16[2,2,2,1,64,512]{5,4,3,2,1,0:T(8,128)(2,1)} %get-tuple-element.330), channel_id=1, source_target_pairs={{0,2},{2,0},{1,3},{3,1},{4,6},{6,4},{5,7},{7,5},{8,10},{10,8},{9,1... | collective-permute-start | bytes 1572872 | tf_op jit(solution)/shard_map/ppermute | solution.py:1068
  301.5 23.6 %collective-permute-start.29 = (bf16[2,2,2,1,64,512]{5,4,2,1,3,0:T(8,128)(2,1)}, bf16[2,2,2,1,64,512]{5,4,2,1,3,0:T(8,128)(2,1)S(1)}, u32[]{:S(2)}, u32[]{:S(2)}) collective-permute-start(bf16[2,2,2,1,64,512]{5,4,2,1,3,0:T(8,128)(2,1)} %bitcast.282), channel_id=1, source_target_pairs={{0,2},{2,0},{1,3},{3,1},{4,6},{6,4},{5,7},{7,5},{8,10},{10,8},{9,1... | collective-permute-start | bytes 1572872 | tf_op jit(solution)/shard_map/ppermute | solution.py:1068
  326.1 16.9 %collective-permute-start.30 = (bf16[2,2,2,1,64,512]{5,4,3,2,1,0:T(8,128)(2,1)S(1)}, bf16[2,2,2,1,64,512]{5,4,3,2,1,0:T(8,128)(2,1)}, u32[]{:S(2)}, u32[]{:S(2)}) collective-permute-start(bf16[2,2,2,1,64,512]{5,4,3,2,1,0:T(8,128)(2,1)S(1)} %add.325), channel_id=1, source_target_pairs={{0,4},{4,0},{1,5},{5,1},{2,6},{6,2},{3,7},{7,3},{8,12},{12,8},{9,1... | collective-permute-start | bytes 1572872 | tf_op jit(solution)/shard_map/ppermute | solution.py:1068
  343.0 26.4 %collective-permute-start.33 = (bf16[3,2,2,2,64,512]{5,4,3,2,1,0:T(8,128)(2,1)}, bf16[3,2,2,2,64,512]{5,4,3,2,1,0:T(8,128)(2,1)}, u32[]{:S(2)}, u32[]{:S(2)}) collective-permute-start(bf16[3,2,2,2,64,512]{5,4,3,2,1,0:T(8,128)(2,1)} %get-tuple-element.362), channel_id=1, source_target_pairs={{0,2},{2,0},{1,3},{3,1},{4,6},{6,4},{5,7},{7,5},{8,10},{10,8},{9,1... | collective-permute-start | bytes 4718600 | tf_op jit(solution)/shard_map/ppermute | solution.py:1068
  343.0 26.4 %collective-permute-start.34 = (bf16[3,2,2,2,64,512]{5,4,3,2,1,0:T(8,128)(2,1)}, bf16[3,2,2,2,64,512]{5,4,3,2,1,0:T(8,128)(2,1)S(1)}, u32[]{:S(2)}, u32[]{:S(2)}) collective-permute-start(bf16[3,2,2,2,64,512]{5,4,3,2,1,0:T(8,128)(2,1)} %get-tuple-element.363), channel_id=1, source_target_pairs={{0,2},{2,0},{1,3},{3,1},{4,6},{6,4},{5,7},{7,5},{8,10},{10,8},{9,1... | collective-permute-start | bytes 4718600 | tf_op jit(solution)/shard_map/ppermute | solution.py:1068
  345.3 24.1 %collective-permute-start.32 = (bf16[2,2,1,64,512]{4,3,1,0,2:T(8,128)(2,1)}, bf16[2,2,1,64,512]{4,3,1,0,2:T(8,128)(2,1)S(1)}, u32[]{:S(2)}, u32[]{:S(2)}) collective-permute-start(bf16[2,2,1,64,512]{4,3,1,0,2:T(8,128)(2,1)} %fusion.13), channel_id=1, source_target_pairs={{0,1},{1,0},{2,3},{3,2},{4,5},{5,4},{6,7},{7,6},{8,9},{9,8},{10,11... | collective-permute-start | bytes 786440 | tf_op jit(solution)/shard_map/ppermute | solution.py:1068
  351.1 42.4 %collective-permute-start.31 = (bf16[2,2,2,64,1024]{4,3,2,1,0:T(8,128)(2,1)}, bf16[2,2,2,64,1024]{4,3,2,1,0:T(8,128)(2,1)}, u32[]{:S(2)}, u32[]{:S(2)}) collective-permute-start(bf16[2,2,2,64,1024]{4,3,2,1,0:T(8,128)(2,1)} %get-tuple-element.433), channel_id=1, source_target_pairs={{0,4},{4,0},{1,5},{5,1},{2,6},{6,2},{3,7},{7,3},{8,12},{12,8},{9,1... | collective-permute-start | bytes 3145736 | tf_op jit(solution)/shard_map/ppermute | solution.py:1068
  372.5 21.0 %collective-permute-start.36 = (bf16[2,2,2,64,512]{4,3,2,1,0:T(8,128)(2,1)}, bf16[2,2,2,64,512]{4,3,2,1,0:T(8,128)(2,1)S(1)}, u32[]{:S(2)}, u32[]{:S(2)}) collective-permute-start(bf16[2,2,2,64,512]{4,3,2,1,0:T(8,128)(2,1)} %get-tuple-element.447), channel_id=1, source_target_pairs={{0,4},{4,0},{1,5},{5,1},{2,6},{6,2},{3,7},{7,3},{8,12},{12,8},{9,1... | collective-permute-start | bytes 1572872 | tf_op jit(solution)/shard_map/ppermute | solution.py:1068
  373.2 20.4 %collective-permute-start.37 = (bf16[2,2,2,64,512]{4,3,2,1,0:T(8,128)(2,1)}, bf16[2,2,2,64,512]{4,3,2,1,0:T(8,128)(2,1)S(1)}, u32[]{:S(2)}, u32[]{:S(2)}) collective-permute-start(bf16[2,2,2,64,512]{4,3,2,1,0:T(8,128)(2,1)} %get-tuple-element.446), channel_id=1, source_target_pairs={{0,1},{1,0},{2,3},{3,2},{4,5},{5,4},{6,7},{7,6},{8,9},{9,8},{10,11... | collective-permute-start | bytes 1572872 | tf_op jit(solution)/shard_map/ppermute | solution.py:1068
  374.6 19.0 %collective-permute-start.38 = (bf16[2,2,2,64,512]{4,3,2,1,0:T(8,128)(2,1)S(1)}, bf16[2,2,2,64,512]{4,3,2,1,0:T(8,128)(2,1)S(1)}, u32[]{:S(2)}, u32[]{:S(2)}) collective-permute-start(bf16[2,2,2,64,512]{4,3,2,1,0:T(8,128)(2,1)S(1)} %get-tuple-element.445), channel_id=1, source_target_pairs={{0,8},{8,0},{1,9},{9,1},{2,10},{10,2},{3,11},{11,3},{4,12},{12,4},... | collective-permute-start | bytes 1572872 | tf_op jit(solution)/shard_map/ppermute | solution.py:1068
  377.2 16.3 %collective-permute-start.35 = (bf16[2,1,64,512]{3,2,0,1:T(8,128)(2,1)S(1)}, bf16[2,1,64,512]{3,2,0,1:T(8,128)(2,1)S(1)}, u32[]{:S(2)}, u32[]{:S(2)}) collective-permute-start(bf16[2,1,64,512]{3,2,0,1:T(8,128)(2,1)S(1)} %fusion.24), channel_id=1, source_target_pairs={{0,8},{8,0},{1,9},{9,1},{2,10},{10,2},{3,11},{11,3},{4,12},{12,4},... | collective-permute-start | bytes 393224 | tf_op jit(solution)/shard_map/ppermute | solution.py:1068
  393.6 7.7 %collective-permute-start.45 = (f32[12,1024]{1,0:T(8,128)}, f32[12,1024]{1,0:T(8,128)S(1)}, u32[]{:S(2)}, u32[]{:S(2)}) collective-permute-start(f32[12,1024]{1,0:T(8,128)} %get-tuple-element.395), channel_id=1, source_target_pairs={{0,16},{16,0},{1,17},{17,1},{2,18},{18,2},{3,19},{19,3},{4,20},{20... | collective-permute-start | bytes 147464 | tf_op jit(solution)/shard_map/ppermute | solution.py:1068
  396.2 16.3 %collective-permute-start.39 = (bf16[2,2,64,1024]{3,2,1,0:T(8,128)(2,1)S(1)}, bf16[2,2,64,1024]{3,2,1,0:T(8,128)(2,1)S(1)}, u32[]{:S(2)}, u32[]{:S(2)}) collective-permute-start(bf16[2,2,64,1024]{3,2,1,0:T(8,128)(2,1)S(1)} %get-tuple-element.449), channel_id=1, source_target_pairs={{0,8},{8,0},{1,9},{9,1},{2,10},{10,2},{3,11},{11,3},{4,12},{12,4},... | collective-permute-start | bytes 1572872 | tf_op jit(solution)/shard_map/ppermute | solution.py:1068
  397.4 22.1 %collective-permute-start.42 = (bf16[2,2,64,512]{3,2,1,0:T(8,128)(2,1)S(1)}, bf16[2,2,64,512]{3,2,1,0:T(8,128)(2,1)S(1)}, u32[]{:S(2)}, u32[]{:S(2)}) collective-permute-start(bf16[2,2,64,512]{3,2,1,0:T(8,128)(2,1)S(1)} %get-tuple-element.444), channel_id=1, source_target_pairs={{0,8},{8,0},{1,9},{9,1},{2,10},{10,2},{3,11},{11,3},{4,12},{12,4},... | collective-permute-start | bytes 786440 | tf_op jit(solution)/shard_map/ppermute | solution.py:1068
  399.2 20.3 %collective-permute-start.43 = (bf16[2,2,64,512]{3,2,1,0:T(8,128)(2,1)S(1)}, bf16[2,2,64,512]{3,2,1,0:T(8,128)(2,1)S(1)}, u32[]{:S(2)}, u32[]{:S(2)}) collective-permute-start(bf16[2,2,64,512]{3,2,1,0:T(8,128)(2,1)S(1)} %get-tuple-element.442), channel_id=1, source_target_pairs={{0,4},{4,0},{1,5},{5,1},{2,6},{6,2},{3,7},{7,3},{8,12},{12,8},{9,1... | collective-permute-start | bytes 786440 | tf_op jit(solution)/shard_map/ppermute | solution.py:1068
  401.2 18.3 %collective-permute-start.44 = (bf16[2,2,64,512]{3,2,1,0:T(8,128)(2,1)S(1)}, bf16[2,2,64,512]{3,2,1,0:T(8,128)(2,1)S(1)}, u32[]{:S(2)}, u32[]{:S(2)}) collective-permute-start(bf16[2,2,64,512]{3,2,1,0:T(8,128)(2,1)S(1)} %get-tuple-element.435), channel_id=1, source_target_pairs={{0,1},{1,0},{2,3},{3,2},{4,5},{5,4},{6,7},{7,6},{8,9},{9,8},{10,11... | collective-permute-start | bytes 786440 | tf_op jit(solution)/shard_map/ppermute | solution.py:1068
  402.6 13.5 %collective-permute-start.41 = (bf16[1,64,512]{2,1,0:T(8,128)(2,1)S(1)}, bf16[1,64,512]{2,1,0:T(8,128)(2,1)S(1)}, u32[]{:S(2)}, u32[]{:S(2)}) collective-permute-start(bf16[1,64,512]{2,1,0:T(8,128)(2,1)S(1)} %fusion.30), channel_id=1, source_target_pairs={{0,16},{16,0},{1,17},{17,1},{2,18},{18,2},{3,19},{19,3},{4,20},{20... | collective-permute-start | bytes 196616 | tf_op jit(solution)/shard_map/ppermute | solution.py:1068
  412.7 17.1 %collective-permute-start.40 = (bf16[2,64,1024]{2,1,0:T(8,128)(2,1)S(1)}, bf16[2,64,1024]{2,1,0:T(8,128)(2,1)S(1)}, u32[]{:S(2)}, u32[]{:S(2)}) collective-permute-start(bf16[2,64,1024]{2,1,0:T(8,128)(2,1)S(1)} %get-tuple-element.452), channel_id=1, source_target_pairs={{0,16},{16,0},{1,17},{17,1},{2,18},{18,2},{3,19},{19,3},{4,20},{20... | collective-permute-start | bytes 786440 | tf_op jit(solution)/shard_map/ppermute | solution.py:1068
  420.6 9.1 %collective-permute-start.51 = (bf16[64,2560]{1,0:T(8,128)(2,1)S(1)}, bf16[64,2560]{1,0:T(8,128)(2,1)S(1)}, u32[]{:S(2)}, u32[]{:S(2)}) collective-permute-start(bf16[64,2560]{1,0:T(8,128)(2,1)S(1)} %dynamic-slice_bitcast_fusion), channel_id=1, source_target_pairs={{0,1},{1,0},{2,3},{3,2},{4,5},{5,4},{6,7},{7,6},{8,9},{9,8},{10,11... | collective-permute-start | bytes 983048 | tf_op jit(solution)/shard_map/ppermute | solution.py:1068
  432.3 9.4 %collective-permute-start.52 = (bf16[3,64,512]{2,1,0:T(8,128)(2,1)S(1)}, bf16[3,64,512]{2,1,0:T(8,128)(2,1)S(1)}, u32[]{:S(2)}, u32[]{:S(2)}) collective-permute-start(bf16[3,64,512]{2,1,0:T(8,128)(2,1)S(1)} %pad_maximum_fusion.12), channel_id=1, source_target_pairs={{0,16},{16,0},{1,17},{17,1},{2,18},{18,2},{3,19},{19,3},{4,20},{20... | collective-permute-start | bytes 589832 | tf_op jit(solution)/shard_map/ppermute | solution.py:1068
  (44 other events, 432.5 us)
Sparse Core Ops, SparseCore 0:
  11.0 104.9 all-gather.4
  118.9 68.7 all-gather.6
  238.2 122.1 reduce-scatter.1

commit v7 on v6

--- a/solution.py
+++ b/solution.py
@@ -606,12 +606,18 @@
     )(co, *models, *chans)
 
 
-def channel_back_kernel(co, dkv, mixed, hidden, active, *refs, layout, part, order):
-    recept, refs = refs[: 2 * (1 - part)], refs[2 * (1 - part) :]
+def channel_back_kernel(co, dkv, mixed, active, *refs, layout, part, order):
+    if part == 0:
+        (hidden, hidden_1, *recept), refs = refs[:4], refs[4:]
     arrays, refs = take_refs(refs, layout)
-    dkey, *targets, grads, narrow, sems, whole, sems_in = refs
+    dkey, targets, refs = refs[0], refs[1:5], refs[5:]
+    if part == 0:
+        blocks, *refs = refs
+        grads, narrow, *refs = refs
+    other, sems, whole, sems_in = refs
     j = pl.program_id(0)
-    per_half = grads.shape[4] // WIDE
+    wide = other.shape[3]
+    per_half = wide // WIDE
     columns = pl.ds(pl.multiple_of(lax.rem(j, per_half) * WIDE, WIDE), WIDE)
     turn = lax.div(j, per_half)
     half = co[4] ^ turn
@@ -620,10 +626,12 @@
     def _():
         start_weight(co, arrays, whole, sems_in, layout)
 
-    def keep(n, values):
-        grads[n, half, :, :, columns] = values.astype(BF).reshape(16, SLOT, WIDE)
-
-    keep(0, dot(dkv[...], hidden[...], TN))
+    def cut(values):
+        return values.astype(BF).reshape(16, SLOT, WIDE)
+
+    if part == 0:
+        other[half, :, :, columns] = cut(dot(dkv[...], hidden_1[...], TN))
+        grads[0, half, :, :, columns] = cut(dot(dkv[...], hidden[...], TN))
 
     for which in (0, 1):
 
@@ -634,23 +642,32 @@
     back = dot(dkv[...], rows_of(whole, half, columns), NN)
     back = (2.0 * active[...].astype(F32) * back).astype(BF)
     dkey[...] = back
-    keep(1, dot(mixed[...], back, TN))
-
-    wide = grads.shape[4]
-
-    def narrow_copy(turn):
-        return pltpu.make_async_copy(
-            narrow.at[turn],
-            targets[0].at[:, co[4] ^ turn, :, pl.ds(2 * wide, narrow.shape[3])],
-            sems.at[2 + turn],
-        )
-
+    found = cut(dot(mixed[...], back, TN))
     if part == 0:
+        grads[1, half, :, :, columns] = found
+    else:
+        other[half, :, :, columns] = found
+
+    for which in (0, 1):
+
+        @pl.when(j == (which + 1) * per_half - 1)
+        def _(which=which):
+            start_grads(co, other, targets, 0, sems.at[0], order, which, True)
+
+    if part == 0:
+
+        def narrow_copy(turn):
+            return pltpu.make_async_copy(
+                narrow.at[turn],
+                blocks.at[:, co[4] ^ turn, :, pl.ds(2 * wide, narrow.shape[3])],
+                sems.at[3 + turn],
+            )
+
         for n in (0, 1):
             pltpu.make_async_copy(
                 grads.at[n, half, :, :, columns],
-                targets[0].at[:, half, :, pl.ds(pl.multiple_of(n * wide + columns.start, WIDE), WIDE)],
-                sems.at[n],
+                blocks.at[:, half, :, pl.ds(pl.multiple_of(n * wide + columns.start, WIDE), WIDE)],
+                sems.at[1 + n],
             ).start()
 
         @pl.when(lax.rem(j, per_half) == 0)
@@ -660,66 +677,53 @@
             narrow[turn] = found.astype(BF).reshape(16, SLOT, size)
             narrow_copy(turn).start()
 
-    for which in range(2 * part):
-
-        @pl.when(turn == which)
-        def _(which=which):
-            for array, index, rel in rel_slots(order):
-                if rel["x"] == which:
-                    block, at = slot_place(co, rel)
-                    for n in (0, 1):
-                        pltpu.make_async_copy(
-                            grads.at[n, at, block, :, columns],
-                            targets[array].at[index + (n, slice(None), columns)],
-                            sems.at[n],
-                        ).start()
-
     @pl.when(j == pl.num_programs(0) - 1)
     def _():
-        for n in (0, 1):
-            wait_bytes(grads.at[n], sems.at[n])
-            if part == 0:
+        wait_bytes(other, sems.at[0])
+        if part == 0:
+            for n in (0, 1):
+                wait_bytes(grads.at[n], sems.at[1 + n])
                 narrow_copy(n).wait()
 
 
 def channel_back(co, dkv, mixed, hidden, active, recept, weight, half, part, order):
     tokens, width = dkv.shape
     per_half = half // WIDE
-    skip, stride = part * per_half, hidden.shape[1] // 2 // WIDE
-
-    def tile(j, co):
-        return 0, (co[4] ^ lax.div(j, per_half)) * stride + skip + lax.rem(j, per_half)
+    stride = active.shape[1] // 2 // WIDE
+
+    def tile_of(skip):
+        return lambda j, co: (
+            0,
+            (co[4] ^ lax.div(j, per_half)) * stride + skip + lax.rem(j, per_half),
+        )
 
     fixed = pl.BlockSpec((tokens, width), lambda j, co: (0, 0))
-    block = pl.BlockSpec((tokens, WIDE), tile)
+    own, other = (pl.BlockSpec((tokens, WIDE), tile_of(n * per_half)) for n in (part, 1 - part))
+    first = part == 0
     return pl.pallas_call(
         functools.partial(channel_back_kernel, layout=weight[0], part=part, order=order),
         grid_spec=pltpu.PrefetchScalarGridSpec(
             num_scalar_prefetch=1,
             grid=(2 * per_half,),
-            in_specs=[fixed, fixed, block, block]
-            + [fixed] * len(recept)
+            in_specs=[fixed, fixed, own]
+            + [own, other, fixed, fixed] * first
             + [anywhere()] * len(weight[1]),
             out_specs=[pl.BlockSpec((tokens, WIDE), column_tile(per_half))]
-            + [anywhere()] * (1 + 3 * part),
+            + [anywhere()] * (4 + first),
             scratch_shapes=[
                 pltpu.VMEM((2, 2, 16, SLOT, half), BF),
                 pltpu.VMEM((2, 16, SLOT, width // 2), BF),
-                pltpu.SemaphoreType.DMA((4,)),
             ]
+            * first
+            + [pltpu.VMEM((2, 16, SLOT, half), BF), pltpu.SemaphoreType.DMA((5,))]
             + weight_scratch(weight),
         ),
-        out_shape=[
-            jax.ShapeDtypeStruct((tokens, 2 * half), BF),
-            *(
-                [jax.ShapeDtypeStruct((2, 2, 2, 2, SLOT, half), BF)] * 4
-                if part
-                else [jax.ShapeDtypeStruct((16, 2, SLOT, 2 * half + width // 2), BF)]
-            ),
-        ],
+        out_shape=[jax.ShapeDtypeStruct((tokens, 2 * half), BF)]
+        + [jax.ShapeDtypeStruct((2, 2, 2, 1, SLOT, half), BF)] * 4
+        + [jax.ShapeDtypeStruct((16, 2, SLOT, 2 * half + width // 2), BF)] * first,
         compiler_params=params(),
         cost_estimate=cost(half / 512 * 3.3, half / 512 * (14 << 20)),
-    )(co, dkv, mixed, hidden, active, *recept, *weight[1])
+    )(co, dkv, mixed, active, *(hidden, hidden, *recept)[: 4 * first], *weight[1])
 
 
 def middle_back_kernel(
@@ -1414,7 +1418,7 @@
         return lax.dynamic_update_slice_in_dim(kept, arrived, (1 - side) * tokens, 0)
 
     back = functools.partial(channel_back, co)
-    order_b, order_c = "wuyx", "wuxy"
+    order_b, order_c = "wuyx", "wuyx"
     edge = jnp.zeros((8, width), F32)
 
     def input_back_part(dmix, part, after, before, found):
@@ -1423,42 +1427,45 @@
         )
 
     if fast:
-        dkey_0, blocks = back(
+        dkey_0, *found, blocks = back(
             dkv, mixed_k2, hidden, active, (mixed_r2, drec2), cvalue_w[0], split, 0, order_b
         )
-        dkv, arrived, blocks = seal(dkv, arrived, blocks)
+        group_v = Merged(found, order_b)
+        dkv, arrived, blocks = seal_all((group_v,), dkv, arrived, blocks)
         blocks = scatter_rows(blocks)
-        dkey_1, *found = back(dkv, mixed_k2, hidden, active, (), cvalue_w[1], split, 1, order_b)
+        group_v.step()
+        dkey_1, *found = back(dkv, mixed_k2, None, active, (), cvalue_w[1], split, 1, order_b)
         group_b = Merged(found, order_b)
-        (dkey_1,) = seal_all((group_b,), dkey_1)
-        group_b.step()
+        (dkey_1,) = seal_all((group_v, group_b), dkey_1)
+        step_all(group_v, group_b)
         outputs = outputs_of(kept, arrived)
         dmid, dtime, sums2 = middle_back(
             co, (dkey_0, dkey_1), drec2, middle, dres, lead, vectors, ckey_w, crecept_w
         )
-        (dtime,) = seal_all((group_b,), dtime)
-        group_b.step()
+        (dtime,) = seal_all((group_v, group_b), dtime)
+        step_all(group_v, group_b)
         found = weight_grads(co, ((dtime, gated, order_c),), merged=True)
         group_c = Merged(found, order_c)
         dtime, outputs = seal_all((group_c,), dtime, outputs)
         group_c.step()
         *dmix, sums_t = time_back(co, dtime, saved, vectors, masks_up, output_w)
-        (dmix, dmid) = seal_all((group_c,), dmix, dmid)
-        group_c.step()
+        (dmix, dmid) = seal_all((group_v, group_b, group_c), dmix, dmid)
+        step_all(group_v, group_b, group_c)
         found = weight_grads(co, [(m, d, order) for m, d, order in zip(mixed, dmix, three_orders)])
         group_t = Reduce(found, three_orders)
-        (dmix,) = seal_all((group_b, group_c, group_t), dmix)
+        (dmix,) = seal_all((group_v, group_b, group_c, group_t), dmix)
+        step_all(group_v, group_b, group_c, group_t)
+        found, totals, edge = input_back_part(dmix, 0, edge, (sums_t, sums2, loss_rows), dres)
+        (dmix, edge, found) = seal_all((group_v, group_b, group_c, group_t), dmix, edge, found)
         step_all(group_b, group_c, group_t)
-        found, totals, edge = input_back_part(dmix, 0, edge, (sums_t, sums2, loss_rows), dres)
-        (dmix, edge, found) = seal_all((group_c, group_t), dmix, edge, found)
-        step_all(group_c, group_t)
         input_grad, totals, _ = input_back_part(dmix, 1, edge, (totals,), found)
     else:
-        dkey_1, *found = back(dkv, mixed_k2, hidden, active, (), cvalue_w[1], split, 1, order_b)
-        dkey_0, blocks = back(
+        dkey_0, *found, blocks = back(
             dkv, mixed_k2, hidden, active, (mixed_r2, drec2), cvalue_w[0], split, 0, order_b
         )
-        value_1, ckey_1 = reduce_merged(found, order_b)
+        (value_1,) = reduce_merged(found, order_b)
+        dkey_1, *found = back(dkv, mixed_k2, None, active, (), cvalue_w[1], split, 1, order_b)
+        (ckey_1,) = reduce_merged(found, order_b)
         value_0, ckey_0 = (
             reduce_blocks(blocks[..., n * split : (n + 1) * split]) for n in (0, 1)
         )
@@ -1492,7 +1499,7 @@
                 totals, blocks = seal_all((group_b, group_c, group_t), totals, blocks)
                 cvalue_g, ckey_g = (
                     jnp.concatenate([blocks[:, n * split : (n + 1) * split], found], axis=1)
-                    for n, found in enumerate(group_b.finish())
+                    for n, found in enumerate(group_v.finish() + group_b.finish())
                 )
                 cvalue_g = cvalue_g.T
             elif axes == "wc":

time: 459 us -> 455 us (level)
  waiting for transfers between devices: 79.5 us -> 64 us
  starting transfers between devices: 55 us -> 60.1 us
  other arithmetic: 38.3 us -> 43.2 us
    ppermute x55 -> x61, waiting for transfers between devices: 54.3 us -> 39.2 us  [swap(): return lax.ppermute(values, axis, SWAP)]
    ppermute x55 -> x61, starting transfers between devices: 54.8 us -> 60 us  [swap(): return lax.ppermute(values, axis, SWAP)]
    convert_element_type x9 -> x15, other arithmetic: 10.3 us -> 14.2 us  [step(): sum((part[place].astype(F32) for part in self.state)).astype(BF)]
  transfers between devices with their start and end apart: 58 -> 64, of which waited for: 18 -> 16; matrix products, arithmetic and copies ran while one was open for 12% -> 13% of each run, Pallas kernels for 47% -> 47%
where the time goes in v7:
time: 455 us; the launch traced here: 449 us
  Pallas kernels  237 us (52%)
  waiting for transfers between devices  64 us (14%)
  starting transfers between devices  60.1 us (13%)
  other arithmetic  43.2 us (9%)
  local copies, waits for them, and re-layouts  26.5 us (6%)
  between operations  18.4 us (4%)
    ppermute x61, starting transfers between devices, swap(): return lax.ppermute(values, axis, SWAP)  60 us
    pallas_call x2, Pallas kernels, channel_back(): pl.pallas_call(functools.partial(channel_back_kernel, layout=weight[0], p...  48.2 us
    ppermute x61, waiting for transfers between devices, swap(): return lax.ppermute(values, axis, SWAP)  39.2 us
    pallas_call x2, Pallas kernels, input_back(): pl.pallas_call(functools.partial(input_back_kernel, layouts=[w[0] for w i...  30.3 us
    pallas_call x1, Pallas kernels, middle_back(): pl.pallas_call(functools.partial(middle_back_kernel, layouts=[weight[0],...  28.9 us
    pallas_call x1, Pallas kernels, time_forward(): pl.pallas_call(functools.partial(time_forward_kernel, layouts=[w[0] for w...  26.4 us
    pallas_call x1, Pallas kernels, result_step(): pl.pallas_call(functools.partial(result_kernel, layouts=[weight[0], recep...  23.6 us
    pallas_call x1, Pallas kernels, time_back(): pl.pallas_call(functools.partial(time_back_kernel, layout=weight[0]), gri...  23 us
  transfers between devices with their start and end apart: 64, of which 16 were waited for; matrix products, arithmetic and copies ran while one was open for 13% of the time, Pallas kernels for 47%

profile of v7, /device:TPU:0, one launch (start us, length us, event | category | flops | bytes accessed | tf_op | source)
XLA Modules:
  0.0 449.1 jit_solution(13178316193896920209)
XLA Ops:
  7.2 1.6 pad_maximum_fusion.10
  13.7 3.0 collective-permute-start.3
  16.7 2.7 constant_dynamic-slice_fusion.1
  19.5 3.1 collective-permute-start
  22.8 2.9 collective-permute-start.2
  35.8 1.5 pad_maximum_fusion.11
  40.1 1.5 collective-permute-start.5
  41.7 2.0 collective-permute-done.5
  43.8 1.6 collective-permute-start.6
  45.4 2.1 collective-permute-done.6
  47.6 2.1 broadcast_in_dim.142.masks
  49.7 1.9 broadcast_in_dim.134.masks
  55.5 1.6 collective-permute-start.10
  57.1 1.6 collective-permute-start.9
  58.7 1.6 collective-permute-start.8
  61.1 6.9 %collective-permute-done.11 = f32[16,512]{1,0:T(8,128)S(1)} collective-permute-done((f32[16,512]{1,0:T(8,128)S(1)}, f32[16,512]{1,0:T(8,128)S(1)}, u32[]{:S(2)}, u32[]{:S(2)}) %collective-permute-start.11) | collective-permute-done | bytes 32800 | tf_op jit(solution)/shard_map/ppermute | solution.py:1072
  70.1 3.9 collective-permute-start.14
  75.9 7.4 %shard_map.364 = (bf16[1024,1024]{1,0:T(8,128)(2,1)}, bf16[1024,1024]{1,0:T(8,128)(2,1)}, bf16[1024,1024]{1,0:T(8,128)(2,1)}) custom-call(bf16[1024,1024]{1,0:T(8,128)(2,1)} %x_ref.7, f32[1024,128]{1,0:T(8,128)} %broadcast_in_dim.143.carry_ref, f32[16,1024]{1,0:T(8,128)} %maximum_select_fusion.1.vec_ref.vec), custom_call_target="tpu_custom_call" | custom-call | bytes 83886 | tf_op jit(solution)/shard_map/pallas_call | solution.py:211
  83.3 4.1 collective-permute-done.14
  87.4 10.3 %collective-permute-done.13 = bf16[2,2,64,1024]{3,2,1,0:T(8,128)(2,1)S(1)} collective-permute-done((bf16[2,2,64,1024]{3,2,1,0:T(8,128)(2,1)S(1)}, bf16[2,2,64,1024]{3,2,1,0:T(8,128)(2,1)S(1)}, u32[]{:S(2)}, u32[]{:S(2)}) %collective-permute-start.13) | collective-permute-done | bytes 524320 | tf_op jit(solution)/shard_map/ppermute | solution.py:1072
  97.8 18.2 %all-gather.5.cloned.1.call-done = bf16[2048,2048]{1,0:T(8,128)(2,1)} async-done(((bf16[64,2048]{1,0:T(8,128)(2,1)}), bf16[2048,2048]{1,0:T(8,128)(2,1)}) %all-gather.5.cloned.1.call-update) | async-done | bytes 8388624 | tf_op jit(solution)/shard_map/all_gather | solution.py:1352
  120.1 26.4 %shard_map.365 = (f32[1024,1024]{1,0:T(8,128)}, f32[1024,1024]{1,0:T(8,128)}, f32[1024,1024]{1,0:T(8,128)}, f32[1024,1024]{1,0:T(8,128)}, f32[1024,1024]{1,0:T(8,128)}, /*index=5*/bf16[1024,1024]{1,0:T(8,128)(2,1)}) custom-call(s32[5]{0:T(128)} %stack.159.co, bf16[1024,1024]{1,0:T(8,128)(2,1)} %get-tuple-element.281.mk.refs_0_, ...), custom_call_target="tpu_custom_call" | custom-call | flops 171798688 | bytes 356515 | tf_op jit(solution)/shard_map/pallas_call | solution.py:316
  147.6 12.4 %shard_map.366 = (f32[1024,1024]{1,0:T(8,128)}, bf16[1024,1024]{1,0:T(8,128)(2,1)}, bf16[1024,1024]{1,0:T(8,128)(2,1)}) custom-call(s32[5]{0:T(128)} %stack.159.co, bf16[1024,1024]{1,0:T(8,128)(2,1)} %get-tuple-element.293.gated.refs_1_, bf16[1024,1024]{1,0:T(8,128)(2,1)} %x_ref.7, f32[1024,128]{1,0:T(8,128)} %broadcast_in_dim.143.carry_ref, ...), custom_call_target="tpu_custom_call" | custom-call | flops 64424508 | bytes 146800 | tf_op jit(solution)/shard_map/pallas_call | solution.py:383
  163.5 17.5 %shard_map.367 = (bf16[1024,4096]{1,0:T(8,128)(2,1)}, bf16[1024,4096]{1,0:T(8,128)(2,1)}) custom-call(s32[5]{0:T(128)} %stack.159.co, bf16[1024,1024]{1,0:T(8,128)(2,1)} %get-tuple-element.299.mk.mixed, bf16[2,2,2,64,1024]{4,3,2,1,0:T(8,128)(2,1)} %copy-done.2, bf16[2,2,2,64,1024]{4,3,2,1,0:T(8,128)(2,1)} %collective-permute-done.15.refs_1_, ...), custom_call_target="tpu_custom_call" | custom-call | flops 96636768 | bytes 272629 | tf_op jit(solution)/shard_map/pallas_call | solution.py:437
  181.0 6.5 %all-gather.7.cloned.1.call-done = bf16[2048,1536]{1,0:T(8,128)(2,1)} async-done(((bf16[64,1536]{1,0:T(8,128)(2,1)}), bf16[2048,1536]{1,0:T(8,128)(2,1)}) %all-gather.7.cloned.1.call-update) | async-done | bytes 6291472 | tf_op jit(solution)/shard_map/all_gather | solution.py:1367
  187.5 23.6 %shard_map.368 = (bf16[2048,512]{1,0:T(8,128)(2,1)}, bf16[1024,512]{1,0:T(8,128)(2,1)}, f32[1024,1024]{1,0:T(8,128)}, bf16[1024,1024]{1,0:T(8,128)(2,1)}, bf16[1024,1024]{1,0:T(8,128)(2,1)}, /*index=5*/f32[8,1024]{1,0:T(8,128)}) custom-call(s32[5]{0:T(128)} %copy-done.40, f32[1]{0:T(128)} %bitcast.38.scale, ...), custom_call_target="tpu_custom_call" | custom-call | flops 150323856 | bytes 398458 | tf_op jit(solution)/shard_map/pallas_call | solution.py:508
  212.6 30.6 %shard_map.369 = (bf16[1024,2048]{1,0:T(8,128)(2,1)}, bf16[2,2,2,1,64,1024]{5,4,3,2,1,0:T(8,128)(2,1)}, bf16[2,2,2,1,64,1024]{5,4,3,2,1,0:T(8,128)(2,1)}, bf16[2...) custom-call(s32[5]{0:T(128)} %stack.159.co, ...), custom_call_target="tpu_custom_call" | custom-call | flops 141733920 | bytes 293601 | tf_op jit(solution)/shard_map/pallas_call | solution.py:703
  244.5 17.6 %shard_map.370 = (bf16[1024,2048]{1,0:T(8,128)(2,1)}, bf16[2,2,2,1,64,1024]{5,4,3,2,1,0:T(8,128)(2,1)}, bf16[2,2,2,1,64,1024]{5,4,3,2,1,0:T(8,128)(2,1)}, bf16[2...) custom-call(s32[5]{0:T(128)} %stack.159.co, bf16[1024,1024]{1,0:T(8,128)(2,1)} %get-tuple-element.334.dkv, ...), custom_call_target="tpu_custom_call" | custom-call | flops 141733920 | bytes 293601 | tf_op jit(solution)/shard_map/pallas_call | solution.py:703
  264.1 28.9 %shard_map.371 = (f32[1024,1024]{1,0:T(8,128)}, bf16[1024,1024]{1,0:T(8,128)(2,1)}, f32[4,8,1024]{2,1,0:T(8,128)}) custom-call(s32[5]{0:T(128)} %stack.159.co, bf16[1024,2048]{1,0:T(8,128)(2,1)} %get-tuple-element.348.dkey_a, bf16[1024,2048]{1,0:T(8,128)(2,1)} %get-tuple-element.349.dkey_b, bf16[1024,1024]{1,0:T(8,128)(2,1)} %get-tuple-element.323.refs_3_.drec, ...), custom_call_target="tpu_custom_call" | custom-call | flops 171798688 | bytes 377487 | tf_op jit(solution)/shard_map/pallas_call | solution.py:806
  293.6 1.7 collective-permute-start.31
  296.3 6.7 %shard_map.372 = (bf16[2,2,2,1,64,512]{5,4,3,2,1,0:T(8,128)(2,1)}, bf16[2,2,2,1,64,512]{5,4,3,2,1,0:T(8,128)(2,1)}, bf16[2,2,2,1,64,512]{5,4,3,2,1,0:T(8,128)(2,1)}, bf16[2,2,2,1,64,512]{5,4,3,2,1,0:T(8,128)(2,1)}) custom-call(s32[5]{0:T(128)} %stack.159.co, bf16[1024,1024]{1,0:T(8,128)(2,1)} %get-tuple-element.372.refs_0_.dtime, ...), custom_call_target="tpu_custom_call" | custom-call | flops 25769804 | bytes 62914 | tf_op jit(solution)/shard_map/pallas_call | solution.py:588
  303.0 2.6 fusion.2
  306.7 23.0 %shard_map.373 = (bf16[1024,1024]{1,0:T(8,128)(2,1)}, bf16[1024,1024]{1,0:T(8,128)(2,1)}, bf16[1024,1024]{1,0:T(8,128)(2,1)}, f32[2,8,1024]{2,1,0:T(8,128)}) custom-call(s32[5]{0:T(128)} %stack.159.co, bf16[1024,1024]{1,0:T(8,128)(2,1)} %get-tuple-element.372.refs_0_.dtime, f32[1024,1024]{1,0:T(8,128)} %get-tuple-element.373.key_ref, ...), custom_call_target="tpu_custom_call" | custom-call | flops 193273536 | bytes 356515 | tf_op jit(solution)/shard_map/pallas_call | solution.py:917
  333.3 1.6 collective-permute-start.34
  334.9 12.5 %shard_map.374 = (bf16[3,2,2,2,64,512]{5,4,3,2,1,0:T(8,128)(2,1)}, bf16[3,2,2,2,64,512]{5,4,3,2,1,0:T(8,128)(2,1)}, bf16[3,2,2,2,64,512]{5,4,3,2,1,0:T(8,128)(2,1)}, bf16[3,2,2,2,64,512]{5,4,3,2,1,0:T(8,128)(2,1)}) custom-call(s32[5]{0:T(128)} %stack.159.co, bf16[1024,1024]{1,0:T(8,128)(2,1)} %get-tuple-element.281.mk.refs_0_, ...), custom_call_target="tpu_custom_call" | custom-call | flops 77309408 | bytes 188743 | tf_op jit(solution)/shard_map/pallas_call | solution.py:588
  350.8 1.9 fusion.17
  354.2 1.7 fusion.18
  357.7 1.9 collective-permute-start.37
  360.2 15.1 %shard_map.375 = (f32[1024,1024]{1,0:T(8,128)}, f32[12,1024]{1,0:T(8,128)}, f32[8,1024]{1,0:T(8,128)}) custom-call(s32[5]{0:T(128)} %stack.159.co, bf16[1024,1024]{1,0:T(8,128)(2,1)} %get-tuple-element.427.refs_3_.dkey, bf16[1024,1024]{1,0:T(8,128)(2,1)} %get-tuple-element.428.refs_4_.dval, ...), custom_call_target="tpu_custom_call", output_to_operand_aliasing={{0}: (12, {})} | custom-call | flops 85899344 | bytes 167772 | tf_op jit(solution)/shard_map/pallas_call | solution.py:1035
  376.5 2.6 add_bitcast_fusion
  387.5 15.1 %shard_map.376 = (f32[1024,1024]{1,0:T(8,128)}, f32[12,1024]{1,0:T(8,128)}, f32[8,1024]{1,0:T(8,128)}) custom-call(s32[5]{0:T(128)} %stack.159.co, bf16[1024,1024]{1,0:T(8,128)(2,1)} %get-tuple-element.427.refs_3_.dkey, bf16[1024,1024]{1,0:T(8,128)(2,1)} %get-tuple-element.428.refs_4_.dval, ...), custom_call_target="tpu_custom_call", output_to_operand_aliasing={{0}: (10, {})} | custom-call | flops 85899344 | bytes 167772 | tf_op jit(solution)/shard_map/pallas_call | solution.py:1035
  403.8 1.6 collective-permute-start.51
  405.3 1.8 fusion.5
  410.1 1.9 collective-permute-start.47
  413.4 2.0 collective-permute-done.47
  417.0 1.8 collective-permute-start.57
  423.1 3.2 collective-permute-done.57
  435.3 3.3 collective-permute-done.60
  (331 shorter events, 83.2 us)
Async XLA Ops:
  7.2 108.8 %all-gather.5.cloned.1.call-start = ((), (), s32[]{:S(2)}) async-start(), calls=%async_computation.2 | async-start | bytes 8650752 | tf_op jit(solution)/shard_map/all_gather | solution.py:1352
  8.9 178.6 %all-gather.7.cloned.1.call-start = ((), (), s32[]{:S(2)}) async-start(), calls=%async_computation.3 | async-start | bytes 6488064 | tf_op jit(solution)/shard_map/all_gather | solution.py:1367
  13.7 24.2 %collective-permute-start.3 = (f32[16,32]{1,0:T(8,128)S(1)}, f32[16,32]{1,0:T(8,128)}, u32[]{:S(2)}, u32[]{:S(2)}) collective-permute-start(f32[16,32]{1,0:T(8,128)S(1)} %concatenate.130), channel_id=1, source_target_pairs={{0,1},{1,0},{2,3},{3,2},{4,5},{5,4},{6,7},{7,6},{8,9},{9,8},{10,11... | collective-permute-start | bytes 6152 | tf_op jit(solution)/shard_map/ppermute | solution.py:1072
  19.5 28.1 %collective-permute-start.7 = (bf16[1024,512]{1,0:T(8,128)(2,1)S(1)}, bf16[1024,512]{1,0:T(8,128)(2,1)S(1)}, u32[]{:S(2)}, u32[]{:S(2)}) collective-permute-start(bf16[1024,512]{1,0:T(8,128)(2,1)S(1)} %get-tuple-element.498), channel_id=1, source_target_pairs={{0,1},{1,0},{2,3},{3,2},{4,5},{5,4},{6,7},{7,6},{8,9},{9,8},{10,11... | collective-permute-start | bytes 3145736 | tf_op jit(solution)/shard_map/ppermute | solution.py:1072
  19.5 28.0 %collective-permute-start = (bf16[64,1024]{1,0:T(8,128)(2,1)S(1)}, bf16[64,1024]{1,0:T(8,128)(2,1)S(1)}, u32[]{:S(2)}, u32[]{:S(2)}) collective-permute-start(bf16[64,1024]{1,0:T(8,128)(2,1)S(1)} %get-tuple-element.255), channel_id=1, source_target_pairs={{0,16},{16,0},{1,17},{17,1},{2,18},{18,2},{3,19},{19,3},{4,20},{20... | collective-permute-start | bytes 393224 | tf_op jit(solution)/shard_map/ppermute | solution.py:1072
  22.7 24.8 %collective-permute-start.1 = (bf16[64,1024]{1,0:T(8,128)(2,1)S(1)}, bf16[64,1024]{1,0:T(8,128)(2,1)S(1)}, u32[]{:S(2)}, u32[]{:S(2)}) collective-permute-start(bf16[64,1024]{1,0:T(8,128)(2,1)S(1)} %get-tuple-element.257), channel_id=1, source_target_pairs={{0,16},{16,0},{1,17},{17,1},{2,18},{18,2},{3,19},{19,3},{4,20},{20... | collective-permute-start | bytes 393224 | tf_op jit(solution)/shard_map/ppermute | solution.py:1072
  22.8 24.7 %collective-permute-start.2 = (bf16[64,1024]{1,0:T(8,128)(2,1)S(1)}, bf16[64,1024]{1,0:T(8,128)(2,1)}, u32[]{:S(2)}, u32[]{:S(2)}) collective-permute-start(bf16[64,1024]{1,0:T(8,128)(2,1)S(1)} %get-tuple-element.259), channel_id=1, source_target_pairs={{0,16},{16,0},{1,17},{17,1},{2,18},{18,2},{3,19},{19,3},{4,20},{20... | collective-permute-start | bytes 393224 | tf_op jit(solution)/shard_map/ppermute | solution.py:1072
  55.5 13.2 %collective-permute-start.10 = (bf16[2,64,1024]{2,1,0:T(8,128)(2,1)S(1)}, bf16[2,64,1024]{2,1,0:T(8,128)(2,1)S(1)}, u32[]{:S(2)}, u32[]{:S(2)}) collective-permute-start(bf16[2,64,1024]{2,1,0:T(8,128)(2,1)S(1)} %pad_maximum_fusion.9), channel_id=1, source_target_pairs={{0,4},{4,0},{1,5},{5,1},{2,6},{6,2},{3,7},{7,3},{8,12},{12,8},{9,1... | collective-permute-start | bytes 786440 | tf_op jit(solution)/shard_map/ppermute | solution.py:1072
  57.1 11.5 %collective-permute-start.9 = (bf16[2,64,1024]{2,1,0:T(8,128)(2,1)S(1)}, bf16[2,64,1024]{2,1,0:T(8,128)(2,1)S(1)}, u32[]{:S(2)}, u32[]{:S(2)}) collective-permute-start(bf16[2,64,1024]{2,1,0:T(8,128)(2,1)S(1)} %pad_maximum_fusion.8), channel_id=1, source_target_pairs={{0,1},{1,0},{2,3},{3,2},{4,5},{5,4},{6,7},{7,6},{8,9},{9,8},{10,11... | collective-permute-start | bytes 786440 | tf_op jit(solution)/shard_map/ppermute | solution.py:1072
  58.7 11.3 %collective-permute-start.8 = (bf16[2,64,1024]{2,1,0:T(8,128)(2,1)S(1)}, bf16[2,64,1024]{2,1,0:T(8,128)(2,1)S(1)}, u32[]{:S(2)}, u32[]{:S(2)}) collective-permute-start(bf16[2,64,1024]{2,1,0:T(8,128)(2,1)S(1)} %pad_maximum_fusion.7), channel_id=1, source_target_pairs={{0,8},{8,0},{1,9},{9,1},{2,10},{10,2},{3,11},{11,3},{4,12},{12,4},... | collective-permute-start | bytes 786440 | tf_op jit(solution)/shard_map/ppermute | solution.py:1072
  70.1 17.4 %collective-permute-start.14 = (bf16[2,2,64,1024]{3,2,1,0:T(8,128)(2,1)S(1)}, bf16[2,2,64,1024]{3,2,1,0:T(8,128)(2,1)S(1)}, u32[]{:S(2)}, u32[]{:S(2)}) collective-permute-start(bf16[2,2,64,1024]{3,2,1,0:T(8,128)(2,1)S(1)} %pad_maximum_fusion.5), channel_id=1, source_target_pairs={{0,1},{1,0},{2,3},{3,2},{4,5},{5,4},{6,7},{7,6},{8,9},{9,8},{10,11... | collective-permute-start | bytes 1572872 | tf_op jit(solution)/shard_map/ppermute | solution.py:1072
  74.0 23.8 %collective-permute-start.13 = (bf16[2,2,64,1024]{3,2,1,0:T(8,128)(2,1)S(1)}, bf16[2,2,64,1024]{3,2,1,0:T(8,128)(2,1)S(1)}, u32[]{:S(2)}, u32[]{:S(2)}) collective-permute-start(bf16[2,2,64,1024]{3,2,1,0:T(8,128)(2,1)S(1)} %pad_maximum_fusion.4), channel_id=1, source_target_pairs={{0,8},{8,0},{1,9},{9,1},{2,10},{10,2},{3,11},{11,3},{4,12},{12,4},... | collective-permute-start | bytes 1572872 | tf_op jit(solution)/shard_map/ppermute | solution.py:1072
  75.4 22.4 %collective-permute-start.12 = (bf16[2,2,64,1024]{3,2,1,0:T(8,128)(2,1)S(1)}, bf16[2,2,64,1024]{3,2,1,0:T(8,128)(2,1)S(1)}, u32[]{:S(2)}, u32[]{:S(2)}) collective-permute-start(bf16[2,2,64,1024]{3,2,1,0:T(8,128)(2,1)S(1)} %pad_maximum_fusion.3), channel_id=1, source_target_pairs={{0,4},{4,0},{1,5},{5,1},{2,6},{6,2},{3,7},{7,3},{8,12},{12,8},{9,1... | collective-permute-start | bytes 1572872 | tf_op jit(solution)/shard_map/ppermute | solution.py:1072
  116.0 299.5 %reduce-scatter.2.cloned.1.call-start = ((), (), s32[]{:S(2)}) async-start(), calls=%async_computation.1 | async-start | bytes 11141120 | tf_op jit(solution)/shard_map/reduce_scatter | solution.py:1214
  116.1 30.4 %collective-permute-start.16 = (bf16[2,2,2,64,1024]{4,3,2,1,0:T(8,128)(2,1)S(1)}, bf16[2,2,2,64,1024]{4,3,2,1,0:T(8,128)(2,1)}, u32[]{:S(2)}, u32[]{:S(2)}) collective-permute-start(bf16[2,2,2,64,1024]{4,3,2,1,0:T(8,128)(2,1)S(1)} %pad_maximum_fusion.1.refs_4_), channel_id=1, source_target_pairs={{0,4},{4,0},{1,5},{5,1},{2,6},{6,2},{3,7},{7,3},{8,12},{12,8},{9,1... | collective-permute-start | bytes 3145736 | tf_op jit(solution)/shard_map/ppermute | solution.py:1072
  117.7 28.9 %collective-permute-start.15 = (bf16[2,2,2,64,1024]{4,3,2,1,0:T(8,128)(2,1)S(1)}, bf16[2,2,2,64,1024]{4,3,2,1,0:T(8,128)(2,1)}, u32[]{:S(2)}, u32[]{:S(2)}) collective-permute-start(bf16[2,2,2,64,1024]{4,3,2,1,0:T(8,128)(2,1)S(1)} %pad_maximum_fusion.refs_0_), channel_id=1, source_target_pairs={{0,1},{1,0},{2,3},{3,2},{4,5},{5,4},{6,7},{7,6},{8,9},{9,8},{10,11... | collective-permute-start | bytes 3145736 | tf_op jit(solution)/shard_map/ppermute | solution.py:1072
  119.9 40.1 %collective-permute-start.21 = (bf16[2,2,2,64,1024]{4,3,2,1,0:T(8,128)(2,1)S(1)}, bf16[2,2,2,64,1024]{4,3,2,1,0:T(8,128)(2,1)}, u32[]{:S(2)}, u32[]{:S(2)}) collective-permute-start(bf16[2,2,2,64,1024]{4,3,2,1,0:T(8,128)(2,1)S(1)} %pad_maximum_fusion.2.refs_1_.refs_0_), channel_id=1, source_target_pairs={{0,8},{8,0},{1,9},{9,1},{2,10},{10,2},{3,11},{11,3},{4,12},{12,4},... | collective-permute-start | bytes 3145736 | tf_op jit(solution)/shard_map/ppermute | solution.py:1072
  146.6 13.5 %collective-permute-start.17 = (bf16[2,2,2,64,1024]{4,3,2,1,0:T(8,128)(2,1)S(1)}, bf16[2,2,2,64,1024]{4,3,2,1,0:T(8,128)(2,1)S(1)}, u32[]{:S(2)}, u32[]{:S(2)}) collective-permute-start(bf16[2,2,2,64,1024]{4,3,2,1,0:T(8,128)(2,1)S(1)} %pad_maximum_fusion.refs_0_), channel_id=1, source_target_pairs={{0,2},{2,0},{1,3},{3,1},{4,6},{6,4},{5,7},{7,5},{8,10},{10,8},{9,1... | collective-permute-start | bytes 3145736 | tf_op jit(solution)/shard_map/ppermute | solution.py:1072
  146.7 13.4 %collective-permute-start.18 = (bf16[2,2,2,64,1024]{4,3,2,1,0:T(8,128)(2,1)}, bf16[2,2,2,64,1024]{4,3,2,1,0:T(8,128)(2,1)S(1)}, u32[]{:S(2)}, u32[]{:S(2)}) collective-permute-start(bf16[2,2,2,64,1024]{4,3,2,1,0:T(8,128)(2,1)} %collective-permute-done.15.refs_1_), channel_id=1, source_target_pairs={{0,2},{2,0},{1,3},{3,1},{4,6},{6,4},{5,7},{7,5},{8,10},{10,8},{9,1... | collective-permute-start | bytes 3145736 | tf_op jit(solution)/shard_map/ppermute | solution.py:1072
  147.1 13.0 %collective-permute-start.19 = (bf16[2,2,2,64,1024]{4,3,2,1,0:T(8,128)(2,1)S(1)}, bf16[2,2,2,64,1024]{4,3,2,1,0:T(8,128)(2,1)}, u32[]{:S(2)}, u32[]{:S(2)}) collective-permute-start(bf16[2,2,2,64,1024]{4,3,2,1,0:T(8,128)(2,1)S(1)} %pad_maximum_fusion.1.refs_4_), channel_id=1, source_target_pairs={{0,2},{2,0},{1,3},{3,1},{4,6},{6,4},{5,7},{7,5},{8,10},{10,8},{9,1... | collective-permute-start | bytes 3145736 | tf_op jit(solution)/shard_map/ppermute | solution.py:1072
  147.2 12.9 %collective-permute-start.20 = (bf16[2,2,2,64,1024]{4,3,2,1,0:T(8,128)(2,1)}, bf16[2,2,2,64,1024]{4,3,2,1,0:T(8,128)(2,1)}, u32[]{:S(2)}, u32[]{:S(2)}) collective-permute-start(bf16[2,2,2,64,1024]{4,3,2,1,0:T(8,128)(2,1)} %collective-permute-done.16.refs_5_), channel_id=1, source_target_pairs={{0,2},{2,0},{1,3},{3,1},{4,6},{6,4},{5,7},{7,5},{8,10},{10,8},{9,1... | collective-permute-start | bytes 3145736 | tf_op jit(solution)/shard_map/ppermute | solution.py:1072
  160.1 20.9 %collective-permute-start.22 = (bf16[2,2,2,64,1024]{4,3,2,1,0:T(8,128)(2,1)S(1)}, bf16[2,2,2,64,1024]{4,3,2,1,0:T(8,128)(2,1)S(1)}, u32[]{:S(2)}, u32[]{:S(2)}) collective-permute-start(bf16[2,2,2,64,1024]{4,3,2,1,0:T(8,128)(2,1)S(1)} %pad_maximum_fusion.2.refs_1_.refs_0_), channel_id=1, source_target_pairs={{0,2},{2,0},{1,3},{3,1},{4,6},{6,4},{5,7},{7,5},{8,10},{10,8},{9,1... | collective-permute-start | bytes 3145736 | tf_op jit(solution)/shard_map/ppermute | solution.py:1072
  161.0 20.0 %collective-permute-start.23 = (bf16[2,2,2,64,1024]{4,3,2,1,0:T(8,128)(2,1)}, bf16[2,2,2,64,1024]{4,3,2,1,0:T(8,128)(2,1)S(1)}, u32[]{:S(2)}, u32[]{:S(2)}) collective-permute-start(bf16[2,2,2,64,1024]{4,3,2,1,0:T(8,128)(2,1)} %collective-permute-done.21.refs_2_.refs_1_), channel_id=1, source_target_pairs={{0,2},{2,0},{1,3},{3,1},{4,6},{6,4},{5,7},{7,5},{8,10},{10,8},{9,1... | collective-permute-start | bytes 3145736 | tf_op jit(solution)/shard_map/ppermute | solution.py:1072
  211.2 32.1 %collective-permute-start.24 = (bf16[1024,512]{1,0:T(8,128)(2,1)}, bf16[1024,512]{1,0:T(8,128)(2,1)S(1)}, u32[]{:S(2)}, u32[]{:S(2)}) collective-permute-start(bf16[1024,512]{1,0:T(8,128)(2,1)} %get-tuple-element.328), channel_id=1, source_target_pairs={{0,1},{1,0},{2,3},{3,2},{4,5},{5,4},{6,7},{7,6},{8,9},{9,8},{10,11... | collective-permute-start | bytes 3145736 | tf_op jit(solution)/shard_map/ppermute | solution.py:1072
  243.3 18.8 %collective-permute-start.25 = (bf16[2,2,2,1,64,1024]{5,4,2,1,3,0:T(8,128)(2,1)}, bf16[2,2,2,1,64,1024]{5,4,2,1,3,0:T(8,128)(2,1)S(1)}, u32[]{:S(2)}, u32[]{:S(2)}) collective-permute-start(bf16[2,2,2,1,64,1024]{5,4,2,1,3,0:T(8,128)(2,1)} %bitcast.319), channel_id=1, source_target_pairs={{0,2},{2,0},{1,3},{3,1},{4,6},{6,4},{5,7},{7,5},{8,10},{10,8},{9,1... | collective-permute-start | bytes 3145736 | tf_op jit(solution)/shard_map/ppermute | solution.py:1072
  244.5 17.6 %collective-permute-start.26 = (bf16[2,2,2,1,64,1024]{5,4,2,1,3,0:T(8,128)(2,1)S(1)}, bf16[2,2,2,1,64,1024]{5,4,2,1,3,0:T(8,128)(2,1)S(1)}, u32[]{:S(2)}, u32[]{:S(2)}) collective-permute-start(bf16[2,2,2,1,64,1024]{5,4,2,1,3,0:T(8,128)(2,1)S(1)} %bitcast.318), channel_id=1, source_target_pairs={{0,2},{2,0},{1,3},{3,1},{4,6},{6,4},{5,7},{7,5},{8,10},{10,8},{9,1... | collective-permute-start | bytes 3145736 | tf_op jit(solution)/shard_map/ppermute | solution.py:1072
  263.2 29.9 %collective-permute-start.27 = (bf16[2,2,2,1,64,1024]{5,4,2,1,3,0:T(8,128)(2,1)S(1)}, bf16[2,2,2,1,64,1024]{5,4,2,1,3,0:T(8,128)(2,1)}, u32[]{:S(2)}, u32[]{:S(2)}) collective-permute-start(bf16[2,2,2,1,64,1024]{5,4,2,1,3,0:T(8,128)(2,1)S(1)} %bitcast_add_fusion.1), channel_id=1, source_target_pairs={{0,1},{1,0},{2,3},{3,2},{4,5},{5,4},{6,7},{7,6},{8,9},{9,8},{10,11... | collective-permute-start | bytes 3145736 | tf_op jit(solution)/shard_map/ppermute | solution.py:1072
  263.6 29.5 %collective-permute-start.28 = (bf16[2,2,2,1,64,1024]{5,4,3,2,1,0:T(8,128)(2,1)}, bf16[2,2,2,1,64,1024]{5,4,3,2,1,0:T(8,128)(2,1)S(1)}, u32[]{:S(2)}, u32[]{:S(2)}) collective-permute-start(bf16[2,2,2,1,64,1024]{5,4,3,2,1,0:T(8,128)(2,1)} %get-tuple-element.346), channel_id=1, source_target_pairs={{0,2},{2,0},{1,3},{3,1},{4,6},{6,4},{5,7},{7,5},{8,10},{10,8},{9,1... | collective-permute-start | bytes 3145736 | tf_op jit(solution)/shard_map/ppermute | solution.py:1072
  263.8 29.4 %collective-permute-start.29 = (bf16[2,2,2,1,64,1024]{5,4,2,1,3,0:T(8,128)(2,1)}, bf16[2,2,2,1,64,1024]{5,4,2,1,3,0:T(8,128)(2,1)S(1)}, u32[]{:S(2)}, u32[]{:S(2)}) collective-permute-start(bf16[2,2,2,1,64,1024]{5,4,2,1,3,0:T(8,128)(2,1)} %bitcast.58), channel_id=1, source_target_pairs={{0,2},{2,0},{1,3},{3,1},{4,6},{6,4},{5,7},{7,5},{8,10},{10,8},{9,1... | collective-permute-start | bytes 3145736 | tf_op jit(solution)/shard_map/ppermute | solution.py:1072
  293.6 36.2 %collective-permute-start.31 = (bf16[2,2,2,1,64,1024]{5,4,3,2,1,0:T(8,128)(2,1)S(1)}, bf16[2,2,2,1,64,1024]{5,4,3,2,1,0:T(8,128)(2,1)}, u32[]{:S(2)}, u32[]{:S(2)}) collective-permute-start(bf16[2,2,2,1,64,1024]{5,4,3,2,1,0:T(8,128)(2,1)S(1)} %add.495), channel_id=1, source_target_pairs={{0,1},{1,0},{2,3},{3,2},{4,5},{5,4},{6,7},{7,6},{8,9},{9,8},{10,11... | collective-permute-start | bytes 3145736 | tf_op jit(solution)/shard_map/ppermute | solution.py:1072
  305.7 24.1 %collective-permute-start.30 = (bf16[2,2,1,64,1024]{4,3,1,2,0:T(8,128)(2,1)}, bf16[2,2,1,64,1024]{4,3,1,2,0:T(8,128)(2,1)S(1)}, u32[]{:S(2)}, u32[]{:S(2)}) collective-permute-start(bf16[2,2,1,64,1024]{4,3,1,2,0:T(8,128)(2,1)} %get-tuple-element.496), channel_id=1, source_target_pairs={{0,4},{4,0},{1,5},{5,1},{2,6},{6,2},{3,7},{7,3},{8,12},{12,8},{9,1... | collective-permute-start | bytes 1572872 | tf_op jit(solution)/shard_map/ppermute | solution.py:1072
  306.2 23.5 %collective-permute-start.32 = (bf16[2,2,2,1,64,512]{5,4,3,2,1,0:T(8,128)(2,1)}, bf16[2,2,2,1,64,512]{5,4,3,2,1,0:T(8,128)(2,1)S(1)}, u32[]{:S(2)}, u32[]{:S(2)}) collective-permute-start(bf16[2,2,2,1,64,512]{5,4,3,2,1,0:T(8,128)(2,1)} %get-tuple-element.370), channel_id=1, source_target_pairs={{0,2},{2,0},{1,3},{3,1},{4,6},{6,4},{5,7},{7,5},{8,10},{10,8},{9,1... | collective-permute-start | bytes 1572872 | tf_op jit(solution)/shard_map/ppermute | solution.py:1072
  306.2 23.5 %collective-permute-start.33 = (bf16[2,2,2,1,64,512]{5,4,2,1,3,0:T(8,128)(2,1)}, bf16[2,2,2,1,64,512]{5,4,2,1,3,0:T(8,128)(2,1)S(1)}, u32[]{:S(2)}, u32[]{:S(2)}) collective-permute-start(bf16[2,2,2,1,64,512]{5,4,2,1,3,0:T(8,128)(2,1)} %bitcast.63), channel_id=1, source_target_pairs={{0,2},{2,0},{1,3},{3,1},{4,6},{6,4},{5,7},{7,5},{8,10},{10,8},{9,1... | collective-permute-start | bytes 1572872 | tf_op jit(solution)/shard_map/ppermute | solution.py:1072
  330.0 18.8 %collective-permute-start.36 = (bf16[2,2,2,1,64,512]{5,4,3,2,1,0:T(8,128)(2,1)S(1)}, bf16[2,2,2,1,64,512]{5,4,3,2,1,0:T(8,128)(2,1)S(1)}, u32[]{:S(2)}, u32[]{:S(2)}) collective-permute-start(bf16[2,2,2,1,64,512]{5,4,3,2,1,0:T(8,128)(2,1)S(1)} %add.502), channel_id=1, source_target_pairs={{0,1},{1,0},{2,3},{3,2},{4,5},{5,4},{6,7},{7,6},{8,9},{9,8},{10,11... | collective-permute-start | bytes 1572872 | tf_op jit(solution)/shard_map/ppermute | solution.py:1072
  332.5 16.3 %collective-permute-start.35 = (bf16[2,2,1,64,1024]{4,3,1,0,2:T(8,128)(2,1)S(1)}, bf16[2,2,1,64,1024]{4,3,1,0,2:T(8,128)(2,1)}, u32[]{:S(2)}, u32[]{:S(2)}) collective-permute-start(bf16[2,2,1,64,1024]{4,3,1,0,2:T(8,128)(2,1)S(1)} %fusion.4), channel_id=1, source_target_pairs={{0,4},{4,0},{1,5},{5,1},{2,6},{6,2},{3,7},{7,3},{8,12},{12,8},{9,1... | collective-permute-start | bytes 1572872 | tf_op jit(solution)/shard_map/ppermute | solution.py:1072
  333.3 15.4 %collective-permute-start.34 = (bf16[2,1,64,1024]{3,2,1,0:T(8,128)(2,1)S(1)}, bf16[2,1,64,1024]{3,2,1,0:T(8,128)(2,1)S(1)}, u32[]{:S(2)}, u32[]{:S(2)}) collective-permute-start(bf16[2,1,64,1024]{3,2,1,0:T(8,128)(2,1)S(1)} %get-tuple-element.500), channel_id=1, source_target_pairs={{0,8},{8,0},{1,9},{9,1},{2,10},{10,2},{3,11},{11,3},{4,12},{12,4},... | collective-permute-start | bytes 786440 | tf_op jit(solution)/shard_map/ppermute | solution.py:1072
  349.6 26.8 %collective-permute-start.40 = (bf16[3,2,2,2,64,512]{5,4,3,2,1,0:T(8,128)(2,1)}, bf16[3,2,2,2,64,512]{5,4,3,2,1,0:T(8,128)(2,1)}, u32[]{:S(2)}, u32[]{:S(2)}) collective-permute-start(bf16[3,2,2,2,64,512]{5,4,3,2,1,0:T(8,128)(2,1)} %get-tuple-element.408), channel_id=1, source_target_pairs={{0,2},{2,0},{1,3},{3,1},{4,6},{6,4},{5,7},{7,5},{8,10},{10,8},{9,1... | collective-permute-start | bytes 4718600 | tf_op jit(solution)/shard_map/ppermute | solution.py:1072
  349.7 26.8 %collective-permute-start.41 = (bf16[3,2,2,2,64,512]{5,4,3,2,1,0:T(8,128)(2,1)}, bf16[3,2,2,2,64,512]{5,4,3,2,1,0:T(8,128)(2,1)S(1)}, u32[]{:S(2)}, u32[]{:S(2)}) collective-permute-start(bf16[3,2,2,2,64,512]{5,4,3,2,1,0:T(8,128)(2,1)} %get-tuple-element.409), channel_id=1, source_target_pairs={{0,2},{2,0},{1,3},{3,1},{4,6},{6,4},{5,7},{7,5},{8,10},{10,8},{9,1... | collective-permute-start | bytes 4718600 | tf_op jit(solution)/shard_map/ppermute | solution.py:1072
  352.8 23.6 %collective-permute-start.39 = (bf16[2,2,1,64,512]{4,3,1,0,2:T(8,128)(2,1)}, bf16[2,2,1,64,512]{4,3,1,0,2:T(8,128)(2,1)S(1)}, u32[]{:S(2)}, u32[]{:S(2)}) collective-permute-start(bf16[2,2,1,64,512]{4,3,1,0,2:T(8,128)(2,1)} %fusion.17), channel_id=1, source_target_pairs={{0,4},{4,0},{1,5},{5,1},{2,6},{6,2},{3,7},{7,3},{8,12},{12,8},{9,1... | collective-permute-start | bytes 786440 | tf_op jit(solution)/shard_map/ppermute | solution.py:1072
  355.9 20.5 %collective-permute-start.38 = (bf16[2,1,64,1024]{3,2,0,1:T(8,128)(2,1)}, bf16[2,1,64,1024]{3,2,0,1:T(8,128)(2,1)S(1)}, u32[]{:S(2)}, u32[]{:S(2)}) collective-permute-start(bf16[2,1,64,1024]{3,2,0,1:T(8,128)(2,1)} %fusion.18), channel_id=1, source_target_pairs={{0,8},{8,0},{1,9},{9,1},{2,10},{10,2},{3,11},{11,3},{4,12},{12,4},... | collective-permute-start | bytes 786440 | tf_op jit(solution)/shard_map/ppermute | solution.py:1072
  357.7 18.7 %collective-permute-start.37 = (bf16[1,64,1024]{2,1,0:T(8,128)(2,1)S(1)}, bf16[1,64,1024]{2,1,0:T(8,128)(2,1)S(1)}, u32[]{:S(2)}, u32[]{:S(2)}) collective-permute-start(bf16[1,64,1024]{2,1,0:T(8,128)(2,1)S(1)} %get-tuple-element.510), channel_id=1, source_target_pairs={{0,16},{16,0},{1,17},{17,1},{2,18},{18,2},{3,19},{19,3},{4,20},{20... | collective-permute-start | bytes 393224 | tf_op jit(solution)/shard_map/ppermute | solution.py:1072
  379.1 24.6 %collective-permute-start.44 = (bf16[2,2,2,64,512]{4,3,2,1,0:T(8,128)(2,1)}, bf16[2,2,2,64,512]{4,3,2,1,0:T(8,128)(2,1)S(1)}, u32[]{:S(2)}, u32[]{:S(2)}) collective-permute-start(bf16[2,2,2,64,512]{4,3,2,1,0:T(8,128)(2,1)} %get-tuple-element.495), channel_id=1, source_target_pairs={{0,4},{4,0},{1,5},{5,1},{2,6},{6,2},{3,7},{7,3},{8,12},{12,8},{9,1... | collective-permute-start | bytes 1572872 | tf_op jit(solution)/shard_map/ppermute | solution.py:1072
  379.8 23.9 %collective-permute-start.45 = (bf16[2,2,2,64,512]{4,3,2,1,0:T(8,128)(2,1)}, bf16[2,2,2,64,512]{4,3,2,1,0:T(8,128)(2,1)S(1)}, u32[]{:S(2)}, u32[]{:S(2)}) collective-permute-start(bf16[2,2,2,64,512]{4,3,2,1,0:T(8,128)(2,1)} %get-tuple-element.494), channel_id=1, source_target_pairs={{0,1},{1,0},{2,3},{3,2},{4,5},{5,4},{6,7},{7,6},{8,9},{9,8},{10,11... | collective-permute-start | bytes 1572872 | tf_op jit(solution)/shard_map/ppermute | solution.py:1072
  381.1 22.6 %collective-permute-start.46 = (bf16[2,2,2,64,512]{4,3,2,1,0:T(8,128)(2,1)S(1)}, bf16[2,2,2,64,512]{4,3,2,1,0:T(8,128)(2,1)}, u32[]{:S(2)}, u32[]{:S(2)}) collective-permute-start(bf16[2,2,2,64,512]{4,3,2,1,0:T(8,128)(2,1)S(1)} %get-tuple-element.493), channel_id=1, source_target_pairs={{0,8},{8,0},{1,9},{9,1},{2,10},{10,2},{3,11},{11,3},{4,12},{12,4},... | collective-permute-start | bytes 1572872 | tf_op jit(solution)/shard_map/ppermute | solution.py:1072
  383.1 20.6 %collective-permute-start.43 = (bf16[2,1,64,512]{3,2,0,1:T(8,128)(2,1)S(1)}, bf16[2,1,64,512]{3,2,0,1:T(8,128)(2,1)S(1)}, u32[]{:S(2)}, u32[]{:S(2)}) collective-permute-start(bf16[2,1,64,512]{3,2,0,1:T(8,128)(2,1)S(1)} %fusion.32), channel_id=1, source_target_pairs={{0,8},{8,0},{1,9},{9,1},{2,10},{10,2},{3,11},{11,3},{4,12},{12,4},... | collective-permute-start | bytes 393224 | tf_op jit(solution)/shard_map/ppermute | solution.py:1072
  386.1 17.6 %collective-permute-start.42 = (bf16[1,64,1024]{2,1,0:T(8,128)(2,1)S(1)}, bf16[1,64,1024]{2,1,0:T(8,128)(2,1)}, u32[]{:S(2)}, u32[]{:S(2)}) collective-permute-start(bf16[1,64,1024]{2,1,0:T(8,128)(2,1)S(1)} %fusion.31), channel_id=1, source_target_pairs={{0,16},{16,0},{1,17},{17,1},{2,18},{18,2},{3,19},{19,3},{4,20},{20... | collective-permute-start | bytes 393224 | tf_op jit(solution)/shard_map/ppermute | solution.py:1072
  417.0 9.3 %collective-permute-start.57 = (bf16[64,2560]{1,0:T(8,128)(2,1)S(1)}, bf16[64,2560]{1,0:T(8,128)(2,1)S(1)}, u32[]{:S(2)}, u32[]{:S(2)}) collective-permute-start(bf16[64,2560]{1,0:T(8,128)(2,1)S(1)} %dynamic-slice_bitcast_fusion), channel_id=1, source_target_pairs={{0,1},{1,0},{2,3},{3,2},{4,5},{5,4},{6,7},{7,6},{8,9},{9,8},{10,11... | collective-permute-start | bytes 983048 | tf_op jit(solution)/shard_map/ppermute | solution.py:1072
  429.3 9.3 %collective-permute-start.58 = (bf16[3,64,512]{2,1,0:T(8,128)(2,1)S(1)}, bf16[3,64,512]{2,1,0:T(8,128)(2,1)S(1)}, u32[]{:S(2)}, u32[]{:S(2)}) collective-permute-start(bf16[3,64,512]{2,1,0:T(8,128)(2,1)S(1)} %pad_maximum_fusion.12), channel_id=1, source_target_pairs={{0,16},{16,0},{1,17},{17,1},{2,18},{18,2},{3,19},{19,3},{4,20},{20... | collective-permute-start | bytes 589832 | tf_op jit(solution)/shard_map/ppermute | solution.py:1072
  (58 other events, 516.2 us)
Sparse Core Ops, SparseCore 0:
  11.0 104.8 all-gather.4
  118.8 68.6 all-gather.6
  243.4 129.9 reduce-scatter.1

commit v8 on v7

--- a/solution.py
+++ b/solution.py
@@ -613,7 +613,7 @@
     dkey, targets, refs = refs[0], refs[1:5], refs[5:]
     if part == 0:
         blocks, *refs = refs
-        grads, narrow, *refs = refs
+        grads, narrow, held, sems_held, *refs = refs
     other, sems, whole, sems_in = refs
     j = pl.program_id(0)
     wide = other.shape[3]
@@ -625,6 +625,9 @@
     @pl.when(j == 0)
     def _():
         start_weight(co, arrays, whole, sems_in, layout)
+        if part == 0:
+            for n in (0, 1):
+                pltpu.make_async_copy(recept[n], held.at[n], sems_held.at[n]).start()
 
     def cut(values):
         return values.astype(BF).reshape(16, SLOT, WIDE)
@@ -670,10 +673,15 @@
                 sems.at[1 + n],
             ).start()
 
-        @pl.when(lax.rem(j, per_half) == 0)
+        @pl.when(j == per_half - 1)
+        def _():
+            for n in (0, 1):
+                pltpu.make_async_copy(recept[n], held.at[n], sems_held.at[n]).wait()
+
+        @pl.when(lax.rem(j, per_half) == per_half - 1)
         def _():
             size = narrow.shape[3]
-            found = dot(recept[0][...], recept[1][:, pl.ds(pl.multiple_of(half * size, size), size)], TN)
+            found = dot(held[0], held[1, :, pl.ds(pl.multiple_of(half * size, size), size)], TN)
             narrow[turn] = found.astype(BF).reshape(16, SLOT, size)
             narrow_copy(turn).start()
 
@@ -706,13 +714,15 @@
             num_scalar_prefetch=1,
             grid=(2 * per_half,),
             in_specs=[fixed, fixed, own]
-            + [own, other, fixed, fixed] * first
+            + [own, other, anywhere(), anywhere()] * first
             + [anywhere()] * len(weight[1]),
             out_specs=[pl.BlockSpec((tokens, WIDE), column_tile(per_half))]
             + [anywhere()] * (4 + first),
             scratch_shapes=[
                 pltpu.VMEM((2, 2, 16, SLOT, half), BF),
                 pltpu.VMEM((2, 16, SLOT, width // 2), BF),
+                pltpu.VMEM((2, tokens, width), BF),
+                pltpu.SemaphoreType.DMA((2,)),
             ]
             * first
             + [pltpu.VMEM((2, 16, SLOT, half), BF), pltpu.SemaphoreType.DMA((5,))]

time: 455 us -> 453 us (level)
  no operation moved by 1% of the time
where the time goes in v8:
time: 453 us; the launch traced here: 447 us
  Pallas kernels  235 us (52%)
  waiting for transfers between devices  63.9 us (14%)
  starting transfers between devices  60.1 us (13%)
  other arithmetic  43.2 us (10%)
  local copies, waits for them, and re-layouts  26.6 us (6%)
  between operations  18.4 us (4%)
    ppermute x61, starting transfers between devices, swap(): return lax.ppermute(values, axis, SWAP)  60 us
    pallas_call x2, Pallas kernels, channel_back(): pl.pallas_call(functools.partial(channel_back_kernel, layout=weight[0], p...  46 us
    ppermute x61, waiting for transfers between devices, swap(): return lax.ppermute(values, axis, SWAP)  39.2 us
    pallas_call x2, Pallas kernels, input_back(): pl.pallas_call(functools.partial(input_back_kernel, layouts=[w[0] for w i...  30.3 us
    pallas_call x1, Pallas kernels, middle_back(): pl.pallas_call(functools.partial(middle_back_kernel, layouts=[weight[0],...  28.9 us
    pallas_call x1, Pallas kernels, time_forward(): pl.pallas_call(functools.partial(time_forward_kernel, layouts=[w[0] for w...  26.4 us
    pallas_call x1, Pallas kernels, result_step(): pl.pallas_call(functools.partial(result_kernel, layouts=[weight[0], recep...  23.6 us
    pallas_call x1, Pallas kernels, time_back(): pl.pallas_call(functools.partial(time_back_kernel, layout=weight[0]), gri...  23 us
  transfers between devices with their start and end apart: 64, of which 16 were waited for; matrix products, arithmetic and copies ran while one was open for 13% of the time, Pallas kernels for 47%

profile of v8, /device:TPU:0, one launch (start us, length us, event | category | flops | bytes accessed | tf_op | source)
XLA Modules:
  0.0 447.0 jit_solution(11590337847033212956)
XLA Ops:
  7.2 1.6 pad_maximum_fusion.10
  13.7 3.0 collective-permute-start.3
  16.7 2.7 constant_dynamic-slice_fusion.1
  19.5 3.1 collective-permute-start
  22.8 2.9 collective-permute-start.2
  35.8 1.5 pad_maximum_fusion.11
  41.7 2.0 collective-permute-done.5
  43.8 1.6 collective-permute-start.6
  45.4 2.1 collective-permute-done.6
  47.6 2.1 broadcast_in_dim.142.masks
  49.7 1.9 broadcast_in_dim.134.masks
  55.5 1.6 collective-permute-start.10
  57.1 1.6 collective-permute-start.9
  58.7 1.6 collective-permute-start.8
  61.1 6.9 %collective-permute-done.11 = f32[16,512]{1,0:T(8,128)S(1)} collective-permute-done((f32[16,512]{1,0:T(8,128)S(1)}, f32[16,512]{1,0:T(8,128)S(1)}, u32[]{:S(2)}, u32[]{:S(2)}) %collective-permute-start.11) | collective-permute-done | bytes 32800 | tf_op jit(solution)/shard_map/ppermute | solution.py:1082
  70.1 3.9 collective-permute-start.14
  75.9 7.4 %shard_map.364 = (bf16[1024,1024]{1,0:T(8,128)(2,1)}, bf16[1024,1024]{1,0:T(8,128)(2,1)}, bf16[1024,1024]{1,0:T(8,128)(2,1)}) custom-call(bf16[1024,1024]{1,0:T(8,128)(2,1)} %x_ref.7, f32[1024,128]{1,0:T(8,128)} %broadcast_in_dim.143.carry_ref, f32[16,1024]{1,0:T(8,128)} %maximum_select_fusion.1.vec_ref.vec), custom_call_target="tpu_custom_call" | custom-call | bytes 83886 | tf_op jit(solution)/shard_map/pallas_call | solution.py:211
  83.3 4.1 collective-permute-done.14
  87.4 10.3 %collective-permute-done.13 = bf16[2,2,64,1024]{3,2,1,0:T(8,128)(2,1)S(1)} collective-permute-done((bf16[2,2,64,1024]{3,2,1,0:T(8,128)(2,1)S(1)}, bf16[2,2,64,1024]{3,2,1,0:T(8,128)(2,1)S(1)}, u32[]{:S(2)}, u32[]{:S(2)}) %collective-permute-start.13) | collective-permute-done | bytes 524320 | tf_op jit(solution)/shard_map/ppermute | solution.py:1082
  97.8 18.2 %all-gather.5.cloned.1.call-done = bf16[2048,2048]{1,0:T(8,128)(2,1)} async-done(((bf16[64,2048]{1,0:T(8,128)(2,1)}), bf16[2048,2048]{1,0:T(8,128)(2,1)}) %all-gather.5.cloned.1.call-update) | async-done | bytes 8388624 | tf_op jit(solution)/shard_map/all_gather | solution.py:1362
  120.1 26.4 %shard_map.365 = (f32[1024,1024]{1,0:T(8,128)}, f32[1024,1024]{1,0:T(8,128)}, f32[1024,1024]{1,0:T(8,128)}, f32[1024,1024]{1,0:T(8,128)}, f32[1024,1024]{1,0:T(8,128)}, /*index=5*/bf16[1024,1024]{1,0:T(8,128)(2,1)}) custom-call(s32[5]{0:T(128)} %stack.159.co, bf16[1024,1024]{1,0:T(8,128)(2,1)} %get-tuple-element.281.mk.refs_0_, ...), custom_call_target="tpu_custom_call" | custom-call | flops 171798688 | bytes 356515 | tf_op jit(solution)/shard_map/pallas_call | solution.py:316
  147.6 12.4 %shard_map.366 = (f32[1024,1024]{1,0:T(8,128)}, bf16[1024,1024]{1,0:T(8,128)(2,1)}, bf16[1024,1024]{1,0:T(8,128)(2,1)}) custom-call(s32[5]{0:T(128)} %stack.159.co, bf16[1024,1024]{1,0:T(8,128)(2,1)} %get-tuple-element.293.gated.refs_1_, bf16[1024,1024]{1,0:T(8,128)(2,1)} %x_ref.7, f32[1024,128]{1,0:T(8,128)} %broadcast_in_dim.143.carry_ref, ...), custom_call_target="tpu_custom_call" | custom-call | flops 64424508 | bytes 146800 | tf_op jit(solution)/shard_map/pallas_call | solution.py:383
  163.5 17.5 %shard_map.367 = (bf16[1024,4096]{1,0:T(8,128)(2,1)}, bf16[1024,4096]{1,0:T(8,128)(2,1)}) custom-call(s32[5]{0:T(128)} %stack.159.co, bf16[1024,1024]{1,0:T(8,128)(2,1)} %get-tuple-element.299.mk.mixed, bf16[2,2,2,64,1024]{4,3,2,1,0:T(8,128)(2,1)} %copy-done.2, bf16[2,2,2,64,1024]{4,3,2,1,0:T(8,128)(2,1)} %collective-permute-done.15.refs_1_, ...), custom_call_target="tpu_custom_call" | custom-call | flops 96636768 | bytes 272629 | tf_op jit(solution)/shard_map/pallas_call | solution.py:437
  181.0 6.5 %all-gather.7.cloned.1.call-done = bf16[2048,1536]{1,0:T(8,128)(2,1)} async-done(((bf16[64,1536]{1,0:T(8,128)(2,1)}), bf16[2048,1536]{1,0:T(8,128)(2,1)}) %all-gather.7.cloned.1.call-update) | async-done | bytes 6291472 | tf_op jit(solution)/shard_map/all_gather | solution.py:1377
  187.5 23.6 %shard_map.368 = (bf16[2048,512]{1,0:T(8,128)(2,1)}, bf16[1024,512]{1,0:T(8,128)(2,1)}, f32[1024,1024]{1,0:T(8,128)}, bf16[1024,1024]{1,0:T(8,128)(2,1)}, bf16[1024,1024]{1,0:T(8,128)(2,1)}, /*index=5*/f32[8,1024]{1,0:T(8,128)}) custom-call(s32[5]{0:T(128)} %copy-done.40, f32[1]{0:T(128)} %bitcast.38.scale, ...), custom_call_target="tpu_custom_call" | custom-call | flops 150323856 | bytes 398458 | tf_op jit(solution)/shard_map/pallas_call | solution.py:508
  212.6 28.4 %shard_map.369 = (bf16[1024,2048]{1,0:T(8,128)(2,1)}, bf16[2,2,2,1,64,1024]{5,4,3,2,1,0:T(8,128)(2,1)}, bf16[2,2,2,1,64,1024]{5,4,3,2,1,0:T(8,128)(2,1)}, bf16[2...) custom-call(s32[5]{0:T(128)} %stack.159.co, ...), custom_call_target="tpu_custom_call" | custom-call | flops 141733920 | bytes 293601 | tf_op jit(solution)/shard_map/pallas_call | solution.py:711
  242.3 17.6 %shard_map.370 = (bf16[1024,2048]{1,0:T(8,128)(2,1)}, bf16[2,2,2,1,64,1024]{5,4,3,2,1,0:T(8,128)(2,1)}, bf16[2,2,2,1,64,1024]{5,4,3,2,1,0:T(8,128)(2,1)}, bf16[2...) custom-call(s32[5]{0:T(128)} %stack.159.co, bf16[1024,1024]{1,0:T(8,128)(2,1)} %get-tuple-element.334.dkv, ...), custom_call_target="tpu_custom_call" | custom-call | flops 141733920 | bytes 293601 | tf_op jit(solution)/shard_map/pallas_call | solution.py:711
  262.0 28.9 %shard_map.371 = (f32[1024,1024]{1,0:T(8,128)}, bf16[1024,1024]{1,0:T(8,128)(2,1)}, f32[4,8,1024]{2,1,0:T(8,128)}) custom-call(s32[5]{0:T(128)} %stack.159.co, bf16[1024,2048]{1,0:T(8,128)(2,1)} %get-tuple-element.348.dkey_a, bf16[1024,2048]{1,0:T(8,128)(2,1)} %get-tuple-element.349.dkey_b, bf16[1024,1024]{1,0:T(8,128)(2,1)} %get-tuple-element.323.refs_3_.drec, ...), custom_call_target="tpu_custom_call" | custom-call | flops 171798688 | bytes 377487 | tf_op jit(solution)/shard_map/pallas_call | solution.py:816
  291.4 1.7 collective-permute-start.31
  294.2 6.7 %shard_map.372 = (bf16[2,2,2,1,64,512]{5,4,3,2,1,0:T(8,128)(2,1)}, bf16[2,2,2,1,64,512]{5,4,3,2,1,0:T(8,128)(2,1)}, bf16[2,2,2,1,64,512]{5,4,3,2,1,0:T(8,128)(2,1)}, bf16[2,2,2,1,64,512]{5,4,3,2,1,0:T(8,128)(2,1)}) custom-call(s32[5]{0:T(128)} %stack.159.co, bf16[1024,1024]{1,0:T(8,128)(2,1)} %get-tuple-element.372.refs_0_.dtime, ...), custom_call_target="tpu_custom_call" | custom-call | flops 25769804 | bytes 62914 | tf_op jit(solution)/shard_map/pallas_call | solution.py:588
  300.9 2.6 fusion.2
  304.6 23.0 %shard_map.373 = (bf16[1024,1024]{1,0:T(8,128)(2,1)}, bf16[1024,1024]{1,0:T(8,128)(2,1)}, bf16[1024,1024]{1,0:T(8,128)(2,1)}, f32[2,8,1024]{2,1,0:T(8,128)}) custom-call(s32[5]{0:T(128)} %stack.159.co, bf16[1024,1024]{1,0:T(8,128)(2,1)} %get-tuple-element.372.refs_0_.dtime, f32[1024,1024]{1,0:T(8,128)} %get-tuple-element.373.key_ref, ...), custom_call_target="tpu_custom_call" | custom-call | flops 193273536 | bytes 356515 | tf_op jit(solution)/shard_map/pallas_call | solution.py:927
  331.2 1.6 collective-permute-start.34
  332.8 12.5 %shard_map.374 = (bf16[3,2,2,2,64,512]{5,4,3,2,1,0:T(8,128)(2,1)}, bf16[3,2,2,2,64,512]{5,4,3,2,1,0:T(8,128)(2,1)}, bf16[3,2,2,2,64,512]{5,4,3,2,1,0:T(8,128)(2,1)}, bf16[3,2,2,2,64,512]{5,4,3,2,1,0:T(8,128)(2,1)}) custom-call(s32[5]{0:T(128)} %stack.159.co, bf16[1024,1024]{1,0:T(8,128)(2,1)} %get-tuple-element.281.mk.refs_0_, ...), custom_call_target="tpu_custom_call" | custom-call | flops 77309408 | bytes 188743 | tf_op jit(solution)/shard_map/pallas_call | solution.py:588
  348.7 1.9 fusion.17
  352.1 1.7 fusion.18
  355.6 1.9 collective-permute-start.37
  358.1 15.1 %shard_map.375 = (f32[1024,1024]{1,0:T(8,128)}, f32[12,1024]{1,0:T(8,128)}, f32[8,1024]{1,0:T(8,128)}) custom-call(s32[5]{0:T(128)} %stack.159.co, bf16[1024,1024]{1,0:T(8,128)(2,1)} %get-tuple-element.427.refs_3_.dkey, bf16[1024,1024]{1,0:T(8,128)(2,1)} %get-tuple-element.428.refs_4_.dval, ...), custom_call_target="tpu_custom_call", output_to_operand_aliasing={{0}: (12, {})} | custom-call | flops 85899344 | bytes 167772 | tf_op jit(solution)/shard_map/pallas_call | solution.py:1045
  374.4 2.6 add_bitcast_fusion
  383.9 1.5 collective-permute-start.42
  385.4 15.2 %shard_map.376 = (f32[1024,1024]{1,0:T(8,128)}, f32[12,1024]{1,0:T(8,128)}, f32[8,1024]{1,0:T(8,128)}) custom-call(s32[5]{0:T(128)} %stack.159.co, bf16[1024,1024]{1,0:T(8,128)(2,1)} %get-tuple-element.427.refs_3_.dkey, bf16[1024,1024]{1,0:T(8,128)(2,1)} %get-tuple-element.428.refs_4_.dval, ...), custom_call_target="tpu_custom_call", output_to_operand_aliasing={{0}: (10, {})} | custom-call | flops 85899344 | bytes 167772 | tf_op jit(solution)/shard_map/pallas_call | solution.py:1045
  401.6 1.5 collective-permute-start.51
  403.2 1.8 fusion.5
  408.0 1.9 collective-permute-start.47
  411.2 2.0 collective-permute-done.47
  414.8 1.8 collective-permute-start.57
  420.9 3.2 collective-permute-done.57
  433.1 3.3 collective-permute-done.60
  (331 shorter events, 83.2 us)
Async XLA Ops:
  7.2 108.8 %all-gather.5.cloned.1.call-start = ((), (), s32[]{:S(2)}) async-start(), calls=%async_computation.2 | async-start | bytes 8650752 | tf_op jit(solution)/shard_map/all_gather | solution.py:1362
  8.9 178.6 %all-gather.7.cloned.1.call-start = ((), (), s32[]{:S(2)}) async-start(), calls=%async_computation.3 | async-start | bytes 6488064 | tf_op jit(solution)/shard_map/all_gather | solution.py:1377
  13.7 24.2 %collective-permute-start.3 = (f32[16,32]{1,0:T(8,128)S(1)}, f32[16,32]{1,0:T(8,128)}, u32[]{:S(2)}, u32[]{:S(2)}) collective-permute-start(f32[16,32]{1,0:T(8,128)S(1)} %concatenate.130), channel_id=1, source_target_pairs={{0,1},{1,0},{2,3},{3,2},{4,5},{5,4},{6,7},{7,6},{8,9},{9,8},{10,11... | collective-permute-start | bytes 6152 | tf_op jit(solution)/shard_map/ppermute | solution.py:1082
  19.5 28.1 %collective-permute-start.7 = (bf16[1024,512]{1,0:T(8,128)(2,1)S(1)}, bf16[1024,512]{1,0:T(8,128)(2,1)S(1)}, u32[]{:S(2)}, u32[]{:S(2)}) collective-permute-start(bf16[1024,512]{1,0:T(8,128)(2,1)S(1)} %get-tuple-element.498), channel_id=1, source_target_pairs={{0,1},{1,0},{2,3},{3,2},{4,5},{5,4},{6,7},{7,6},{8,9},{9,8},{10,11... | collective-permute-start | bytes 3145736 | tf_op jit(solution)/shard_map/ppermute | solution.py:1082
  19.5 28.0 %collective-permute-start = (bf16[64,1024]{1,0:T(8,128)(2,1)S(1)}, bf16[64,1024]{1,0:T(8,128)(2,1)S(1)}, u32[]{:S(2)}, u32[]{:S(2)}) collective-permute-start(bf16[64,1024]{1,0:T(8,128)(2,1)S(1)} %get-tuple-element.255), channel_id=1, source_target_pairs={{0,16},{16,0},{1,17},{17,1},{2,18},{18,2},{3,19},{19,3},{4,20},{20... | collective-permute-start | bytes 393224 | tf_op jit(solution)/shard_map/ppermute | solution.py:1082
  22.7 24.8 %collective-permute-start.1 = (bf16[64,1024]{1,0:T(8,128)(2,1)S(1)}, bf16[64,1024]{1,0:T(8,128)(2,1)S(1)}, u32[]{:S(2)}, u32[]{:S(2)}) collective-permute-start(bf16[64,1024]{1,0:T(8,128)(2,1)S(1)} %get-tuple-element.257), channel_id=1, source_target_pairs={{0,16},{16,0},{1,17},{17,1},{2,18},{18,2},{3,19},{19,3},{4,20},{20... | collective-permute-start | bytes 393224 | tf_op jit(solution)/shard_map/ppermute | solution.py:1082
  22.8 24.7 %collective-permute-start.2 = (bf16[64,1024]{1,0:T(8,128)(2,1)S(1)}, bf16[64,1024]{1,0:T(8,128)(2,1)}, u32[]{:S(2)}, u32[]{:S(2)}) collective-permute-start(bf16[64,1024]{1,0:T(8,128)(2,1)S(1)} %get-tuple-element.259), channel_id=1, source_target_pairs={{0,16},{16,0},{1,17},{17,1},{2,18},{18,2},{3,19},{19,3},{4,20},{20... | collective-permute-start | bytes 393224 | tf_op jit(solution)/shard_map/ppermute | solution.py:1082
  55.5 13.2 %collective-permute-start.10 = (bf16[2,64,1024]{2,1,0:T(8,128)(2,1)S(1)}, bf16[2,64,1024]{2,1,0:T(8,128)(2,1)S(1)}, u32[]{:S(2)}, u32[]{:S(2)}) collective-permute-start(bf16[2,64,1024]{2,1,0:T(8,128)(2,1)S(1)} %pad_maximum_fusion.9), channel_id=1, source_target_pairs={{0,4},{4,0},{1,5},{5,1},{2,6},{6,2},{3,7},{7,3},{8,12},{12,8},{9,1... | collective-permute-start | bytes 786440 | tf_op jit(solution)/shard_map/ppermute | solution.py:1082
  57.1 11.5 %collective-permute-start.9 = (bf16[2,64,1024]{2,1,0:T(8,128)(2,1)S(1)}, bf16[2,64,1024]{2,1,0:T(8,128)(2,1)S(1)}, u32[]{:S(2)}, u32[]{:S(2)}) collective-permute-start(bf16[2,64,1024]{2,1,0:T(8,128)(2,1)S(1)} %pad_maximum_fusion.8), channel_id=1, source_target_pairs={{0,1},{1,0},{2,3},{3,2},{4,5},{5,4},{6,7},{7,6},{8,9},{9,8},{10,11... | collective-permute-start | bytes 786440 | tf_op jit(solution)/shard_map/ppermute | solution.py:1082
  58.7 11.3 %collective-permute-start.8 = (bf16[2,64,1024]{2,1,0:T(8,128)(2,1)S(1)}, bf16[2,64,1024]{2,1,0:T(8,128)(2,1)S(1)}, u32[]{:S(2)}, u32[]{:S(2)}) collective-permute-start(bf16[2,64,1024]{2,1,0:T(8,128)(2,1)S(1)} %pad_maximum_fusion.7), channel_id=1, source_target_pairs={{0,8},{8,0},{1,9},{9,1},{2,10},{10,2},{3,11},{11,3},{4,12},{12,4},... | collective-permute-start | bytes 786440 | tf_op jit(solution)/shard_map/ppermute | solution.py:1082
  70.1 17.4 %collective-permute-start.14 = (bf16[2,2,64,1024]{3,2,1,0:T(8,128)(2,1)S(1)}, bf16[2,2,64,1024]{3,2,1,0:T(8,128)(2,1)S(1)}, u32[]{:S(2)}, u32[]{:S(2)}) collective-permute-start(bf16[2,2,64,1024]{3,2,1,0:T(8,128)(2,1)S(1)} %pad_maximum_fusion.5), channel_id=1, source_target_pairs={{0,1},{1,0},{2,3},{3,2},{4,5},{5,4},{6,7},{7,6},{8,9},{9,8},{10,11... | collective-permute-start | bytes 1572872 | tf_op jit(solution)/shard_map/ppermute | solution.py:1082
  74.0 23.8 %collective-permute-start.13 = (bf16[2,2,64,1024]{3,2,1,0:T(8,128)(2,1)S(1)}, bf16[2,2,64,1024]{3,2,1,0:T(8,128)(2,1)S(1)}, u32[]{:S(2)}, u32[]{:S(2)}) collective-permute-start(bf16[2,2,64,1024]{3,2,1,0:T(8,128)(2,1)S(1)} %pad_maximum_fusion.4), channel_id=1, source_target_pairs={{0,8},{8,0},{1,9},{9,1},{2,10},{10,2},{3,11},{11,3},{4,12},{12,4},... | collective-permute-start | bytes 1572872 | tf_op jit(solution)/shard_map/ppermute | solution.py:1082
  75.4 22.4 %collective-permute-start.12 = (bf16[2,2,64,1024]{3,2,1,0:T(8,128)(2,1)S(1)}, bf16[2,2,64,1024]{3,2,1,0:T(8,128)(2,1)S(1)}, u32[]{:S(2)}, u32[]{:S(2)}) collective-permute-start(bf16[2,2,64,1024]{3,2,1,0:T(8,128)(2,1)S(1)} %pad_maximum_fusion.3), channel_id=1, source_target_pairs={{0,4},{4,0},{1,5},{5,1},{2,6},{6,2},{3,7},{7,3},{8,12},{12,8},{9,1... | collective-permute-start | bytes 1572872 | tf_op jit(solution)/shard_map/ppermute | solution.py:1082
  116.0 297.3 %reduce-scatter.2.cloned.1.call-start = ((), (), s32[]{:S(2)}) async-start(), calls=%async_computation.1 | async-start | bytes 11141120 | tf_op jit(solution)/shard_map/reduce_scatter | solution.py:1224
  116.1 30.4 %collective-permute-start.16 = (bf16[2,2,2,64,1024]{4,3,2,1,0:T(8,128)(2,1)S(1)}, bf16[2,2,2,64,1024]{4,3,2,1,0:T(8,128)(2,1)}, u32[]{:S(2)}, u32[]{:S(2)}) collective-permute-start(bf16[2,2,2,64,1024]{4,3,2,1,0:T(8,128)(2,1)S(1)} %pad_maximum_fusion.1.refs_4_), channel_id=1, source_target_pairs={{0,4},{4,0},{1,5},{5,1},{2,6},{6,2},{3,7},{7,3},{8,12},{12,8},{9,1... | collective-permute-start | bytes 3145736 | tf_op jit(solution)/shard_map/ppermute | solution.py:1082
  117.7 28.9 %collective-permute-start.15 = (bf16[2,2,2,64,1024]{4,3,2,1,0:T(8,128)(2,1)S(1)}, bf16[2,2,2,64,1024]{4,3,2,1,0:T(8,128)(2,1)}, u32[]{:S(2)}, u32[]{:S(2)}) collective-permute-start(bf16[2,2,2,64,1024]{4,3,2,1,0:T(8,128)(2,1)S(1)} %pad_maximum_fusion.refs_0_), channel_id=1, source_target_pairs={{0,1},{1,0},{2,3},{3,2},{4,5},{5,4},{6,7},{7,6},{8,9},{9,8},{10,11... | collective-permute-start | bytes 3145736 | tf_op jit(solution)/shard_map/ppermute | solution.py:1082
  119.9 40.1 %collective-permute-start.21 = (bf16[2,2,2,64,1024]{4,3,2,1,0:T(8,128)(2,1)S(1)}, bf16[2,2,2,64,1024]{4,3,2,1,0:T(8,128)(2,1)}, u32[]{:S(2)}, u32[]{:S(2)}) collective-permute-start(bf16[2,2,2,64,1024]{4,3,2,1,0:T(8,128)(2,1)S(1)} %pad_maximum_fusion.2.refs_1_.refs_0_), channel_id=1, source_target_pairs={{0,8},{8,0},{1,9},{9,1},{2,10},{10,2},{3,11},{11,3},{4,12},{12,4},... | collective-permute-start | bytes 3145736 | tf_op jit(solution)/shard_map/ppermute | solution.py:1082
  146.6 13.5 %collective-permute-start.17 = (bf16[2,2,2,64,1024]{4,3,2,1,0:T(8,128)(2,1)S(1)}, bf16[2,2,2,64,1024]{4,3,2,1,0:T(8,128)(2,1)S(1)}, u32[]{:S(2)}, u32[]{:S(2)}) collective-permute-start(bf16[2,2,2,64,1024]{4,3,2,1,0:T(8,128)(2,1)S(1)} %pad_maximum_fusion.refs_0_), channel_id=1, source_target_pairs={{0,2},{2,0},{1,3},{3,1},{4,6},{6,4},{5,7},{7,5},{8,10},{10,8},{9,1... | collective-permute-start | bytes 3145736 | tf_op jit(solution)/shard_map/ppermute | solution.py:1082
  146.7 13.4 %collective-permute-start.18 = (bf16[2,2,2,64,1024]{4,3,2,1,0:T(8,128)(2,1)}, bf16[2,2,2,64,1024]{4,3,2,1,0:T(8,128)(2,1)S(1)}, u32[]{:S(2)}, u32[]{:S(2)}) collective-permute-start(bf16[2,2,2,64,1024]{4,3,2,1,0:T(8,128)(2,1)} %collective-permute-done.15.refs_1_), channel_id=1, source_target_pairs={{0,2},{2,0},{1,3},{3,1},{4,6},{6,4},{5,7},{7,5},{8,10},{10,8},{9,1... | collective-permute-start | bytes 3145736 | tf_op jit(solution)/shard_map/ppermute | solution.py:1082
  147.1 13.0 %collective-permute-start.19 = (bf16[2,2,2,64,1024]{4,3,2,1,0:T(8,128)(2,1)S(1)}, bf16[2,2,2,64,1024]{4,3,2,1,0:T(8,128)(2,1)}, u32[]{:S(2)}, u32[]{:S(2)}) collective-permute-start(bf16[2,2,2,64,1024]{4,3,2,1,0:T(8,128)(2,1)S(1)} %pad_maximum_fusion.1.refs_4_), channel_id=1, source_target_pairs={{0,2},{2,0},{1,3},{3,1},{4,6},{6,4},{5,7},{7,5},{8,10},{10,8},{9,1... | collective-permute-start | bytes 3145736 | tf_op jit(solution)/shard_map/ppermute | solution.py:1082
  147.2 12.9 %collective-permute-start.20 = (bf16[2,2,2,64,1024]{4,3,2,1,0:T(8,128)(2,1)}, bf16[2,2,2,64,1024]{4,3,2,1,0:T(8,128)(2,1)}, u32[]{:S(2)}, u32[]{:S(2)}) collective-permute-start(bf16[2,2,2,64,1024]{4,3,2,1,0:T(8,128)(2,1)} %collective-permute-done.16.refs_5_), channel_id=1, source_target_pairs={{0,2},{2,0},{1,3},{3,1},{4,6},{6,4},{5,7},{7,5},{8,10},{10,8},{9,1... | collective-permute-start | bytes 3145736 | tf_op jit(solution)/shard_map/ppermute | solution.py:1082
  160.1 20.9 %collective-permute-start.22 = (bf16[2,2,2,64,1024]{4,3,2,1,0:T(8,128)(2,1)S(1)}, bf16[2,2,2,64,1024]{4,3,2,1,0:T(8,128)(2,1)S(1)}, u32[]{:S(2)}, u32[]{:S(2)}) collective-permute-start(bf16[2,2,2,64,1024]{4,3,2,1,0:T(8,128)(2,1)S(1)} %pad_maximum_fusion.2.refs_1_.refs_0_), channel_id=1, source_target_pairs={{0,2},{2,0},{1,3},{3,1},{4,6},{6,4},{5,7},{7,5},{8,10},{10,8},{9,1... | collective-permute-start | bytes 3145736 | tf_op jit(solution)/shard_map/ppermute | solution.py:1082
  161.0 20.0 %collective-permute-start.23 = (bf16[2,2,2,64,1024]{4,3,2,1,0:T(8,128)(2,1)}, bf16[2,2,2,64,1024]{4,3,2,1,0:T(8,128)(2,1)S(1)}, u32[]{:S(2)}, u32[]{:S(2)}) collective-permute-start(bf16[2,2,2,64,1024]{4,3,2,1,0:T(8,128)(2,1)} %collective-permute-done.21.refs_2_.refs_1_), channel_id=1, source_target_pairs={{0,2},{2,0},{1,3},{3,1},{4,6},{6,4},{5,7},{7,5},{8,10},{10,8},{9,1... | collective-permute-start | bytes 3145736 | tf_op jit(solution)/shard_map/ppermute | solution.py:1082
  211.2 29.9 %collective-permute-start.24 = (bf16[1024,512]{1,0:T(8,128)(2,1)}, bf16[1024,512]{1,0:T(8,128)(2,1)S(1)}, u32[]{:S(2)}, u32[]{:S(2)}) collective-permute-start(bf16[1024,512]{1,0:T(8,128)(2,1)} %get-tuple-element.328), channel_id=1, source_target_pairs={{0,1},{1,0},{2,3},{3,2},{4,5},{5,4},{6,7},{7,6},{8,9},{9,8},{10,11... | collective-permute-start | bytes 3145736 | tf_op jit(solution)/shard_map/ppermute | solution.py:1082
  241.1 18.8 %collective-permute-start.25 = (bf16[2,2,2,1,64,1024]{5,4,2,1,3,0:T(8,128)(2,1)}, bf16[2,2,2,1,64,1024]{5,4,2,1,3,0:T(8,128)(2,1)S(1)}, u32[]{:S(2)}, u32[]{:S(2)}) collective-permute-start(bf16[2,2,2,1,64,1024]{5,4,2,1,3,0:T(8,128)(2,1)} %bitcast.319), channel_id=1, source_target_pairs={{0,2},{2,0},{1,3},{3,1},{4,6},{6,4},{5,7},{7,5},{8,10},{10,8},{9,1... | collective-permute-start | bytes 3145736 | tf_op jit(solution)/shard_map/ppermute | solution.py:1082
  242.3 17.6 %collective-permute-start.26 = (bf16[2,2,2,1,64,1024]{5,4,2,1,3,0:T(8,128)(2,1)S(1)}, bf16[2,2,2,1,64,1024]{5,4,2,1,3,0:T(8,128)(2,1)S(1)}, u32[]{:S(2)}, u32[]{:S(2)}) collective-permute-start(bf16[2,2,2,1,64,1024]{5,4,2,1,3,0:T(8,128)(2,1)S(1)} %bitcast.318), channel_id=1, source_target_pairs={{0,2},{2,0},{1,3},{3,1},{4,6},{6,4},{5,7},{7,5},{8,10},{10,8},{9,1... | collective-permute-start | bytes 3145736 | tf_op jit(solution)/shard_map/ppermute | solution.py:1082
  261.1 29.9 %collective-permute-start.27 = (bf16[2,2,2,1,64,1024]{5,4,2,1,3,0:T(8,128)(2,1)S(1)}, bf16[2,2,2,1,64,1024]{5,4,2,1,3,0:T(8,128)(2,1)}, u32[]{:S(2)}, u32[]{:S(2)}) collective-permute-start(bf16[2,2,2,1,64,1024]{5,4,2,1,3,0:T(8,128)(2,1)S(1)} %bitcast_add_fusion.1), channel_id=1, source_target_pairs={{0,1},{1,0},{2,3},{3,2},{4,5},{5,4},{6,7},{7,6},{8,9},{9,8},{10,11... | collective-permute-start | bytes 3145736 | tf_op jit(solution)/shard_map/ppermute | solution.py:1082
  261.5 29.5 %collective-permute-start.28 = (bf16[2,2,2,1,64,1024]{5,4,3,2,1,0:T(8,128)(2,1)}, bf16[2,2,2,1,64,1024]{5,4,3,2,1,0:T(8,128)(2,1)S(1)}, u32[]{:S(2)}, u32[]{:S(2)}) collective-permute-start(bf16[2,2,2,1,64,1024]{5,4,3,2,1,0:T(8,128)(2,1)} %get-tuple-element.346), channel_id=1, source_target_pairs={{0,2},{2,0},{1,3},{3,1},{4,6},{6,4},{5,7},{7,5},{8,10},{10,8},{9,1... | collective-permute-start | bytes 3145736 | tf_op jit(solution)/shard_map/ppermute | solution.py:1082
  261.6 29.3 %collective-permute-start.29 = (bf16[2,2,2,1,64,1024]{5,4,2,1,3,0:T(8,128)(2,1)}, bf16[2,2,2,1,64,1024]{5,4,2,1,3,0:T(8,128)(2,1)S(1)}, u32[]{:S(2)}, u32[]{:S(2)}) collective-permute-start(bf16[2,2,2,1,64,1024]{5,4,2,1,3,0:T(8,128)(2,1)} %bitcast.58), channel_id=1, source_target_pairs={{0,2},{2,0},{1,3},{3,1},{4,6},{6,4},{5,7},{7,5},{8,10},{10,8},{9,1... | collective-permute-start | bytes 3145736 | tf_op jit(solution)/shard_map/ppermute | solution.py:1082
  291.4 36.2 %collective-permute-start.31 = (bf16[2,2,2,1,64,1024]{5,4,3,2,1,0:T(8,128)(2,1)S(1)}, bf16[2,2,2,1,64,1024]{5,4,3,2,1,0:T(8,128)(2,1)}, u32[]{:S(2)}, u32[]{:S(2)}) collective-permute-start(bf16[2,2,2,1,64,1024]{5,4,3,2,1,0:T(8,128)(2,1)S(1)} %add.495), channel_id=1, source_target_pairs={{0,1},{1,0},{2,3},{3,2},{4,5},{5,4},{6,7},{7,6},{8,9},{9,8},{10,11... | collective-permute-start | bytes 3145736 | tf_op jit(solution)/shard_map/ppermute | solution.py:1082
  303.6 24.0 %collective-permute-start.30 = (bf16[2,2,1,64,1024]{4,3,1,2,0:T(8,128)(2,1)}, bf16[2,2,1,64,1024]{4,3,1,2,0:T(8,128)(2,1)S(1)}, u32[]{:S(2)}, u32[]{:S(2)}) collective-permute-start(bf16[2,2,1,64,1024]{4,3,1,2,0:T(8,128)(2,1)} %get-tuple-element.496), channel_id=1, source_target_pairs={{0,4},{4,0},{1,5},{5,1},{2,6},{6,2},{3,7},{7,3},{8,12},{12,8},{9,1... | collective-permute-start | bytes 1572872 | tf_op jit(solution)/shard_map/ppermute | solution.py:1082
  304.1 23.5 %collective-permute-start.32 = (bf16[2,2,2,1,64,512]{5,4,3,2,1,0:T(8,128)(2,1)}, bf16[2,2,2,1,64,512]{5,4,3,2,1,0:T(8,128)(2,1)S(1)}, u32[]{:S(2)}, u32[]{:S(2)}) collective-permute-start(bf16[2,2,2,1,64,512]{5,4,3,2,1,0:T(8,128)(2,1)} %get-tuple-element.370), channel_id=1, source_target_pairs={{0,2},{2,0},{1,3},{3,1},{4,6},{6,4},{5,7},{7,5},{8,10},{10,8},{9,1... | collective-permute-start | bytes 1572872 | tf_op jit(solution)/shard_map/ppermute | solution.py:1082
  304.1 23.5 %collective-permute-start.33 = (bf16[2,2,2,1,64,512]{5,4,2,1,3,0:T(8,128)(2,1)}, bf16[2,2,2,1,64,512]{5,4,2,1,3,0:T(8,128)(2,1)S(1)}, u32[]{:S(2)}, u32[]{:S(2)}) collective-permute-start(bf16[2,2,2,1,64,512]{5,4,2,1,3,0:T(8,128)(2,1)} %bitcast.63), channel_id=1, source_target_pairs={{0,2},{2,0},{1,3},{3,1},{4,6},{6,4},{5,7},{7,5},{8,10},{10,8},{9,1... | collective-permute-start | bytes 1572872 | tf_op jit(solution)/shard_map/ppermute | solution.py:1082
  327.8 18.8 %collective-permute-start.36 = (bf16[2,2,2,1,64,512]{5,4,3,2,1,0:T(8,128)(2,1)S(1)}, bf16[2,2,2,1,64,512]{5,4,3,2,1,0:T(8,128)(2,1)S(1)}, u32[]{:S(2)}, u32[]{:S(2)}) collective-permute-start(bf16[2,2,2,1,64,512]{5,4,3,2,1,0:T(8,128)(2,1)S(1)} %add.502), channel_id=1, source_target_pairs={{0,1},{1,0},{2,3},{3,2},{4,5},{5,4},{6,7},{7,6},{8,9},{9,8},{10,11... | collective-permute-start | bytes 1572872 | tf_op jit(solution)/shard_map/ppermute | solution.py:1082
  330.4 16.3 %collective-permute-start.35 = (bf16[2,2,1,64,1024]{4,3,1,0,2:T(8,128)(2,1)S(1)}, bf16[2,2,1,64,1024]{4,3,1,0,2:T(8,128)(2,1)}, u32[]{:S(2)}, u32[]{:S(2)}) collective-permute-start(bf16[2,2,1,64,1024]{4,3,1,0,2:T(8,128)(2,1)S(1)} %fusion.4), channel_id=1, source_target_pairs={{0,4},{4,0},{1,5},{5,1},{2,6},{6,2},{3,7},{7,3},{8,12},{12,8},{9,1... | collective-permute-start | bytes 1572872 | tf_op jit(solution)/shard_map/ppermute | solution.py:1082
  331.2 15.4 %collective-permute-start.34 = (bf16[2,1,64,1024]{3,2,1,0:T(8,128)(2,1)S(1)}, bf16[2,1,64,1024]{3,2,1,0:T(8,128)(2,1)S(1)}, u32[]{:S(2)}, u32[]{:S(2)}) collective-permute-start(bf16[2,1,64,1024]{3,2,1,0:T(8,128)(2,1)S(1)} %get-tuple-element.500), channel_id=1, source_target_pairs={{0,8},{8,0},{1,9},{9,1},{2,10},{10,2},{3,11},{11,3},{4,12},{12,4},... | collective-permute-start | bytes 786440 | tf_op jit(solution)/shard_map/ppermute | solution.py:1082
  347.5 26.8 %collective-permute-start.40 = (bf16[3,2,2,2,64,512]{5,4,3,2,1,0:T(8,128)(2,1)}, bf16[3,2,2,2,64,512]{5,4,3,2,1,0:T(8,128)(2,1)}, u32[]{:S(2)}, u32[]{:S(2)}) collective-permute-start(bf16[3,2,2,2,64,512]{5,4,3,2,1,0:T(8,128)(2,1)} %get-tuple-element.408), channel_id=1, source_target_pairs={{0,2},{2,0},{1,3},{3,1},{4,6},{6,4},{5,7},{7,5},{8,10},{10,8},{9,1... | collective-permute-start | bytes 4718600 | tf_op jit(solution)/shard_map/ppermute | solution.py:1082
  347.5 26.8 %collective-permute-start.41 = (bf16[3,2,2,2,64,512]{5,4,3,2,1,0:T(8,128)(2,1)}, bf16[3,2,2,2,64,512]{5,4,3,2,1,0:T(8,128)(2,1)S(1)}, u32[]{:S(2)}, u32[]{:S(2)}) collective-permute-start(bf16[3,2,2,2,64,512]{5,4,3,2,1,0:T(8,128)(2,1)} %get-tuple-element.409), channel_id=1, source_target_pairs={{0,2},{2,0},{1,3},{3,1},{4,6},{6,4},{5,7},{7,5},{8,10},{10,8},{9,1... | collective-permute-start | bytes 4718600 | tf_op jit(solution)/shard_map/ppermute | solution.py:1082
  350.6 23.6 %collective-permute-start.39 = (bf16[2,2,1,64,512]{4,3,1,0,2:T(8,128)(2,1)}, bf16[2,2,1,64,512]{4,3,1,0,2:T(8,128)(2,1)S(1)}, u32[]{:S(2)}, u32[]{:S(2)}) collective-permute-start(bf16[2,2,1,64,512]{4,3,1,0,2:T(8,128)(2,1)} %fusion.17), channel_id=1, source_target_pairs={{0,4},{4,0},{1,5},{5,1},{2,6},{6,2},{3,7},{7,3},{8,12},{12,8},{9,1... | collective-permute-start | bytes 786440 | tf_op jit(solution)/shard_map/ppermute | solution.py:1082
  353.8 20.5 %collective-permute-start.38 = (bf16[2,1,64,1024]{3,2,0,1:T(8,128)(2,1)}, bf16[2,1,64,1024]{3,2,0,1:T(8,128)(2,1)S(1)}, u32[]{:S(2)}, u32[]{:S(2)}) collective-permute-start(bf16[2,1,64,1024]{3,2,0,1:T(8,128)(2,1)} %fusion.18), channel_id=1, source_target_pairs={{0,8},{8,0},{1,9},{9,1},{2,10},{10,2},{3,11},{11,3},{4,12},{12,4},... | collective-permute-start | bytes 786440 | tf_op jit(solution)/shard_map/ppermute | solution.py:1082
  355.6 18.7 %collective-permute-start.37 = (bf16[1,64,1024]{2,1,0:T(8,128)(2,1)S(1)}, bf16[1,64,1024]{2,1,0:T(8,128)(2,1)S(1)}, u32[]{:S(2)}, u32[]{:S(2)}) collective-permute-start(bf16[1,64,1024]{2,1,0:T(8,128)(2,1)S(1)} %get-tuple-element.510), channel_id=1, source_target_pairs={{0,16},{16,0},{1,17},{17,1},{2,18},{18,2},{3,19},{19,3},{4,20},{20... | collective-permute-start | bytes 393224 | tf_op jit(solution)/shard_map/ppermute | solution.py:1082
  377.0 24.6 %collective-permute-start.44 = (bf16[2,2,2,64,512]{4,3,2,1,0:T(8,128)(2,1)}, bf16[2,2,2,64,512]{4,3,2,1,0:T(8,128)(2,1)S(1)}, u32[]{:S(2)}, u32[]{:S(2)}) collective-permute-start(bf16[2,2,2,64,512]{4,3,2,1,0:T(8,128)(2,1)} %get-tuple-element.495), channel_id=1, source_target_pairs={{0,4},{4,0},{1,5},{5,1},{2,6},{6,2},{3,7},{7,3},{8,12},{12,8},{9,1... | collective-permute-start | bytes 1572872 | tf_op jit(solution)/shard_map/ppermute | solution.py:1082
  377.7 23.9 %collective-permute-start.45 = (bf16[2,2,2,64,512]{4,3,2,1,0:T(8,128)(2,1)}, bf16[2,2,2,64,512]{4,3,2,1,0:T(8,128)(2,1)S(1)}, u32[]{:S(2)}, u32[]{:S(2)}) collective-permute-start(bf16[2,2,2,64,512]{4,3,2,1,0:T(8,128)(2,1)} %get-tuple-element.494), channel_id=1, source_target_pairs={{0,1},{1,0},{2,3},{3,2},{4,5},{5,4},{6,7},{7,6},{8,9},{9,8},{10,11... | collective-permute-start | bytes 1572872 | tf_op jit(solution)/shard_map/ppermute | solution.py:1082
  379.0 22.6 %collective-permute-start.46 = (bf16[2,2,2,64,512]{4,3,2,1,0:T(8,128)(2,1)S(1)}, bf16[2,2,2,64,512]{4,3,2,1,0:T(8,128)(2,1)}, u32[]{:S(2)}, u32[]{:S(2)}) collective-permute-start(bf16[2,2,2,64,512]{4,3,2,1,0:T(8,128)(2,1)S(1)} %get-tuple-element.493), channel_id=1, source_target_pairs={{0,8},{8,0},{1,9},{9,1},{2,10},{10,2},{3,11},{11,3},{4,12},{12,4},... | collective-permute-start | bytes 1572872 | tf_op jit(solution)/shard_map/ppermute | solution.py:1082
  380.9 20.7 %collective-permute-start.43 = (bf16[2,1,64,512]{3,2,0,1:T(8,128)(2,1)S(1)}, bf16[2,1,64,512]{3,2,0,1:T(8,128)(2,1)S(1)}, u32[]{:S(2)}, u32[]{:S(2)}) collective-permute-start(bf16[2,1,64,512]{3,2,0,1:T(8,128)(2,1)S(1)} %fusion.32), channel_id=1, source_target_pairs={{0,8},{8,0},{1,9},{9,1},{2,10},{10,2},{3,11},{11,3},{4,12},{12,4},... | collective-permute-start | bytes 393224 | tf_op jit(solution)/shard_map/ppermute | solution.py:1082
  383.9 17.7 %collective-permute-start.42 = (bf16[1,64,1024]{2,1,0:T(8,128)(2,1)S(1)}, bf16[1,64,1024]{2,1,0:T(8,128)(2,1)}, u32[]{:S(2)}, u32[]{:S(2)}) collective-permute-start(bf16[1,64,1024]{2,1,0:T(8,128)(2,1)S(1)} %fusion.31), channel_id=1, source_target_pairs={{0,16},{16,0},{1,17},{17,1},{2,18},{18,2},{3,19},{19,3},{4,20},{20... | collective-permute-start | bytes 393224 | tf_op jit(solution)/shard_map/ppermute | solution.py:1082
  414.8 9.3 %collective-permute-start.57 = (bf16[64,2560]{1,0:T(8,128)(2,1)S(1)}, bf16[64,2560]{1,0:T(8,128)(2,1)S(1)}, u32[]{:S(2)}, u32[]{:S(2)}) collective-permute-start(bf16[64,2560]{1,0:T(8,128)(2,1)S(1)} %dynamic-slice_bitcast_fusion), channel_id=1, source_target_pairs={{0,1},{1,0},{2,3},{3,2},{4,5},{5,4},{6,7},{7,6},{8,9},{9,8},{10,11... | collective-permute-start | bytes 983048 | tf_op jit(solution)/shard_map/ppermute | solution.py:1082
  427.1 9.3 %collective-permute-start.58 = (bf16[3,64,512]{2,1,0:T(8,128)(2,1)S(1)}, bf16[3,64,512]{2,1,0:T(8,128)(2,1)S(1)}, u32[]{:S(2)}, u32[]{:S(2)}) collective-permute-start(bf16[3,64,512]{2,1,0:T(8,128)(2,1)S(1)} %pad_maximum_fusion.12), channel_id=1, source_target_pairs={{0,16},{16,0},{1,17},{17,1},{2,18},{18,2},{3,19},{19,3},{4,20},{20... | collective-permute-start | bytes 589832 | tf_op jit(solution)/shard_map/ppermute | solution.py:1082
  (58 other events, 516.2 us)
Sparse Core Ops, SparseCore 0:
  11.0 104.8 all-gather.4
  118.8 68.6 all-gather.6
  241.2 129.9 reduce-scatter.1
